TPU v7x, 32 devices: a whole 2x2x4 slice. The times are simulated.
32 devices in a mesh: grp: 2 (over y), gx: 8 (over z, x), gy: 2 (over core).
Axes of the slice: x: 2, y: 2, z: 4, core: 2. Of those that a mesh axis runs over, the one named last changes fastest.
Arguments:
- density: float32 [32, 128, 256], P('gx', ('grp', 'gy')), may hold values from 1 to 2
- momentum: float32 [3, 32, 128, 256], P(None, 'gx', ('grp', 'gy')), may hold values from -0.5 to 0.5
- energy: float32 [32, 128, 256], P('gx', ('grp', 'gy')), may hold values from 3 to 6
- displacement: float32 [3, 72, 68, 512], P(None, 'gx', ('grp', 'gy')), as said below
- velocity_field: float32 [3, 72, 68, 512], P(None, 'gx', ('grp', 'gy')), as said below
- acceleration: float32 [3, 72, 68, 512], P(None, 'gx', ('grp', 'gy')), as said below
- material: float32 [3, 8], replicated, may hold values from 1 to 4
- element_region_index: int32 [16, 16, 128], P('gx', ('grp', 'gy')), may hold values from 0 to 7
- face_dest: int32 [32, 128, 1], P(('grp', 'gx', 'gy')), may hold values from 0 to 31; in each aligned block of 128 rows (0 to 127, 128 to 255, ..., all dimensions but the last counted through in order) at most 8 rows name the same one
- face_slot: int32 [32, 128], P(('grp', 'gx', 'gy')), may hold values from 0 to 152
Outputs:
- hydro_final: float32 [5, 32, 128, 256], P(None, 'gx', ('grp', 'gy'))
- displacement_out: float32 [3, 72, 68, 512], P(None, 'gx', ('grp', 'gy'))
- velocity_out: float32 [3, 72, 68, 512], P(None, 'gx', ('grp', 'gy'))
- acceleration_out: float32 [3, 72, 68, 512], P(None, 'gx', ('grp', 'gy'))
Inputs may be any that keep to these rules, and one draw needn't show every extreme that they name: `face_dest`: among the 128 rows of one device no owner is named more than 8 times; some owner is named exactly 8 times by some device. `displacement`: copies of one node held by neighbouring blocks are equal. `velocity_field`: copies of one node held by neighbouring blocks are equal. `acceleration`: copies of one node held by neighbouring blocks are equal.
All inputs are finite; a program needn't handle non-finite values.
Results may differ from a plain program's by a relative error of at most 0.0003.
Values sent between devices are 32-bit elements; how exact they have to be, the bound alone decides.
No kernel may reach another device: no remote copies, remote signals or barrier semaphores. Data moves between devices by JAX's collectives and lax.ppermute only.
A program may use at most 128 MiB of HBM per device.

v0:
```python
import jax
import jax.numpy as jnp
import numpy as np
from jax import lax
from jax.sharding import PartitionSpec as P

gamma_gas = 1.4
cell_ratio = 0.05
half_size = 2.0
time_step = 0.1
face_area = 2.0


def extended_2(array, sides, width):
    for axis, dim in sides:
        count, length = (lax.axis_size(axis), array.shape[dim])
        up = [(i, (i + 1) % count) for i in range(count - 1)]
        down = [(j, i) for i, j in up]
        last = lax.slice_in_dim(array, length - width, length, axis=dim)
        first = lax.slice_in_dim(array, 0, width, axis=dim)
        before = lax.ppermute(last, axis, up)
        after = lax.ppermute(first, axis, down)
        array = jnp.concatenate([before, array, after], axis=dim)
    return array


def gll_tables():
    gll_root = np.sqrt(3.0 / 7.0)
    points = np.array([-1.0, -gll_root, 0.0, gll_root, 1.0])
    weights = np.array([0.1, 49.0 / 90.0, 32.0 / 45.0, 49.0 / 90.0, 0.1])
    products = np.array(
        [
            np.prod(
                [points[row_num] - points[col_num] for col_num in range(5) if col_num != row_num]
            )
            for row_num in range(5)
        ]
    )
    derivative = np.zeros((5, 5))
    for row_num in range(5):
        for col_num in range(5):
            if row_num != col_num:
                derivative[row_num, col_num] = (
                    products[row_num] / products[col_num] / (points[row_num] - points[col_num])
                )
        derivative[row_num, row_num] = sum(
            (
                1.0 / (points[row_num] - points[col_num])
                for col_num in range(5)
                if col_num != row_num
            )
        )
    return (jnp.asarray(derivative, dtype=jnp.float32), jnp.asarray(weights, dtype=jnp.float32))


def pressure_of(hydro_state):
    velocity = hydro_state[1:4] / hydro_state[0]
    pressure = (gamma_gas - 1.0) * (
        hydro_state[4] - 0.5 * jnp.sum(hydro_state[1:4] * velocity, axis=0)
    )
    return (velocity, pressure)


def euler_flux(hydro_state, axis_num):
    velocity, pressure = pressure_of(hydro_state)
    sound_speed = jnp.sqrt(gamma_gas * pressure / hydro_state[0])
    normal_vel = velocity[axis_num]
    unit_row = jnp.eye(3, dtype=jnp.float32)[axis_num].reshape(3, 1, 1, 1)
    momentum_flux = hydro_state[1:4] * normal_vel + pressure * unit_row
    energy_flux = (hydro_state[4] + pressure) * normal_vel
    flux_all = jnp.concatenate(
        [hydro_state[1 + axis_num][None], momentum_flux, energy_flux[None]], axis=0
    )
    return (flux_all, jnp.abs(normal_vel) + sound_speed)


def advance(padded):
    interior = padded[:, 1:-1, 1:-1, 1:-1]
    change = jnp.zeros_like(interior)
    for axis_num in range(3):
        pencil = padded
        for other_axis in range(3):
            if other_axis != axis_num:
                pencil = lax.slice_in_dim(
                    pencil, 1, pencil.shape[other_axis + 1] - 1, axis=other_axis + 1
                )
        flux_all, wave_speed = euler_flux(pencil, axis_num)
        length = pencil.shape[axis_num + 1]
        low_state = lax.slice_in_dim(pencil, 0, length - 1, axis=axis_num + 1)
        high_state = lax.slice_in_dim(pencil, 1, length, axis=axis_num + 1)
        low_flux = lax.slice_in_dim(flux_all, 0, length - 1, axis=axis_num + 1)
        high_flux = lax.slice_in_dim(flux_all, 1, length, axis=axis_num + 1)
        fastest = jnp.maximum(
            lax.slice_in_dim(wave_speed, 0, length - 1, axis=axis_num),
            lax.slice_in_dim(wave_speed, 1, length, axis=axis_num),
        )
        face_flux = 0.5 * (low_flux + high_flux) - 0.5 * fastest * (high_state - low_state)
        change = (
            change
            + lax.slice_in_dim(face_flux, 1, length - 1, axis=axis_num + 1)
            - lax.slice_in_dim(face_flux, 0, length - 2, axis=axis_num + 1)
        )
    return interior - cell_ratio * change


def surface_traction(hydro_state):
    bottom = hydro_state[:, :, :, -1]
    velocity, pressure = pressure_of(bottom[:, :, :, None])
    vertical = velocity[2, :, :, 0]
    return (
        jnp.stack(
            [bottom[1] * vertical, bottom[2] * vertical, bottom[3] * vertical + pressure[:, :, 0]]
        )
        * face_area
    )


def split_points(field, axis_num, elements):
    return jnp.stack(
        [
            lax.slice_in_dim(field, offset, offset + 4 * elements - 3, stride=4, axis=axis_num)
            for offset in range(5)
        ],
        axis=1,
    )


def depth_points(nodes):
    leading = nodes.shape[:3]
    elements = nodes.shape[3] // 4
    blocks = jnp.moveaxis(nodes.reshape(leading + (elements, 4)), 4, 1)
    fifth = jnp.concatenate(
        [blocks[:, 0, :, :, 1:], jnp.zeros(leading + (1,), nodes.dtype)], axis=3
    )
    return jnp.concatenate([blocks, fifth[:, None]], axis=1)


def scatter_to_elements(nodes, count_x, count_y):
    along_z = depth_points(nodes)
    along_y = split_points(along_z, 3, count_y)
    return split_points(along_y, 3, count_x)


def fold_points(values, elem_axis):
    pieces = [values[:, offset] for offset in range(5)]
    axis_num = elem_axis - 1
    widths = [(0, 0)] * pieces[0].ndim
    pad_after = list(widths)
    pad_after[axis_num] = (0, 1)
    pad_before = list(widths)
    pad_before[axis_num] = (1, 0)
    head_part = jnp.pad(pieces[0], pad_after) + jnp.pad(pieces[4], pad_before)
    stacked = jnp.stack(
        [head_part] + [jnp.pad(portion, pad_after) for portion in pieces[1:4]], axis=axis_num + 1
    )
    new_shape = (
        stacked.shape[:axis_num] + (stacked.shape[axis_num] * 4,) + stacked.shape[axis_num + 2 :]
    )
    merged = stacked.reshape(new_shape)
    return lax.slice_in_dim(merged, 0, merged.shape[axis_num] - 3, axis=axis_num)


def depth_fold(values):
    leading = values.shape[:1] + values.shape[2:4]
    elements = values.shape[4]
    shifted = jnp.concatenate(
        [jnp.zeros(leading + (1,), values.dtype), values[:, 4, :, :, :-1]], axis=3
    )
    head_part = values[:, 0] + shifted
    stacked = jnp.stack([head_part, values[:, 1], values[:, 2], values[:, 3]], axis=-1)
    return stacked.reshape(leading + (elements * 4,))


def gather_to_nodes(values):
    return depth_fold(fold_points(fold_points(values, 4), 4))


def cell_weight(weights):
    cube = weights[:, None, None] * weights[None, :, None] * weights[None, None, :] * half_size**3
    return cube[:, :, :, None, None, None]


def material_fields(material, element_region_index):
    regions = jnp.arange(material.shape[1], dtype=jnp.int32)
    onehot = (element_region_index[None] == regions[:, None, None, None]).astype(jnp.float32)
    return [
        jnp.sum(onehot * material[material_row][:, None, None, None], axis=0)
        for material_row in range(3)
    ]


def forces_per_element(elem_disp, first_lame_modulus, shear_lame_modulus):
    derivative, weights = gll_tables()
    inv_half = 1.0 / half_size
    highest = lax.Precision.HIGHEST
    gradients = [
        inv_half * jnp.einsum("ap,cpjkxyz->cajkxyz", derivative, elem_disp, precision=highest),
        inv_half * jnp.einsum("ap,cipkxyz->ciakxyz", derivative, elem_disp, precision=highest),
        inv_half * jnp.einsum("ap,cijpxyz->cijaxyz", derivative, elem_disp, precision=highest),
    ]
    dilation = gradients[0][0] + gradients[1][1] + gradients[2][2]
    weighting = cell_weight(weights)
    forces = []
    for component in range(3):
        stress_row = [
            shear_lame_modulus * (gradients[direction][component] + gradients[component][direction])
            for direction in range(3)
        ]
        stress_row[component] = stress_row[component] + first_lame_modulus * dilation
        total = jnp.einsum(
            "pa,pjkxyz->ajkxyz", derivative, weighting * stress_row[0], precision=highest
        )
        total = total + jnp.einsum(
            "pa,ipkxyz->iakxyz", derivative, weighting * stress_row[1], precision=highest
        )
        total = total + jnp.einsum(
            "pa,ijpxyz->ijaxyz", derivative, weighting * stress_row[2], precision=highest
        )
        forces.append(inv_half * total)
    return jnp.stack(forces)


def fix_edges(padded, depth):
    placings = (
        (lax.axis_index("gx"), lax.axis_size("gx"), 1),
        (lax.axis_index(("grp", "gy")), lax.axis_size(("grp", "gy")), 2),
    )
    for position, extent, axis_num in placings:
        length = padded.shape[axis_num]
        inner_low = lax.slice_in_dim(padded, depth, depth + 1, axis=axis_num)
        inner_high = lax.slice_in_dim(padded, length - depth - 1, length - depth, axis=axis_num)
        place = lax.broadcasted_iota(jnp.int32, padded.shape, axis_num)
        padded = jnp.where((position == 0) & (place < depth), inner_low, padded)
        padded = jnp.where((position == extent - 1) & (place >= length - depth), inner_high, padded)
    return padded


def pad_depth(padded):
    return jnp.pad(padded, ((0, 0), (0, 0), (0, 0), (1, 1)), mode="edge")


def fold_rim(extended, axis_num):
    length = extended.shape[axis_num]
    middle = lax.slice_in_dim(extended, 1, length - 1, axis=axis_num)
    low_rim = lax.slice_in_dim(extended, 0, 1, axis=axis_num)
    high_rim = lax.slice_in_dim(extended, length - 1, length, axis=axis_num)
    widths = [(0, 0)] * extended.ndim
    pad_after = list(widths)
    pad_after[axis_num] = (0, length - 3)
    pad_before = list(widths)
    pad_before[axis_num] = (length - 3, 0)
    return middle + jnp.pad(low_rim, pad_after) + jnp.pad(high_rim, pad_before)


def assemble(local_sum):
    extended = extended_2(local_sum, (("gx", 1), (("grp", "gy"), 2)), 1)
    return fold_rim(fold_rim(extended, 1), 2)


def shards(
    density,
    momentum,
    energy,
    displacement,
    velocity_field,
    acceleration,
    material,
    element_region_index,
    face_dest,
    face_slot,
):
    hydro_state = jnp.concatenate([density[None], momentum, energy[None]], axis=0)
    for repeat in range(2):
        padded = extended_2(hydro_state, (("gx", 1), (("grp", "gy"), 2)), 1)
        hydro_state = advance(pad_depth(fix_edges(padded, 1)))
    traction = surface_traction(hydro_state).reshape(3, -1)
    own_rank = lax.axis_index(("grp", "gx", "gy"))
    node_rows = displacement.shape[1]
    node_cols = displacement.shape[2]
    depth_nodes = displacement.shape[3]
    surface_nodes = node_rows * node_cols
    targets = face_dest[0, :, 0]
    slot_ids = face_slot[0]
    combined = (targets * surface_nodes + slot_ids).astype(jnp.float32)
    whole_traction, whole_codes = (
        lax.all_gather(traction[:, None, :], ("grp", "gx", "gy"), axis=1, tiled=True),
        lax.all_gather(combined[None, None, :], ("grp", "gx", "gy"), axis=1, tiled=True),
    )
    target_codes = whole_codes.reshape(-1).astype(jnp.int32)
    is_mine = target_codes // surface_nodes == own_rank
    landing = jnp.where(is_mine, target_codes - own_rank * surface_nodes, 0)
    arriving = jnp.where(is_mine[None], whole_traction.reshape(3, -1), 0.0)
    deposited = jax.ops.segment_sum(arriving.T, landing, num_segments=surface_nodes).T
    surface_force = jnp.concatenate(
        [
            deposited.reshape(3, node_rows, node_cols, 1),
            jnp.zeros((3, node_rows, node_cols, depth_nodes - 1), jnp.float32),
        ],
        axis=3,
    )
    count_x, count_y, count_z = element_region_index.shape
    rock_density, first_lame_modulus, shear_lame_modulus = material_fields(
        material, element_region_index
    )
    _, weights = gll_tables()
    elem_mass = (rock_density * cell_weight(weights))[None]
    current_displacement, veloc_now, accel_now = (displacement, velocity_field, acceleration)
    mass_nodes = None
    for repeat in range(2):
        current_displacement = (
            current_displacement + time_step * veloc_now + 0.5 * time_step**2 * accel_now
        )
        internal_forces = gather_to_nodes(
            forces_per_element(
                scatter_to_elements(current_displacement, count_x, count_y),
                first_lame_modulus,
                shear_lame_modulus,
            )
        )
        if repeat == 0:
            summed = assemble(
                jnp.concatenate(
                    [surface_force - internal_forces, gather_to_nodes(elem_mass)], axis=0
                )
            )
            mass_nodes = summed[3]
            net_force = summed[:3]
        else:
            net_force = assemble(surface_force - internal_forces)
        accel_new = net_force / mass_nodes
        veloc_now = veloc_now + 0.5 * time_step * (accel_now + accel_new)
        accel_now = accel_new
    return (hydro_state, current_displacement, veloc_now, accel_now)


def solution(mesh):
    placed = (
        P("gx", ("grp", "gy"), None),
        P(None, "gx", ("grp", "gy"), None),
        P("gx", ("grp", "gy"), None),
        P(None, "gx", ("grp", "gy"), None),
        P(None, "gx", ("grp", "gy"), None),
        P(None, "gx", ("grp", "gy"), None),
        P(),
        P("gx", ("grp", "gy"), None),
        P(("grp", "gx", "gy"), None, None),
        P(("grp", "gx", "gy"), None),
    )
    return jax.shard_map(
        shards,
        mesh=mesh,
        in_specs=placed,
        out_specs=(
            P(None, "gx", ("grp", "gy"), None),
            P(None, "gx", ("grp", "gy"), None),
            P(None, "gx", ("grp", "gy"), None),
            P(None, "gx", ("grp", "gy"), None),
        ),
        check_vma=False,
    )
```

profile of v0, /device:TPU:9, one launch (start us, length us, event | category | flops | bytes accessed | tf_op | source)
XLA Modules:
  0.0 368.2 jit_solution(17011309073964725883)
XLA Ops:
  0.6 1.8 pad_maximum_fusion.45
  2.4 3.1 collective-permute-start
  5.6 3.1 collective-permute-start.1
  15.9 4.3 %copy.1095 = f32[3,9,17,512]{2,3,1,0:T(8,128)} copy(f32[3,9,17,512]{3,2,1,0:T(8,128)S(1)} %fusion.20) | data formatting | bytes 1880064 | tf_op jit(solution)/shard_map/add | solution.py:311
  20.2 5.8 %copy.1252 = f32[3,9,17,128,4]{3,2,1,4,0:T(8,128)S(1)} copy(f32[3,9,17,128,4]{2,4,3,1,0:T(4,128)} %bitcast.712) | data formatting | bytes 1880064 | tf_op jit(solution)/shard_map/transpose | solution.py:131
  26.0 5.8 %copy.1096 = f32[3,9,17,128,4]{3,2,1,0,4:T(8,128)S(1)} copy(f32[3,9,17,128,4]{2,4,3,1,0:T(4,128)} %bitcast.713) | data formatting | bytes 1880064 | tf_op jit(solution)/shard_map/reshape | solution.py:131
  36.2 6.4 %stack.231 = f32[3,5,5,5,2,4,128]{6,1,5,4,3,2,0:T(8,128)S(1)} concatenate(f32[3,1,5,5,2,4,128]{6,1,5,4,3,2,0:T(1,128)} %bitcast.845, f32[3,1,5,5,2,4,128]{6,1,5,4,3,2,0:T(1,128)} %bitcast.844, f32[3,1,5,5,2,4,128]{6,1,5,4,3,2,0:T(1,128)} %bitcast.843, f32[3,1,5,5,2,4,128]{6,1,5,4,3,2,0:T(1,128)S(1)} %bitcast.842, f32[3,1,5,5,2,4,128]{6,1,5,4,3,2,0:T(1,128)S(1)} %bitcast.841), dimensions={1} | concatenate | bytes 3072000 | tf_op jit(solution)/shard_map/stack | solution.py:119
  42.6 2.3 multiply_bitcast_fusion
  44.9 3.1 fusion.6
  48.0 3.1 fusion.9
  71.5 1.7 reshape.531
  74.3 38.0 %all_gather.6 = f32[1,32,128]{2,0,1:T(1,128)S(1)} all-gather(f32[1,1,128]{2,0,1:T(1,128)S(1)} %fusion.184), channel_id=1, replica_groups=mesh['grp'=2,'gx'=8,'gy'=2] {'grp','gx','gy'}, dimensions={1}, use_global_device_ids=true | all-gather | bytes 16896 | tf_op jit(solution)/shard_map/all_gather | solution.py:287
  113.9 2.2 collective-permute-start.2
  116.1 2.1 collective-permute-start.3
  118.2 3.1 collective-permute-done.3
  128.7 1.9 collective-permute-start.4
  130.6 4.3 %collective-permute-start.5 = (f32[5,1,32,256]{3,2,0,1:T(8,128)S(1)}, f32[5,1,32,256]{3,2,0,1:T(8,128)S(1)}, u32[]{:S(2)}, u32[]{:S(2)}) collective-permute-start(f32[5,1,32,256]{3,2,0,1:T(8,128)S(1)} %get-tuple-element.138), channel_id=1, source_target_pairs={{2,0},{4,2},{6,4},{8,6},{10,8},{12,10},{14,12},{3,1},{5,3},{7,5},{... | collective-permute-start | bytes 491528 | tf_op jit(solution)/shard_map/ppermute | solution.py:22
  137.4 2.3 collective-permute-done.5
  140.3 1.9 collective-permute-start.6
  142.2 2.4 collective-permute-start.7
  145.7 2.9 copy.1156
  150.1 6.6 %copy.1146 = f32[3,9,17,128,4]{2,4,3,1,0:T(4,128)} copy(f32[3,9,17,128,4]{3,2,1,0,4:T(8,128)} %pad_maximum_fusion.9) | data formatting | bytes 1880064 | tf_op jit(solution)/shard_map/stack | solution.py:170
  156.7 5.2 %copy.1147 = f32[3,9,17,512]{3,0,2,1:T(4,128)S(1)} copy(f32[3,9,17,512]{2,3,1,0:T(8,128)} %bitcast.754) | data formatting | bytes 1880064 | tf_op jit(solution)/shard_map/reshape | solution.py:171
  171.7 34.9 %all_gather.7 = f32[3,32,128]{2,0,1:T(4,128)S(1)} all-gather(f32[3,1,128]{2,0,1:T(4,128)S(1)} %copy.1091), channel_id=1, replica_groups=mesh['grp'=2,'gx'=8,'gy'=2] {'grp','gx','gy'}, dimensions={1}, use_global_device_ids=true | all-gather | bytes 50688 | tf_op jit(solution)/shard_map/all_gather | solution.py:286
  206.7 2.0 copy.1092
  208.7 28.5 %scatter_custom_fusion = f32[153,3]{1,0:T(8,128)S(1)} fusion(s32[4096]{0:T(1024)} %bitcast.857, f32[4096,3]{1,0:T(8,128)} %copy.1092, f32[]{:T(128)} %constant.36.clone.1), kind=kCustom, calls=%fused_computation.449 | custom fusion | flops 12288 | bytes 2348 | tf_op jit(solution)/shard_map/scatter-add | solution.py:293
  238.6 1.9 collective-permute-start.8
  240.5 4.3 %collective-permute-start.9 = (f32[4,1,17,512]{3,0,2,1:T(4,128)S(1)}, f32[4,1,17,512]{3,0,2,1:T(4,128)S(1)}, u32[]{:S(2)}, u32[]{:S(2)}) collective-permute-start(f32[4,1,17,512]{3,0,2,1:T(4,128)S(1)} %get-tuple-element.100), channel_id=1, source_target_pairs={{2,0},{4,2},{6,4},{8,6},{10,8},{12,10},{14,12},{3,1},{5,3},{7,5},{... | collective-permute-start | bytes 417800 | tf_op jit(solution)/shard_map/ppermute | solution.py:22
  246.5 3.5 collective-permute-done.9
  250.1 5.4 %collective-permute-start.10 = (f32[4,11,1,512]{3,0,2,1:T(4,128)S(1)}, f32[4,11,1,512]{3,0,2,1:T(4,128)S(1)}, u32[]{:S(2)}, u32[]{:S(2)}) collective-permute-start(f32[4,11,1,512]{3,0,2,1:T(4,128)S(1)} %get-tuple-element.79), channel_id=1, source_target_pairs={{0,1},{1,16},{16,17},{2,3},{3,18},{18,19},{4,5},{5,20},{20,21},{6,... | collective-permute-start | bytes 270344 | tf_op jit(solution)/shard_map/ppermute | solution.py:21
  255.5 1.9 collective-permute-start.11
  257.4 3.9 %collective-permute-done.11 = f32[4,11,1,512]{3,0,2,1:T(4,128)S(1)} collective-permute-done((f32[4,11,1,512]{3,0,2,1:T(4,128)S(1)}, f32[4,11,1,512]{3,0,2,1:T(4,128)S(1)}, u32[]{:S(2)}, u32[]{:S(2)}) %collective-permute-start.11) | collective-permute-done | bytes 90144 | tf_op jit(solution)/shard_map/ppermute | solution.py:22
  267.8 4.3 %copy.1163 = f32[3,9,17,512]{2,3,1,0:T(8,128)} copy(f32[3,9,17,512]{3,2,1,0:T(8,128)S(1)} %multiply_add_fusion.1) | data formatting | bytes 1880064 | tf_op jit(solution)/shard_map/add | solution.py:311
  272.1 5.8 %copy.1262 = f32[3,9,17,128,4]{3,2,1,4,0:T(8,128)S(1)} copy(f32[3,9,17,128,4]{2,4,3,1,0:T(4,128)} %bitcast.714) | data formatting | bytes 1880064 | tf_op jit(solution)/shard_map/transpose | solution.py:131
  277.9 5.8 %copy.1164 = f32[3,9,17,128,4]{3,2,1,0,4:T(8,128)S(1)} copy(f32[3,9,17,128,4]{2,4,3,1,0:T(4,128)} %bitcast.715) | data formatting | bytes 1880064 | tf_op jit(solution)/shard_map/reshape | solution.py:131
  286.3 5.0 %slice.1014 = f32[3,5,9,4,128]{4,3,2,1,0:T(4,128)} slice(f32[3,5,9,17,128]{4,3,2,1,0:T(8,128)S(1)} %pad_maximum_fusion.6), slice={[0:3:1], [0:5:1], [0:9:1], [0:13:4], [0:128:1]} | slice | bytes 552960 | tf_op jit(solution)/shard_map/slice | solution.py:121
  293.7 6.4 %stack.271 = f32[3,5,5,5,2,4,128]{6,1,5,4,3,2,0:T(8,128)S(1)} concatenate(f32[3,1,5,5,2,4,128]{6,1,5,4,3,2,0:T(1,128)} %bitcast.850, f32[3,1,5,5,2,4,128]{6,1,5,4,3,2,0:T(1,128)} %bitcast.849, f32[3,1,5,5,2,4,128]{6,1,5,4,3,2,0:T(1,128)} %bitcast.848, f32[3,1,5,5,2,4,128]{6,1,5,4,3,2,0:T(1,128)} %bitcast.847, f32[3,1,5,5,2,4,128]{6,1,5,4,3,2,0:T(1,128)S(1)} %bitcast.846), dimensions={1} | concatenate | bytes 3072000 | tf_op jit(solution)/shard_map/stack | solution.py:119
  300.1 3.1 fusion.1
  303.1 3.1 fusion.3
  306.2 2.3 fusion.197
  323.1 2.0 fusion.32
  330.9 5.0 %copy.1215 = f32[3,9,17,128,4]{2,4,3,1,0:T(4,128)} copy(f32[3,9,17,128,4]{3,2,1,0,4:T(8,128)S(1)} %pad_maximum_fusion.10) | data formatting | bytes 1880064 | tf_op jit(solution)/shard_map/stack | solution.py:170
  336.0 5.3 %copy.1216 = f32[3,9,17,512]{3,0,2,1:T(4,128)S(1)} copy(f32[3,9,17,512]{2,3,1,0:T(8,128)} %bitcast.755) | data formatting | bytes 1880064 | tf_op jit(solution)/shard_map/reshape | solution.py:171
  341.8 3.4 collective-permute-start.13
  345.3 1.9 collective-permute-start.12
  347.3 4.3 %collective-permute-done.12 = f32[3,1,17,512]{3,1,2,0:T(1,128)S(1)} collective-permute-done((f32[3,1,17,512]{3,1,2,0:T(1,128)S(1)}, f32[3,1,17,512]{3,1,2,0:T(1,128)S(1)}, u32[]{:S(2)}, u32[]{:S(2)}) %collective-permute-start.12) | collective-permute-done | bytes 104480 | tf_op jit(solution)/shard_map/ppermute | solution.py:21
  352.3 2.1 collective-permute-start.15
  354.4 3.6 collective-permute-start.14
  (336 shorter events, 102.1 us)
Async XLA Ops:
  2.4 111.3 %collective-permute-start = (f32[5,1,32,256]{3,2,0,1:T(8,128)}, f32[5,1,32,256]{3,2,0,1:T(8,128)S(1)}, u32[]{:S(2)}, u32[]{:S(2)}) collective-permute-start(f32[5,1,32,256]{3,2,0,1:T(8,128)} %get-tuple-element.139), channel_id=1, source_target_pairs={{0,2},{2,4},{4,6},{6,8},{8,10},{10,12},{12,14},{1,3},{3,5},{5,7},{... | collective-permute-start | bytes 491528 | tf_op jit(solution)/shard_map/ppermute | solution.py:21
  5.6 108.2 %collective-permute-start.1 = (f32[5,1,32,256]{3,2,0,1:T(8,128)}, f32[5,1,32,256]{3,2,0,1:T(8,128)S(1)}, u32[]{:S(2)}, u32[]{:S(2)}) collective-permute-start(f32[5,1,32,256]{3,2,0,1:T(8,128)} %get-tuple-element.140), channel_id=1, source_target_pairs={{2,0},{4,2},{6,4},{8,6},{10,8},{12,10},{14,12},{3,1},{5,3},{7,5},{... | collective-permute-start | bytes 491528 | tf_op jit(solution)/shard_map/ppermute | solution.py:22
  12.4 2.5 copy-start.16
  12.6 2.3 copy-start.10
  12.7 2.2 copy-start.7
  36.2 6.4 %copy-start.29 = (f32[5,5,1,1,1,1,1]{1,0,6,5,4,3,2:T(8,128)S(1)}, f32[5,5,1,1,1,1,1]{1,0,6,5,4,3,2:T(8,128)}, u32[]{:S(2)}) copy-start(f32[5,5,1,1,1,1,1]{1,0,6,5,4,3,2:T(8,128)} %constant.189) | copy-start | bytes 304
  53.3 1.4 copy-start.21
  73.3 40.5 %copy-start = (f32[3,4,32,256]{3,2,1,0:T(8,128)S(1)}, f32[3,4,32,256]{3,2,1,0:T(8,128)}, u32[]{:S(2)}) copy-start(f32[3,4,32,256]{3,2,1,0:T(8,128)} %param.16) | copy-start | bytes 1179652
  73.3 40.5 %copy-start.1 = (f32[4,32,256]{2,1,0:T(8,128)S(1)}, f32[4,32,256]{2,1,0:T(8,128)}, u32[]{:S(2)}) copy-start(f32[4,32,256]{2,1,0:T(8,128)} %param.17) | copy-start | bytes 393220
  73.3 40.5 %copy-start.2 = (f32[4,32,256]{2,1,0:T(8,128)S(1)}, f32[4,32,256]{2,1,0:T(8,128)}, u32[]{:S(2)}) copy-start(f32[4,32,256]{2,1,0:T(8,128)} %param.15) | copy-start | bytes 393220
  113.7 12.3 %copy-start.33 = (f32[3]{0:T(128)}, f32[3]{0:T(128)S(1)}, u32[]{:S(2)}) copy-start(f32[3]{0:T(128)S(1)} %get-tuple-element.166) | copy-start | bytes 40
  113.7 13.2 %copy-start.35 = (f32[3]{0:T(128)}, f32[3]{0:T(128)S(1)}, u32[]{:S(2)}) copy-start(f32[3]{0:T(128)S(1)} %get-tuple-element.164) | copy-start | bytes 40
  113.7 13.6 %copy-start.31 = (f32[3]{0:T(128)}, f32[3]{0:T(128)S(1)}, u32[]{:S(2)}) copy-start(f32[3]{0:T(128)S(1)} %get-tuple-element.165) | copy-start | bytes 40
  113.9 4.4 %collective-permute-start.2 = (f32[5,6,1,256]{3,2,0,1:T(1,128)S(1)}, f32[5,6,1,256]{3,2,0,1:T(1,128)S(1)}, u32[]{:S(2)}, u32[]{:S(2)}) collective-permute-start(f32[5,6,1,256]{3,2,0,1:T(1,128)S(1)} %get-tuple-element.135), channel_id=1, source_target_pairs={{0,1},{1,16},{16,17},{2,3},{3,18},{18,19},{4,5},{5,20},{20,21},{6,... | collective-permute-start | bytes 92168 | tf_op jit(solution)/shard_map/ppermute | solution.py:21
  116.1 5.2 %collective-permute-start.3 = (f32[5,6,1,256]{3,2,0,1:T(1,128)S(1)}, f32[5,6,1,256]{3,2,0,1:T(1,128)S(1)}, u32[]{:S(2)}, u32[]{:S(2)}) collective-permute-start(f32[5,6,1,256]{3,2,0,1:T(1,128)S(1)} %get-tuple-element.136), channel_id=1, source_target_pairs={{1,0},{16,1},{17,16},{3,2},{18,3},{19,18},{5,4},{20,5},{21,20},{7,... | collective-permute-start | bytes 92168 | tf_op jit(solution)/shard_map/ppermute | solution.py:22
  128.2 6.7 %copy-start.28 = (f32[1,9,17,127]{3,0,2,1:T(1,128)S(1)}, f32[1,9,17,127]{3,0,2,1:T(1,128)}, u32[]{:S(2)}) copy-start(f32[1,9,17,127]{3,0,2,1:T(1,128)} %slice_bitcast_fusion.49) | copy-start | bytes 233176
  128.2 7.8 %copy-start.22 = (f32[3,9,17,128,1]{3,2,1,0,4:T(8,128)S(1)}, f32[3,9,17,128,1]{3,2,1,0,4:T(8,128)}, u32[]{:S(2)}) copy-start(f32[3,9,17,128,1]{3,2,1,0,4:T(8,128)} %get-tuple-element.96) | copy-start | bytes 705028
  128.3 7.8 %copy-start.23 = (f32[3,9,17,128,1]{3,2,1,0,4:T(8,128)S(1)}, f32[3,9,17,128,1]{3,2,1,0,4:T(8,128)}, u32[]{:S(2)}) copy-start(f32[3,9,17,128,1]{3,2,1,0,4:T(8,128)} %get-tuple-element.97) | copy-start | bytes 705028
  128.3 7.8 %copy-start.24 = (f32[3,9,17,128,1]{3,2,1,0,4:T(8,128)S(1)}, f32[3,9,17,128,1]{3,2,1,0,4:T(8,128)}, u32[]{:S(2)}) copy-start(f32[3,9,17,128,1]{3,2,1,0,4:T(8,128)} %get-tuple-element.98) | copy-start | bytes 705028
  128.7 8.6 %collective-permute-start.4 = (f32[5,1,32,256]{3,2,0,1:T(8,128)S(1)}, f32[5,1,32,256]{3,2,0,1:T(8,128)S(1)}, u32[]{:S(2)}, u32[]{:S(2)}) collective-permute-start(f32[5,1,32,256]{3,2,0,1:T(8,128)S(1)} %get-tuple-element.137), channel_id=1, source_target_pairs={{0,2},{2,4},{4,6},{6,8},{8,10},{10,12},{12,14},{1,3},{3,5},{5,7},{... | collective-permute-start | bytes 491528 | tf_op jit(solution)/shard_map/ppermute | solution.py:21
  130.6 9.0 %collective-permute-start.5 = (f32[5,1,32,256]{3,2,0,1:T(8,128)S(1)}, f32[5,1,32,256]{3,2,0,1:T(8,128)S(1)}, u32[]{:S(2)}, u32[]{:S(2)}) collective-permute-start(f32[5,1,32,256]{3,2,0,1:T(8,128)S(1)} %get-tuple-element.138), channel_id=1, source_target_pairs={{2,0},{4,2},{6,4},{8,6},{10,8},{12,10},{14,12},{3,1},{5,3},{7,5},{... | collective-permute-start | bytes 491528 | tf_op jit(solution)/shard_map/ppermute | solution.py:22
  136.1 8.6 %copy-start.25 = (f32[1,9,17,128,1]{3,0,4,2,1:T(1,128)S(1)}, f32[1,9,17,128,1]{3,0,4,2,1:T(1,128)}, u32[]{:S(2)}) copy-start(f32[1,9,17,128,1]{3,0,4,2,1:T(1,128)} %get-tuple-element.155) | copy-start | bytes 235012
  136.1 8.6 %copy-start.26 = (f32[1,9,17,128,1]{3,0,4,2,1:T(1,128)S(1)}, f32[1,9,17,128,1]{3,0,4,2,1:T(1,128)}, u32[]{:S(2)}) copy-start(f32[1,9,17,128,1]{3,0,4,2,1:T(1,128)} %get-tuple-element.156) | copy-start | bytes 235012
  136.1 8.6 %copy-start.27 = (f32[1,9,17,128,1]{3,0,4,2,1:T(1,128)S(1)}, f32[1,9,17,128,1]{3,0,4,2,1:T(1,128)}, u32[]{:S(2)}) copy-start(f32[1,9,17,128,1]{3,0,4,2,1:T(1,128)} %get-tuple-element.157) | copy-start | bytes 235012
  140.3 21.6 %collective-permute-start.6 = (f32[5,6,1,256]{3,2,0,1:T(1,128)}, f32[5,6,1,256]{3,2,0,1:T(1,128)S(1)}, u32[]{:S(2)}, u32[]{:S(2)}) collective-permute-start(f32[5,6,1,256]{3,2,0,1:T(1,128)} %get-tuple-element.133), channel_id=1, source_target_pairs={{0,1},{1,16},{16,17},{2,3},{3,18},{18,19},{4,5},{5,20},{20,21},{6,... | collective-permute-start | bytes 92168 | tf_op jit(solution)/shard_map/ppermute | solution.py:21
  142.2 19.7 %collective-permute-start.7 = (f32[5,6,1,256]{3,2,0,1:T(1,128)S(1)}, f32[5,6,1,256]{3,2,0,1:T(1,128)S(1)}, u32[]{:S(2)}, u32[]{:S(2)}) collective-permute-start(f32[5,6,1,256]{3,2,0,1:T(1,128)S(1)} %get-tuple-element.134), channel_id=1, source_target_pairs={{1,0},{16,1},{17,16},{3,2},{18,3},{19,18},{5,4},{20,5},{21,20},{7,... | collective-permute-start | bytes 92168 | tf_op jit(solution)/shard_map/ppermute | solution.py:22
  170.1 36.5 %copy-start.30 = (pred[4096]{0:T(1024)(128)(4,1)S(1)}, pred[4096]{0:T(1024)(128)(4,1)}, u32[]{:S(2)}) copy-start(pred[4096]{0:T(1024)(128)(4,1)} %get-tuple-element.39) | copy-start | bytes 12292
  170.5 38.1 %copy-start.14 = (f32[5,4,32,256]{3,2,0,1:T(8,128)}, f32[5,4,32,256]{3,2,0,1:T(8,128)S(1)}, u32[]{:S(2)}) copy-start(f32[5,4,32,256]{3,2,0,1:T(8,128)S(1)} %fusion.119) | copy-start | bytes 1966084
  237.4 1.1 copy-start.13
  238.6 7.9 %collective-permute-start.8 = (f32[4,1,17,512]{3,0,2,1:T(4,128)S(1)}, f32[4,1,17,512]{3,0,2,1:T(4,128)S(1)}, u32[]{:S(2)}, u32[]{:S(2)}) collective-permute-start(f32[4,1,17,512]{3,0,2,1:T(4,128)S(1)} %get-tuple-element.99), channel_id=1, source_target_pairs={{0,2},{2,4},{4,6},{6,8},{8,10},{10,12},{12,14},{1,3},{3,5},{5,7},{... | collective-permute-start | bytes 417800 | tf_op jit(solution)/shard_map/ppermute | solution.py:21
  240.5 9.5 %collective-permute-start.9 = (f32[4,1,17,512]{3,0,2,1:T(4,128)S(1)}, f32[4,1,17,512]{3,0,2,1:T(4,128)S(1)}, u32[]{:S(2)}, u32[]{:S(2)}) collective-permute-start(f32[4,1,17,512]{3,0,2,1:T(4,128)S(1)} %get-tuple-element.100), channel_id=1, source_target_pairs={{2,0},{4,2},{6,4},{8,6},{10,8},{12,10},{14,12},{3,1},{5,3},{7,5},{... | collective-permute-start | bytes 417800 | tf_op jit(solution)/shard_map/ppermute | solution.py:22
  250.1 7.3 %collective-permute-start.10 = (f32[4,11,1,512]{3,0,2,1:T(4,128)S(1)}, f32[4,11,1,512]{3,0,2,1:T(4,128)S(1)}, u32[]{:S(2)}, u32[]{:S(2)}) collective-permute-start(f32[4,11,1,512]{3,0,2,1:T(4,128)S(1)} %get-tuple-element.79), channel_id=1, source_target_pairs={{0,1},{1,16},{16,17},{2,3},{3,18},{18,19},{4,5},{5,20},{20,21},{6,... | collective-permute-start | bytes 270344 | tf_op jit(solution)/shard_map/ppermute | solution.py:21
  255.5 5.8 %collective-permute-start.11 = (f32[4,11,1,512]{3,0,2,1:T(4,128)S(1)}, f32[4,11,1,512]{3,0,2,1:T(4,128)S(1)}, u32[]{:S(2)}, u32[]{:S(2)}) collective-permute-start(f32[4,11,1,512]{3,0,2,1:T(4,128)S(1)} %get-tuple-element.80), channel_id=1, source_target_pairs={{1,0},{16,1},{17,16},{3,2},{18,3},{19,18},{5,4},{20,5},{21,20},{7,... | collective-permute-start | bytes 270344 | tf_op jit(solution)/shard_map/ppermute | solution.py:22
  263.9 1.8 copy-start.8
  263.9 2.3 copy-start.11
  263.9 2.7 copy-start.17
  264.3 1.3 copy-start.3
  267.8 4.3 %copy-start.5 = (f32[3,9,17,512]{3,2,1,0:T(8,128)}, f32[3,9,17,512]{3,2,1,0:T(8,128)S(1)}, u32[]{:S(2)}) copy-start(f32[3,9,17,512]{3,2,1,0:T(8,128)S(1)} %multiply_add_fusion.1) | copy-start | bytes 2820100
  336.0 5.3 %copy-start.19 = (f32[3,9,17,1]{3,0,2,1:T(4,128)S(1)}, f32[3,9,17,1]{3,0,2,1:T(4,128)}, u32[]{:S(2)}) copy-start(f32[3,9,17,1]{3,0,2,1:T(4,128)} %copy-done.18) | copy-start | bytes 5512
  341.8 5.5 %collective-permute-start.13 = (f32[3,1,17,512]{3,1,2,0:T(1,128)S(1)}, f32[3,1,17,512]{3,1,2,0:T(1,128)S(1)}, u32[]{:S(2)}, u32[]{:S(2)}) collective-permute-start(f32[3,1,17,512]{3,1,2,0:T(1,128)S(1)} %copy.1218), channel_id=1, source_target_pairs={{2,0},{4,2},{6,4},{8,6},{10,8},{12,10},{14,12},{3,1},{5,3},{7,5},{... | collective-permute-start | bytes 313352 | tf_op jit(solution)/shard_map/ppermute | solution.py:22
  345.3 6.3 %collective-permute-start.12 = (f32[3,1,17,512]{3,1,2,0:T(1,128)S(1)}, f32[3,1,17,512]{3,1,2,0:T(1,128)S(1)}, u32[]{:S(2)}, u32[]{:S(2)}) collective-permute-start(f32[3,1,17,512]{3,1,2,0:T(1,128)S(1)} %copy.1217), channel_id=1, source_target_pairs={{0,2},{2,4},{4,6},{6,8},{8,10},{10,12},{12,14},{1,3},{3,5},{5,7},{... | collective-permute-start | bytes 313352 | tf_op jit(solution)/shard_map/ppermute | solution.py:21
  351.7 6.3 %copy-start.15 = (f32[5,4,32,256]{3,2,0,1:T(8,128)S(1)}, f32[5,4,32,256]{3,2,0,1:T(8,128)}, u32[]{:S(2)}) copy-start(f32[5,4,32,256]{3,2,0,1:T(8,128)} %copy-done.14) | copy-start | bytes 1966084
  352.1 6.8 %copy-start.6 = (f32[3,9,17,512]{3,2,1,0:T(8,128)S(1)}, f32[3,9,17,512]{3,2,1,0:T(8,128)}, u32[]{:S(2)}) copy-start(f32[3,9,17,512]{3,2,1,0:T(8,128)} %copy-done.5) | copy-start | bytes 2820100
  352.3 8.7 %collective-permute-start.15 = (f32[3,11,1,512]{3,2,1,0:T(1,128)S(1)}, f32[3,11,1,512]{3,2,1,0:T(1,128)S(1)}, u32[]{:S(2)}, u32[]{:S(2)}) collective-permute-start(f32[3,11,1,512]{3,2,1,0:T(1,128)S(1)} %copy.1222), channel_id=1, source_target_pairs={{1,0},{16,1},{17,16},{3,2},{18,3},{19,18},{5,4},{20,5},{21,20},{7,... | collective-permute-start | bytes 202760 | tf_op jit(solution)/shard_map/ppermute | solution.py:22
  354.4 6.7 %collective-permute-start.14 = (f32[3,11,1,512]{3,2,1,0:T(1,128)S(1)}, f32[3,11,1,512]{3,2,1,0:T(1,128)S(1)}, u32[]{:S(2)}, u32[]{:S(2)}) collective-permute-start(f32[3,11,1,512]{3,2,1,0:T(1,128)S(1)} %copy.1221), channel_id=1, source_target_pairs={{0,1},{1,16},{16,17},{2,3},{3,18},{18,19},{4,5},{5,20},{20,21},{6,... | collective-permute-start | bytes 202760 | tf_op jit(solution)/shard_map/ppermute | solution.py:21
  361.3 1.5 copy-start.4
  361.3 1.8 copy-start.9
  361.3 2.2 copy-start.12
  (9 other events, 7.2 us)
where the time goes:
time: 375 us; the launch traced here: 368 us
  local copies, waits for them, and re-layouts  112 us (30%)
  other arithmetic  75.1 us (20%)
  blocking collectives  73 us (19%)
  starting transfers between devices  45.5 us (12%)
  matrix products  40.3 us (11%)
  waiting for transfers between devices  18.9 us (5%)
    all_gather x1, blocking collectives, shards(): lax.all_gather(combined[None, None, :], ('grp', 'gx', 'gy'), axis=1, tile...  38 us
    all_gather x1, blocking collectives, shards(): lax.all_gather(traction[:, None, :], ('grp', 'gx', 'gy'), axis=1, tiled=T...  34.9 us
    scatter-add x1, other arithmetic, shards(): jax.ops.segment_sum(arriving.T, landing, num_segments=surface_nodes)  28.5 us
    ppermute x8, starting transfers between devices, extended_2(): after = lax.ppermute(first, axis, down)  23.5 us
    ppermute x8, starting transfers between devices, extended_2(): before = lax.ppermute(last, axis, up)  22 us
    another operation x6, local copies, waits for them, and re-layouts, depth_fold(): jnp.stack([head_part, values[:, 1], values[:, 2], values[:, 3]], axis=-1)  16.2 us
    unnamed x95, local copies, waits for them, and re-layouts  13.7 us
    another operation x4, local copies, waits for them, and re-layouts, split_points(): jnp.stack([lax.slice_in_dim(field, offset, offset + 4 * elements - 3, str...  12.9 us
  transfers between devices with their start and end apart: 16, of which 6 were waited for; matrix products, arithmetic and copies ran while one was open for 24% of the time, Pallas kernels for 0%

commit v1 on v0

v1 whole, which is shorter than its diff:
```python
import functools

import jax
import jax.numpy as jnp
import numpy as np
from jax import lax
from jax.experimental import pallas as pl
from jax.experimental.pallas import tpu as pltpu
from jax.sharding import PartitionSpec as P

gamma_gas = 1.4
cell_ratio = 0.05
half_size = 2.0
time_step = 0.1
face_area = 2.0
vmem_bytes = 40 * 1024 * 1024


def gll_tables():
    root = np.sqrt(3.0 / 7.0)
    points = np.array([-1.0, -root, 0.0, root, 1.0])
    weights = np.array([0.1, 49.0 / 90.0, 32.0 / 45.0, 49.0 / 90.0, 0.1])
    products = [np.prod([points[r] - points[c] for c in range(5) if c != r]) for r in range(5)]
    derivative = np.zeros((5, 5))
    for r in range(5):
        for c in range(5):
            if r != c:
                derivative[r, c] = products[r] / products[c] / (points[r] - points[c])
        derivative[r, r] = sum(1.0 / (points[r] - points[c]) for c in range(5) if c != r)
    derivative[2, 2] = 0.0
    return derivative, weights


deriv, quad = gll_tables()
deriv_t = deriv.T
kind = [0, 1, 2, 1, 0]
f32 = jnp.float32


def line(matrix, v):
    even, odd = (matrix + matrix[:, ::-1]) / 2, (matrix - matrix[:, ::-1]) / 2
    e0, e1, o0, o1 = v[0] + v[4], v[1] + v[3], v[0] - v[4], v[1] - v[3]
    top = [float(even[i, 0]) * e0 + float(even[i, 1]) * e1 + float(matrix[i, 2]) * v[2] for i in range(2)]
    low = [float(odd[i, 0]) * o0 + float(odd[i, 1]) * o1 for i in range(2)]
    centre = float(matrix[2, 0]) * o0 + float(matrix[2, 1]) * o1
    return [top[0] + low[0], top[1] + low[1], centre, low[1] - top[1], low[0] - top[0]]


def rows_of(shape=(8, 128)):
    return lax.broadcasted_iota(jnp.int32, shape, 0)


def lanes_of(shape=(8, 128)):
    return lax.broadcasted_iota(jnp.int32, shape, 1)


def deeper(x):
    return jnp.where(lanes_of() == 127, 0.0, pltpu.roll(x, 127, 1))


def shallower(x):
    return jnp.where(lanes_of() == 0, 0.0, pltpu.roll(x, 1, 1))


def split_three(x):
    high = x.astype(jnp.bfloat16)
    rest = x - high.astype(f32)
    middle = rest.astype(jnp.bfloat16)
    return high, middle, (rest - middle.astype(f32)).astype(jnp.bfloat16)


def one_hot_dot(x, table, dims=(((1,), (0,)), ((), ()))):
    return sum(lax.dot_general(part, table, dims, preferred_element_type=f32) for part in split_three(x))


def depth_table(back=False):
    a = lax.broadcasted_iota(jnp.int32, (512, 512), 1 if back else 0)
    b = lax.broadcasted_iota(jnp.int32, (512, 512), 0 if back else 1)
    return jnp.where(a == 4 * (b & 127) + (b >> 7), 1.0, 0.0).astype(jnp.bfloat16)


def to_elements(nodes, table, tall, put):
    for i in range(5):
        for j in range(5):
            for ex in range(2):
                for t in range(4):
                    tall[i, j, 4 * ex : 4 * ex + 4, 128 * t : 128 * t + 128] = nodes[t, 4 * ex + i, pl.ds(j, 4, stride=4), :]
    out = one_hot_dot(tall[...].reshape(200, 512), table)
    for k in range(4):
        put(k, out[:, 128 * k : 128 * k + 128].reshape(5, 5, 8, 128))


def to_nodes(get, table, tall, nodes):
    wide = jnp.concatenate([get(k).reshape(200, 128) for k in range(4)], axis=1)
    tall[...] = one_hot_dot(wide, table).reshape(5, 5, 8, 512)
    for i in range(5):
        for j in range(5):
            for ex in range(2):
                if i == 4 and ex == 0:
                    continue
                for t in range(4):
                    lanes = slice(128 * t, 128 * t + 128)
                    if j < 4:
                        nodes[t, 4 * ex + i, pl.ds(j, 4, stride=4), :] = tall[i, j, 4 * ex : 4 * ex + 4, lanes]
                    else:
                        nodes[t, 4 * ex + i, 16:17, :] = tall[i, j, 4 * ex + 3 : 4 * ex + 4, lanes]


def lookup(material, row, region):
    total = jnp.zeros_like(region)
    for m in range(material.shape[1]):
        total = jnp.where(region == float(m + 1), material[row, m], total)
    return total


def internal(u, out, lame, shear, gx, gz, cross, planes, side):
    def depth_lines(i, carry):
        for j in range(5):
            for c in range(3):
                v = [u[c, i, j, k] for k in range(4)]
                v.append(deeper(v[0]))
                u[c, i, j, 4] = v[4]
                for k, g in enumerate(line(deriv, v)):
                    gz[c, i, j, k] = g
        return carry

    lax.fori_loop(0, 5, depth_lines, 0)

    def plane(k, carry):
        weight = jnp.where((k == 0) | (k == 4), float(quad[0]), jnp.where(k == 2, float(quad[2]), float(quad[1])))
        lame_k, shear_k = lame * (2.0 * weight), shear * (2.0 * weight)
        pairs = {}
        for a in range(3):
            for b in range(a, 3):
                w = float(quad[a] * quad[b])
                pairs[a, b] = pairs[b, a] = (lame_k * w, shear_k * w, shear_k * (2.0 * w))
        for c in range(3):
            for j in range(5):
                for i, g in enumerate(line(deriv, [u[c, i, j, k] for i in range(5)])):
                    gx[c, i, j] = g
        for i in range(5):
            gy = [line(deriv, [u[c, i, j, k] for j in range(5)]) for c in range(3)]
            ys = [[], [], []]
            for j in range(5):
                lw, mw, mw2 = pairs[kind[i], kind[j]]
                g0, g1, g2 = [[gx[c, i, j], gy[c][j], gz[c, i, j, k]] for c in range(3)]
                dilated = lw * (g0[0] + g1[1] + g2[2])
                s01 = mw * (g0[1] + g1[0])
                s02 = mw * (g0[2] + g2[0])
                s12 = mw * (g1[2] + g2[1])
                side[0, i, j] = dilated + mw2 * g0[0]
                side[1, i, j] = s01
                cross[0, i, j, k] = s02
                cross[1, i, j, k] = s12
                cross[2, i, j, k] = dilated + mw2 * g2[2]
                ys[0].append(s01)
                ys[1].append(dilated + mw2 * g1[1])
                ys[2].append(s12)
            for c in range(3):
                for j, value in enumerate(line(deriv_t, ys[c])):
                    planes[c, i, j, k] = value
        for j in range(5):
            for c in range(3):
                v = [side[c, i, j] if c < 2 else cross[0, i, j, k] for i in range(5)]
                for i, value in enumerate(line(deriv_t, v)):
                    planes[c, i, j, k] += value
        return carry

    lax.fori_loop(0, 5, plane, 0)

    def depth_sums(i, carry):
        for j in range(5):
            for c in range(3):
                v = line(deriv_t, [cross[c, i, j, k] for k in range(5)])
                v = [v[k] + planes[c, i, j, k] for k in range(5)]
                out[c, i, j, 0] = v[0] + shallower(v[4])
                for k in range(1, 4):
                    out[c, i, j, k] = v[k]
        return carry

    lax.fori_loop(0, 5, depth_sums, 0)
    sub = rows_of()

    def fold(k, carry):
        for c in range(3):
            for i in range(5):
                low, high = out[c, i, 0, k], out[c, i, 4, k]
                out[c, i, 0, k] = low + jnp.where(sub % 4 == 0, 0.0, pltpu.roll(high, 1, 0))
                out[c, i, 4, k] = high + jnp.where(sub % 4 == 3, 0.0, pltpu.roll(low, 7, 0))
            for j in range(5):
                low, high = out[c, 0, j, k], out[c, 4, j, k]
                out[c, 0, j, k] = low + jnp.where(sub < 4, 0.0, pltpu.roll(high, 4, 0))
                out[c, 4, j, k] = high + jnp.where(sub < 4, pltpu.roll(low, 4, 0), 0.0)
        return carry

    lax.fori_loop(0, 4, fold, 0)


def rolled(x, amount, axis=0):
    amount = amount % x.shape[axis]
    return pltpu.roll(x, amount, axis) if amount else x


def pack_x(force, low, high):
    sub = rows_of()
    for c in range(3):
        for j in range(5):
            for half in range(2):
                at = (c * 5 + j) * 2 + half
                a, b = force[c, 0, j, 2 * half], force[c, 0, j, 2 * half + 1]
                low[at] = jnp.where(sub < 4, a, rolled(b, 4))
                a, b = force[c, 4, j, 2 * half], force[c, 4, j, 2 * half + 1]
                high[at] = jnp.where(sub < 4, rolled(a, 4), b)


def pack_y(force, low, high):
    sub = rows_of()
    for c in range(3):
        for i in range(5):
            a, b = force[c, i, 0, 0], rolled(force[c, i, 4, 0], -3)
            for k in range(1, 4):
                a = jnp.where(sub % 4 == k, rolled(force[c, i, 0, k], k), a)
                b = jnp.where(sub % 4 == k, rolled(force[c, i, 4, k], k - 3), b)
            low[c * 5 + i] = a
            high[c * 5 + i] = b


def add_x(force, from_low, from_high):
    sub = rows_of()
    for c in range(3):
        for j in range(5):
            for half in range(2):
                at = (c * 5 + j) * 2 + half
                r, s = from_low[at], from_high[at]
                force[c, 0, j, 2 * half] += jnp.where(sub < 4, r, 0.0)
                force[c, 0, j, 2 * half + 1] += jnp.where(sub < 4, rolled(r, 4), 0.0)
                force[c, 4, j, 2 * half] += jnp.where(sub < 4, 0.0, rolled(s, 4))
                force[c, 4, j, 2 * half + 1] += jnp.where(sub < 4, 0.0, s)


def add_y(force, from_low, from_high):
    sub = rows_of()
    for c in range(3):
        for i in range(5):
            r, s = from_low[c * 5 + i], from_high[c * 5 + i]
            for k in range(4):
                force[c, i, 0, k] += jnp.where(sub % 4 == 0, rolled(r, -k), 0.0)
                force[c, i, 4, k] += jnp.where(sub % 4 == 3, rolled(s, 3 - k), 0.0)


def edge_kernel(extra, low, high, from_low, from_high, *outs):
    out_low, out_high = outs
    sub = rows_of()
    for c in range(3):
        for i in range(5):
            out_low[c * 5 + i] = low[c * 5 + i]
            out_high[c * 5 + i] = high[c * 5 + i]
        for i, came, first in ((0, from_low, 0), (4, from_high, 4)):
            for j, out, row in ((0, out_low, 0), (4, out_high, 3)):
                total = out[c * 5 + i]
                for k in range(4):
                    r = rolled(came[(c * 5 + j) * 2 + k // 2], first + k - (4 * (k % 2) + row))
                    total = total + jnp.where(sub == first + k, r, 0.0)
                out[c * 5 + i] = total
    if extra:
        for out, mine in ((out_low, low), (out_high, high)):
            out[15] = mine[15]
            out[16] = from_low[30]
            out[17] = from_high[30]


def region_grid(own, xl, xh, yl, yh):
    return [[yl[16], xl[30], yh[16]], [yl[15], own, yh[15]], [yl[17], xh[30], yh[17]]]


def shared_density(grid):
    sub = rows_of()
    across = []
    for y in range(3):
        low, mid, high = grid[0][y], grid[1][y], grid[2][y]
        turned = rolled(mid, 4)
        across.append([jnp.where(sub < 4, rolled(low, 4), turned), mid, jnp.where(sub < 4, turned, rolled(high, 4))])
    found = [[None] * 3 for _ in range(3)]
    for x in range(3):
        low, mid, high = across[0][x], across[1][x], across[2][x]
        found[x][0] = jnp.where(sub % 4 == 0, rolled(low, -3), rolled(mid, 1))
        found[x][1] = mid
        found[x][2] = jnp.where(sub % 4 == 3, rolled(high, 3), rolled(mid, -1))
    sums = []
    for x in ((1,), (0, 1), (1, 2)):
        row = []
        for y in ((1,), (0, 1), (1, 2)):
            total = sum(found[a][b] for a in x for b in y)
            row.append((total + shallower(total), total))
        sums.append(row)
    return sums


def mass_scales(sums):
    return [[[1.0 / s for s in pair] for pair in row] for row in sums]


def edge_kind(i):
    return 1 if i == 0 else 2 if i == 4 else 0


def accel_scale(i, j, k):
    return float(-1.0 / (half_size**3 * quad[i] * quad[j] * quad[k]))


def first_kernel(u, v, a, region, material, b_out, f_out, x_low, x_high, y_low, y_high,
                 elem, gx, gz, cross, planes, side, tall, nodes):
    table = depth_table()
    region_now = jnp.concatenate([region[0], region[1]], axis=0).astype(f32) + 1.0

    def one(c, carry):
        for t in range(4):
            lanes = slice(128 * t, 128 * t + 128)
            nodes[t] = u[c, :, :, lanes] + time_step * v[c, :, :, lanes] + 0.5 * time_step**2 * a[c, :, :, lanes]

        def put_u(k, value):
            elem[c, :, :, k] = value

        to_elements(nodes, table, tall, put_u)
        for t in range(4):
            lanes = slice(128 * t, 128 * t + 128)
            nodes[t] = u[c, :, :, lanes] + 2.0 * time_step * v[c, :, :, lanes] + time_step**2 * a[c, :, :, lanes]

        def put_b(k, value):
            b_out[c, :, :, k] = value

        to_elements(nodes, table, tall, put_b)
        return carry

    lax.fori_loop(0, 3, one, 0)
    internal(elem, f_out, lookup(material, 1, region_now), lookup(material, 2, region_now), gx, gz, cross, planes, side)
    pack_x(f_out, x_low, x_high)
    pack_y(f_out, y_low, y_high)
    x_low[30] = region_now
    x_high[30] = region_now
    y_low[15] = region_now
    y_high[15] = region_now


def second_kernel(b, f, xl, xh, yl, yh, region, material, a_out, f_out, x_low, x_high, y_low, y_high, scales,
                  elem, gx, gz, cross, planes, side):
    region_now = jnp.concatenate([region[0], region[1]], axis=0).astype(f32) + 1.0
    a_out[...] = f[...]
    add_x(a_out, xl, xh)
    add_y(a_out, yl, yh)
    grid = region_grid(region_now, xl, xh, yl, yh)
    inverse = mass_scales(shared_density([[lookup(material, 0, r) for r in row] for row in grid]))
    for x in range(3):
        for y in range(3):
            for z in range(2):
                scales[x, y, z] = inverse[x][y][z]
    for i in range(5):
        for j in range(5):
            for k in range(4):
                scale = scales[edge_kind(i), edge_kind(j), min(k, 1)] * accel_scale(i, j, k)
                for c in range(3):
                    value = a_out[c, i, j, k] * scale
                    a_out[c, i, j, k] = value
                    elem[c, i, j, k] = b[c, i, j, k] + time_step**2 * value
    internal(elem, f_out, lookup(material, 1, region_now), lookup(material, 2, region_now), gx, gz, cross, planes, side)
    pack_x(f_out, x_low, x_high)
    pack_y(f_out, y_low, y_high)


def last_kernel(a1, f, xl, xh, yl, yh, scales, surf1, surf2, u, v, a, u_out, v_out, a_out, tall, nodes, nodes2, force):
    table = depth_table(back=True)
    force[...] = f[...]
    add_x(force, xl, xh)
    add_y(force, yl, yh)
    for i in range(5):
        for j in range(5):
            for k in range(4):
                scale = scales[edge_kind(i), edge_kind(j), min(k, 1)] * accel_scale(i, j, k)
                for c in range(3):
                    force[c, i, j, k] = force[c, i, j, k] * scale
    lane = lanes_of((17, 128))
    for c in range(3):
        to_nodes(lambda k: a1[c, :, :, k], table, tall, nodes)
        to_nodes(lambda k: force[c, :, :, k], table, tall, nodes2)
        for x in range(9):
            at = 8 * (c * 9 + x)
            tile, shift = at // 128, (128 - at % 128) % 128
            moved = [rolled(s[0:17, 128 * tile : 128 * tile + 128], shift, 1) for s in (surf1, surf2)]
            direct = jnp.where(lane < 1, moved[0], 0.0)
            nodes[0, x] += direct
            nodes2[0, x] += direct + jnp.where(lane < 5, moved[1], 0.0)
        for t in range(4):
            at = (c, slice(None), slice(None), slice(128 * t, 128 * t + 128))
            first, second = nodes[t], nodes2[t]
            a_out[at] = second
            u_out[at] = u[at] + 2.0 * time_step * v[at] + time_step**2 * (a[at] + first)
            v_out[at] = v[at] + 0.5 * time_step * (a[at] + 2.0 * first + second)


def whole():
    return pl.BlockSpec(memory_space=pltpu.VMEM)


def scalars():
    return pl.BlockSpec(memory_space=pltpu.SMEM)


def call(kernel, ins, outs, scratch, smem=()):
    return pl.pallas_call(
        kernel,
        out_shape=[jax.ShapeDtypeStruct(s, f32) for s in outs],
        in_specs=[scalars() if n in smem else whole() for n in range(len(ins))],
        out_specs=[whole() for _ in outs],
        scratch_shapes=[pltpu.VMEM(s, f32) for s in scratch],
        compiler_params=pltpu.CompilerParams(vmem_limit_bytes=vmem_bytes),
    )(*ins)


element_shape = (3, 5, 5, 4, 8, 128)
lines_shape = (3, 5, 5, 5, 8, 128)
internal_scratch = [lines_shape, (3, 5, 5, 8, 128), lines_shape, lines_shape, lines_shape, (2, 5, 5, 8, 128)]


def exchange(axis, to_low, to_high):
    count = lax.axis_size(axis)
    up = [(i, i + 1) for i in range(count - 1)]
    down = [(j, i) for i, j in up]
    return lax.ppermute(to_high, axis, up), lax.ppermute(to_low, axis, down)


def extended_2(array, sides, width):
    for axis, dim in sides:
        count, length = (lax.axis_size(axis), array.shape[dim])
        up = [(i, (i + 1) % count) for i in range(count - 1)]
        down = [(j, i) for i, j in up]
        last = lax.slice_in_dim(array, length - width, length, axis=dim)
        first = lax.slice_in_dim(array, 0, width, axis=dim)
        before = lax.ppermute(last, axis, up)
        after = lax.ppermute(first, axis, down)
        array = jnp.concatenate([before, array, after], axis=dim)
    return array


def pressure_of(hydro_state):
    velocity = hydro_state[1:4] / hydro_state[0]
    pressure = (gamma_gas - 1.0) * (
        hydro_state[4] - 0.5 * jnp.sum(hydro_state[1:4] * velocity, axis=0)
    )
    return (velocity, pressure)


def euler_flux(hydro_state, axis_num):
    velocity, pressure = pressure_of(hydro_state)
    sound_speed = jnp.sqrt(gamma_gas * pressure / hydro_state[0])
    normal_vel = velocity[axis_num]
    unit_row = jnp.eye(3, dtype=jnp.float32)[axis_num].reshape(3, 1, 1, 1)
    momentum_flux = hydro_state[1:4] * normal_vel + pressure * unit_row
    energy_flux = (hydro_state[4] + pressure) * normal_vel
    flux_all = jnp.concatenate(
        [hydro_state[1 + axis_num][None], momentum_flux, energy_flux[None]], axis=0
    )
    return (flux_all, jnp.abs(normal_vel) + sound_speed)


def advance(padded):
    interior = padded[:, 1:-1, 1:-1, 1:-1]
    change = jnp.zeros_like(interior)
    for axis_num in range(3):
        pencil = padded
        for other_axis in range(3):
            if other_axis != axis_num:
                pencil = lax.slice_in_dim(
                    pencil, 1, pencil.shape[other_axis + 1] - 1, axis=other_axis + 1
                )
        flux_all, wave_speed = euler_flux(pencil, axis_num)
        length = pencil.shape[axis_num + 1]
        low_state = lax.slice_in_dim(pencil, 0, length - 1, axis=axis_num + 1)
        high_state = lax.slice_in_dim(pencil, 1, length, axis=axis_num + 1)
        low_flux = lax.slice_in_dim(flux_all, 0, length - 1, axis=axis_num + 1)
        high_flux = lax.slice_in_dim(flux_all, 1, length, axis=axis_num + 1)
        fastest = jnp.maximum(
            lax.slice_in_dim(wave_speed, 0, length - 1, axis=axis_num),
            lax.slice_in_dim(wave_speed, 1, length, axis=axis_num),
        )
        face_flux = 0.5 * (low_flux + high_flux) - 0.5 * fastest * (high_state - low_state)
        change = (
            change
            + lax.slice_in_dim(face_flux, 1, length - 1, axis=axis_num + 1)
            - lax.slice_in_dim(face_flux, 0, length - 2, axis=axis_num + 1)
        )
    return interior - cell_ratio * change


def surface_traction(hydro_state):
    bottom = hydro_state[:, :, :, -1]
    velocity, pressure = pressure_of(bottom[:, :, :, None])
    vertical = velocity[2, :, :, 0]
    return (
        jnp.stack(
            [bottom[1] * vertical, bottom[2] * vertical, bottom[3] * vertical + pressure[:, :, 0]]
        )
        * face_area
    )


def fix_edges(padded, depth):
    placings = (
        (lax.axis_index("gx"), lax.axis_size("gx"), 1),
        (lax.axis_index(("grp", "gy")), lax.axis_size(("grp", "gy")), 2),
    )
    for position, extent, axis_num in placings:
        length = padded.shape[axis_num]
        inner_low = lax.slice_in_dim(padded, depth, depth + 1, axis=axis_num)
        inner_high = lax.slice_in_dim(padded, length - depth - 1, length - depth, axis=axis_num)
        place = lax.broadcasted_iota(jnp.int32, padded.shape, axis_num)
        padded = jnp.where((position == 0) & (place < depth), inner_low, padded)
        padded = jnp.where((position == extent - 1) & (place >= length - depth), inner_high, padded)
    return padded


def pad_depth(padded):
    return jnp.pad(padded, ((0, 0), (0, 0), (0, 0), (1, 1)), mode="edge")


def surface_tables():
    lane = np.arange(128)
    j, ey = lane // 8, lane % 8
    used = (j < 5) & (ey < 6)
    place = np.where(used, ey + 1, -9)
    source = lane[:, None]
    centre = source == place
    meet = centre | ((j == 0) & (source == place - 1)) | ((j == 4) & (source == place + 1))
    along = np.zeros((128, 128))
    for a in range(40):
        for b in range(40):
            if a % 8 == b % 8 and a % 8 < 6:
                along[a, b] = deriv[b // 8, a // 8]
    node = np.where(used, 4 * (ey - 1) + j, -9)
    fold = (lane[:, None] == node) & (lane[:, None] < 17)
    keep = fold & ((j < 4) & (ey < 5) | (j == 4) & (ey == 4))
    return np.stack([centre, meet, along, along.T, fold, keep]).astype(np.float32)


def full_dot(x, y, back=False):
    dims = (((1,), (1 if back else 0,)), ((), ()))
    return lax.dot_general(x, y, dims, precision=lax.Precision.HIGHEST, preferred_element_type=f32)


def deposit(faces, nodes_y, base_x, base_y, total):
    rows = faces.shape[1]
    sub = rows_of((8, 512)).astype(f32)
    total[...] = jnp.zeros_like(total)

    def one(step, carry):
        def wide(q):
            block = faces[q, pl.ds(4 * step, 4), :]
            return jnp.concatenate([block[n : n + 1] for n in range(4)], axis=1)

        ids = wide(3)
        node_x = jnp.floor((ids + 0.5) * (1.0 / nodes_y))
        rel_y = jnp.broadcast_to(ids - node_x * nodes_y - base_y, (8, 512))
        rel_x = jnp.broadcast_to(node_x - base_x, (8, 512))
        left = []
        hits = [(rel_x - i == 4.0 * sub) & (sub < 4.0) for i in range(5)]
        parts = [split_three(wide(c)) for c in range(3)]
        for part in range(3):
            for c in range(3):
                value = jnp.broadcast_to(parts[c][part].astype(f32), (8, 512))
                left += [jnp.where(hit, value, 0.0) for hit in hits]
        right = [jnp.where((rel_y - j == 4.0 * sub) & (sub < 6.0), 1.0, 0.0) for j in range(5)]
        right.append(jnp.zeros((88, 512), f32))
        left, right = jnp.concatenate(left, axis=0), jnp.concatenate(right, axis=0)
        total[...] += lax.dot_general(
            left.astype(jnp.bfloat16), right.astype(jnp.bfloat16), (((1,), (1,)), ((), ())), preferred_element_type=f32
        )
        return carry

    lax.fori_loop(0, rows // 4, one, 0)


def top_grid(grid, z):
    sub, lane = rows_of(), lanes_of()
    out = jnp.zeros((8, 128), f32)
    for x in range(3):
        total = jnp.zeros((8, 128), f32)
        for y in range(3):
            column = jnp.broadcast_to(grid[x][y][:, z : z + 1], (8, 128))
            total = total + jnp.where((lane == 4 * y + (sub & 3) - 2), column, 0.0)
        total = total + rolled(total, -1)
        total = total + rolled(total, -2)
        for ex in range(2):
            out = jnp.where(sub == 2 * x + ex, rolled(total, 2 * x + ex - 4 * ex), out)
    return out


def respond(total, grid, material, tables, out1, out2):
    sub, lane = rows_of(), lanes_of()
    top, below = top_grid(grid, 0), top_grid(grid, 1)
    centre, meet, along, along_t, fold, keep = [tables[n] for n in range(6)]
    sums0 = full_dot(lookup(material, 0, top), meet)
    sums1 = full_dot(lookup(material, 0, below), meet)
    lame = rolled(full_dot(lookup(material, 1, top), centre), -1)
    shear = rolled(full_dot(lookup(material, 2, top), centre), -1)
    weight_y = jnp.ones((8, 128), f32)
    for j in range(5):
        weight_y = jnp.where(lane // 8 == j, float(quad[j]), weight_y)

    def inverse(sums):
        mid = rolled(sums, -1)
        found = {0: mid + sums, 1: mid, 4: mid + rolled(sums, -2)}
        found = {i: jnp.where(s > 0.0, 1.0 / (s * weight_y), 0.0) for i, s in found.items()}
        found[2] = found[3] = found[1]
        return found

    light, heavy = inverse(sums0), inverse(sums0 + sums1)
    first = [[None] * 5 for _ in range(3)]
    moved = [[None] * 5 for _ in range(3)]
    for c in range(3):
        for i in range(5):
            at = (c * 5 + i) * 8
            force = total[at : at + 8] + total[at + 120 : at + 128] + total[at + 240 : at + 248]
            first[c][i] = force * light[i] * -accel_scale(i, 2, 0) * float(quad[2])
            moved[c][i] = first[c][i] * time_step**2
    gx = [line(deriv, moved[c]) for c in range(3)]
    gy = full_dot(jnp.concatenate([moved[c][i] for c in range(3) for i in range(5)], axis=0), along)
    gy = [[gy[(c * 5 + i) * 8 : (c * 5 + i) * 8 + 8] for i in range(5)] for c in range(3)]
    lame_w, shear_w = lame * weight_y * 2.0, shear * weight_y * 2.0
    d00 = float(deriv[0, 0])
    sx = [[], [], []]
    sy = [[], [], []]
    sz = [[], [], []]
    qs = [[], [], []]
    pressed = []
    for i in range(5):
        lw, mw = lame_w * float(quad[i]), shear_w * float(quad[i])
        d = [moved[c][i] for c in range(3)]
        gz = [d00 * x for x in d]
        dilated = lw * (gx[0][i] + gy[1][i] + gz[2])
        s01 = mw * (gx[1][i] + gy[0][i])
        s02 = mw * (gx[2][i] + gz[0])
        s12 = mw * (gy[2][i] + gz[1])
        for c, value in enumerate((dilated + 2.0 * mw * gx[0][i], s01, s02)):
            sx[c].append(value)
        for c, value in enumerate((s01, dilated + 2.0 * mw * gy[1][i], s12)):
            sy[c].append(value)
        for c, value in enumerate((s02, s12, dilated + 2.0 * mw * gz[2])):
            sz[c].append(value)
        for c, value in enumerate((mw * d[0], mw * d[1], (lw + 2.0 * mw) * d[2])):
            qs[c].append(value)
        pressed.append(lw * d[2])
    ydiv = full_dot(jnp.concatenate(sy[0] + sy[1] + sy[2] + pressed + qs[1], axis=0), along_t)
    ydiv = [[ydiv[(n * 5 + i) * 8 : (n * 5 + i) * 8 + 8] for i in range(5)] for n in range(5)]
    xdiv = [line(deriv_t, v) for v in sx + [pressed, qs[0]]]
    base = [xdiv[3], ydiv[3], [p + q for p, q in zip(xdiv[4], ydiv[4])]]
    second = {}
    for c in range(3):
        for i in range(5):
            for l in range(5):
                stiff = float(sum(deriv[k, l] * quad[k] * deriv[k, 0] for k in range(1, 5)))
                value = float(deriv[0, l] * quad[0]) * sz[c][i] + stiff * qs[c][i]
                if l:
                    value = value + float(deriv[l, 0] * quad[l]) * base[c][i]
                else:
                    value = value + float(quad[0]) * (xdiv[c][i] + ydiv[c][i])
                scale = (heavy if l == 4 else light)[i]
                second[c, i, l] = value * scale * (accel_scale(i, 2, l) * float(quad[2]))
    rows1, rows2 = [], []
    for c in range(3):
        for x in range(9):
            own = 1 if x < 4 else 2
            rows1.append(jnp.where(sub == 0, rolled(first[c][x - 4 * (own - 1)], -own), 0.0))
            block = jnp.zeros((8, 128), f32)
            for l in range(5):
                for ex in range(4):
                    i = x - 4 * (ex - 1)
                    if 0 <= i <= 4:
                        block = block + jnp.where(sub == l, rolled(second[c, i, l], l - ex), 0.0)
            rows2.append(block)
    blank = [jnp.zeros((40, 128), f32)]
    out1[...] = full_dot(keep[0:24], jnp.concatenate(rows1 + blank, axis=0), back=True)
    out2[...] = full_dot(fold[0:24], jnp.concatenate(rows2 + blank, axis=0), back=True)


def surface_kernel(nodes_y, faces, here, region, xl, xh, yl, yh, material, tables, out1, out2, total):
    base_x = (8 * here[0] - 4).astype(f32)
    base_y = (16 * here[1] - 4).astype(f32)
    deposit(faces, nodes_y, base_x, base_y, total)
    region_now = jnp.concatenate([region[0], region[1]], axis=0).astype(f32) + 1.0
    respond(total, region_grid(region_now, xl, xh, yl, yh), material, tables, out1, out2)


def shards(density, momentum, energy, displacement, velocity_field, acceleration, material, element_region_index,
           face_dest, face_slot):
    along_y = ("grp", "gy")
    place_x, place_y = lax.axis_index("gx"), lax.axis_index(along_y)
    nodes_y = 16 * lax.axis_size(along_y) + 1
    region = element_region_index
    b, f, x_low, x_high, y_low, y_high = call(
        first_kernel,
        (displacement, velocity_field, acceleration, region, material),
        [element_shape, element_shape, (31, 8, 128), (31, 8, 128), (16, 8, 128), (16, 8, 128)],
        internal_scratch + [(5, 5, 8, 512), (4, 9, 17, 128)],
        smem=(4,),
    )
    xl, xh = exchange("gx", x_low, x_high)
    y_low, y_high = call(
        functools.partial(edge_kernel, True), (y_low, y_high, xl, xh), [(18, 8, 128), (18, 8, 128)], []
    )
    yl, yh = exchange(along_y, y_low, y_high)
    hydro_state = jnp.concatenate([density[None], momentum, energy[None]], axis=0)
    for repeat in range(2):
        padded = extended_2(hydro_state, (("gx", 1), (("grp", "gy"), 2)), 1)
        hydro_state = advance(pad_depth(fix_edges(padded, 1)))
    traction = surface_traction(hydro_state).reshape(3, -1)
    targets, slots = face_dest[0, :, 0], face_slot[0]
    count_x, count_gy = lax.axis_size("gx"), lax.axis_size("gy")
    node_x = targets // count_gy % count_x * 8 + slots // 17
    node_y = (targets // (count_gy * count_x) * count_gy + targets % count_gy) * 16 + slots % 17
    ids = (node_x * nodes_y + node_y).astype(f32)
    faces = lax.all_gather(
        jnp.concatenate([traction, ids[None]], axis=0)[:, None, :], ("grp", "gx", "gy"), axis=1, tiled=True
    )
    here = jnp.stack([place_x, place_y]).astype(jnp.int32)
    surf1, surf2 = call(
        functools.partial(surface_kernel, float(nodes_y)),
        (faces, here, region, xl, xh, yl, yh, material, jnp.asarray(surface_tables())),
        [(24, 256), (24, 256)],
        [(360, 128)],
        smem=(1, 7),
    )
    a1, f2, x_low, x_high, y_low, y_high, scales = call(
        second_kernel,
        (b, f, xl, xh, yl, yh, region, material),
        [element_shape, element_shape, (30, 8, 128), (30, 8, 128), (15, 8, 128), (15, 8, 128), (3, 3, 2, 8, 128)],
        internal_scratch,
        smem=(7,),
    )
    xl2, xh2 = exchange("gx", x_low, x_high)
    y_low, y_high = call(
        functools.partial(edge_kernel, False), (y_low, y_high, xl2, xh2), [(15, 8, 128), (15, 8, 128)], []
    )
    yl2, yh2 = exchange(along_y, y_low, y_high)
    u_out, v_out, a_out = call(
        last_kernel,
        (a1, f2, xl2, xh2, yl2, yh2, scales, surf1, surf2, displacement, velocity_field, acceleration),
        [displacement.shape] * 3,
        [(5, 5, 8, 512), (4, 9, 17, 128), (4, 9, 17, 128), element_shape],
    )
    return hydro_state, u_out, v_out, a_out


def solution(mesh):
    field = P(None, "gx", ("grp", "gy"), None)
    cells = P("gx", ("grp", "gy"), None)
    rank = ("grp", "gx", "gy")
    return jax.shard_map(
        shards,
        mesh=mesh,
        in_specs=(cells, field, cells, field, field, field, P(), cells, P(rank, None, None), P(rank, None)),
        out_specs=(field, field, field, field),
        check_vma=False,
    )
```

time: 375 us -> 169 us (0.45)
  the two profiles are of different devices: /device:TPU:9 before, /device:TPU:0 now
where the time goes in v1:
time: 169 us; the launch traced here: 167 us
  blocking collectives  45 us (27%)
  starting transfers between devices  42.8 us (25%)
  other arithmetic  31 us (18%)
  local copies, waits for them, and re-layouts  23.5 us (14%)
  Pallas kernels  20.2 us (12%)
  waiting for transfers between devices  3.05 us (2%)
  between operations  1.71 us (1%)
    all_gather x1, blocking collectives, shards(): lax.all_gather(jnp.concatenate([traction, ids[None]], axis=0)[:, None, :]...  45 us
    ppermute x8, starting transfers between devices, exchange(): return (lax.ppermute(to_high, axis, up), lax.ppermute(to_low, axis, down))  22.4 us
    pallas_call x6, Pallas kernels, call(): pl.pallas_call(kernel, out_shape=[jax.ShapeDtypeStruct(s, f32) for s in o...  20.2 us
    unnamed x64, local copies, waits for them, and re-layouts  16.7 us
    ppermute x4, starting transfers between devices, extended_2(): before = lax.ppermute(last, axis, up)  15.1 us
    ppermute x4, starting transfers between devices, extended_2(): after = lax.ppermute(first, axis, down)  5.3 us
    reduce_sum x7, other arithmetic, pressure_of(): jnp.sum(hydro_state[1:4] * velocity, axis=0)  4 us
  transfers between devices with their start and end apart: 16, of which 2 were waited for; matrix products, arithmetic and copies ran while one was open for 24% of the time, Pallas kernels for 10%

profile of v1, /device:TPU:0, one launch (start us, length us, event | category | flops | bytes accessed | tf_op | source)
XLA Modules:
  0.0 167.3 jit_solution(7773889719929568434)
XLA Ops:
  0.6 1.8 %pad_maximum_fusion.19 = (f32[5,1,32,256]{3,2,0,1:T(8,128)}, f32[5,1,32,256]{3,2,0,1:T(8,128)}) fusion(f32[1,4,32,256]{3,2,0,1:T(8,128)} %bitcast.238, f32[1,4,32,256]{3,2,0,1:T(8,128)} %bitcast.257, f32[3,4,32,256]{3,2,1,0:T(8,128)} %param.12), kind=kLoop, calls=%fused_computation.151 | loop fusion | flops 163840 | bytes 983040 | tf_op jit(solution)/shard_map/slice | solution.py:436
  2.4 4.8 %collective-permute-start = (f32[5,1,32,256]{3,2,0,1:T(8,128)}, f32[5,1,32,256]{3,2,0,1:T(8,128)S(1)}, u32[]{:S(2)}, u32[]{:S(2)}) collective-permute-start(f32[5,1,32,256]{3,2,0,1:T(8,128)} %get-tuple-element.108), channel_id=1, source_target_pairs={{0,2},{2,4},{4,6},{6,8},{8,10},{10,12},{12,14},{1,3},{3,5},{5,7},{... | collective-permute-start | bytes 491528 | tf_op jit(solution)/shard_map/ppermute | solution.py:438
  7.3 1.4 collective-permute-start.1
  8.7 1.6 copy.126.u
  10.7 0.9 copy-done.25
  12.3 7.5 %shard_map.138 = (f32[3,5,5,4,8,128]{5,4,3,2,1,0:T(8,128)S(1)}, f32[3,5,5,4,8,128]{5,4,3,2,1,0:T(8,128)S(1)}, f32[31,8,128]{2,1,0:T(8,128)S(1)}, f32[31,8,128]{2...) custom-call(f32[3,9,17,512]{3,2,1,0:T(8,128)S(1)} %copy.126.u, f32[3,9,17,512]{3,2,1,0:T(8,128)S(1)} %copy.127.v, ...), custom_call_target="tpu_custom_call" | custom-call | tf_op jit(solution)/shard_map/pallas_call | solution.py:409
  19.9 1.0 copy-done.6
  20.9 1.0 copy-done.8
  21.9 4.5 %collective-permute-start.8 = (f32[31,8,128]{2,1,0:T(8,128)S(1)}, f32[31,8,128]{2,1,0:T(8,128)S(1)}, u32[]{:S(2)}, u32[]{:S(2)}) collective-permute-start(f32[31,8,128]{2,1,0:T(8,128)S(1)} %get-tuple-element.28), channel_id=1, source_target_pairs={{0,2},{2,4},{4,6},{6,8},{8,10},{10,12},{12,14},{1,3},{3,5},{5,7},{... | collective-permute-start | bytes 380936 | tf_op jit(solution)/shard_map/ppermute | solution.py:428
  26.5 1.3 collective-permute-start.9
  27.9 1.2 pad_maximum_fusion.27
  29.0 1.3 collective-permute-start.2
  30.3 1.3 collective-permute-start.3
  31.7 2.0 %collective-permute-done.9.from_high.xh = f32[31,8,128]{2,1,0:T(8,128)S(1)} collective-permute-done((f32[31,8,128]{2,1,0:T(8,128)S(1)}, f32[31,8,128]{2,1,0:T(8,128)S(1)}, u32[]{:S(2)}, u32[]{:S(2)}) %collective-permute-start.9) | collective-permute-done | bytes 127008 | tf_op jit(solution)/shard_map/ppermute | solution.py:428
  33.7 2.8 %collective-permute-start.10 = (f32[18,8,128]{2,1,0:T(8,128)S(1)}, f32[18,8,128]{2,1,0:T(8,128)S(1)}, u32[]{:S(2)}, u32[]{:S(2)}) collective-permute-start(f32[18,8,128]{2,1,0:T(8,128)S(1)} %get-tuple-element.32), channel_id=1, source_target_pairs={{0,1},{1,16},{16,17},{2,3},{3,18},{18,19},{4,5},{5,20},{20,21},{6,... | collective-permute-start | bytes 221192 | tf_op jit(solution)/shard_map/ppermute | solution.py:428
  36.5 1.3 collective-permute-start.11
  37.8 1.1 pad_maximum_fusion
  39.0 1.2 select_select_fusion.3
  40.2 1.5 fusion.78
  44.5 1.3 multiply_reduce_fusion.3
  45.9 1.1 fusion.43
  47.0 1.4 select_select_fusion.2
  49.3 0.9 bitcast_multiply_fusion.1
  52.8 5.1 %collective-permute-start.4 = (f32[5,1,32,256]{3,2,0,1:T(8,128)S(1)}, f32[5,1,32,256]{3,2,0,1:T(8,128)S(1)}, u32[]{:S(2)}, u32[]{:S(2)}) collective-permute-start(f32[5,1,32,256]{3,2,0,1:T(8,128)S(1)} %get-tuple-element.106), channel_id=1, source_target_pairs={{0,2},{2,4},{4,6},{6,8},{8,10},{10,12},{12,14},{1,3},{3,5},{5,7},{... | collective-permute-start | bytes 491528 | tf_op jit(solution)/shard_map/ppermute | solution.py:438
  58.0 1.3 collective-permute-start.5
  59.8 3.9 %shard_map.140 = (f32[3,5,5,4,8,128]{5,4,3,2,1,0:T(8,128)S(1)}, f32[3,5,5,4,8,128]{5,4,3,2,1,0:T(8,128)S(1)}, f32[30,8,128]{2,1,0:T(8,128)S(1)}, f32[30,8,128]{2...) custom-call(f32[3,5,5,4,8,128]{5,4,3,2,1,0:T(8,128)S(1)} %copy-done.7, ...), custom_call_target="tpu_custom_call" | custom-call | tf_op jit(solution)/shard_map/pallas_call | solution.py:409
  63.9 5.4 %collective-permute-start.12 = (f32[30,8,128]{2,1,0:T(8,128)S(1)}, f32[30,8,128]{2,1,0:T(8,128)S(1)}, u32[]{:S(2)}, u32[]{:S(2)}) collective-permute-start(f32[30,8,128]{2,1,0:T(8,128)S(1)} %get-tuple-element.36), channel_id=1, source_target_pairs={{0,2},{2,4},{4,6},{6,8},{8,10},{10,12},{12,14},{1,3},{3,5},{5,7},{... | collective-permute-start | bytes 368648 | tf_op jit(solution)/shard_map/ppermute | solution.py:428
  69.3 1.3 collective-permute-start.13
  70.7 3.9 %collective-permute-start.6 = (f32[5,6,1,256]{3,2,0,1:T(1,128)S(1)}, f32[5,6,1,256]{3,2,0,1:T(1,128)S(1)}, u32[]{:S(2)}, u32[]{:S(2)}) collective-permute-start(f32[5,6,1,256]{3,2,0,1:T(1,128)S(1)} %get-tuple-element.102), channel_id=1, source_target_pairs={{0,1},{1,16},{16,17},{2,3},{3,18},{18,19},{4,5},{5,20},{20,21},{6,... | collective-permute-start | bytes 92168 | tf_op jit(solution)/shard_map/ppermute | solution.py:438
  74.6 1.3 collective-permute-start.7
  76.6 0.9 collective-permute-done.13.from_high.xh
  78.2 4.5 %collective-permute-start.14 = (f32[15,8,128]{2,1,0:T(8,128)}, f32[15,8,128]{2,1,0:T(8,128)}, u32[]{:S(2)}, u32[]{:S(2)}) collective-permute-start(f32[15,8,128]{2,1,0:T(8,128)} %get-tuple-element.40), channel_id=1, source_target_pairs={{0,1},{1,16},{16,17},{2,3},{3,18},{18,19},{4,5},{5,20},{20,21},{6,... | collective-permute-start | bytes 184328 | tf_op jit(solution)/shard_map/ppermute | solution.py:428
  82.7 1.3 collective-permute-start.15
  93.6 1.3 mul.683
  94.8 1.8 %fusion.63 = (f32[4,32]{1,0:T(4,128)}, f32[4,32]{1,0:T(4,128)}, f32[4,32]{1,0:T(4,128)}, f32[4,32]{1,0:T(4,128)}) fusion(f32[5,4,32,256]{3,2,0,1:T(8,128)} %copy-done.23, f32[3,4,32,1]{3,2,0,1:T(8,128)} %get-tuple-element.65), kind=kLoop, calls=%fused_computation.180 | loop fusion | flops 384 | bytes 4608 | tf_op jit(solution)/shard_map/mul | solution.py:500
  96.7 1.3 mul.675
  98.0 1.3 mul.679
  99.3 1.3 mul.677
  100.5 1.3 squeeze.22
  103.9 2.0 %copy.132 = f32[5,4,32,256]{3,2,1,0:T(8,128)} copy(f32[5,4,32,256]{3,2,0,1:T(8,128)} %copy-done.23) | data formatting | bytes 1310720
  105.9 45.0 %all-gather = f32[4,4096]{1,0:T(4,128)S(1)} all-gather(f32[4,128]{1,0:T(4,128)S(1)} %pad_maximum_fusion.28), channel_id=2, replica_groups=mesh['grp'=2,'gx'=8,'gy'=2] {'grp','gx','gy'}, dimensions={1}, use_global_device_ids=true | all-gather | bytes 67584 | tf_op jit(solution)/shard_map/all_gather | solution.py:720
  151.6 4.1 %shard_map.142 = (f32[24,256]{1,0:T(8,128)S(1)}, f32[24,256]{1,0:T(8,128)S(1)}) custom-call(f32[4,32,128]{2,1,0:T(8,128)S(1)} %bitcast.237, s32[2]{0:T(128)S(1)} %copy-done.19, s32[2,4,128]{2,1,0:T(4,128)S(1)} %copy-done.17, f32[31,8,128]{2,1,0:T(8,128)S(1)} %collective-permute-done.8.from_low.xl, f32[31,8,128]{2,1,0:T(8,128)S(1)} %collective-permute-done.9.from_high.xh, ...), custom_call_target="tpu_custom_call" | custom-call | tf_op jit(solution)/shard_map/pallas_call | solution.py:409
  155.7 1.3 copy-done.3
  157.0 1.3 copy-done.5
  158.3 4.0 %shard_map.143 = (f32[3,9,17,512]{3,2,1,0:T(8,128)S(1)}, f32[3,9,17,512]{3,2,1,0:T(8,128)S(1)}, f32[3,9,17,512]{3,2,1,0:T(8,128)S(1)}) custom-call(f32[3,5,5,4,8,128]{5,4,3,2,1,0:T(8,128)S(1)} %copy-done.3, f32[3,5,5,4,8,128]{5,4,3,2,1,0:T(8,128)S(1)} %copy-done.5, f32[30,8,128]{2,1,0:T(8,128)S(1)} %collective-permute-done.12.from_low.xl, ...), custom_call_target="tpu_custom_call" | custom-call | tf_op jit(solution)/shard_map/pallas_call | solution.py:409
  162.3 1.7 %copy.133 = f32[3,9,17,512]{3,0,2,1:T(4,128)} copy(f32[3,9,17,512]{3,2,1,0:T(8,128)S(1)} %get-tuple-element.57) | data formatting | bytes 1880064
  164.0 1.7 %copy.134 = f32[3,9,17,512]{3,0,2,1:T(4,128)} copy(f32[3,9,17,512]{3,2,1,0:T(8,128)S(1)} %get-tuple-element.58) | data formatting | bytes 1880064
  165.6 1.7 %copy.135 = f32[3,9,17,512]{3,0,2,1:T(4,128)} copy(f32[3,9,17,512]{3,2,1,0:T(8,128)S(1)} %get-tuple-element.59) | data formatting | bytes 1880064
  (150 shorter events, 21.5 us)
Async XLA Ops:
  2.4 25.5 %collective-permute-start = (f32[5,1,32,256]{3,2,0,1:T(8,128)}, f32[5,1,32,256]{3,2,0,1:T(8,128)S(1)}, u32[]{:S(2)}, u32[]{:S(2)}) collective-permute-start(f32[5,1,32,256]{3,2,0,1:T(8,128)} %get-tuple-element.108), channel_id=1, source_target_pairs={{0,2},{2,4},{4,6},{6,8},{8,10},{10,12},{12,14},{1,3},{3,5},{5,7},{... | collective-permute-start | bytes 491528 | tf_op jit(solution)/shard_map/ppermute | solution.py:438
  7.2 3.1 %copy-start.24 = (f32[3,9,17,512]{3,0,2,1:T(4,128)S(1)}, f32[3,9,17,512]{3,0,2,1:T(4,128)}, u32[]{:S(2)}) copy-start(f32[3,9,17,512]{3,0,2,1:T(4,128)} %param.15) | copy-start | bytes 2820100
  7.3 20.6 %collective-permute-start.1 = (f32[5,1,32,256]{3,2,0,1:T(8,128)}, f32[5,1,32,256]{3,2,0,1:T(8,128)}, u32[]{:S(2)}, u32[]{:S(2)}) collective-permute-start(f32[5,1,32,256]{3,2,0,1:T(8,128)} %get-tuple-element.109), channel_id=1, source_target_pairs={{2,0},{4,2},{6,4},{8,6},{10,8},{12,10},{14,12},{3,1},{5,3},{7,5},{... | collective-permute-start | bytes 491528 | tf_op jit(solution)/shard_map/ppermute | solution.py:439
  10.3 1.3 copy-start.25
  11.6 0.7 copy-start.17
  11.6 0.7 copy-start.18
  12.3 7.5 %copy-start = (f32[3,9,17,512]{3,2,1,0:T(8,128)}, f32[3,9,17,512]{3,2,1,0:T(8,128)S(1)}, u32[]{:S(2)}) copy-start(f32[3,9,17,512]{3,2,1,0:T(8,128)S(1)} %copy.128.a) | copy-start | bytes 2820100
  19.8 1.0 copy-start.6
  20.9 1.0 copy-start.8
  21.9 9.7 %collective-permute-start.8 = (f32[31,8,128]{2,1,0:T(8,128)S(1)}, f32[31,8,128]{2,1,0:T(8,128)S(1)}, u32[]{:S(2)}, u32[]{:S(2)}) collective-permute-start(f32[31,8,128]{2,1,0:T(8,128)S(1)} %get-tuple-element.28), channel_id=1, source_target_pairs={{0,2},{2,4},{4,6},{6,8},{8,10},{10,12},{12,14},{1,3},{3,5},{5,7},{... | collective-permute-start | bytes 380936 | tf_op jit(solution)/shard_map/ppermute | solution.py:428
  26.5 7.2 %collective-permute-start.9 = (f32[31,8,128]{2,1,0:T(8,128)S(1)}, f32[31,8,128]{2,1,0:T(8,128)S(1)}, u32[]{:S(2)}, u32[]{:S(2)}) collective-permute-start(f32[31,8,128]{2,1,0:T(8,128)S(1)} %get-tuple-element.29), channel_id=1, source_target_pairs={{2,0},{4,2},{6,4},{8,6},{10,8},{12,10},{14,12},{3,1},{5,3},{7,5},{... | collective-permute-start | bytes 380936 | tf_op jit(solution)/shard_map/ppermute | solution.py:428
  27.8 10.0 %copy-start.20 = (f32[3,4,32,256]{3,2,1,0:T(8,128)S(1)}, f32[3,4,32,256]{3,2,1,0:T(8,128)}, u32[]{:S(2)}) copy-start(f32[3,4,32,256]{3,2,1,0:T(8,128)} %param.12) | copy-start | bytes 1179652
  27.8 10.0 %copy-start.21 = (f32[4,32,256]{2,1,0:T(8,128)S(1)}, f32[4,32,256]{2,1,0:T(8,128)}, u32[]{:S(2)}) copy-start(f32[4,32,256]{2,1,0:T(8,128)} %param.13) | copy-start | bytes 393220
  27.8 10.0 %copy-start.22 = (f32[4,32,256]{2,1,0:T(8,128)S(1)}, f32[4,32,256]{2,1,0:T(8,128)}, u32[]{:S(2)}) copy-start(f32[4,32,256]{2,1,0:T(8,128)} %param.11) | copy-start | bytes 393220
  29.0 8.8 %collective-permute-start.2 = (f32[5,6,1,256]{3,2,0,1:T(1,128)S(1)}, f32[5,6,1,256]{3,2,0,1:T(1,128)S(1)}, u32[]{:S(2)}, u32[]{:S(2)}) collective-permute-start(f32[5,6,1,256]{3,2,0,1:T(1,128)S(1)} %get-tuple-element.104), channel_id=1, source_target_pairs={{0,1},{1,16},{16,17},{2,3},{3,18},{18,19},{4,5},{5,20},{20,21},{6,... | collective-permute-start | bytes 92168 | tf_op jit(solution)/shard_map/ppermute | solution.py:438
  30.3 7.5 %collective-permute-start.3 = (f32[5,6,1,256]{3,2,0,1:T(1,128)S(1)}, f32[5,6,1,256]{3,2,0,1:T(1,128)S(1)}, u32[]{:S(2)}, u32[]{:S(2)}) collective-permute-start(f32[5,6,1,256]{3,2,0,1:T(1,128)S(1)} %get-tuple-element.105), channel_id=1, source_target_pairs={{1,0},{16,1},{17,16},{3,2},{18,3},{19,18},{5,4},{20,5},{21,20},{7,... | collective-permute-start | bytes 92168 | tf_op jit(solution)/shard_map/ppermute | solution.py:439
  33.7 26.1 %collective-permute-start.10 = (f32[18,8,128]{2,1,0:T(8,128)S(1)}, f32[18,8,128]{2,1,0:T(8,128)S(1)}, u32[]{:S(2)}, u32[]{:S(2)}) collective-permute-start(f32[18,8,128]{2,1,0:T(8,128)S(1)} %get-tuple-element.32), channel_id=1, source_target_pairs={{0,1},{1,16},{16,17},{2,3},{3,18},{18,19},{4,5},{5,20},{20,21},{6,... | collective-permute-start | bytes 221192 | tf_op jit(solution)/shard_map/ppermute | solution.py:428
  36.5 23.3 %collective-permute-start.11 = (f32[18,8,128]{2,1,0:T(8,128)S(1)}, f32[18,8,128]{2,1,0:T(8,128)S(1)}, u32[]{:S(2)}, u32[]{:S(2)}) collective-permute-start(f32[18,8,128]{2,1,0:T(8,128)S(1)} %get-tuple-element.33), channel_id=1, source_target_pairs={{1,0},{16,1},{17,16},{3,2},{18,3},{19,18},{5,4},{20,5},{21,20},{7,... | collective-permute-start | bytes 221192 | tf_op jit(solution)/shard_map/ppermute | solution.py:428
  52.4 6.9 %copy-start.26 = (s32[1,128]{1,0:T(1,128)S(1)}, s32[1,128]{1,0:T(1,128)}, u32[]{:S(2)}) copy-start(s32[1,128]{1,0:T(1,128)} %param.20) | copy-start | bytes 1540
  52.4 6.9 %copy-start.27 = (s32[1,128,1]{1,2,0:T(1,128)S(1)}, s32[1,128,1]{1,2,0:T(1,128)}, u32[]{:S(2)}) copy-start(s32[1,128,1]{1,2,0:T(1,128)} %param.19) | copy-start | bytes 1540
  52.4 7.4 %copy-start.7 = (f32[3,5,5,4,8,128]{5,4,3,2,1,0:T(8,128)S(1)}, f32[3,5,5,4,8,128]{5,4,3,2,1,0:T(8,128)}, u32[]{:S(2)}) copy-start(f32[3,5,5,4,8,128]{5,4,3,2,1,0:T(8,128)} %copy-done.6) | copy-start | bytes 3686404
  52.4 7.4 %copy-start.9 = (f32[3,5,5,4,8,128]{5,4,3,2,1,0:T(8,128)S(1)}, f32[3,5,5,4,8,128]{5,4,3,2,1,0:T(8,128)}, u32[]{:S(2)}) copy-start(f32[3,5,5,4,8,128]{5,4,3,2,1,0:T(8,128)} %copy-done.8) | copy-start | bytes 3686404
  52.8 17.8 %collective-permute-start.4 = (f32[5,1,32,256]{3,2,0,1:T(8,128)S(1)}, f32[5,1,32,256]{3,2,0,1:T(8,128)S(1)}, u32[]{:S(2)}, u32[]{:S(2)}) collective-permute-start(f32[5,1,32,256]{3,2,0,1:T(8,128)S(1)} %get-tuple-element.106), channel_id=1, source_target_pairs={{0,2},{2,4},{4,6},{6,8},{8,10},{10,12},{12,14},{1,3},{3,5},{5,7},{... | collective-permute-start | bytes 491528 | tf_op jit(solution)/shard_map/ppermute | solution.py:438
  58.0 12.7 %collective-permute-start.5 = (f32[5,1,32,256]{3,2,0,1:T(8,128)S(1)}, f32[5,1,32,256]{3,2,0,1:T(8,128)S(1)}, u32[]{:S(2)}, u32[]{:S(2)}) collective-permute-start(f32[5,1,32,256]{3,2,0,1:T(8,128)S(1)} %get-tuple-element.107), channel_id=1, source_target_pairs={{2,0},{4,2},{6,4},{8,6},{10,8},{12,10},{14,12},{3,1},{5,3},{7,5},{... | collective-permute-start | bytes 491528 | tf_op jit(solution)/shard_map/ppermute | solution.py:439
  59.8 4.0 %copy-start.11 = (f32[18,8,128]{2,1,0:T(8,128)}, f32[18,8,128]{2,1,0:T(8,128)S(1)}, u32[]{:S(2)}) copy-start(f32[18,8,128]{2,1,0:T(8,128)S(1)} %collective-permute-done.10.yl) | copy-start | bytes 221188
  59.8 4.0 %copy-start.13 = (f32[18,8,128]{2,1,0:T(8,128)}, f32[18,8,128]{2,1,0:T(8,128)S(1)}, u32[]{:S(2)}) copy-start(f32[18,8,128]{2,1,0:T(8,128)S(1)} %collective-permute-done.11.yh) | copy-start | bytes 221188
  63.8 20.3 %copy-start.2 = (f32[3,5,5,4,8,128]{5,4,3,2,1,0:T(8,128)}, f32[3,5,5,4,8,128]{5,4,3,2,1,0:T(8,128)S(1)}, u32[]{:S(2)}) copy-start(f32[3,5,5,4,8,128]{5,4,3,2,1,0:T(8,128)S(1)} %get-tuple-element.34.a1) | copy-start | bytes 3686404
  63.8 20.3 %copy-start.4 = (f32[3,5,5,4,8,128]{5,4,3,2,1,0:T(8,128)}, f32[3,5,5,4,8,128]{5,4,3,2,1,0:T(8,128)S(1)}, u32[]{:S(2)}) copy-start(f32[3,5,5,4,8,128]{5,4,3,2,1,0:T(8,128)S(1)} %get-tuple-element.35.f) | copy-start | bytes 3686404
  63.8 20.3 %copy-start.15 = (f32[3,3,2,8,128]{4,3,2,1,0:T(8,128)}, f32[3,3,2,8,128]{4,3,2,1,0:T(8,128)S(1)}, u32[]{:S(2)}) copy-start(f32[3,3,2,8,128]{4,3,2,1,0:T(8,128)S(1)} %get-tuple-element.42.scales) | copy-start | bytes 221188
  63.9 12.7 %collective-permute-start.12 = (f32[30,8,128]{2,1,0:T(8,128)S(1)}, f32[30,8,128]{2,1,0:T(8,128)S(1)}, u32[]{:S(2)}, u32[]{:S(2)}) collective-permute-start(f32[30,8,128]{2,1,0:T(8,128)S(1)} %get-tuple-element.36), channel_id=1, source_target_pairs={{0,2},{2,4},{4,6},{6,8},{8,10},{10,12},{12,14},{1,3},{3,5},{5,7},{... | collective-permute-start | bytes 368648 | tf_op jit(solution)/shard_map/ppermute | solution.py:428
  69.3 8.2 %collective-permute-start.13 = (f32[30,8,128]{2,1,0:T(8,128)S(1)}, f32[30,8,128]{2,1,0:T(8,128)S(1)}, u32[]{:S(2)}, u32[]{:S(2)}) collective-permute-start(f32[30,8,128]{2,1,0:T(8,128)S(1)} %get-tuple-element.37), channel_id=1, source_target_pairs={{2,0},{4,2},{6,4},{8,6},{10,8},{12,10},{14,12},{3,1},{5,3},{7,5},{... | collective-permute-start | bytes 368648 | tf_op jit(solution)/shard_map/ppermute | solution.py:428
  70.7 13.3 %collective-permute-start.6 = (f32[5,6,1,256]{3,2,0,1:T(1,128)S(1)}, f32[5,6,1,256]{3,2,0,1:T(1,128)S(1)}, u32[]{:S(2)}, u32[]{:S(2)}) collective-permute-start(f32[5,6,1,256]{3,2,0,1:T(1,128)S(1)} %get-tuple-element.102), channel_id=1, source_target_pairs={{0,1},{1,16},{16,17},{2,3},{3,18},{18,19},{4,5},{5,20},{20,21},{6,... | collective-permute-start | bytes 92168 | tf_op jit(solution)/shard_map/ppermute | solution.py:438
  74.6 9.4 %collective-permute-start.7 = (f32[5,6,1,256]{3,2,0,1:T(1,128)S(1)}, f32[5,6,1,256]{3,2,0,1:T(1,128)S(1)}, u32[]{:S(2)}, u32[]{:S(2)}) collective-permute-start(f32[5,6,1,256]{3,2,0,1:T(1,128)S(1)} %get-tuple-element.103), channel_id=1, source_target_pairs={{1,0},{16,1},{17,16},{3,2},{18,3},{19,18},{5,4},{20,5},{21,20},{7,... | collective-permute-start | bytes 92168 | tf_op jit(solution)/shard_map/ppermute | solution.py:439
  78.2 77.5 %collective-permute-start.14 = (f32[15,8,128]{2,1,0:T(8,128)}, f32[15,8,128]{2,1,0:T(8,128)}, u32[]{:S(2)}, u32[]{:S(2)}) collective-permute-start(f32[15,8,128]{2,1,0:T(8,128)} %get-tuple-element.40), channel_id=1, source_target_pairs={{0,1},{1,16},{16,17},{2,3},{3,18},{18,19},{4,5},{5,20},{20,21},{6,... | collective-permute-start | bytes 184328 | tf_op jit(solution)/shard_map/ppermute | solution.py:428
  82.7 73.0 %collective-permute-start.15 = (f32[15,8,128]{2,1,0:T(8,128)}, f32[15,8,128]{2,1,0:T(8,128)}, u32[]{:S(2)}, u32[]{:S(2)}) collective-permute-start(f32[15,8,128]{2,1,0:T(8,128)} %get-tuple-element.41), channel_id=1, source_target_pairs={{1,0},{16,1},{17,16},{3,2},{18,3},{19,18},{5,4},{20,5},{21,20},{7,... | collective-permute-start | bytes 184328 | tf_op jit(solution)/shard_map/ppermute | solution.py:428
  91.4 0.8 copy-start.23
  91.4 59.5 %copy-start.10 = (f32[6,128,128]{2,1,0:T(8,128)S(1)}, f32[6,128,128]{2,1,0:T(8,128)}, u32[]{:S(2)}) copy-start(f32[6,128,128]{2,1,0:T(8,128)} %constant.121.clone.tables) | copy-start | bytes 1179652
  101.8 49.1 %copy-start.12 = (f32[18,8,128]{2,1,0:T(8,128)S(1)}, f32[18,8,128]{2,1,0:T(8,128)}, u32[]{:S(2)}) copy-start(f32[18,8,128]{2,1,0:T(8,128)} %copy-done.11) | copy-start | bytes 221188
  101.8 49.1 %copy-start.14 = (f32[18,8,128]{2,1,0:T(8,128)S(1)}, f32[18,8,128]{2,1,0:T(8,128)}, u32[]{:S(2)}) copy-start(f32[18,8,128]{2,1,0:T(8,128)} %copy-done.13) | copy-start | bytes 221188
  101.8 53.9 %copy-start.1 = (f32[3,9,17,512]{3,2,1,0:T(8,128)S(1)}, f32[3,9,17,512]{3,2,1,0:T(8,128)}, u32[]{:S(2)}) copy-start(f32[3,9,17,512]{3,2,1,0:T(8,128)} %copy-done) | copy-start | bytes 2820100
  101.8 53.9 %copy-start.16 = (f32[3,3,2,8,128]{4,3,2,1,0:T(8,128)S(1)}, f32[3,3,2,8,128]{4,3,2,1,0:T(8,128)}, u32[]{:S(2)}) copy-start(f32[3,3,2,8,128]{4,3,2,1,0:T(8,128)} %copy-done.15) | copy-start | bytes 221188
  150.9 0.7 copy-start.19
  155.7 1.3 copy-start.3
  157.0 1.3 copy-start.5

commit v2 on v1

--- a/solution.py
+++ b/solution.py
@@ -717,9 +717,10 @@
     node_x = targets // count_gy % count_x * 8 + slots // 17
     node_y = (targets // (count_gy * count_x) * count_gy + targets % count_gy) * 16 + slots % 17
     ids = (node_x * nodes_y + node_y).astype(f32)
-    faces = lax.all_gather(
-        jnp.concatenate([traction, ids[None]], axis=0)[:, None, :], ("grp", "gx", "gy"), axis=1, tiled=True
-    )
+    rank = ("grp", "gx", "gy")
+    mine = jnp.concatenate([traction, ids[None]], axis=0)
+    copies = jnp.broadcast_to(mine, (lax.axis_size(rank),) + mine.shape)
+    faces = jnp.swapaxes(lax.all_to_all(copies, rank, 0, 0, tiled=True), 0, 1)
     here = jnp.stack([place_x, place_y]).astype(jnp.int32)
     surf1, surf2 = call(
         functools.partial(surface_kernel, float(nodes_y)),

time: 169 us -> 140 us (0.83)
  the two profiles are of different devices: /device:TPU:0 before, /device:TPU:3 now
where the time goes in v2:
time: 140 us; the launch traced here: 138 us
  starting transfers between devices  51.6 us (37%)
  local copies, waits for them, and re-layouts  27.3 us (20%)
  other arithmetic  22.4 us (16%)
  Pallas kernels  20.9 us (15%)
  waiting for transfers between devices  13.9 us (10%)
  between operations  1.63 us (1%)
    ppermute x8, starting transfers between devices, exchange(): return (lax.ppermute(to_high, axis, up), lax.ppermute(to_low, axis, down))  22.4 us
    pallas_call x6, Pallas kernels, call(): pl.pallas_call(kernel, out_shape=[jax.ShapeDtypeStruct(s, f32) for s in o...  20.9 us
    unnamed x65, local copies, waits for them, and re-layouts  19 us
    ppermute x4, starting transfers between devices, extended_2(): before = lax.ppermute(last, axis, up)  15.2 us
    ppermute x4, starting transfers between devices, extended_2(): after = lax.ppermute(first, axis, down)  8 us
    ppermute x4, waiting for transfers between devices, extended_2(): after = lax.ppermute(first, axis, down)  7.03 us
    all_to_all x1, starting transfers between devices, shards(): faces = jnp.swapaxes(lax.all_to_all(copies, rank, 0, 0, tiled=True), 0, 1)  5.98 us
    ppermute x8, waiting for transfers between devices, exchange(): return (lax.ppermute(to_high, axis, up), lax.ppermute(to_low, axis, down))  5.24 us
  transfers between devices with their start and end apart: 17, of which 5 were waited for; matrix products, arithmetic and copies ran while one was open for 18% of the time, Pallas kernels for 12%

profile of v2, /device:TPU:3, one launch (start us, length us, event | category | flops | bytes accessed | tf_op | source)
XLA Modules:
  0.0 137.7 jit_solution(13477884522400276832)
XLA Ops:
  0.7 1.1 pad_maximum_fusion.19
  1.8 3.2 %collective-permute-start = (f32[5,1,32,256]{3,2,0,1:T(8,128)S(1)}, f32[5,1,32,256]{3,2,0,1:T(8,128)S(1)}, u32[]{:S(2)}, u32[]{:S(2)}) collective-permute-start(f32[5,1,32,256]{3,2,0,1:T(8,128)S(1)} %get-tuple-element.112), channel_id=1, source_target_pairs={{0,2},{2,4},{4,6},{6,8},{8,10},{10,12},{12,14},{1,3},{3,5},{5,7},{... | collective-permute-start | bytes 491528 | tf_op jit(solution)/shard_map/ppermute | solution.py:438
  5.0 2.1 %collective-permute-start.1 = (f32[5,1,32,256]{3,2,0,1:T(8,128)S(1)}, f32[5,1,32,256]{3,2,0,1:T(8,128)S(1)}, u32[]{:S(2)}, u32[]{:S(2)}) collective-permute-start(f32[5,1,32,256]{3,2,0,1:T(8,128)S(1)} %get-tuple-element.113), channel_id=1, source_target_pairs={{2,0},{4,2},{6,4},{8,6},{10,8},{12,10},{14,12},{3,1},{5,3},{7,5},{... | collective-permute-start | bytes 491528 | tf_op jit(solution)/shard_map/ppermute | solution.py:439
  7.1 1.6 %collective-permute-done = f32[5,1,32,256]{3,2,0,1:T(8,128)S(1)} collective-permute-done((f32[5,1,32,256]{3,2,0,1:T(8,128)S(1)}, f32[5,1,32,256]{3,2,0,1:T(8,128)S(1)}, u32[]{:S(2)}, u32[]{:S(2)}) %collective-permute-start) | collective-permute-done | bytes 163872 | tf_op jit(solution)/shard_map/ppermute | solution.py:438
  8.7 3.8 %collective-permute-done.1 = f32[5,1,32,256]{3,2,0,1:T(8,128)S(1)} collective-permute-done((f32[5,1,32,256]{3,2,0,1:T(8,128)S(1)}, f32[5,1,32,256]{3,2,0,1:T(8,128)S(1)}, u32[]{:S(2)}, u32[]{:S(2)}) %collective-permute-start.1) | collective-permute-done | bytes 163872 | tf_op jit(solution)/shard_map/ppermute | solution.py:439
  12.5 0.9 pad_maximum_fusion.27
  13.4 4.9 %collective-permute-start.2 = (f32[5,6,1,256]{3,2,0,1:T(1,128)S(1)}, f32[5,6,1,256]{3,2,0,1:T(1,128)S(1)}, u32[]{:S(2)}, u32[]{:S(2)}) collective-permute-start(f32[5,6,1,256]{3,2,0,1:T(1,128)S(1)} %get-tuple-element.108), channel_id=1, source_target_pairs={{0,1},{1,16},{16,17},{2,3},{3,18},{18,19},{4,5},{5,20},{20,21},{6,... | collective-permute-start | bytes 92168 | tf_op jit(solution)/shard_map/ppermute | solution.py:438
  18.3 1.9 %collective-permute-start.3 = (f32[5,6,1,256]{3,2,0,1:T(1,128)S(1)}, f32[5,6,1,256]{3,2,0,1:T(1,128)S(1)}, u32[]{:S(2)}, u32[]{:S(2)}) collective-permute-start(f32[5,6,1,256]{3,2,0,1:T(1,128)S(1)} %get-tuple-element.109), channel_id=1, source_target_pairs={{1,0},{16,1},{17,16},{3,2},{18,3},{19,18},{5,4},{20,5},{21,20},{7,... | collective-permute-start | bytes 92168 | tf_op jit(solution)/shard_map/ppermute | solution.py:439
  20.2 3.3 %collective-permute-done.3 = f32[5,6,1,256]{3,2,0,1:T(1,128)S(1)} collective-permute-done((f32[5,6,1,256]{3,2,0,1:T(1,128)S(1)}, f32[5,6,1,256]{3,2,0,1:T(1,128)S(1)}, u32[]{:S(2)}, u32[]{:S(2)}) %collective-permute-start.3) | collective-permute-done | bytes 30752 | tf_op jit(solution)/shard_map/ppermute | solution.py:439
  30.7 3.5 %collective-permute-start.4 = (f32[5,1,32,256]{3,2,0,1:T(8,128)S(1)}, f32[5,1,32,256]{3,2,0,1:T(8,128)S(1)}, u32[]{:S(2)}, u32[]{:S(2)}) collective-permute-start(f32[5,1,32,256]{3,2,0,1:T(8,128)S(1)} %get-tuple-element.110), channel_id=1, source_target_pairs={{0,2},{2,4},{4,6},{6,8},{8,10},{10,12},{12,14},{1,3},{3,5},{5,7},{... | collective-permute-start | bytes 491528 | tf_op jit(solution)/shard_map/ppermute | solution.py:438
  34.2 2.1 %collective-permute-start.5 = (f32[5,1,32,256]{3,2,0,1:T(8,128)S(1)}, f32[5,1,32,256]{3,2,0,1:T(8,128)S(1)}, u32[]{:S(2)}, u32[]{:S(2)}) collective-permute-start(f32[5,1,32,256]{3,2,0,1:T(8,128)S(1)} %get-tuple-element.111), channel_id=1, source_target_pairs={{2,0},{4,2},{6,4},{8,6},{10,8},{12,10},{14,12},{3,1},{5,3},{7,5},{... | collective-permute-start | bytes 491528 | tf_op jit(solution)/shard_map/ppermute | solution.py:439
  37.0 0.9 copy-done.26
  38.7 7.5 %shard_map.138 = (f32[3,5,5,4,8,128]{5,4,3,2,1,0:T(8,128)S(1)}, f32[3,5,5,4,8,128]{5,4,3,2,1,0:T(8,128)S(1)}, f32[31,8,128]{2,1,0:T(8,128)S(1)}, f32[31,8,128]{2...) custom-call(f32[3,9,17,512]{3,2,1,0:T(8,128)S(1)} %copy.182.u, f32[3,9,17,512]{3,2,1,0:T(8,128)S(1)} %copy.183.v, ...), custom_call_target="tpu_custom_call" | custom-call | tf_op jit(solution)/shard_map/pallas_call | solution.py:409
  46.2 4.3 %collective-permute-start.8 = (f32[31,8,128]{2,1,0:T(8,128)S(1)}, f32[31,8,128]{2,1,0:T(8,128)S(1)}, u32[]{:S(2)}, u32[]{:S(2)}) collective-permute-start(f32[31,8,128]{2,1,0:T(8,128)S(1)} %get-tuple-element.28), channel_id=1, source_target_pairs={{0,2},{2,4},{4,6},{6,8},{8,10},{10,12},{12,14},{1,3},{3,5},{5,7},{... | collective-permute-start | bytes 380936 | tf_op jit(solution)/shard_map/ppermute | solution.py:428
  50.5 1.9 %collective-permute-start.9 = (f32[31,8,128]{2,1,0:T(8,128)S(1)}, f32[31,8,128]{2,1,0:T(8,128)S(1)}, u32[]{:S(2)}, u32[]{:S(2)}) collective-permute-start(f32[31,8,128]{2,1,0:T(8,128)S(1)} %get-tuple-element.29), channel_id=1, source_target_pairs={{2,0},{4,2},{6,4},{8,6},{10,8},{12,10},{14,12},{3,1},{5,3},{7,5},{... | collective-permute-start | bytes 380936 | tf_op jit(solution)/shard_map/ppermute | solution.py:428
  52.6 5.0 %collective-permute-done.9.from_high.xh = f32[31,8,128]{2,1,0:T(8,128)S(1)} collective-permute-done((f32[31,8,128]{2,1,0:T(8,128)S(1)}, f32[31,8,128]{2,1,0:T(8,128)S(1)}, u32[]{:S(2)}, u32[]{:S(2)}) %collective-permute-start.9) | collective-permute-done | bytes 127008 | tf_op jit(solution)/shard_map/ppermute | solution.py:428
  57.7 3.3 %collective-permute-start.10 = (f32[18,8,128]{2,1,0:T(8,128)S(1)}, f32[18,8,128]{2,1,0:T(8,128)S(1)}, u32[]{:S(2)}, u32[]{:S(2)}) collective-permute-start(f32[18,8,128]{2,1,0:T(8,128)S(1)} %get-tuple-element.32), channel_id=1, source_target_pairs={{0,1},{1,16},{16,17},{2,3},{3,18},{18,19},{4,5},{5,20},{20,21},{6,... | collective-permute-start | bytes 221192 | tf_op jit(solution)/shard_map/ppermute | solution.py:428
  61.0 1.9 %collective-permute-start.11 = (f32[18,8,128]{2,1,0:T(8,128)S(1)}, f32[18,8,128]{2,1,0:T(8,128)S(1)}, u32[]{:S(2)}, u32[]{:S(2)}) collective-permute-start(f32[18,8,128]{2,1,0:T(8,128)S(1)} %get-tuple-element.33), channel_id=1, source_target_pairs={{1,0},{16,1},{17,16},{3,2},{18,3},{19,18},{5,4},{20,5},{21,20},{7,... | collective-permute-start | bytes 221192 | tf_op jit(solution)/shard_map/ppermute | solution.py:428
  63.0 3.6 %collective-permute-start.6 = (f32[5,6,1,256]{3,2,0,1:T(1,128)S(1)}, f32[5,6,1,256]{3,2,0,1:T(1,128)S(1)}, u32[]{:S(2)}, u32[]{:S(2)}) collective-permute-start(f32[5,6,1,256]{3,2,0,1:T(1,128)S(1)} %get-tuple-element.106), channel_id=1, source_target_pairs={{0,1},{1,16},{16,17},{2,3},{3,18},{18,19},{4,5},{5,20},{20,21},{6,... | collective-permute-start | bytes 92168 | tf_op jit(solution)/shard_map/ppermute | solution.py:438
  66.7 1.9 %collective-permute-start.7 = (f32[5,6,1,256]{3,2,0,1:T(1,128)S(1)}, f32[5,6,1,256]{3,2,0,1:T(1,128)S(1)}, u32[]{:S(2)}, u32[]{:S(2)}) collective-permute-start(f32[5,6,1,256]{3,2,0,1:T(1,128)S(1)} %get-tuple-element.107), channel_id=1, source_target_pairs={{1,0},{16,1},{17,16},{3,2},{18,3},{19,18},{5,4},{20,5},{21,20},{7,... | collective-permute-start | bytes 92168 | tf_op jit(solution)/shard_map/ppermute | solution.py:439
  69.2 4.7 %shard_map.140 = (f32[3,5,5,4,8,128]{5,4,3,2,1,0:T(8,128)S(1)}, f32[3,5,5,4,8,128]{5,4,3,2,1,0:T(8,128)S(1)}, f32[30,8,128]{2,1,0:T(8,128)}, f32[30,8,128]{2,1,0...) custom-call(f32[3,5,5,4,8,128]{5,4,3,2,1,0:T(8,128)S(1)} %get-tuple-element.26.b, ...), custom_call_target="tpu_custom_call" | custom-call | tf_op jit(solution)/shard_map/pallas_call | solution.py:409
  74.0 1.9 %collective-permute-start.12 = (f32[30,8,128]{2,1,0:T(8,128)}, f32[30,8,128]{2,1,0:T(8,128)S(1)}, u32[]{:S(2)}, u32[]{:S(2)}) collective-permute-start(f32[30,8,128]{2,1,0:T(8,128)} %get-tuple-element.36), channel_id=1, source_target_pairs={{0,2},{2,4},{4,6},{6,8},{8,10},{10,12},{12,14},{1,3},{3,5},{5,7},{... | collective-permute-start | bytes 368648 | tf_op jit(solution)/shard_map/ppermute | solution.py:428
  75.9 3.5 %collective-permute-start.13 = (f32[30,8,128]{2,1,0:T(8,128)}, f32[30,8,128]{2,1,0:T(8,128)S(1)}, u32[]{:S(2)}, u32[]{:S(2)}) collective-permute-start(f32[30,8,128]{2,1,0:T(8,128)} %get-tuple-element.37), channel_id=1, source_target_pairs={{2,0},{4,2},{6,4},{8,6},{10,8},{12,10},{14,12},{3,1},{5,3},{7,5},{... | collective-permute-start | bytes 368648 | tf_op jit(solution)/shard_map/ppermute | solution.py:428
  87.7 0.8 multiply_reduce_fusion.6
  89.1 1.3 mul.683
  90.3 1.8 %fusion.63 = (f32[4,32]{1,0:T(4,128)}, f32[4,32]{1,0:T(4,128)}, f32[4,32]{1,0:T(4,128)}, f32[4,32]{1,0:T(4,128)}) fusion(f32[5,4,32,256]{3,2,0,1:T(8,128)} %copy-done.23, f32[3,4,32,1]{3,2,0,1:T(8,128)} %get-tuple-element.69), kind=kLoop, calls=%fused_computation.179 | loop fusion | flops 384 | bytes 4608 | tf_op jit(solution)/shard_map/mul | solution.py:500
  92.2 1.3 mul.675
  93.5 1.3 mul.679
  94.8 1.3 mul.677
  96.1 1.3 squeeze.22
  100.0 6.0 %all-to-all-start = ((f32[32,4,128]{2,1,0:T(4,128)}), f32[32,4,128]{2,1,0:T(4,128)}, u32[]{:S(2)}, u32[]{:S(2)}) async-start(f32[32,4,128]{2,1,0:T(4,128)} %broadcast_in_dim.108), calls=%async_computation | async-start | bytes 131072 | tf_op jit(solution)/shard_map/all_to_all | solution.py:723
  106.0 0.8 copy-done.14
  106.9 0.8 copy-done.16
  108.4 3.3 %collective-permute-start.14 = (f32[15,8,128]{2,1,0:T(8,128)}, f32[15,8,128]{2,1,0:T(8,128)}, u32[]{:S(2)}, u32[]{:S(2)}) collective-permute-start(f32[15,8,128]{2,1,0:T(8,128)} %get-tuple-element.40), channel_id=1, source_target_pairs={{0,1},{1,16},{16,17},{2,3},{3,18},{18,19},{4,5},{5,20},{20,21},{6,... | collective-permute-start | bytes 184328 | tf_op jit(solution)/shard_map/ppermute | solution.py:428
  111.7 2.1 %collective-permute-start.15 = (f32[15,8,128]{2,1,0:T(8,128)}, f32[15,8,128]{2,1,0:T(8,128)}, u32[]{:S(2)}, u32[]{:S(2)}) collective-permute-start(f32[15,8,128]{2,1,0:T(8,128)} %get-tuple-element.41), channel_id=1, source_target_pairs={{1,0},{16,1},{17,16},{3,2},{18,3},{19,18},{5,4},{20,5},{21,20},{7,... | collective-permute-start | bytes 184328 | tf_op jit(solution)/shard_map/ppermute | solution.py:428
  114.5 2.0 %copy.189 = f32[5,4,32,256]{3,2,1,0:T(8,128)} copy(f32[5,4,32,256]{3,2,0,1:T(8,128)} %copy-done.23) | data formatting | bytes 1310720
  116.5 0.8 copy.360
  117.4 0.9 copy-done.8
  118.2 0.9 copy-done.10
  119.8 4.0 %shard_map.142 = (f32[24,256]{1,0:T(8,128)S(1)}, f32[24,256]{1,0:T(8,128)S(1)}) custom-call(f32[4,32,128]{2,1,0:T(8,128)S(1)} %bitcast.236, s32[2]{0:T(128)S(1)} %copy-done.19, s32[2,4,128]{2,1,0:T(4,128)S(1)} %copy-done.17, f32[31,8,128]{2,1,0:T(8,128)S(1)} %collective-permute-done.8.from_low.xl, f32[31,8,128]{2,1,0:T(8,128)S(1)} %collective-permute-done.9.from_high.xh, ...), custom_call_target="tpu_custom_call" | custom-call | tf_op jit(solution)/shard_map/pallas_call | solution.py:409
  123.9 1.3 copy-done.1
  125.2 1.3 copy-done.3
  126.5 1.3 copy-done.5
  127.8 0.9 copy-done.12
  128.7 4.0 %shard_map.143 = (f32[3,9,17,512]{3,2,1,0:T(8,128)S(1)}, f32[3,9,17,512]{3,2,1,0:T(8,128)S(1)}, f32[3,9,17,512]{3,2,1,0:T(8,128)S(1)}) custom-call(f32[3,5,5,4,8,128]{5,4,3,2,1,0:T(8,128)S(1)} %copy-done.3, f32[3,5,5,4,8,128]{5,4,3,2,1,0:T(8,128)S(1)} %copy-done.5, f32[30,8,128]{2,1,0:T(8,128)S(1)} %collective-permute-done.12.from_low.xl, ...), custom_call_target="tpu_custom_call" | custom-call | tf_op jit(solution)/shard_map/pallas_call | solution.py:409
  132.6 1.7 %copy.190 = f32[3,9,17,512]{3,0,2,1:T(4,128)} copy(f32[3,9,17,512]{3,2,1,0:T(8,128)S(1)} %get-tuple-element.61) | data formatting | bytes 1880064
  134.3 1.7 %copy.191 = f32[3,9,17,512]{3,0,2,1:T(4,128)} copy(f32[3,9,17,512]{3,2,1,0:T(8,128)S(1)} %get-tuple-element.62) | data formatting | bytes 1880064
  136.0 1.7 %copy.192 = f32[3,9,17,512]{3,0,2,1:T(4,128)} copy(f32[3,9,17,512]{3,2,1,0:T(8,128)S(1)} %get-tuple-element.63) | data formatting | bytes 1880064
  (154 shorter events, 22.6 us)
Async XLA Ops:
  0.6 11.9 %copy-start.20 = (f32[3,4,32,256]{3,2,1,0:T(8,128)S(1)}, f32[3,4,32,256]{3,2,1,0:T(8,128)}, u32[]{:S(2)}) copy-start(f32[3,4,32,256]{3,2,1,0:T(8,128)} %param.12) | copy-start | bytes 1179652
  0.6 22.8 %copy-start.21 = (f32[4,32,256]{2,1,0:T(8,128)S(1)}, f32[4,32,256]{2,1,0:T(8,128)}, u32[]{:S(2)}) copy-start(f32[4,32,256]{2,1,0:T(8,128)} %param.13) | copy-start | bytes 393220
  0.7 22.8 %copy-start.22 = (f32[4,32,256]{2,1,0:T(8,128)S(1)}, f32[4,32,256]{2,1,0:T(8,128)}, u32[]{:S(2)}) copy-start(f32[4,32,256]{2,1,0:T(8,128)} %param.11) | copy-start | bytes 393220
  1.8 7.0 %collective-permute-start = (f32[5,1,32,256]{3,2,0,1:T(8,128)S(1)}, f32[5,1,32,256]{3,2,0,1:T(8,128)S(1)}, u32[]{:S(2)}, u32[]{:S(2)}) collective-permute-start(f32[5,1,32,256]{3,2,0,1:T(8,128)S(1)} %get-tuple-element.112), channel_id=1, source_target_pairs={{0,2},{2,4},{4,6},{6,8},{8,10},{10,12},{12,14},{1,3},{3,5},{5,7},{... | collective-permute-start | bytes 491528 | tf_op jit(solution)/shard_map/ppermute | solution.py:438
  5.0 7.5 %collective-permute-start.1 = (f32[5,1,32,256]{3,2,0,1:T(8,128)S(1)}, f32[5,1,32,256]{3,2,0,1:T(8,128)S(1)}, u32[]{:S(2)}, u32[]{:S(2)}) collective-permute-start(f32[5,1,32,256]{3,2,0,1:T(8,128)S(1)} %get-tuple-element.113), channel_id=1, source_target_pairs={{2,0},{4,2},{6,4},{8,6},{10,8},{12,10},{14,12},{3,1},{5,3},{7,5},{... | collective-permute-start | bytes 491528 | tf_op jit(solution)/shard_map/ppermute | solution.py:439
  13.4 6.9 %collective-permute-start.2 = (f32[5,6,1,256]{3,2,0,1:T(1,128)S(1)}, f32[5,6,1,256]{3,2,0,1:T(1,128)S(1)}, u32[]{:S(2)}, u32[]{:S(2)}) collective-permute-start(f32[5,6,1,256]{3,2,0,1:T(1,128)S(1)} %get-tuple-element.108), channel_id=1, source_target_pairs={{0,1},{1,16},{16,17},{2,3},{3,18},{18,19},{4,5},{5,20},{20,21},{6,... | collective-permute-start | bytes 92168 | tf_op jit(solution)/shard_map/ppermute | solution.py:438
  18.3 5.2 %collective-permute-start.3 = (f32[5,6,1,256]{3,2,0,1:T(1,128)S(1)}, f32[5,6,1,256]{3,2,0,1:T(1,128)S(1)}, u32[]{:S(2)}, u32[]{:S(2)}) collective-permute-start(f32[5,6,1,256]{3,2,0,1:T(1,128)S(1)} %get-tuple-element.109), channel_id=1, source_target_pairs={{1,0},{16,1},{17,16},{3,2},{18,3},{19,18},{5,4},{20,5},{21,20},{7,... | collective-permute-start | bytes 92168 | tf_op jit(solution)/shard_map/ppermute | solution.py:439
  30.3 6.0 %copy-start.24 = (f32[3,9,17,512]{3,0,2,1:T(4,128)S(1)}, f32[3,9,17,512]{3,0,2,1:T(4,128)}, u32[]{:S(2)}) copy-start(f32[3,9,17,512]{3,0,2,1:T(4,128)} %param.14) | copy-start | bytes 2820100
  30.7 32.2 %collective-permute-start.4 = (f32[5,1,32,256]{3,2,0,1:T(8,128)S(1)}, f32[5,1,32,256]{3,2,0,1:T(8,128)S(1)}, u32[]{:S(2)}, u32[]{:S(2)}) collective-permute-start(f32[5,1,32,256]{3,2,0,1:T(8,128)S(1)} %get-tuple-element.110), channel_id=1, source_target_pairs={{0,2},{2,4},{4,6},{6,8},{8,10},{10,12},{12,14},{1,3},{3,5},{5,7},{... | collective-permute-start | bytes 491528 | tf_op jit(solution)/shard_map/ppermute | solution.py:438
  34.2 2.4 %copy-start.25 = (f32[3,9,17,512]{3,0,2,1:T(4,128)S(1)}, f32[3,9,17,512]{3,0,2,1:T(4,128)}, u32[]{:S(2)}) copy-start(f32[3,9,17,512]{3,0,2,1:T(4,128)} %param.15) | copy-start | bytes 2820100
  34.2 28.7 %collective-permute-start.5 = (f32[5,1,32,256]{3,2,0,1:T(8,128)S(1)}, f32[5,1,32,256]{3,2,0,1:T(8,128)S(1)}, u32[]{:S(2)}, u32[]{:S(2)}) collective-permute-start(f32[5,1,32,256]{3,2,0,1:T(8,128)S(1)} %get-tuple-element.111), channel_id=1, source_target_pairs={{2,0},{4,2},{6,4},{8,6},{10,8},{12,10},{14,12},{3,1},{5,3},{7,5},{... | collective-permute-start | bytes 491528 | tf_op jit(solution)/shard_map/ppermute | solution.py:439
  36.7 1.3 copy-start.26
  38.0 0.7 copy-start.17
  38.0 0.7 copy-start.18
  38.7 7.5 %copy-start = (f32[3,9,17,512]{3,2,1,0:T(8,128)}, f32[3,9,17,512]{3,2,1,0:T(8,128)S(1)}, u32[]{:S(2)}) copy-start(f32[3,9,17,512]{3,2,1,0:T(8,128)S(1)} %copy.184.a) | copy-start | bytes 2820100
  46.2 22.4 %copy-start.27 = (s32[1,128]{1,0:T(1,128)S(1)}, s32[1,128]{1,0:T(1,128)}, u32[]{:S(2)}) copy-start(s32[1,128]{1,0:T(1,128)} %param.20) | copy-start | bytes 1540
  46.2 22.4 %copy-start.28 = (s32[1,128,1]{1,2,0:T(1,128)S(1)}, s32[1,128,1]{1,2,0:T(1,128)}, u32[]{:S(2)}) copy-start(s32[1,128,1]{1,2,0:T(1,128)} %param.19) | copy-start | bytes 1540
  46.2 6.4 %collective-permute-start.8 = (f32[31,8,128]{2,1,0:T(8,128)S(1)}, f32[31,8,128]{2,1,0:T(8,128)S(1)}, u32[]{:S(2)}, u32[]{:S(2)}) collective-permute-start(f32[31,8,128]{2,1,0:T(8,128)S(1)} %get-tuple-element.28), channel_id=1, source_target_pairs={{0,2},{2,4},{4,6},{6,8},{8,10},{10,12},{12,14},{1,3},{3,5},{5,7},{... | collective-permute-start | bytes 380936 | tf_op jit(solution)/shard_map/ppermute | solution.py:428
  50.5 7.1 %collective-permute-start.9 = (f32[31,8,128]{2,1,0:T(8,128)S(1)}, f32[31,8,128]{2,1,0:T(8,128)S(1)}, u32[]{:S(2)}, u32[]{:S(2)}) collective-permute-start(f32[31,8,128]{2,1,0:T(8,128)S(1)} %get-tuple-element.29), channel_id=1, source_target_pairs={{2,0},{4,2},{6,4},{8,6},{10,8},{12,10},{14,12},{3,1},{5,3},{7,5},{... | collective-permute-start | bytes 380936 | tf_op jit(solution)/shard_map/ppermute | solution.py:428
  57.7 11.6 %collective-permute-start.10 = (f32[18,8,128]{2,1,0:T(8,128)S(1)}, f32[18,8,128]{2,1,0:T(8,128)S(1)}, u32[]{:S(2)}, u32[]{:S(2)}) collective-permute-start(f32[18,8,128]{2,1,0:T(8,128)S(1)} %get-tuple-element.32), channel_id=1, source_target_pairs={{0,1},{1,16},{16,17},{2,3},{3,18},{18,19},{4,5},{5,20},{20,21},{6,... | collective-permute-start | bytes 221192 | tf_op jit(solution)/shard_map/ppermute | solution.py:428
  61.0 8.2 %collective-permute-start.11 = (f32[18,8,128]{2,1,0:T(8,128)S(1)}, f32[18,8,128]{2,1,0:T(8,128)S(1)}, u32[]{:S(2)}, u32[]{:S(2)}) collective-permute-start(f32[18,8,128]{2,1,0:T(8,128)S(1)} %get-tuple-element.33), channel_id=1, source_target_pairs={{1,0},{16,1},{17,16},{3,2},{18,3},{19,18},{5,4},{20,5},{21,20},{7,... | collective-permute-start | bytes 221192 | tf_op jit(solution)/shard_map/ppermute | solution.py:428
  63.0 16.4 %collective-permute-start.6 = (f32[5,6,1,256]{3,2,0,1:T(1,128)S(1)}, f32[5,6,1,256]{3,2,0,1:T(1,128)S(1)}, u32[]{:S(2)}, u32[]{:S(2)}) collective-permute-start(f32[5,6,1,256]{3,2,0,1:T(1,128)S(1)} %get-tuple-element.106), channel_id=1, source_target_pairs={{0,1},{1,16},{16,17},{2,3},{3,18},{18,19},{4,5},{5,20},{20,21},{6,... | collective-permute-start | bytes 92168 | tf_op jit(solution)/shard_map/ppermute | solution.py:438
  66.7 12.8 %collective-permute-start.7 = (f32[5,6,1,256]{3,2,0,1:T(1,128)S(1)}, f32[5,6,1,256]{3,2,0,1:T(1,128)S(1)}, u32[]{:S(2)}, u32[]{:S(2)}) collective-permute-start(f32[5,6,1,256]{3,2,0,1:T(1,128)S(1)} %get-tuple-element.107), channel_id=1, source_target_pairs={{1,0},{16,1},{17,16},{3,2},{18,3},{19,18},{5,4},{20,5},{21,20},{7,... | collective-permute-start | bytes 92168 | tf_op jit(solution)/shard_map/ppermute | solution.py:439
  69.2 4.7 %copy-start.7 = (f32[18,8,128]{2,1,0:T(8,128)}, f32[18,8,128]{2,1,0:T(8,128)S(1)}, u32[]{:S(2)}) copy-start(f32[18,8,128]{2,1,0:T(8,128)S(1)} %collective-permute-done.10.yl) | copy-start | bytes 221188
  69.2 4.7 %copy-start.9 = (f32[18,8,128]{2,1,0:T(8,128)}, f32[18,8,128]{2,1,0:T(8,128)S(1)}, u32[]{:S(2)}) copy-start(f32[18,8,128]{2,1,0:T(8,128)S(1)} %collective-permute-done.11.yh) | copy-start | bytes 221188
  73.9 5.8 %copy-start.2 = (f32[3,5,5,4,8,128]{5,4,3,2,1,0:T(8,128)}, f32[3,5,5,4,8,128]{5,4,3,2,1,0:T(8,128)S(1)}, u32[]{:S(2)}) copy-start(f32[3,5,5,4,8,128]{5,4,3,2,1,0:T(8,128)S(1)} %get-tuple-element.34.a1) | copy-start | bytes 3686404
  73.9 5.8 %copy-start.4 = (f32[3,5,5,4,8,128]{5,4,3,2,1,0:T(8,128)}, f32[3,5,5,4,8,128]{5,4,3,2,1,0:T(8,128)S(1)}, u32[]{:S(2)}) copy-start(f32[3,5,5,4,8,128]{5,4,3,2,1,0:T(8,128)S(1)} %get-tuple-element.35.f) | copy-start | bytes 3686404
  73.9 5.8 %copy-start.11 = (f32[3,3,2,8,128]{4,3,2,1,0:T(8,128)}, f32[3,3,2,8,128]{4,3,2,1,0:T(8,128)S(1)}, u32[]{:S(2)}) copy-start(f32[3,3,2,8,128]{4,3,2,1,0:T(8,128)S(1)} %get-tuple-element.42.scales) | copy-start | bytes 221188
  73.9 5.8 %copy-start.13 = (f32[15,8,128]{2,1,0:T(8,128)}, f32[15,8,128]{2,1,0:T(8,128)S(1)}, u32[]{:S(2)}) copy-start(f32[15,8,128]{2,1,0:T(8,128)S(1)} %get-tuple-element.38.low) | copy-start | bytes 184324
  73.9 5.8 %copy-start.15 = (f32[15,8,128]{2,1,0:T(8,128)}, f32[15,8,128]{2,1,0:T(8,128)S(1)}, u32[]{:S(2)}) copy-start(f32[15,8,128]{2,1,0:T(8,128)S(1)} %get-tuple-element.39.high) | copy-start | bytes 184324
  74.0 32.1 %collective-permute-start.12 = (f32[30,8,128]{2,1,0:T(8,128)}, f32[30,8,128]{2,1,0:T(8,128)S(1)}, u32[]{:S(2)}, u32[]{:S(2)}) collective-permute-start(f32[30,8,128]{2,1,0:T(8,128)} %get-tuple-element.36), channel_id=1, source_target_pairs={{0,2},{2,4},{4,6},{6,8},{8,10},{10,12},{12,14},{1,3},{3,5},{5,7},{... | collective-permute-start | bytes 368648 | tf_op jit(solution)/shard_map/ppermute | solution.py:428
  75.9 30.1 %collective-permute-start.13 = (f32[30,8,128]{2,1,0:T(8,128)}, f32[30,8,128]{2,1,0:T(8,128)S(1)}, u32[]{:S(2)}, u32[]{:S(2)}) collective-permute-start(f32[30,8,128]{2,1,0:T(8,128)} %get-tuple-element.37), channel_id=1, source_target_pairs={{2,0},{4,2},{6,4},{8,6},{10,8},{12,10},{14,12},{3,1},{5,3},{7,5},{... | collective-permute-start | bytes 368648 | tf_op jit(solution)/shard_map/ppermute | solution.py:428
  86.8 0.8 copy-start.23
  88.5 28.8 %copy-start.6 = (f32[6,128,128]{2,1,0:T(8,128)S(1)}, f32[6,128,128]{2,1,0:T(8,128)}, u32[]{:S(2)}) copy-start(f32[6,128,128]{2,1,0:T(8,128)} %constant.121.clone.tables) | copy-start | bytes 1179652
  100.0 16.5 %all-to-all-start = ((f32[32,4,128]{2,1,0:T(4,128)}), f32[32,4,128]{2,1,0:T(4,128)}, u32[]{:S(2)}, u32[]{:S(2)}) async-start(f32[32,4,128]{2,1,0:T(4,128)} %broadcast_in_dim.108), calls=%async_computation | async-start | bytes 131072 | tf_op jit(solution)/shard_map/all_to_all | solution.py:723
  106.0 0.8 copy-start.14
  106.9 0.8 copy-start.16
  108.4 15.5 %collective-permute-start.14 = (f32[15,8,128]{2,1,0:T(8,128)}, f32[15,8,128]{2,1,0:T(8,128)}, u32[]{:S(2)}, u32[]{:S(2)}) collective-permute-start(f32[15,8,128]{2,1,0:T(8,128)} %get-tuple-element.40), channel_id=1, source_target_pairs={{0,1},{1,16},{16,17},{2,3},{3,18},{18,19},{4,5},{5,20},{20,21},{6,... | collective-permute-start | bytes 184328 | tf_op jit(solution)/shard_map/ppermute | solution.py:428
  111.7 12.2 %collective-permute-start.15 = (f32[15,8,128]{2,1,0:T(8,128)}, f32[15,8,128]{2,1,0:T(8,128)}, u32[]{:S(2)}, u32[]{:S(2)}) collective-permute-start(f32[15,8,128]{2,1,0:T(8,128)} %get-tuple-element.41), channel_id=1, source_target_pairs={{1,0},{16,1},{17,16},{3,2},{18,3},{19,18},{5,4},{20,5},{21,20},{7,... | collective-permute-start | bytes 184328 | tf_op jit(solution)/shard_map/ppermute | solution.py:428
  117.4 0.9 copy-start.8
  118.2 0.9 copy-start.10
  119.1 0.7 copy-start.19
  123.9 1.3 copy-start.1
  125.2 1.3 copy-start.3
  126.5 1.3 copy-start.5
  127.8 0.9 copy-start.12

commit v3 on v1

--- a/solution.py
+++ b/solution.py
@@ -426,100 +426,6 @@
     up = [(i, i + 1) for i in range(count - 1)]
     down = [(j, i) for i, j in up]
     return lax.ppermute(to_high, axis, up), lax.ppermute(to_low, axis, down)
-
-
-def extended_2(array, sides, width):
-    for axis, dim in sides:
-        count, length = (lax.axis_size(axis), array.shape[dim])
-        up = [(i, (i + 1) % count) for i in range(count - 1)]
-        down = [(j, i) for i, j in up]
-        last = lax.slice_in_dim(array, length - width, length, axis=dim)
-        first = lax.slice_in_dim(array, 0, width, axis=dim)
-        before = lax.ppermute(last, axis, up)
-        after = lax.ppermute(first, axis, down)
-        array = jnp.concatenate([before, array, after], axis=dim)
-    return array
-
-
-def pressure_of(hydro_state):
-    velocity = hydro_state[1:4] / hydro_state[0]
-    pressure = (gamma_gas - 1.0) * (
-        hydro_state[4] - 0.5 * jnp.sum(hydro_state[1:4] * velocity, axis=0)
-    )
-    return (velocity, pressure)
-
-
-def euler_flux(hydro_state, axis_num):
-    velocity, pressure = pressure_of(hydro_state)
-    sound_speed = jnp.sqrt(gamma_gas * pressure / hydro_state[0])
-    normal_vel = velocity[axis_num]
-    unit_row = jnp.eye(3, dtype=jnp.float32)[axis_num].reshape(3, 1, 1, 1)
-    momentum_flux = hydro_state[1:4] * normal_vel + pressure * unit_row
-    energy_flux = (hydro_state[4] + pressure) * normal_vel
-    flux_all = jnp.concatenate(
-        [hydro_state[1 + axis_num][None], momentum_flux, energy_flux[None]], axis=0
-    )
-    return (flux_all, jnp.abs(normal_vel) + sound_speed)
-
-
-def advance(padded):
-    interior = padded[:, 1:-1, 1:-1, 1:-1]
-    change = jnp.zeros_like(interior)
-    for axis_num in range(3):
-        pencil = padded
-        for other_axis in range(3):
-            if other_axis != axis_num:
-                pencil = lax.slice_in_dim(
-                    pencil, 1, pencil.shape[other_axis + 1] - 1, axis=other_axis + 1
-                )
-        flux_all, wave_speed = euler_flux(pencil, axis_num)
-        length = pencil.shape[axis_num + 1]
-        low_state = lax.slice_in_dim(pencil, 0, length - 1, axis=axis_num + 1)
-        high_state = lax.slice_in_dim(pencil, 1, length, axis=axis_num + 1)
-        low_flux = lax.slice_in_dim(flux_all, 0, length - 1, axis=axis_num + 1)
-        high_flux = lax.slice_in_dim(flux_all, 1, length, axis=axis_num + 1)
-        fastest = jnp.maximum(
-            lax.slice_in_dim(wave_speed, 0, length - 1, axis=axis_num),
-            lax.slice_in_dim(wave_speed, 1, length, axis=axis_num),
-        )
-        face_flux = 0.5 * (low_flux + high_flux) - 0.5 * fastest * (high_state - low_state)
-        change = (
-            change
-            + lax.slice_in_dim(face_flux, 1, length - 1, axis=axis_num + 1)
-            - lax.slice_in_dim(face_flux, 0, length - 2, axis=axis_num + 1)
-        )
-    return interior - cell_ratio * change
-
-
-def surface_traction(hydro_state):
-    bottom = hydro_state[:, :, :, -1]
-    velocity, pressure = pressure_of(bottom[:, :, :, None])
-    vertical = velocity[2, :, :, 0]
-    return (
-        jnp.stack(
-            [bottom[1] * vertical, bottom[2] * vertical, bottom[3] * vertical + pressure[:, :, 0]]
-        )
-        * face_area
-    )
-
-
-def fix_edges(padded, depth):
-    placings = (
-        (lax.axis_index("gx"), lax.axis_size("gx"), 1),
-        (lax.axis_index(("grp", "gy")), lax.axis_size(("grp", "gy")), 2),
-    )
-    for position, extent, axis_num in placings:
-        length = padded.shape[axis_num]
-        inner_low = lax.slice_in_dim(padded, depth, depth + 1, axis=axis_num)
-        inner_high = lax.slice_in_dim(padded, length - depth - 1, length - depth, axis=axis_num)
-        place = lax.broadcasted_iota(jnp.int32, padded.shape, axis_num)
-        padded = jnp.where((position == 0) & (place < depth), inner_low, padded)
-        padded = jnp.where((position == extent - 1) & (place >= length - depth), inner_high, padded)
-    return padded
-
-
-def pad_depth(padded):
-    return jnp.pad(padded, ((0, 0), (0, 0), (0, 0), (1, 1)), mode="edge")
 
 
 def surface_tables():
@@ -681,9 +587,267 @@
     out2[...] = full_dot(fold[0:24], jnp.concatenate(rows2 + blank, axis=0), back=True)
 
 
-def surface_kernel(nodes_y, faces, here, region, xl, xh, yl, yh, material, tables, out1, out2, total):
-    base_x = (8 * here[0] - 4).astype(f32)
-    base_y = (16 * here[1] - 4).astype(f32)
+def position(axis):
+    return lax.axis_index(axis)
+
+
+def along_y():
+    return lax.axis_index("grp") * lax.axis_size("gy") + lax.axis_index("gy")
+
+
+def primitives(state):
+    inverse = 1.0 / state[0]
+    v = [state[1 + c] * inverse for c in range(3)]
+    p = (gamma_gas - 1.0) * (state[4] - 0.5 * (state[1] * v[0] + state[2] * v[1] + state[3] * v[2]))
+    return v + [p, jnp.sqrt(gamma_gas * p * inverse), state[4] + p]
+
+
+def flux(state, prim, d):
+    out = [state[1 + d]] + [state[1 + c] * prim[d] for c in range(3)] + [prim[5] * prim[d]]
+    out[1 + d] = out[1 + d] + prim[3]
+    return out, jnp.abs(prim[d]) + prim[4]
+
+
+def twice_face(low, high):
+    fastest = jnp.maximum(low[2], high[2])
+    return [fl + fh - fastest * (uh - ul) for ul, uh, fl, fh in zip(low[0], high[0], low[1], high[1])]
+
+
+def turned_change(state, prim, d, axis, ends):
+    size = state[0].shape[axis]
+    fluxes, speed = flux(state, prim, d)
+    up = lambda x: pltpu.roll(x, size - 1, axis)
+    high = ([up(x) for x in state], [up(x) for x in fluxes], up(speed))
+    upper = twice_face((state, fluxes, speed), high)
+    if ends is None:
+        return [g - pltpu.roll(g, 1, axis) for g in upper]
+    upper = [jnp.where(ends[1], 2.0 * f, g) for f, g in zip(fluxes, upper)]
+    return [g - jnp.where(ends[0], 2.0 * f, pltpu.roll(g, 1, axis)) for f, g in zip(fluxes, upper)]
+
+
+def field_of(f, density, momentum, energy):
+    return density if f == 0 else energy if f == 4 else momentum.at[f - 1]
+
+
+def start_kernel(nodes_y, density, momentum, energy, dest, slot, bottoms, rows):
+    lane = lanes_of()
+    pick = jnp.where(lane == 125 + rows_of(), 1.0, 0.0)
+    pieces = []
+    place = along_y()
+    for f in range(5):
+        field = field_of(f, density, momentum, energy)
+        columns = jnp.concatenate([field[x, :, 128:256] for x in range(4)], axis=0)
+        pieces.append(full_dot(pick, columns, back=True)[0:3])
+        low = jnp.concatenate([field[x, r : r + 1, :] for r in (0, 1) for x in range(4)], axis=0)
+        high = jnp.concatenate([field[x, r : r + 1, :] for r in (31, 30) for x in range(4)], axis=0)
+        for p in range(4):
+            rows[p, f] = jnp.where(p < place, low, high)
+    count_gy, count_x = lax.axis_size("gy"), lax.axis_size("gx")
+    target, node = dest[...].astype(f32), slot[...].astype(f32)
+    grp = jnp.floor((target + 0.5) * (1.0 / (count_gy * count_x)))
+    rest = target - grp * (count_gy * count_x)
+    gx = jnp.floor((rest + 0.5) * (1.0 / count_gy))
+    gy = rest - gx * count_gy
+    i = jnp.floor((node + 0.5) * (1.0 / 17.0))
+    j = node - 17.0 * i
+    pieces.append((8.0 * gx + i) * nodes_y + 16.0 * (grp * count_gy + gy) + j)
+    block = jnp.concatenate(pieces, axis=0)
+    for n in range(bottoms.shape[0]):
+        bottoms[n] = block
+
+
+def widen_kernel(density, momentum, energy, came, own, first, second):
+    place, last = along_y(), lax.axis_size("grp") * lax.axis_size("gy") - 1
+    odd = position("gx") % 2
+    low_slot, high_slot = jnp.maximum(place - 1, 0), jnp.minimum(place + 1, last)
+    for f in range(5):
+        field = field_of(f, density, momentum, energy)
+        low, high = came[low_slot, f], came[high_slot, f]
+        for x in range(4):
+            own[f, x, 0:32, :] = field[x]
+            bottom, top = field[x, 0:1, :], field[x, 31:32, :]
+            own[f, x, 39:40, :] = jnp.where(place == 0, bottom, low[x : x + 1])
+            own[f, x, 38:39, :] = jnp.where(place == 0, bottom, low[4 + x : 5 + x])
+            own[f, x, 32:33, :] = jnp.where(place == last, top, high[x : x + 1])
+            own[f, x, 33:34, :] = jnp.where(place == last, top, high[4 + x : 5 + x])
+            own[f, x, 34:38, :] = jnp.broadcast_to(top, (4, 256))
+        for out, low_way in ((first, odd), (second, 1 - odd)):
+            near = jnp.where(low_way == 1, 0, 3)
+            far = jnp.where(low_way == 1, 1, 2)
+            out[f, 0:40, :] = own[f, near]
+            out[f, 40:72, :] = own[f, far, 0:32, :]
+
+
+def crater_kernel(own, came1, came2, out, wide, mid, prims, face, fluxes):
+    place, last_y = along_y(), lax.axis_size("grp") * lax.axis_size("gy") - 1
+    gx, last_x = position("gx"), lax.axis_size("gx") - 1
+    odd = gx % 2
+    for f in range(5):
+        for x in range(4):
+            wide[f, 2 + x] = own[f, x]
+
+    def spread(came, near, far):
+        for f in range(5):
+            wide[f, near] = came[f, 0:40, :]
+            wide[f, far, 0:32, :] = came[f, 40:72, :]
+            wide[f, far, 32:40, :] = came[f, 32:40, :]
+
+    @pl.when(odd == 1)
+    def _():
+        spread(came1, 1, 0)
+        spread(came2, 6, 7)
+
+    @pl.when(odd == 0)
+    def _():
+        spread(came2, 1, 0)
+        spread(came1, 6, 7)
+
+    @pl.when(gx == 0)
+    def _():
+        for f in range(5):
+            wide[f, 0] = own[f, 0]
+            wide[f, 1] = own[f, 0]
+
+    @pl.when(gx == last_x)
+    def _():
+        for f in range(5):
+            wide[f, 6] = own[f, 3]
+            wide[f, 7] = own[f, 3]
+
+    lane = lanes_of((40, 256))
+    ends = (lane == 0, lane == 255)
+
+    def step(source, low, high, put):
+        def along_x(p):
+            state = [source[f, p] for f in range(5)]
+            prim = primitives(state)
+            return state, prim, flux(state, prim, 0)
+
+        state, prim, (fx, speed) = along_x(low - 1)
+        next_state, next_prim, (next_fx, next_speed) = along_x(low)
+        g = twice_face((state, fx, speed), (next_state, next_fx, next_speed))
+        for f in range(5):
+            face[f] = g[f]
+            fluxes[f] = next_fx[f]
+        for n in range(6):
+            prims[n] = next_prim[n]
+        fluxes[5] = next_speed
+
+        def plane(p, carry):
+            state = [source[f, p] for f in range(5)]
+            prim = [prims[n] for n in range(6)]
+            next_state, next_prim, (next_fx, next_speed) = along_x(p + 1)
+            g = twice_face((state, [fluxes[f] for f in range(5)], fluxes[5]), (next_state, next_fx, next_speed))
+            change = [g[f] - face[f] for f in range(5)]
+            for f in range(5):
+                face[f] = g[f]
+                fluxes[f] = next_fx[f]
+            for n in range(6):
+                prims[n] = next_prim[n]
+            fluxes[5] = next_speed
+            change = [a + b for a, b in zip(change, turned_change(state, prim, 1, 0, None))]
+            change = [a + b for a, b in zip(change, turned_change(state, prim, 2, 1, ends))]
+            for f in range(5):
+                put(f, p, state[f] - (0.5 * cell_ratio) * change[f])
+            return carry
+
+        lax.fori_loop(low, high, plane, 0)
+
+    def put_mid(f, p, value):
+        mid[f, p] = value
+
+    def put_out(f, p, value):
+        out[f, p - 2] = value[0:32]
+
+    step(wide, 1, 7, put_mid)
+
+    @pl.when(gx == 0)
+    def _():
+        for f in range(5):
+            mid[f, 1] = mid[f, 2]
+
+    @pl.when(gx == last_x)
+    def _():
+        for f in range(5):
+            mid[f, 6] = mid[f, 5]
+
+    for f in range(5):
+        for p in range(2, 6):
+            edge = mid[f, p, 39:40, :]
+            mid[f, p, 39:40, :] = jnp.where(place == 0, mid[f, p, 0:1, :], edge)
+            edge = mid[f, p, 32:33, :]
+            mid[f, p, 32:33, :] = jnp.where(place == last_y, mid[f, p, 31:32, :], edge)
+    step(mid, 2, 6, put_out)
+
+
+def bottom_tractions(bottoms, count_x, faces):
+    shape = (count_x, 128)
+    sub, lane = rows_of(shape), lanes_of(shape)
+    count_gy = lax.axis_size("gy")
+
+    def columns(q):
+        parts = []
+        for y in range(4):
+            start = (y // count_gy * count_x * count_gy + y % count_gy) * 16 + q
+            parts.append(bottoms[pl.ds(start, count_x, stride=16 * count_gy), :])
+        found = []
+        for x in range(4):
+            total = rolled(parts[0], -32 * x, 1)
+            for y in range(1, 4):
+                total = jnp.where(lane // 32 == y, rolled(parts[y], 32 * (y - x), 1), total)
+            found.append(total)
+        return found
+
+    cells = [[columns(f * 3 + z) for f in range(5)] for z in range(3)]
+    state = [[[cells[z][f][x] for f in range(5)] for x in range(4)] for z in range(3)]
+    ends_y = (lane == 0, lane == 127)
+
+    def across_x(states, prims):
+        fluxes = [flux(s, p, 0) for s, p in zip(states, prims)]
+        data = [(s, f, a) for s, (f, a) in zip(states, fluxes)]
+        up = lambda x: rolled(x, -1)
+        wrap = ([up(v) for v in data[0][0]], [up(v) for v in data[0][1]], up(data[0][2]))
+        upper = [twice_face(data[x], data[x + 1] if x < 3 else wrap) for x in range(4)]
+        upper[3] = [jnp.where(sub == count_x - 1, 2.0 * f, g) for f, g in zip(data[3][1], upper[3])]
+        below = [jnp.where(sub == 0, 2.0 * f, rolled(g, 1)) for f, g in zip(data[0][1], upper[3])]
+        lower = [below] + upper[:3]
+        return [[a - b for a, b in zip(u, l)] for u, l in zip(upper, lower)]
+
+    def advanced(above, here, under, prim_above, prim_here, prim_under):
+        changes = across_x(here, prim_here)
+        out = []
+        for x in range(4):
+            change = [a + b for a, b in zip(changes[x], turned_change(here[x], prim_here[x], 1, 1, ends_y))]
+            fz, az = flux(here[x], prim_here[x], 2)
+            fa, aa = flux(above[x], prim_above[x], 2)
+            lower = twice_face((above[x], fa, aa), (here[x], fz, az))
+            if under is None:
+                upper = [2.0 * f for f in fz]
+            else:
+                fu, au = flux(under[x], prim_under[x], 2)
+                upper = twice_face((here[x], fz, az), (under[x], fu, au))
+            out.append([s - (0.5 * cell_ratio) * (c + u - l) for s, c, u, l in zip(here[x], change, upper, lower)])
+        return out
+
+    prims = [[primitives(state[z][x]) for x in range(4)] for z in range(3)]
+    middle = advanced(state[0], state[1], state[2], prims[0], prims[1], prims[2])
+    deepest = advanced(state[1], state[2], None, prims[1], prims[2], None)
+    prim_mid, prim_deep = [primitives(s) for s in middle], [primitives(s) for s in deepest]
+    final = advanced(middle, deepest, None, prim_mid, prim_deep, None)
+    ids = columns(15)
+    for x in range(4):
+        s, prim = final[x], primitives(final[x])
+        at = pl.ds(x * count_x, count_x)
+        faces[0, at, :] = face_area * s[1] * prim[2]
+        faces[1, at, :] = face_area * s[2] * prim[2]
+        faces[2, at, :] = face_area * (s[3] * prim[2] + prim[3])
+        faces[3, at, :] = ids[x]
+
+
+def surface_kernel(nodes_y, count_x, bottoms, region, xl, xh, yl, yh, material, tables, out1, out2, total, faces):
+    base_x = (8 * position("gx") - 4).astype(f32)
+    base_y = (16 * along_y() - 4).astype(f32)
+    bottom_tractions(bottoms, count_x, faces)
     deposit(faces, nodes_y, base_x, base_y, total)
     region_now = jnp.concatenate([region[0], region[1]], axis=0).astype(f32) + 1.0
     respond(total, region_grid(region_now, xl, xh, yl, yh), material, tables, out1, out2)
@@ -691,9 +855,23 @@
 
 def shards(density, momentum, energy, displacement, velocity_field, acceleration, material, element_region_index,
            face_dest, face_slot):
-    along_y = ("grp", "gy")
-    place_x, place_y = lax.axis_index("gx"), lax.axis_index(along_y)
-    nodes_y = 16 * lax.axis_size(along_y) + 1
+    along = ("grp", "gy")
+    nodes_y = 16 * lax.axis_size(along) + 1
+    count_x, rank = lax.axis_size("gx"), ("grp", "gx", "gy")
+    devices = lax.axis_size(rank)
+    crater = (density, momentum, energy)
+    bottoms, rows = call(
+        functools.partial(start_kernel, float(nodes_y)),
+        crater + (face_dest.reshape(1, -1), face_slot),
+        [(devices, 16, 128), (4, 5, 8, 256)],
+        [],
+    )
+    bottoms = lax.all_to_all(bottoms, rank, 0, 0, tiled=True)
+    rows = lax.all_to_all(rows, along, 0, 0, tiled=True)
+    own, first, second = call(widen_kernel, crater + (rows,), [(5, 4, 40, 256), (5, 72, 256), (5, 72, 256)], [])
+    first = lax.ppermute(first, "gx", [(i, i ^ 1) for i in range(count_x)])
+    pairs = [(i, i + 1) for i in range(1, count_x - 1, 2)]
+    second = lax.ppermute(second, "gx", pairs + [(j, i) for i, j in pairs])
     region = element_region_index
     b, f, x_low, x_high, y_low, y_high = call(
         first_kernel,
@@ -706,27 +884,19 @@
     y_low, y_high = call(
         functools.partial(edge_kernel, True), (y_low, y_high, xl, xh), [(18, 8, 128), (18, 8, 128)], []
     )
-    yl, yh = exchange(along_y, y_low, y_high)
-    hydro_state = jnp.concatenate([density[None], momentum, energy[None]], axis=0)
-    for repeat in range(2):
-        padded = extended_2(hydro_state, (("gx", 1), (("grp", "gy"), 2)), 1)
-        hydro_state = advance(pad_depth(fix_edges(padded, 1)))
-    traction = surface_traction(hydro_state).reshape(3, -1)
-    targets, slots = face_dest[0, :, 0], face_slot[0]
-    count_x, count_gy = lax.axis_size("gx"), lax.axis_size("gy")
-    node_x = targets // count_gy % count_x * 8 + slots // 17
-    node_y = (targets // (count_gy * count_x) * count_gy + targets % count_gy) * 16 + slots % 17
-    ids = (node_x * nodes_y + node_y).astype(f32)
-    faces = lax.all_gather(
-        jnp.concatenate([traction, ids[None]], axis=0)[:, None, :], ("grp", "gx", "gy"), axis=1, tiled=True
+    yl, yh = exchange(along, y_low, y_high)
+    (hydro_state,) = call(
+        crater_kernel,
+        (own, first, second),
+        [(5, 4, 32, 256)],
+        [(5, 8, 40, 256), (5, 8, 40, 256), (6, 40, 256), (5, 40, 256), (6, 40, 256)],
     )
-    here = jnp.stack([place_x, place_y]).astype(jnp.int32)
     surf1, surf2 = call(
-        functools.partial(surface_kernel, float(nodes_y)),
-        (faces, here, region, xl, xh, yl, yh, material, jnp.asarray(surface_tables())),
+        functools.partial(surface_kernel, float(nodes_y), count_x),
+        (bottoms.reshape(devices * 16, 128), region, xl, xh, yl, yh, material, jnp.asarray(surface_tables())),
         [(24, 256), (24, 256)],
-        [(360, 128)],
-        smem=(1, 7),
+        [(360, 128), (4, 4 * count_x, 128)],
+        smem=(6,),
     )
     a1, f2, x_low, x_high, y_low, y_high, scales = call(
         second_kernel,
@@ -739,7 +909,7 @@
     y_low, y_high = call(
         functools.partial(edge_kernel, False), (y_low, y_high, xl2, xh2), [(15, 8, 128), (15, 8, 128)], []
     )
-    yl2, yh2 = exchange(along_y, y_low, y_high)
+    yl2, yh2 = exchange(along, y_low, y_high)
     u_out, v_out, a_out = call(
         last_kernel,
         (a1, f2, xl2, xh2, yl2, yh2, scales, surf1, surf2, displacement, velocity_field, acceleration),

time: 169 us -> 99.3 us (0.59)
  the two profiles are of different devices: /device:TPU:0 before, /device:TPU:3 now
where the time goes in v3:
time: 99.3 us; the launch traced here: 98.3 us
  starting transfers between devices  31.8 us (32%)
  Pallas kernels  27.3 us (27%)
  local copies, waits for them, and re-layouts  21.8 us (22%)
  waiting for transfers between devices  8.71 us (9%)
  blocking collectives  7.67 us (8%)
    pallas_call x9, Pallas kernels, call(): pl.pallas_call(kernel, out_shape=[jax.ShapeDtypeStruct(s, f32) for s in o...  27.3 us
    ppermute x8, starting transfers between devices, exchange(): return (lax.ppermute(to_high, axis, up), lax.ppermute(to_low, axis, down))  22.1 us
    unnamed x56, local copies, waits for them, and re-layouts  21.8 us
    ppermute x8, waiting for transfers between devices, exchange(): return (lax.ppermute(to_high, axis, up), lax.ppermute(to_low, axis, down))  8.7 us
    all_to_all x1, blocking collectives, shards(): rows = lax.all_to_all(rows, along, 0, 0, tiled=True)  7.67 us
    all_to_all x1, starting transfers between devices, shards(): bottoms = lax.all_to_all(bottoms, rank, 0, 0, tiled=True)  5.38 us
    ppermute x1, starting transfers between devices, shards(): second = lax.ppermute(second, 'gx', pairs + [(j, i) for i, j in pairs])  4.25 us
  transfers between devices with their start and end apart: 11, of which 4 were waited for; matrix products, arithmetic and copies ran while one was open for 1% of the time, Pallas kernels for 22%

profile of v3, /device:TPU:3, one launch (start us, length us, event | category | flops | bytes accessed | tf_op | source)
XLA Modules:
  0.0 98.3 jit_solution(13030333498742216028)
XLA Ops:
  0.6 1.0 %copy-done.2 = f32[3,4,32,256]{3,2,1,0:T(8,128)S(1)} copy-done((f32[3,4,32,256]{3,2,1,0:T(8,128)S(1)}, f32[3,4,32,256]{3,2,1,0:T(8,128)}, u32[]{:S(2)}) %copy-start.2) | copy-done | bytes 393240
  1.6 0.9 copy-done.8
  2.5 0.9 copy-done.10
  3.4 0.7 copy-done.20
  4.1 0.7 copy-done.21
  4.8 1.3 %shard_map.138 = (f32[32,16,128]{2,1,0:T(8,128)}, f32[4,5,8,256]{3,2,1,0:T(8,128)S(1)}) custom-call(f32[4,32,256]{2,1,0:T(8,128)S(1)} %copy-done.8, f32[3,4,32,256]{3,2,1,0:T(8,128)S(1)} %copy-done.2, f32[4,32,256]{2,1,0:T(8,128)S(1)} %copy-done.10, s32[1,128]{1,0:T(1,128)S(1)} %bitcast.3, s32[1,128]{1,0:T(1,128)S(1)} %copy-done.21), custom_call_target="tpu_custom_call" | custom-call | tf_op jit(solution)/shard_map/pallas_call | solution.py:409
  6.1 7.7 %all_to_all.10.came = f32[4,5,8,256]{3,2,1,0:T(8,128)S(1)} all-to-all(f32[4,5,8,256]{3,2,1,0:T(8,128)S(1)} %get-tuple-element.31), channel_id=1, replica_groups=mesh['grp'=2,'gx'=8,'gy'=2] {'grp','gy'}, dimensions={0} | all-to-all | bytes 327680 | tf_op jit(solution)/shard_map/all_to_all | solution.py:870
  13.8 5.4 %all-to-all-start.1 = ((f32[32,16,128]{2,1,0:T(8,128)}), f32[32,16,128]{2,1,0:T(8,128)S(1)}, u32[]{:S(2)}, u32[]{:S(2)}) async-start(f32[32,16,128]{2,1,0:T(8,128)} %get-tuple-element.52), calls=%async_computation.1 | async-start | bytes 524288 | tf_op jit(solution)/shard_map/all_to_all | solution.py:869
  19.2 0.3 copy.15.u
  19.5 0.9 copy-done.23
  20.5 0.3 copy.16.v
  20.8 1.0 copy-done.24
  21.8 0.3 copy.17.a
  22.1 0.3 copy-done.17
  22.5 7.5 %shard_map.141 = (f32[3,5,5,4,8,128]{5,4,3,2,1,0:T(8,128)S(1)}, f32[3,5,5,4,8,128]{5,4,3,2,1,0:T(8,128)S(1)}, f32[31,8,128]{2,1,0:T(8,128)S(1)}, f32[31,8,128]{2...) custom-call(f32[3,9,17,512]{3,2,1,0:T(8,128)S(1)} %copy.15.u, f32[3,9,17,512]{3,2,1,0:T(8,128)S(1)} %copy.16.v, ...), custom_call_target="tpu_custom_call" | custom-call | tf_op jit(solution)/shard_map/pallas_call | solution.py:409
  30.0 3.1 %collective-permute-start.2 = (f32[31,8,128]{2,1,0:T(8,128)S(1)}, f32[31,8,128]{2,1,0:T(8,128)S(1)}, u32[]{:S(2)}, u32[]{:S(2)}) collective-permute-start(f32[31,8,128]{2,1,0:T(8,128)S(1)} %get-tuple-element.37), channel_id=1, source_target_pairs={{0,2},{2,4},{4,6},{6,8},{8,10},{10,12},{12,14},{1,3},{3,5},{5,7},{... | collective-permute-start | bytes 380936 | tf_op jit(solution)/shard_map/ppermute | solution.py:428
  33.1 2.2 %collective-permute-start.3 = (f32[31,8,128]{2,1,0:T(8,128)S(1)}, f32[31,8,128]{2,1,0:T(8,128)S(1)}, u32[]{:S(2)}, u32[]{:S(2)}) collective-permute-start(f32[31,8,128]{2,1,0:T(8,128)S(1)} %get-tuple-element.38), channel_id=1, source_target_pairs={{2,0},{4,2},{6,4},{8,6},{10,8},{12,10},{14,12},{3,1},{5,3},{7,5},{... | collective-permute-start | bytes 380936 | tf_op jit(solution)/shard_map/ppermute | solution.py:428
  35.3 0.2 shard_map.139
  35.5 0.1 collective-permute-start
  35.6 4.3 %collective-permute-start.1 = (f32[5,72,256]{2,1,0:T(8,128)S(1)}, f32[5,72,256]{2,1,0:T(8,128)S(1)}, u32[]{:S(2)}, u32[]{:S(2)}) collective-permute-start(f32[5,72,256]{2,1,0:T(8,128)S(1)} %get-tuple-element.34), channel_id=1, source_target_pairs={{2,4},{6,8},{10,12},{4,2},{8,6},{12,10},{3,5},{7,9},{11,13},{5,3},... | collective-permute-start | bytes 1105928 | tf_op jit(solution)/shard_map/ppermute | solution.py:874
  39.8 0.4 collective-permute-done.3.from_high.xh
  40.3 4.7 %collective-permute-start.4 = (f32[18,8,128]{2,1,0:T(8,128)S(1)}, f32[18,8,128]{2,1,0:T(8,128)S(1)}, u32[]{:S(2)}, u32[]{:S(2)}) collective-permute-start(f32[18,8,128]{2,1,0:T(8,128)S(1)} %get-tuple-element.41), channel_id=1, source_target_pairs={{0,1},{1,16},{16,17},{2,3},{3,18},{18,19},{4,5},{5,20},{20,21},{6,... | collective-permute-start | bytes 221192 | tf_op jit(solution)/shard_map/ppermute | solution.py:428
  45.0 1.9 %collective-permute-start.5 = (f32[18,8,128]{2,1,0:T(8,128)S(1)}, f32[18,8,128]{2,1,0:T(8,128)S(1)}, u32[]{:S(2)}, u32[]{:S(2)}) collective-permute-start(f32[18,8,128]{2,1,0:T(8,128)S(1)} %get-tuple-element.42), channel_id=1, source_target_pairs={{1,0},{16,1},{17,16},{3,2},{18,3},{19,18},{5,4},{20,5},{21,20},{7,... | collective-permute-start | bytes 221192 | tf_op jit(solution)/shard_map/ppermute | solution.py:428
  47.0 4.0 %collective-permute-done.5.yh = f32[18,8,128]{2,1,0:T(8,128)S(1)} collective-permute-done((f32[18,8,128]{2,1,0:T(8,128)S(1)}, f32[18,8,128]{2,1,0:T(8,128)S(1)}, u32[]{:S(2)}, u32[]{:S(2)}) %collective-permute-start.5) | collective-permute-done | bytes 73760 | tf_op jit(solution)/shard_map/ppermute | solution.py:428
  51.0 3.9 %shard_map.143 = (f32[3,5,5,4,8,128]{5,4,3,2,1,0:T(8,128)S(1)}, f32[3,5,5,4,8,128]{5,4,3,2,1,0:T(8,128)S(1)}, f32[30,8,128]{2,1,0:T(8,128)S(1)}, f32[30,8,128]{2...) custom-call(f32[3,5,5,4,8,128]{5,4,3,2,1,0:T(8,128)S(1)} %get-tuple-elemen, ...), custom_call_target="tpu_custom_call" | custom-call | tf_op jit(solution)/shard_map/pallas_call | solution.py:409
  55.0 1.0 %copy-done.4 = f32[3,5,5,4,8,128]{5,4,3,2,1,0:T(8,128)} copy-done((f32[3,5,5,4,8,128]{5,4,3,2,1,0:T(8,128)}, f32[3,5,5,4,8,128]{5,4,3,2,1,0:T(8,128)S(1)}, u32[]{:S(2)}) %copy-start.4) | copy-done | bytes 1228824
  56.0 1.0 %copy-done.6 = f32[3,5,5,4,8,128]{5,4,3,2,1,0:T(8,128)} copy-done((f32[3,5,5,4,8,128]{5,4,3,2,1,0:T(8,128)}, f32[3,5,5,4,8,128]{5,4,3,2,1,0:T(8,128)S(1)}, u32[]{:S(2)}) %copy-start.6) | copy-done | bytes 1228824
  57.0 3.0 %collective-permute-start.6 = (f32[30,8,128]{2,1,0:T(8,128)S(1)}, f32[30,8,128]{2,1,0:T(8,128)S(1)}, u32[]{:S(2)}, u32[]{:S(2)}) collective-permute-start(f32[30,8,128]{2,1,0:T(8,128)S(1)} %get-tuple-element.45), channel_id=1, source_target_pairs={{0,2},{2,4},{4,6},{6,8},{8,10},{10,12},{12,14},{1,3},{3,5},{5,7},{... | collective-permute-start | bytes 368648 | tf_op jit(solution)/shard_map/ppermute | solution.py:428
  60.0 2.3 %collective-permute-start.7 = (f32[30,8,128]{2,1,0:T(8,128)S(1)}, f32[30,8,128]{2,1,0:T(8,128)S(1)}, u32[]{:S(2)}, u32[]{:S(2)}) collective-permute-start(f32[30,8,128]{2,1,0:T(8,128)S(1)} %get-tuple-element.46), channel_id=1, source_target_pairs={{2,0},{4,2},{6,4},{8,6},{10,8},{12,10},{14,12},{3,1},{5,3},{7,5},{... | collective-permute-start | bytes 368648 | tf_op jit(solution)/shard_map/ppermute | solution.py:428
  62.3 0.3 collective-permute-done.6.from_low.xl
  62.7 3.9 %collective-permute-done.7.from_high.xh = f32[30,8,128]{2,1,0:T(8,128)S(1)} collective-permute-done((f32[30,8,128]{2,1,0:T(8,128)S(1)}, f32[30,8,128]{2,1,0:T(8,128)S(1)}, u32[]{:S(2)}, u32[]{:S(2)}) %collective-permute-start.7) | collective-permute-done | bytes 122912 | tf_op jit(solution)/shard_map/ppermute | solution.py:428
  66.5 0.7 shard_map.144
  67.2 3.0 %collective-permute-start.8 = (f32[15,8,128]{2,1,0:T(8,128)}, f32[15,8,128]{2,1,0:T(8,128)S(1)}, u32[]{:S(2)}, u32[]{:S(2)}) collective-permute-start(f32[15,8,128]{2,1,0:T(8,128)} %get-tuple-element.49), channel_id=1, source_target_pairs={{0,1},{1,16},{16,17},{2,3},{3,18},{18,19},{4,5},{5,20},{20,21},{6,... | collective-permute-start | bytes 184328 | tf_op jit(solution)/shard_map/ppermute | solution.py:428
  70.2 1.9 %collective-permute-start.9 = (f32[15,8,128]{2,1,0:T(8,128)}, f32[15,8,128]{2,1,0:T(8,128)}, u32[]{:S(2)}, u32[]{:S(2)}) collective-permute-start(f32[15,8,128]{2,1,0:T(8,128)} %get-tuple-element.50), channel_id=1, source_target_pairs={{1,0},{16,1},{17,16},{3,2},{18,3},{19,18},{5,4},{20,5},{21,20},{7,... | collective-permute-start | bytes 184328 | tf_op jit(solution)/shard_map/ppermute | solution.py:428
  72.1 4.9 %shard_map.140 = f32[5,4,32,256]{3,2,1,0:T(8,128)} custom-call(f32[5,4,40,256]{3,2,1,0:T(8,128)S(1)} %get-tuple-element.32.own, f32[5,72,256]{2,1,0:T(8,128)S(1)} %collective-permute-done.came1, f32[5,72,256]{2,1,0:T(8,128)S(1)} %collective-permute-done.1.came2), custom_call_target="tpu_custom_call" | custom-call | tf_op jit(solution)/shard_map/pallas_call | solution.py:409
  77.1 1.0 %copy-done.12 = f32[6,128,128]{2,1,0:T(8,128)S(1)} copy-done((f32[6,128,128]{2,1,0:T(8,128)S(1)}, f32[6,128,128]{2,1,0:T(8,128)}, u32[]{:S(2)}) %copy-start.12) | copy-done | bytes 393240
  78.1 0.9 copy-done.14
  79.0 0.7 copy-done.19
  79.7 4.8 %shard_map.145 = (f32[24,256]{1,0:T(8,128)S(1)}, f32[24,256]{1,0:T(8,128)S(1)}) custom-call(f32[512,128]{1,0:T(8,128)S(1)} %bitcast.2, s32[2,4,128]{2,1,0:T(4,128)S(1)} %copy-done.17, f32[31,8,128]{2,1,0:T(8,128)S(1)} %collective-permute-done.2.from_low.xl, f32[31,8,128]{2,1,0:T(8,128)S(1)} %collective-permute-done.3.from_high.xh, ...), custom_call_target="tpu_custom_call" | custom-call | tf_op jit(solution)/shard_map/pallas_call | solution.py:409
  84.5 0.0 collective-permute-done.9.yh
  84.5 1.3 %copy-done.1 = f32[3,9,17,512]{3,2,1,0:T(8,128)S(1)} copy-done((f32[3,9,17,512]{3,2,1,0:T(8,128)S(1)}, f32[3,9,17,512]{3,2,1,0:T(8,128)}, u32[]{:S(2)}) %copy-start.1) | copy-done | bytes 940056
  85.8 1.3 %copy-done.5 = f32[3,5,5,4,8,128]{5,4,3,2,1,0:T(8,128)S(1)} copy-done((f32[3,5,5,4,8,128]{5,4,3,2,1,0:T(8,128)S(1)}, f32[3,5,5,4,8,128]{5,4,3,2,1,0:T(8,128)}, u32[]{:S(2)}) %copy-start.5) | copy-done | bytes 1228824
  87.1 1.3 %copy-done.7 = f32[3,5,5,4,8,128]{5,4,3,2,1,0:T(8,128)S(1)} copy-done((f32[3,5,5,4,8,128]{5,4,3,2,1,0:T(8,128)S(1)}, f32[3,5,5,4,8,128]{5,4,3,2,1,0:T(8,128)}, u32[]{:S(2)}) %copy-start.7) | copy-done | bytes 1228824
  88.4 0.9 copy-done.16
  89.3 3.9 %shard_map.146 = (f32[3,9,17,512]{3,2,1,0:T(8,128)S(1)}, f32[3,9,17,512]{3,2,1,0:T(8,128)S(1)}, f32[3,9,17,512]{3,2,1,0:T(8,128)S(1)}) custom-call(f32[3,5,5,4,8,128]{5,4,3,2,1,0:T(8,128)S(1)} %copy-done.5, f32[3,5,5,4,8,128]{5,4,3,2,1,0:T(8,128)S(1)} %copy-done.7, f32[30,8,128]{2,1,0:T(8,128)S(1)} %collective-permute-done.6.from_low.xl, ...), custom_call_target="tpu_custom_call" | custom-call | tf_op jit(solution)/shard_map/pallas_call | solution.py:409
  93.2 1.7 %copy.21 = f32[3,9,17,512]{3,0,2,1:T(4,128)} copy(f32[3,9,17,512]{3,2,1,0:T(8,128)S(1)} %get-tuple-element.59) | data formatting | bytes 1880064
  94.9 1.7 %copy.22 = f32[3,9,17,512]{3,0,2,1:T(4,128)} copy(f32[3,9,17,512]{3,2,1,0:T(8,128)S(1)} %get-tuple-element.60) | data formatting | bytes 1880064
  96.6 1.7 %copy.23 = f32[3,9,17,512]{3,0,2,1:T(4,128)} copy(f32[3,9,17,512]{3,2,1,0:T(8,128)S(1)} %get-tuple-element.61) | data formatting | bytes 1880064
  (40 shorter events, 0.1 us)
Async XLA Ops:
  0.6 1.0 %copy-start.2 = (f32[3,4,32,256]{3,2,1,0:T(8,128)S(1)}, f32[3,4,32,256]{3,2,1,0:T(8,128)}, u32[]{:S(2)}) copy-start(f32[3,4,32,256]{3,2,1,0:T(8,128)} %momentum.3) | copy-start | bytes 1179652
  1.6 0.9 copy-start.8
  2.5 0.9 copy-start.10
  3.4 0.7 copy-start.20
  4.1 0.7 copy-start.21
  4.8 14.4 %copy-start.22 = (f32[3,9,17,512]{3,0,2,1:T(4,128)S(1)}, f32[3,9,17,512]{3,0,2,1:T(4,128)}, u32[]{:S(2)}) copy-start(f32[3,9,17,512]{3,0,2,1:T(4,128)} %param.14) | copy-start | bytes 2820100
  13.8 63.3 %all-to-all-start.1 = ((f32[32,16,128]{2,1,0:T(8,128)}), f32[32,16,128]{2,1,0:T(8,128)S(1)}, u32[]{:S(2)}, u32[]{:S(2)}) async-start(f32[32,16,128]{2,1,0:T(8,128)} %get-tuple-element.52), calls=%async_computation.1 | async-start | bytes 524288 | tf_op jit(solution)/shard_map/all_to_all | solution.py:869
  19.2 1.3 %copy-start.23 = (f32[3,9,17,512]{3,0,2,1:T(4,128)S(1)}, f32[3,9,17,512]{3,0,2,1:T(4,128)}, u32[]{:S(2)}) copy-start(f32[3,9,17,512]{3,0,2,1:T(4,128)} %param.15) | copy-start | bytes 2820100
  20.5 1.3 %copy-start.24 = (f32[3,9,17,512]{3,0,2,1:T(4,128)S(1)}, f32[3,9,17,512]{3,0,2,1:T(4,128)}, u32[]{:S(2)}) copy-start(f32[3,9,17,512]{3,0,2,1:T(4,128)} %param.16) | copy-start | bytes 2820100
  21.7 0.7 copy-start.17
  21.8 0.7 copy-start.18
  22.4 7.5 %copy-start = (f32[3,9,17,512]{3,2,1,0:T(8,128)}, f32[3,9,17,512]{3,2,1,0:T(8,128)S(1)}, u32[]{:S(2)}) copy-start(f32[3,9,17,512]{3,2,1,0:T(8,128)S(1)} %copy.17.a) | copy-start | bytes 2820100
  22.4 12.8 %copy-start.3 = (f32[3,4,32,256]{3,2,1,0:T(8,128)S(1)}, f32[3,4,32,256]{3,2,1,0:T(8,128)}, u32[]{:S(2)}) copy-start(f32[3,4,32,256]{3,2,1,0:T(8,128)} %momentum.3) | copy-start | bytes 1179652
  22.5 12.8 %copy-start.9 = (f32[4,32,256]{2,1,0:T(8,128)S(1)}, f32[4,32,256]{2,1,0:T(8,128)}, u32[]{:S(2)}) copy-start(f32[4,32,256]{2,1,0:T(8,128)} %density.3) | copy-start | bytes 393220
  22.5 12.8 %copy-start.11 = (f32[4,32,256]{2,1,0:T(8,128)S(1)}, f32[4,32,256]{2,1,0:T(8,128)}, u32[]{:S(2)}) copy-start(f32[4,32,256]{2,1,0:T(8,128)} %energy.3) | copy-start | bytes 393220
  30.0 9.8 %collective-permute-start.2 = (f32[31,8,128]{2,1,0:T(8,128)S(1)}, f32[31,8,128]{2,1,0:T(8,128)S(1)}, u32[]{:S(2)}, u32[]{:S(2)}) collective-permute-start(f32[31,8,128]{2,1,0:T(8,128)S(1)} %get-tuple-element.37), channel_id=1, source_target_pairs={{0,2},{2,4},{4,6},{6,8},{8,10},{10,12},{12,14},{1,3},{3,5},{5,7},{... | collective-permute-start | bytes 380936 | tf_op jit(solution)/shard_map/ppermute | solution.py:428
  33.1 7.2 %collective-permute-start.3 = (f32[31,8,128]{2,1,0:T(8,128)S(1)}, f32[31,8,128]{2,1,0:T(8,128)S(1)}, u32[]{:S(2)}, u32[]{:S(2)}) collective-permute-start(f32[31,8,128]{2,1,0:T(8,128)S(1)} %get-tuple-element.38), channel_id=1, source_target_pairs={{2,0},{4,2},{6,4},{8,6},{10,8},{12,10},{14,12},{3,1},{5,3},{7,5},{... | collective-permute-start | bytes 380936 | tf_op jit(solution)/shard_map/ppermute | solution.py:428
  35.5 36.6 %collective-permute-start = (f32[5,72,256]{2,1,0:T(8,128)S(1)}, f32[5,72,256]{2,1,0:T(8,128)S(1)}, u32[]{:S(2)}, u32[]{:S(2)}) collective-permute-start(f32[5,72,256]{2,1,0:T(8,128)S(1)} %get-tuple-element.33), channel_id=1, source_target_pairs={{0,2},{2,0},{4,6},{6,4},{8,10},{10,8},{12,14},{14,12},{1,3},{3,1},... | collective-permute-start | bytes 1105928 | tf_op jit(solution)/shard_map/ppermute | solution.py:872
  35.6 36.6 %collective-permute-start.1 = (f32[5,72,256]{2,1,0:T(8,128)S(1)}, f32[5,72,256]{2,1,0:T(8,128)S(1)}, u32[]{:S(2)}, u32[]{:S(2)}) collective-permute-start(f32[5,72,256]{2,1,0:T(8,128)S(1)} %get-tuple-element.34), channel_id=1, source_target_pairs={{2,4},{6,8},{10,12},{4,2},{8,6},{12,10},{3,5},{7,9},{11,13},{5,3},... | collective-permute-start | bytes 1105928 | tf_op jit(solution)/shard_map/ppermute | solution.py:874
  40.3 6.7 %collective-permute-start.4 = (f32[18,8,128]{2,1,0:T(8,128)S(1)}, f32[18,8,128]{2,1,0:T(8,128)S(1)}, u32[]{:S(2)}, u32[]{:S(2)}) collective-permute-start(f32[18,8,128]{2,1,0:T(8,128)S(1)} %get-tuple-element.41), channel_id=1, source_target_pairs={{0,1},{1,16},{16,17},{2,3},{3,18},{18,19},{4,5},{5,20},{20,21},{6,... | collective-permute-start | bytes 221192 | tf_op jit(solution)/shard_map/ppermute | solution.py:428
  45.0 6.0 %collective-permute-start.5 = (f32[18,8,128]{2,1,0:T(8,128)S(1)}, f32[18,8,128]{2,1,0:T(8,128)S(1)}, u32[]{:S(2)}, u32[]{:S(2)}) collective-permute-start(f32[18,8,128]{2,1,0:T(8,128)S(1)} %get-tuple-element.42), channel_id=1, source_target_pairs={{1,0},{16,1},{17,16},{3,2},{18,3},{19,18},{5,4},{20,5},{21,20},{7,... | collective-permute-start | bytes 221192 | tf_op jit(solution)/shard_map/ppermute | solution.py:428
  51.0 4.0 %copy-start.13 = (f32[18,8,128]{2,1,0:T(8,128)}, f32[18,8,128]{2,1,0:T(8,128)S(1)}, u32[]{:S(2)}) copy-start(f32[18,8,128]{2,1,0:T(8,128)S(1)} %collective-permute-done.5.yh) | copy-start | bytes 221188
  55.0 1.0 %copy-start.4 = (f32[3,5,5,4,8,128]{5,4,3,2,1,0:T(8,128)}, f32[3,5,5,4,8,128]{5,4,3,2,1,0:T(8,128)S(1)}, u32[]{:S(2)}) copy-start(f32[3,5,5,4,8,128]{5,4,3,2,1,0:T(8,128)S(1)} %get-tuple-element.43.a1) | copy-start | bytes 3686404
  56.0 1.0 %copy-start.6 = (f32[3,5,5,4,8,128]{5,4,3,2,1,0:T(8,128)}, f32[3,5,5,4,8,128]{5,4,3,2,1,0:T(8,128)S(1)}, u32[]{:S(2)}) copy-start(f32[3,5,5,4,8,128]{5,4,3,2,1,0:T(8,128)S(1)} %get-tuple-element.44.f) | copy-start | bytes 3686404
  57.0 15.1 %copy-start.15 = (f32[3,3,2,8,128]{4,3,2,1,0:T(8,128)}, f32[3,3,2,8,128]{4,3,2,1,0:T(8,128)S(1)}, u32[]{:S(2)}) copy-start(f32[3,3,2,8,128]{4,3,2,1,0:T(8,128)S(1)} %get-tuple-element.51.scales) | copy-start | bytes 221188
  57.0 5.6 %collective-permute-start.6 = (f32[30,8,128]{2,1,0:T(8,128)S(1)}, f32[30,8,128]{2,1,0:T(8,128)S(1)}, u32[]{:S(2)}, u32[]{:S(2)}) collective-permute-start(f32[30,8,128]{2,1,0:T(8,128)S(1)} %get-tuple-element.45), channel_id=1, source_target_pairs={{0,2},{2,4},{4,6},{6,8},{8,10},{10,12},{12,14},{1,3},{3,5},{5,7},{... | collective-permute-start | bytes 368648 | tf_op jit(solution)/shard_map/ppermute | solution.py:428
  60.0 6.5 %collective-permute-start.7 = (f32[30,8,128]{2,1,0:T(8,128)S(1)}, f32[30,8,128]{2,1,0:T(8,128)S(1)}, u32[]{:S(2)}, u32[]{:S(2)}) collective-permute-start(f32[30,8,128]{2,1,0:T(8,128)S(1)} %get-tuple-element.46), channel_id=1, source_target_pairs={{2,0},{4,2},{6,4},{8,6},{10,8},{12,10},{14,12},{3,1},{5,3},{7,5},{... | collective-permute-start | bytes 368648 | tf_op jit(solution)/shard_map/ppermute | solution.py:428
  67.2 17.3 %collective-permute-start.8 = (f32[15,8,128]{2,1,0:T(8,128)}, f32[15,8,128]{2,1,0:T(8,128)S(1)}, u32[]{:S(2)}, u32[]{:S(2)}) collective-permute-start(f32[15,8,128]{2,1,0:T(8,128)} %get-tuple-element.49), channel_id=1, source_target_pairs={{0,1},{1,16},{16,17},{2,3},{3,18},{18,19},{4,5},{5,20},{20,21},{6,... | collective-permute-start | bytes 184328 | tf_op jit(solution)/shard_map/ppermute | solution.py:428
  70.2 14.3 %collective-permute-start.9 = (f32[15,8,128]{2,1,0:T(8,128)}, f32[15,8,128]{2,1,0:T(8,128)}, u32[]{:S(2)}, u32[]{:S(2)}) collective-permute-start(f32[15,8,128]{2,1,0:T(8,128)} %get-tuple-element.50), channel_id=1, source_target_pairs={{1,0},{16,1},{17,16},{3,2},{18,3},{19,18},{5,4},{20,5},{21,20},{7,... | collective-permute-start | bytes 184328 | tf_op jit(solution)/shard_map/ppermute | solution.py:428
  77.1 1.0 %copy-start.12 = (f32[6,128,128]{2,1,0:T(8,128)S(1)}, f32[6,128,128]{2,1,0:T(8,128)}, u32[]{:S(2)}) copy-start(f32[6,128,128]{2,1,0:T(8,128)} %constant.2.clone.tables) | copy-start | bytes 1179652
  78.1 0.9 copy-start.14
  79.0 0.7 copy-start.19
  84.5 1.3 %copy-start.1 = (f32[3,9,17,512]{3,2,1,0:T(8,128)S(1)}, f32[3,9,17,512]{3,2,1,0:T(8,128)}, u32[]{:S(2)}) copy-start(f32[3,9,17,512]{3,2,1,0:T(8,128)} %copy-done) | copy-start | bytes 2820100
  85.8 1.3 %copy-start.5 = (f32[3,5,5,4,8,128]{5,4,3,2,1,0:T(8,128)S(1)}, f32[3,5,5,4,8,128]{5,4,3,2,1,0:T(8,128)}, u32[]{:S(2)}) copy-start(f32[3,5,5,4,8,128]{5,4,3,2,1,0:T(8,128)} %copy-done.4) | copy-start | bytes 3686404
  87.1 1.3 %copy-start.7 = (f32[3,5,5,4,8,128]{5,4,3,2,1,0:T(8,128)S(1)}, f32[3,5,5,4,8,128]{5,4,3,2,1,0:T(8,128)}, u32[]{:S(2)}) copy-start(f32[3,5,5,4,8,128]{5,4,3,2,1,0:T(8,128)} %copy-done.6) | copy-start | bytes 3686404
  88.4 0.9 copy-start.16

commit v4 on v3

--- a/solution.py
+++ b/solution.py
@@ -13,7 +13,6 @@
 half_size = 2.0
 time_step = 0.1
 face_area = 2.0
-vmem_bytes = 40 * 1024 * 1024
 
 
 def gll_tables():
@@ -201,16 +200,29 @@
     return pltpu.roll(x, amount, axis) if amount else x
 
 
-def pack_x(force, low, high):
-    sub = rows_of()
+def parity_x():
+    return position("gx") % 2
+
+
+def parity_y():
+    return along_y() % 2
+
+
+def sort_out(odd, low, high):
+    return jnp.where(odd == 1, low, high), jnp.where(odd == 1, high, low)
+
+
+def pack_x(force, first, second):
+    sub, odd = rows_of(), parity_x()
     for c in range(3):
         for j in range(5):
             for half in range(2):
                 at = (c * 5 + j) * 2 + half
                 a, b = force[c, 0, j, 2 * half], force[c, 0, j, 2 * half + 1]
-                low[at] = jnp.where(sub < 4, a, rolled(b, 4))
+                low = jnp.where(sub < 4, a, rolled(b, 4))
                 a, b = force[c, 4, j, 2 * half], force[c, 4, j, 2 * half + 1]
-                high[at] = jnp.where(sub < 4, rolled(a, 4), b)
+                high = jnp.where(sub < 4, rolled(a, 4), b)
+                first[at], second[at] = sort_out(odd, low, high)
 
 
 def pack_y(force, low, high):
@@ -225,52 +237,73 @@
             high[c * 5 + i] = b
 
 
-def add_x(force, from_low, from_high):
-    sub = rows_of()
+def add_x(force, first, second):
+    sub, odd = rows_of(), parity_x()
     for c in range(3):
         for j in range(5):
             for half in range(2):
                 at = (c * 5 + j) * 2 + half
-                r, s = from_low[at], from_high[at]
+                r, s = sort_out(odd, first[at], second[at])
                 force[c, 0, j, 2 * half] += jnp.where(sub < 4, r, 0.0)
                 force[c, 0, j, 2 * half + 1] += jnp.where(sub < 4, rolled(r, 4), 0.0)
                 force[c, 4, j, 2 * half] += jnp.where(sub < 4, 0.0, rolled(s, 4))
                 force[c, 4, j, 2 * half + 1] += jnp.where(sub < 4, 0.0, s)
 
 
-def add_y(force, from_low, from_high):
-    sub = rows_of()
+def add_y(force, first, second):
+    sub, odd = rows_of(), parity_y()
     for c in range(3):
         for i in range(5):
-            r, s = from_low[c * 5 + i], from_high[c * 5 + i]
+            r, s = sort_out(odd, first[c * 5 + i], second[c * 5 + i])
             for k in range(4):
                 force[c, i, 0, k] += jnp.where(sub % 4 == 0, rolled(r, -k), 0.0)
                 force[c, i, 4, k] += jnp.where(sub % 4 == 3, rolled(s, 3 - k), 0.0)
 
 
-def edge_kernel(extra, low, high, from_low, from_high, *outs):
-    out_low, out_high = outs
-    sub = rows_of()
+def edge_rows(low, high, came1, came2, first, second):
+    sub, odd, odd_y = rows_of(), parity_x(), parity_y()
     for c in range(3):
+        came = [[sort_out(odd, came1[at], came2[at]) for at in range((c * 5 + j) * 2, (c * 5 + j) * 2 + 2)] for j in (0, 4)]
         for i in range(5):
-            out_low[c * 5 + i] = low[c * 5 + i]
-            out_high[c * 5 + i] = high[c * 5 + i]
-        for i, came, first in ((0, from_low, 0), (4, from_high, 4)):
-            for j, out, row in ((0, out_low, 0), (4, out_high, 3)):
-                total = out[c * 5 + i]
-                for k in range(4):
-                    r = rolled(came[(c * 5 + j) * 2 + k // 2], first + k - (4 * (k % 2) + row))
-                    total = total + jnp.where(sub == first + k, r, 0.0)
-                out[c * 5 + i] = total
-    if extra:
-        for out, mine in ((out_low, low), (out_high, high)):
-            out[15] = mine[15]
-            out[16] = from_low[30]
-            out[17] = from_high[30]
-
-
-def region_grid(own, xl, xh, yl, yh):
-    return [[yl[16], xl[30], yh[16]], [yl[15], own, yh[15]], [yl[17], xh[30], yh[17]]]
+            rows = [low[c * 5 + i], high[c * 5 + i]]
+            if i in (0, 4):
+                start, side = i, i // 4
+                for end, row in ((0, 0), (1, 3)):
+                    for k in range(4):
+                        r = rolled(came[end][k // 2][side], start + k - (4 * (k % 2) + row))
+                        rows[end] = rows[end] + jnp.where(sub == start + k, r, 0.0)
+            first[c * 5 + i], second[c * 5 + i] = sort_out(odd_y, *rows)
+
+
+def first_edge_kernel(low, high, came1, came2, density, momentum, energy, crater1, crater2, after, first, second):
+    edge_rows(low, high, came1, came2, first, second)
+    odd, odd_y = parity_x(), parity_y()
+    regions = sort_out(odd, came1[30], came2[30])
+    for n, value in enumerate((low[15], regions[0], regions[1])):
+        first[15 + n] = value
+        second[15 + n] = value
+    for f in range(5):
+        field = field_of(f, density, momentum, energy)
+        for t in range(2):
+            lanes = slice(128 * t, 128 * t + 128)
+            ends = []
+            for near, far in ((0, 1), (31, 30)):
+                own = [field[x, r : r + 1, lanes] for r in (near, far) for x in range(4)]
+                sides = sort_out(odd, crater1[f, near : near + 1, lanes], crater2[f, near : near + 1, lanes])
+                ends.append((jnp.concatenate(own, axis=0), jnp.concatenate(list(sides) * 4, axis=0)))
+            for h in range(2):
+                at = 18 + f * 4 + t * 2 + h
+                first[at], second[at] = sort_out(odd_y, ends[0][h], ends[1][h])
+
+
+def second_edge_kernel(low, high, came1, came2, after, first, second):
+    edge_rows(low, high, came1, came2, first, second)
+
+
+def region_grid(own, x1, x2, y1, y2):
+    xl, xh = sort_out(parity_x(), x1[30], x2[30])
+    yl, yh = [list(v) for v in zip(*[sort_out(parity_y(), y1[n], y2[n]) for n in (15, 16, 17)])]
+    return [[yl[1], xl, yh[1]], [yl[0], own, yh[0]], [yl[2], xh, yh[2]]]
 
 
 def shared_density(grid):
@@ -308,7 +341,7 @@
     return float(-1.0 / (half_size**3 * quad[i] * quad[j] * quad[k]))
 
 
-def first_kernel(u, v, a, region, material, b_out, f_out, x_low, x_high, y_low, y_high,
+def first_kernel(u, v, a, region, material, b_out, f_out, x1, x2, y_low, y_high,
                  elem, gx, gz, cross, planes, side, tall, nodes):
     table = depth_table()
     region_now = jnp.concatenate([region[0], region[1]], axis=0).astype(f32) + 1.0
@@ -334,21 +367,20 @@
 
     lax.fori_loop(0, 3, one, 0)
     internal(elem, f_out, lookup(material, 1, region_now), lookup(material, 2, region_now), gx, gz, cross, planes, side)
-    pack_x(f_out, x_low, x_high)
+    pack_x(f_out, x1, x2)
     pack_y(f_out, y_low, y_high)
-    x_low[30] = region_now
-    x_high[30] = region_now
+    x1[30] = region_now
+    x2[30] = region_now
     y_low[15] = region_now
-    y_high[15] = region_now
-
-
-def second_kernel(b, f, xl, xh, yl, yh, region, material, a_out, f_out, x_low, x_high, y_low, y_high, scales,
+
+
+def second_kernel(b, f, came_x1, came_x2, came_y1, came_y2, region, material, a_out, f_out, x1, x2, y_low, y_high, scales,
                   elem, gx, gz, cross, planes, side):
     region_now = jnp.concatenate([region[0], region[1]], axis=0).astype(f32) + 1.0
     a_out[...] = f[...]
-    add_x(a_out, xl, xh)
-    add_y(a_out, yl, yh)
-    grid = region_grid(region_now, xl, xh, yl, yh)
+    add_x(a_out, came_x1, came_x2)
+    add_y(a_out, came_y1, came_y2)
+    grid = region_grid(region_now, came_x1, came_x2, came_y1, came_y2)
     inverse = mass_scales(shared_density([[lookup(material, 0, r) for r in row] for row in grid]))
     for x in range(3):
         for y in range(3):
@@ -363,38 +395,48 @@
                     a_out[c, i, j, k] = value
                     elem[c, i, j, k] = b[c, i, j, k] + time_step**2 * value
     internal(elem, f_out, lookup(material, 1, region_now), lookup(material, 2, region_now), gx, gz, cross, planes, side)
-    pack_x(f_out, x_low, x_high)
+    pack_x(f_out, x1, x2)
     pack_y(f_out, y_low, y_high)
 
 
-def last_kernel(a1, f, xl, xh, yl, yh, scales, surf1, surf2, u, v, a, u_out, v_out, a_out, tall, nodes, nodes2, force):
+def add_surface(source, x, c, count):
+    at = 8 * (c * 9 + x)
+    tile, shift = at // 128, (128 - at % 128) % 128
+    moved = rolled(source[0:17, 128 * tile : 128 * tile + 128], shift, 1)
+    return jnp.where(lanes_of((17, 128)) < count, moved, 0.0)
+
+
+def place_kernel(a1, surf1, u, v, a, after, u_out, first, tall, nodes):
+    table = depth_table(back=True)
+    for c in range(3):
+        to_nodes(lambda k: a1[c, :, :, k], table, tall, nodes)
+        for x in range(9):
+            nodes[0, x] += add_surface(surf1, x, c, 1)
+        for t in range(4):
+            at = (c, slice(None), slice(None), slice(128 * t, 128 * t + 128))
+            first[c, t] = nodes[t]
+            u_out[at] = u[at] + 2.0 * time_step * v[at] + time_step**2 * (a[at] + nodes[t])
+
+
+def last_kernel(first, f, x1, x2, y1, y2, scales, surf1, surf2, v, a, v_out, a_out, tall, nodes, force):
     table = depth_table(back=True)
     force[...] = f[...]
-    add_x(force, xl, xh)
-    add_y(force, yl, yh)
+    add_x(force, x1, x2)
+    add_y(force, y1, y2)
     for i in range(5):
         for j in range(5):
             for k in range(4):
                 scale = scales[edge_kind(i), edge_kind(j), min(k, 1)] * accel_scale(i, j, k)
                 for c in range(3):
                     force[c, i, j, k] = force[c, i, j, k] * scale
-    lane = lanes_of((17, 128))
     for c in range(3):
-        to_nodes(lambda k: a1[c, :, :, k], table, tall, nodes)
-        to_nodes(lambda k: force[c, :, :, k], table, tall, nodes2)
+        to_nodes(lambda k: force[c, :, :, k], table, tall, nodes)
         for x in range(9):
-            at = 8 * (c * 9 + x)
-            tile, shift = at // 128, (128 - at % 128) % 128
-            moved = [rolled(s[0:17, 128 * tile : 128 * tile + 128], shift, 1) for s in (surf1, surf2)]
-            direct = jnp.where(lane < 1, moved[0], 0.0)
-            nodes[0, x] += direct
-            nodes2[0, x] += direct + jnp.where(lane < 5, moved[1], 0.0)
+            nodes[0, x] += add_surface(surf1, x, c, 1) + add_surface(surf2, x, c, 5)
         for t in range(4):
             at = (c, slice(None), slice(None), slice(128 * t, 128 * t + 128))
-            first, second = nodes[t], nodes2[t]
-            a_out[at] = second
-            u_out[at] = u[at] + 2.0 * time_step * v[at] + time_step**2 * (a[at] + first)
-            v_out[at] = v[at] + 0.5 * time_step * (a[at] + 2.0 * first + second)
+            a_out[at] = nodes[t]
+            v_out[at] = v[at] + 0.5 * time_step * (a[at] + 2.0 * first[c, t] + nodes[t])
 
 
 def whole():
@@ -405,14 +447,17 @@
     return pl.BlockSpec(memory_space=pltpu.SMEM)
 
 
-def call(kernel, ins, outs, scratch, smem=()):
+def call(kernel, ins, outs, scratch, smem=(), away=(), mib=20):
+    def spec(n):
+        return scalars() if n in smem else pl.BlockSpec(memory_space=pl.ANY) if n in away else whole()
+
     return pl.pallas_call(
         kernel,
         out_shape=[jax.ShapeDtypeStruct(s, f32) for s in outs],
-        in_specs=[scalars() if n in smem else whole() for n in range(len(ins))],
+        in_specs=[spec(n) for n in range(len(ins))],
         out_specs=[whole() for _ in outs],
         scratch_shapes=[pltpu.VMEM(s, f32) for s in scratch],
-        compiler_params=pltpu.CompilerParams(vmem_limit_bytes=vmem_bytes),
+        compiler_params=pltpu.CompilerParams(vmem_limit_bytes=mib * 1024 * 1024),
     )(*ins)
 
 
@@ -421,11 +466,11 @@
 internal_scratch = [lines_shape, (3, 5, 5, 8, 128), lines_shape, lines_shape, lines_shape, (2, 5, 5, 8, 128)]
 
 
-def exchange(axis, to_low, to_high):
+def exchange(axis, first, second):
     count = lax.axis_size(axis)
-    up = [(i, i + 1) for i in range(count - 1)]
-    down = [(j, i) for i, j in up]
-    return lax.ppermute(to_high, axis, up), lax.ppermute(to_low, axis, down)
+    pairs = [(i, i + 1) for i in range(1, count - 1, 2)]
+    first = lax.ppermute(first, axis, [(i, i ^ 1) for i in range(count)])
+    return first, lax.ppermute(second, axis, pairs + [(j, i) for i, j in pairs])
 
 
 def surface_tables():
@@ -484,19 +529,32 @@
     lax.fori_loop(0, rows // 4, one, 0)
 
 
-def top_grid(grid, z):
+def top_grid(rows, z):
     sub, lane = rows_of(), lanes_of()
     out = jnp.zeros((8, 128), f32)
     for x in range(3):
-        total = jnp.zeros((8, 128), f32)
         for y in range(3):
-            column = jnp.broadcast_to(grid[x][y][:, z : z + 1], (8, 128))
-            total = total + jnp.where((lane == 4 * y + (sub & 3) - 2), column, 0.0)
-        total = total + rolled(total, -1)
-        total = total + rolled(total, -2)
-        for ex in range(2):
-            out = jnp.where(sub == 2 * x + ex, rolled(total, 2 * x + ex - 4 * ex), out)
+            row = jnp.broadcast_to(rows[x][y], (8, 128))
+            for ex in range(2):
+                here = (sub == 2 * x + ex) & (lane >= 4 * y - 2) & (lane < 4 * y + 2) & (lane < 8)
+                out = jnp.where(here, rolled(row, 4 * y - 2 - 8 * z - 4 * ex, 1), out)
     return out
+
+
+def region_rows(bottoms, count_x):
+    gx, place, count_gy = position("gx"), along_y(), lax.axis_size("gy")
+    last_y = lax.axis_size("grp") * count_gy - 1
+    found = []
+    for x in range(3):
+        found.append([])
+        for y in range(3):
+            px, py = gx + x - 1, place + y - 1
+            inside = (px >= 0) & (px < count_x) & (py >= 0) & (py <= last_y)
+            cx, cy = jnp.clip(px, 0, count_x - 1), jnp.clip(py, 0, last_y)
+            rank = (cy // count_gy) * (count_x * count_gy) + cx * count_gy + cy % count_gy
+            row = bottoms[pl.ds(pl.multiple_of(rank * 24 + 16, 8), 1), :]
+            found[x].append(jnp.where(inside, row, 0.0))
+    return found
 
 
 def respond(total, grid, material, tables, out1, out2):
@@ -629,19 +687,18 @@
     return density if f == 0 else energy if f == 4 else momentum.at[f - 1]
 
 
-def start_kernel(nodes_y, density, momentum, energy, dest, slot, bottoms, rows):
-    lane = lanes_of()
-    pick = jnp.where(lane == 125 + rows_of(), 1.0, 0.0)
+def start_kernel(nodes_y, density, momentum, energy, dest, slot, region, bottoms, first, second):
+    sub, lane = rows_of(), lanes_of()
+    pick = jnp.where(lane == 125 + sub, 1.0, 0.0)
     pieces = []
-    place = along_y()
+    odd = parity_x()
     for f in range(5):
         field = field_of(f, density, momentum, energy)
         columns = jnp.concatenate([field[x, :, 128:256] for x in range(4)], axis=0)
         pieces.append(full_dot(pick, columns, back=True)[0:3])
-        low = jnp.concatenate([field[x, r : r + 1, :] for r in (0, 1) for x in range(4)], axis=0)
-        high = jnp.concatenate([field[x, r : r + 1, :] for r in (31, 30) for x in range(4)], axis=0)
-        for p in range(4):
-            rows[p, f] = jnp.where(p < place, low, high)
+        for out, down in ((first, odd), (second, 1 - odd)):
+            out[f, 0:32, :] = field[3 - 3 * down]
+            out[f, 32:64, :] = field[2 - down]
     count_gy, count_x = lax.axis_size("gy"), lax.axis_size("gx")
     target, node = dest[...].astype(f32), slot[...].astype(f32)
     grp = jnp.floor((target + 0.5) * (1.0 / (count_gy * count_x)))
@@ -651,68 +708,60 @@
     i = jnp.floor((node + 0.5) * (1.0 / 17.0))
     j = node - 17.0 * i
     pieces.append((8.0 * gx + i) * nodes_y + 16.0 * (grp * count_gy + gy) + j)
+    region_now = jnp.concatenate([region[0], region[1]], axis=0).astype(f32) + 1.0
+    found = jnp.zeros((8, 128), f32)
+    for z in range(2):
+        found = jnp.where(lane == 8 * z + sub, jnp.broadcast_to(region_now[:, z : z + 1], (8, 128)), found)
+    pieces.append(jnp.broadcast_to(jnp.sum(found, axis=0, keepdims=True), (8, 128)))
     block = jnp.concatenate(pieces, axis=0)
     for n in range(bottoms.shape[0]):
         bottoms[n] = block
 
 
-def widen_kernel(density, momentum, energy, came, own, first, second):
-    place, last = along_y(), lax.axis_size("grp") * lax.axis_size("gy") - 1
-    odd = position("gx") % 2
-    low_slot, high_slot = jnp.maximum(place - 1, 0), jnp.minimum(place + 1, last)
+def crater_kernel(density, momentum, energy, came1, came2, rows1, rows2, after, out, wide, mid, prims, face, fluxes):
+    place, last_y = along_y(), lax.axis_size("grp") * lax.axis_size("gy") - 1
+    gx, last_x = position("gx"), lax.axis_size("gx") - 1
+    odd, odd_y = parity_x(), parity_y()
     for f in range(5):
         field = field_of(f, density, momentum, energy)
-        low, high = came[low_slot, f], came[high_slot, f]
+        low, high = sort_out(odd, came1[f], came2[f])
+        for p, value in ((0, low[32:64]), (1, low[0:32]), (6, high[0:32]), (7, high[32:64])):
+            wide[f, p, 0:32, :] = value
+            wide[f, p, 32:40, :] = value[0:8]
         for x in range(4):
-            own[f, x, 0:32, :] = field[x]
-            bottom, top = field[x, 0:1, :], field[x, 31:32, :]
-            own[f, x, 39:40, :] = jnp.where(place == 0, bottom, low[x : x + 1])
-            own[f, x, 38:39, :] = jnp.where(place == 0, bottom, low[4 + x : 5 + x])
-            own[f, x, 32:33, :] = jnp.where(place == last, top, high[x : x + 1])
-            own[f, x, 33:34, :] = jnp.where(place == last, top, high[4 + x : 5 + x])
-            own[f, x, 34:38, :] = jnp.broadcast_to(top, (4, 256))
-        for out, low_way in ((first, odd), (second, 1 - odd)):
-            near = jnp.where(low_way == 1, 0, 3)
-            far = jnp.where(low_way == 1, 1, 2)
-            out[f, 0:40, :] = own[f, near]
-            out[f, 40:72, :] = own[f, far, 0:32, :]
-
-
-def crater_kernel(own, came1, came2, out, wide, mid, prims, face, fluxes):
-    place, last_y = along_y(), lax.axis_size("grp") * lax.axis_size("gy") - 1
-    gx, last_x = position("gx"), lax.axis_size("gx") - 1
-    odd = gx % 2
-    for f in range(5):
-        for x in range(4):
-            wide[f, 2 + x] = own[f, x]
-
-    def spread(came, near, far):
-        for f in range(5):
-            wide[f, near] = came[f, 0:40, :]
-            wide[f, far, 0:32, :] = came[f, 40:72, :]
-            wide[f, far, 32:40, :] = came[f, 32:40, :]
-
-    @pl.when(odd == 1)
-    def _():
-        spread(came1, 1, 0)
-        spread(came2, 6, 7)
-
-    @pl.when(odd == 0)
-    def _():
-        spread(came2, 1, 0)
-        spread(came1, 6, 7)
+            wide[f, 2 + x, 0:32, :] = field[x]
+            wide[f, 2 + x, 32:40, :] = field[x, 24:32, :]
+        for t in range(2):
+            lanes = slice(128 * t, 128 * t + 128)
+            at = 18 + f * 4 + t * 2
+            below, above = sort_out(odd_y, rows1[at], rows2[at])
+            sides_below, sides_above = sort_out(odd_y, rows1[at + 1], rows2[at + 1])
+
+            def put(p, row, edge, value):
+                clamped = jnp.where(edge == 0, place == 0, place == last_y)
+                at_edge = wide[f, p, 31 * edge : 31 * edge + 1, lanes]
+                wide[f, p, row : row + 1, lanes] = jnp.where(clamped, at_edge, value)
+
+            for x in range(4):
+                put(2 + x, 39, 0, below[x : x + 1])
+                put(2 + x, 38, 0, below[4 + x : 5 + x])
+                put(2 + x, 32, 1, above[x : x + 1])
+                put(2 + x, 33, 1, above[4 + x : 5 + x])
+            for p, n in ((1, 0), (6, 1)):
+                put(p, 39, 0, sides_below[n : n + 1])
+                put(p, 32, 1, sides_above[n : n + 1])
 
     @pl.when(gx == 0)
     def _():
         for f in range(5):
-            wide[f, 0] = own[f, 0]
-            wide[f, 1] = own[f, 0]
+            wide[f, 0] = wide[f, 2]
+            wide[f, 1] = wide[f, 2]
 
     @pl.when(gx == last_x)
     def _():
         for f in range(5):
-            wide[f, 6] = own[f, 3]
-            wide[f, 7] = own[f, 3]
+            wide[f, 6] = wide[f, 5]
+            wide[f, 7] = wide[f, 5]
 
     lane = lanes_of((40, 256))
     ends = (lane == 0, lane == 255)
@@ -788,8 +837,8 @@
     def columns(q):
         parts = []
         for y in range(4):
-            start = (y // count_gy * count_x * count_gy + y % count_gy) * 16 + q
-            parts.append(bottoms[pl.ds(start, count_x, stride=16 * count_gy), :])
+            start = (y // count_gy * count_x * count_gy + y % count_gy) * 24 + q
+            parts.append(bottoms[pl.ds(start, count_x, stride=24 * count_gy), :])
         found = []
         for x in range(4):
             total = rolled(parts[0], -32 * x, 1)
@@ -844,77 +893,96 @@
         faces[3, at, :] = ids[x]
 
 
-def surface_kernel(nodes_y, count_x, bottoms, region, xl, xh, yl, yh, material, tables, out1, out2, total, faces):
+def surface_kernel(nodes_y, count_x, bottoms, material, tables, after, out1, out2, total, faces):
     base_x = (8 * position("gx") - 4).astype(f32)
     base_y = (16 * along_y() - 4).astype(f32)
     bottom_tractions(bottoms, count_x, faces)
     deposit(faces, nodes_y, base_x, base_y, total)
-    region_now = jnp.concatenate([region[0], region[1]], axis=0).astype(f32) + 1.0
-    respond(total, region_grid(region_now, xl, xh, yl, yh), material, tables, out1, out2)
+    respond(total, region_rows(bottoms, count_x), material, tables, out1, out2)
 
 
 def shards(density, momentum, energy, displacement, velocity_field, acceleration, material, element_region_index,
            face_dest, face_slot):
-    along = ("grp", "gy")
+    along, rank = ("grp", "gy"), ("grp", "gx", "gy")
     nodes_y = 16 * lax.axis_size(along) + 1
-    count_x, rank = lax.axis_size("gx"), ("grp", "gx", "gy")
-    devices = lax.axis_size(rank)
-    crater = (density, momentum, energy)
-    bottoms, rows = call(
+    count_x, devices = lax.axis_size("gx"), lax.axis_size(rank)
+    crater, region = (density, momentum, energy), element_region_index
+    bottoms, crater1, crater2 = call(
         functools.partial(start_kernel, float(nodes_y)),
-        crater + (face_dest.reshape(1, -1), face_slot),
-        [(devices, 16, 128), (4, 5, 8, 256)],
+        crater + (face_dest.reshape(1, -1), face_slot, region),
+        [(devices, 24, 128), (5, 64, 256), (5, 64, 256)],
         [],
+        mib=12,
     )
     bottoms = lax.all_to_all(bottoms, rank, 0, 0, tiled=True)
-    rows = lax.all_to_all(rows, along, 0, 0, tiled=True)
-    own, first, second = call(widen_kernel, crater + (rows,), [(5, 4, 40, 256), (5, 72, 256), (5, 72, 256)], [])
-    first = lax.ppermute(first, "gx", [(i, i ^ 1) for i in range(count_x)])
-    pairs = [(i, i + 1) for i in range(1, count_x - 1, 2)]
-    second = lax.ppermute(second, "gx", pairs + [(j, i) for i, j in pairs])
-    region = element_region_index
-    b, f, x_low, x_high, y_low, y_high = call(
+    crater1, crater2 = exchange("gx", crater1, crater2)
+    b, f, x1, x2, y_low, y_high = call(
         first_kernel,
         (displacement, velocity_field, acceleration, region, material),
-        [element_shape, element_shape, (31, 8, 128), (31, 8, 128), (16, 8, 128), (16, 8, 128)],
+        [element_shape, element_shape, (31, 8, 128), (31, 8, 128), (16, 8, 128), (15, 8, 128)],
         internal_scratch + [(5, 5, 8, 512), (4, 9, 17, 128)],
         smem=(4,),
-    )
-    xl, xh = exchange("gx", x_low, x_high)
-    y_low, y_high = call(
-        functools.partial(edge_kernel, True), (y_low, y_high, xl, xh), [(18, 8, 128), (18, 8, 128)], []
-    )
-    yl, yh = exchange(along, y_low, y_high)
-    (hydro_state,) = call(
-        crater_kernel,
-        (own, first, second),
-        [(5, 4, 32, 256)],
-        [(5, 8, 40, 256), (5, 8, 40, 256), (6, 40, 256), (5, 40, 256), (6, 40, 256)],
+        mib=24,
     )
     surf1, surf2 = call(
         functools.partial(surface_kernel, float(nodes_y), count_x),
-        (bottoms.reshape(devices * 16, 128), region, xl, xh, yl, yh, material, jnp.asarray(surface_tables())),
+        (bottoms.reshape(devices * 24, 128), material, jnp.asarray(surface_tables()), x1),
         [(24, 256), (24, 256)],
         [(360, 128), (4, 4 * count_x, 128)],
-        smem=(6,),
+        smem=(1,),
+        away=(3,),
+        mib=12,
     )
-    a1, f2, x_low, x_high, y_low, y_high, scales = call(
+    x1, x2 = exchange("gx", x1, x2)
+    y1, y2 = call(
+        first_edge_kernel,
+        (y_low, y_high, x1, x2) + crater + (crater1, crater2, surf1),
+        [(38, 8, 128), (38, 8, 128)],
+        [],
+        away=(9,),
+        mib=12,
+    )
+    y1, y2 = exchange(along, y1, y2)
+    a1, f2, p1, p2, y_low, y_high, scales = call(
         second_kernel,
-        (b, f, xl, xh, yl, yh, region, material),
+        (b, f, x1, x2, y1, y2, region, material),
         [element_shape, element_shape, (30, 8, 128), (30, 8, 128), (15, 8, 128), (15, 8, 128), (3, 3, 2, 8, 128)],
         internal_scratch,
         smem=(7,),
+        mib=24,
     )
-    xl2, xh2 = exchange("gx", x_low, x_high)
-    y_low, y_high = call(
-        functools.partial(edge_kernel, False), (y_low, y_high, xl2, xh2), [(15, 8, 128), (15, 8, 128)], []
+    (hydro_state,) = call(
+        crater_kernel,
+        crater + (crater1, crater2, y1, y2, p1),
+        [(5, 4, 32, 256)],
+        [(5, 8, 40, 256), (5, 8, 40, 256), (6, 40, 256), (5, 40, 256), (6, 40, 256)],
+        away=(7,),
+        mib=16,
     )
-    yl2, yh2 = exchange(along, y_low, y_high)
-    u_out, v_out, a_out = call(
+    p1, p2 = exchange("gx", p1, p2)
+    r1, r2 = call(
+        second_edge_kernel,
+        (y_low, y_high, p1, p2, hydro_state),
+        [(15, 8, 128), (15, 8, 128)],
+        [],
+        away=(4,),
+        mib=8,
+    )
+    u_out, first = call(
+        place_kernel,
+        (a1, surf1, displacement, velocity_field, acceleration, r1),
+        [displacement.shape, (3, 4, 9, 17, 128)],
+        [(5, 5, 8, 512), (4, 9, 17, 128)],
+        away=(5,),
+        mib=20,
+    )
+    r1, r2 = exchange(along, r1, r2)
+    v_out, a_out = call(
         last_kernel,
-        (a1, f2, xl2, xh2, yl2, yh2, scales, surf1, surf2, displacement, velocity_field, acceleration),
-        [displacement.shape] * 3,
-        [(5, 5, 8, 512), (4, 9, 17, 128), (4, 9, 17, 128), element_shape],
+        (first, f2, p1, p2, r1, r2, scales, surf1, surf2, velocity_field, acceleration),
+        [displacement.shape] * 2,
+        [(5, 5, 8, 512), (4, 9, 17, 128), element_shape],
+        mib=22,
     )
     return hydro_state, u_out, v_out, a_out
 

time: 99.3 us -> 82.9 us (0.83)
  the two profiles are of different devices: /device:TPU:3 before, /device:TPU:0 now
where the time goes in v4:
time: 82.9 us; the launch traced here: 82.2 us
  starting transfers between devices  31.2 us (38%)
  Pallas kernels  29.8 us (36%)
  local copies, waits for them, and re-layouts  19.6 us (24%)
  between operations  0.85 us (1%)
    pallas_call x9, Pallas kernels, call(): pl.pallas_call(kernel, out_shape=[jax.ShapeDtypeStruct(s, f32) for s in o...  29.8 us
    unnamed x58, local copies, waits for them, and re-layouts  19.6 us
    ppermute x5, starting transfers between devices, exchange(): first = lax.ppermute(first, axis, [(i, i ^ 1) for i in range(count)])  18.9 us
    all_to_all x1, starting transfers between devices, shards(): bottoms = lax.all_to_all(bottoms, rank, 0, 0, tiled=True)  7.3 us
    ppermute x5, starting transfers between devices, exchange(): lax.ppermute(second, axis, pairs + [(j, i) for i, j in pairs])  5.01 us
  transfers between devices with their start and end apart: 11, of which 1 were waited for; matrix products, arithmetic and copies ran while one was open for 3% of the time, Pallas kernels for 25%

profile of v4, /device:TPU:0, one launch (start us, length us, event | category | flops | bytes accessed | tf_op | source)
XLA Modules:
  0.0 82.2 jit_solution(15793093319197741304)
XLA Ops:
  0.6 0.0 copy-start.2
  0.6 1.0 %copy-done.2 = f32[3,4,32,256]{3,2,1,0:T(8,128)S(1)} copy-done((f32[3,4,32,256]{3,2,1,0:T(8,128)S(1)}, f32[3,4,32,256]{3,2,1,0:T(8,128)}, u32[]{:S(2)}) %copy-start.2) | copy-done | bytes 393240
  1.6 0.9 %copy-done.9 = f32[4,32,256]{2,1,0:T(8,128)S(1)} copy-done((f32[4,32,256]{2,1,0:T(8,128)S(1)}, f32[4,32,256]{2,1,0:T(8,128)}, u32[]{:S(2)}) %copy-start.9) | copy-done | bytes 131096
  2.5 0.9 %copy-done.12 = f32[4,32,256]{2,1,0:T(8,128)S(1)} copy-done((f32[4,32,256]{2,1,0:T(8,128)S(1)}, f32[4,32,256]{2,1,0:T(8,128)}, u32[]{:S(2)}) %copy-start.12) | copy-done | bytes 131096
  3.4 0.7 copy-done.18
  4.1 0.7 copy-done.21
  4.8 0.7 copy-done.22
  5.4 1.5 %shard_map.138 = (f32[32,24,128]{2,1,0:T(8,128)}, f32[5,64,256]{2,1,0:T(8,128)}, f32[5,64,256]{2,1,0:T(8,128)}) custom-call(f32[4,32,256]{2,1,0:T(8,128)S(1)} %copy-done.9, f32[3,4,32,256]{3,2,1,0:T(8,128)S(1)} %copy-done.2, f32[4,32,256]{2,1,0:T(8,128)S(1)} %copy-done.12, s32[1,128]{1,0:T(1,128)S(1)} %bitcast.3, s32[1,128]{1,0:T(1,128)S(1)} %copy-done.22, ...), custom_call_target="tpu_custom_call" | custom-call | tf_op jit(solution)/shard_map/pallas_call | solution.py:454
  6.9 7.3 %all-to-all-start = ((f32[32,24,128]{2,1,0:T(8,128)}), f32[32,24,128]{2,1,0:T(8,128)S(1)}, u32[]{:S(2)}, u32[]{:S(2)}) async-start(f32[32,24,128]{2,1,0:T(8,128)} %get-tuple-element.36), calls=%async_computation | async-start | bytes 786432 | tf_op jit(solution)/shard_map/all_to_all | solution.py:917
  14.2 1.8 %collective-permute-start = (f32[5,64,256]{2,1,0:T(8,128)}, f32[5,64,256]{2,1,0:T(8,128)}, u32[]{:S(2)}, u32[]{:S(2)}) collective-permute-start(f32[5,64,256]{2,1,0:T(8,128)} %get-tuple-element.30), channel_id=1, source_target_pairs={{0,2},{2,0},{4,6},{6,4},{8,10},{10,8},{12,14},{14,12},{1,3},{3,1},... | collective-permute-start | bytes 983048 | tf_op jit(solution)/shard_map/ppermute | solution.py:472
  16.1 1.5 %collective-permute-start.1 = (f32[5,64,256]{2,1,0:T(8,128)}, f32[5,64,256]{2,1,0:T(8,128)}, u32[]{:S(2)}, u32[]{:S(2)}) collective-permute-start(f32[5,64,256]{2,1,0:T(8,128)} %get-tuple-element.31), channel_id=1, source_target_pairs={{2,4},{6,8},{10,12},{4,2},{8,6},{12,10},{3,5},{7,9},{11,13},{5,3},... | collective-permute-start | bytes 983048 | tf_op jit(solution)/shard_map/ppermute | solution.py:473
  17.6 0.3 copy.16.v
  17.9 0.0 copy-start.25
  18.0 0.3 copy.17.a
  18.3 0.9 %copy-done.25 = f32[3,9,17,512]{3,0,2,1:T(4,128)S(1)} copy-done((f32[3,9,17,512]{3,0,2,1:T(4,128)S(1)}, f32[3,9,17,512]{3,0,2,1:T(4,128)}, u32[]{:S(2)}) %copy-start.25) | copy-done | bytes 940056
  19.2 0.3 copy.15.u
  19.6 0.3 copy-done.19
  19.9 0.0 copy-done.20
  19.9 8.2 %shard_map.139 = (f32[3,5,5,4,8,128]{5,4,3,2,1,0:T(8,128)S(1)}, f32[3,5,5,4,8,128]{5,4,3,2,1,0:T(8,128)S(1)}, f32[31,8,128]{2,1,0:T(8,128)}, f32[31,8,128]{2,1,0...) custom-call(f32[3,9,17,512]{3,2,1,0:T(8,128)S(1)} %copy.15.u, f32[3,9,17,512]{3,2,1,0:T(8,128)S(1)} %copy.16.v, ...), custom_call_target="tpu_custom_call" | custom-call | tf_op jit(solution)/shard_map/pallas_call | solution.py:454
  28.2 1.0 %copy-done.5 = f32[3,5,5,4,8,128]{5,4,3,2,1,0:T(8,128)} copy-done((f32[3,5,5,4,8,128]{5,4,3,2,1,0:T(8,128)}, f32[3,5,5,4,8,128]{5,4,3,2,1,0:T(8,128)S(1)}, u32[]{:S(2)}) %copy-start.5) | copy-done | bytes 1228824
  29.2 1.0 %copy-done.7 = f32[3,5,5,4,8,128]{5,4,3,2,1,0:T(8,128)} copy-done((f32[3,5,5,4,8,128]{5,4,3,2,1,0:T(8,128)}, f32[3,5,5,4,8,128]{5,4,3,2,1,0:T(8,128)S(1)}, u32[]{:S(2)}) %copy-start.7) | copy-done | bytes 1228824
  30.2 0.6 copy-done.16
  30.8 1.3 %collective-permute-start.3 = (f32[31,8,128]{2,1,0:T(8,128)}, f32[31,8,128]{2,1,0:T(8,128)}, u32[]{:S(2)}, u32[]{:S(2)}) collective-permute-start(f32[31,8,128]{2,1,0:T(8,128)} %get-tuple-element.35), channel_id=1, source_target_pairs={{2,4},{6,8},{10,12},{4,2},{8,6},{12,10},{3,5},{7,9},{11,13},{5,3},... | collective-permute-start | bytes 380936 | tf_op jit(solution)/shard_map/ppermute | solution.py:473
  32.2 4.4 %collective-permute-start.2 = (f32[31,8,128]{2,1,0:T(8,128)}, f32[31,8,128]{2,1,0:T(8,128)}, u32[]{:S(2)}, u32[]{:S(2)}) collective-permute-start(f32[31,8,128]{2,1,0:T(8,128)} %get-tuple-element.34.after), channel_id=1, source_target_pairs={{0,2},{2,0},{4,6},{6,4},{8,10},{10,8},{12,14},{14,12},{1,3},{3,1},... | collective-permute-start | bytes 380936 | tf_op jit(solution)/shard_map/ppermute | solution.py:472
  36.5 1.0 %copy-done.15 = f32[6,128,128]{2,1,0:T(8,128)S(1)} copy-done((f32[6,128,128]{2,1,0:T(8,128)S(1)}, f32[6,128,128]{2,1,0:T(8,128)}, u32[]{:S(2)}) %copy-start.15) | copy-done | bytes 393240
  37.5 4.8 %shard_map.140 = (f32[24,256]{1,0:T(8,128)S(1)}, f32[24,256]{1,0:T(8,128)S(1)}) custom-call(f32[768,128]{1,0:T(8,128)S(1)} %bitcast.2, f32[3,8]{1,0:T(4,128)S(1)} %copy-done.20, f32[6,128,128]{2,1,0:T(8,128)S(1)} %copy-done.15, f32[31,8,128]{2,1,0:T(8,128)} %get-tuple-element.34.after), custom_call_target="tpu_custom_call" | custom-call | tf_op jit(solution)/shard_map/pallas_call | solution.py:454
  42.4 0.0 collective-permute-done.2.came1.came_x1
  42.4 0.0 copy-start.10
  42.4 0.9 %copy-done.10 = f32[4,32,256]{2,1,0:T(8,128)S(1)} copy-done((f32[4,32,256]{2,1,0:T(8,128)S(1)}, f32[4,32,256]{2,1,0:T(8,128)}, u32[]{:S(2)}) %copy-start.10) | copy-done | bytes 131096
  43.3 0.9 %copy-done.13 = f32[4,32,256]{2,1,0:T(8,128)S(1)} copy-done((f32[4,32,256]{2,1,0:T(8,128)S(1)}, f32[4,32,256]{2,1,0:T(8,128)}, u32[]{:S(2)}) %copy-start.13) | copy-done | bytes 131096
  44.2 0.8 %copy-done.17 = f32[15,8,128]{2,1,0:T(8,128)S(1)} copy-done((f32[15,8,128]{2,1,0:T(8,128)S(1)}, f32[15,8,128]{2,1,0:T(8,128)}, u32[]{:S(2)}) %copy-start.17) | copy-done | bytes 61464
  45.1 1.3 %shard_map.141 = (f32[38,8,128]{2,1,0:T(8,128)S(1)}, f32[38,8,128]{2,1,0:T(8,128)S(1)}) custom-call(f32[16,8,128]{2,1,0:T(8,128)S(1)} %get-tuple-element.32.low, f32[15,8,128]{2,1,0:T(8,128)S(1)} %copy-done.17, f32[31,8,128]{2,1,0:T(8,128)} %collective-permute-done.2.came1.came_x1, f32[31,8,128]{2,1,0:T(8,128)} %collective-permute-done.3.came2.came_x2, ...), custom_call_target="tpu_custom_call" | custom-call | tf_op jit(solution)/shard_map/pallas_call | solution.py:454
  46.4 0.1 collective-permute-start.4
  46.5 0.7 collective-permute-start.5
  47.1 0.7 collective-permute-done.4.came_y1.rows1
  47.8 0.0 copy-start.11
  47.9 4.5 %shard_map.142 = (f32[3,5,5,4,8,128]{5,4,3,2,1,0:T(8,128)S(1)}, f32[3,5,5,4,8,128]{5,4,3,2,1,0:T(8,128)S(1)}, f32[30,8,128]{2,1,0:T(8,128)S(1)}, f32[30,8,128]{2...) custom-call(f32[3,5,5,4,8,128]{5,4,3,2,1,0:T(8,128)S(1)} %copy-done.6, ...), custom_call_target="tpu_custom_call" | custom-call | tf_op jit(solution)/shard_map/pallas_call | solution.py:454
  52.4 0.7 collective-permute-start.7
  53.1 4.5 %collective-permute-start.6 = (f32[30,8,128]{2,1,0:T(8,128)S(1)}, f32[30,8,128]{2,1,0:T(8,128)S(1)}, u32[]{:S(2)}, u32[]{:S(2)}) collective-permute-start(f32[30,8,128]{2,1,0:T(8,128)S(1)} %get-tuple-element.42.after), channel_id=1, source_target_pairs={{0,2},{2,0},{4,6},{6,4},{8,10},{10,8},{12,14},{14,12},{1,3},{3,1},... | collective-permute-start | bytes 368648 | tf_op jit(solution)/shard_map/ppermute | solution.py:472
  57.6 5.9 %shard_map.143.after = f32[5,4,32,256]{3,2,1,0:T(8,128)} custom-call(f32[4,32,256]{2,1,0:T(8,128)S(1)} %copy-done.11, f32[3,4,32,256]{3,2,1,0:T(8,128)S(1)} %copy-done.3, f32[4,32,256]{2,1,0:T(8,128)S(1)} %copy-done.14, f32[5,64,256]{2,1,0:T(8,128)} %collective-permute-done.crater1.came1, f32[5,64,256]{2,1,0:T(8,128)} %collective-permute-done.1.crater2.came2, ...), custom_call_target="tpu_custom_call" | custom-call | tf_op jit(solution)/shard_map/pallas_call | solution.py:454
  63.5 1.1 %copy-done.4 = f32[5,4,32,256]{3,2,1,0:T(8,128)S(1)} copy-done((f32[5,4,32,256]{3,2,1,0:T(8,128)S(1)}, f32[5,4,32,256]{3,2,1,0:T(8,128)}, u32[]{:S(2)}) %copy-start.4) | copy-done | bytes 655384
  64.7 0.8 %collective-permute-start.9 = (f32[15,8,128]{2,1,0:T(8,128)S(1)}, f32[15,8,128]{2,1,0:T(8,128)S(1)}, u32[]{:S(2)}, u32[]{:S(2)}) collective-permute-start(f32[15,8,128]{2,1,0:T(8,128)S(1)} %get-tuple-element.51), channel_id=1, source_target_pairs={{1,16},{16,1},{3,18},{18,3},{5,20},{20,5},{7,22},{22,7},{9,24},{24... | collective-permute-start | bytes 184328 | tf_op jit(solution)/shard_map/ppermute | solution.py:473
  65.5 8.0 %collective-permute-start.8 = (f32[15,8,128]{2,1,0:T(8,128)S(1)}, f32[15,8,128]{2,1,0:T(8,128)S(1)}, u32[]{:S(2)}, u32[]{:S(2)}) collective-permute-start(f32[15,8,128]{2,1,0:T(8,128)S(1)} %get-tuple-element.47.after), channel_id=1, source_target_pairs={{0,1},{1,0},{16,17},{17,16},{2,3},{3,2},{18,19},{19,18},{4,5},{5,4... | collective-permute-start | bytes 184328 | tf_op jit(solution)/shard_map/ppermute | solution.py:472
  73.6 1.7 %shard_map.145 = (f32[3,9,17,512]{3,2,1,0:T(8,128)S(1)}, f32[3,4,9,17,128]{4,3,2,1,0:T(8,128)S(1)}) custom-call(f32[3,5,5,4,8,128]{5,4,3,2,1,0:T(8,128)S(1)} %get-tuple-element.43.a1, f32[24,256]{1,0:T(8,128)S(1)} %get-tuple-element.37.after.surf1, f32[3,9,17,512]{3,2,1,0:T(8,128)S(1)} %copy-done.1, f32[3,9,17,512]{3,2,1,0:T(8,128)S(1)} %copy.16.v, ...), custom_call_target="tpu_custom_call" | custom-call | tf_op jit(solution)/shard_map/pallas_call | solution.py:454
  75.3 1.7 %copy.23 = f32[3,9,17,512]{3,0,2,1:T(4,128)} copy(f32[3,9,17,512]{3,2,1,0:T(8,128)S(1)} %get-tuple-element.57) | data formatting | bytes 1880064
  77.0 1.8 %shard_map.146 = (f32[3,9,17,512]{3,2,1,0:T(8,128)S(1)}, f32[3,9,17,512]{3,2,1,0:T(8,128)S(1)}) custom-call(f32[3,4,9,17,128]{4,3,2,1,0:T(8,128)S(1)} %get-tuple-element.49.first, f32[3,5,5,4,8,128]{5,4,3,2,1,0:T(8,128)S(1)} %get-tuple-element.50.f, f32[30,8,128]{2,1,0:T(8,128)S(1)} %collective-permute-done.6.came1.x1, ...), custom_call_target="tpu_custom_call" | custom-call | tf_op jit(solution)/shard_map/pallas_call | solution.py:454
  78.8 1.7 %copy.24 = f32[3,9,17,512]{3,0,2,1:T(4,128)} copy(f32[3,9,17,512]{3,2,1,0:T(8,128)S(1)} %get-tuple-element.58) | data formatting | bytes 1880064
  80.5 1.7 %copy.25 = f32[3,9,17,512]{3,0,2,1:T(4,128)} copy(f32[3,9,17,512]{3,2,1,0:T(8,128)S(1)} %get-tuple-element.59) | data formatting | bytes 1880064
  (41 shorter events, 0.1 us)
Async XLA Ops:
  0.6 1.0 %copy-start.2 = (f32[3,4,32,256]{3,2,1,0:T(8,128)S(1)}, f32[3,4,32,256]{3,2,1,0:T(8,128)}, u32[]{:S(2)}) copy-start(f32[3,4,32,256]{3,2,1,0:T(8,128)} %momentum.5) | copy-start | bytes 1179652
  1.6 0.9 %copy-start.9 = (f32[4,32,256]{2,1,0:T(8,128)S(1)}, f32[4,32,256]{2,1,0:T(8,128)}, u32[]{:S(2)}) copy-start(f32[4,32,256]{2,1,0:T(8,128)} %density.5) | copy-start | bytes 393220
  2.5 0.9 %copy-start.12 = (f32[4,32,256]{2,1,0:T(8,128)S(1)}, f32[4,32,256]{2,1,0:T(8,128)}, u32[]{:S(2)}) copy-start(f32[4,32,256]{2,1,0:T(8,128)} %energy.5) | copy-start | bytes 393220
  3.4 0.7 copy-start.18
  4.1 0.7 copy-start.21
  4.8 0.7 copy-start.22
  5.4 12.2 %copy-start.23 = (f32[3,9,17,512]{3,0,2,1:T(4,128)S(1)}, f32[3,9,17,512]{3,0,2,1:T(4,128)}, u32[]{:S(2)}) copy-start(f32[3,9,17,512]{3,0,2,1:T(4,128)} %param.15) | copy-start | bytes 2820100
  6.9 29.6 %all-to-all-start = ((f32[32,24,128]{2,1,0:T(8,128)}), f32[32,24,128]{2,1,0:T(8,128)S(1)}, u32[]{:S(2)}, u32[]{:S(2)}) async-start(f32[32,24,128]{2,1,0:T(8,128)} %get-tuple-element.36), calls=%async_computation | async-start | bytes 786432 | tf_op jit(solution)/shard_map/all_to_all | solution.py:917
  14.2 28.2 %collective-permute-start = (f32[5,64,256]{2,1,0:T(8,128)}, f32[5,64,256]{2,1,0:T(8,128)}, u32[]{:S(2)}, u32[]{:S(2)}) collective-permute-start(f32[5,64,256]{2,1,0:T(8,128)} %get-tuple-element.30), channel_id=1, source_target_pairs={{0,2},{2,0},{4,6},{6,4},{8,10},{10,8},{12,14},{14,12},{1,3},{3,1},... | collective-permute-start | bytes 983048 | tf_op jit(solution)/shard_map/ppermute | solution.py:472
  16.1 1.9 %copy-start.24 = (f32[3,9,17,512]{3,0,2,1:T(4,128)S(1)}, f32[3,9,17,512]{3,0,2,1:T(4,128)}, u32[]{:S(2)}) copy-start(f32[3,9,17,512]{3,0,2,1:T(4,128)} %param.16) | copy-start | bytes 2820100
  16.1 26.3 %collective-permute-start.1 = (f32[5,64,256]{2,1,0:T(8,128)}, f32[5,64,256]{2,1,0:T(8,128)}, u32[]{:S(2)}, u32[]{:S(2)}) collective-permute-start(f32[5,64,256]{2,1,0:T(8,128)} %get-tuple-element.31), channel_id=1, source_target_pairs={{2,4},{6,8},{10,12},{4,2},{8,6},{12,10},{3,5},{7,9},{11,13},{5,3},... | collective-permute-start | bytes 983048 | tf_op jit(solution)/shard_map/ppermute | solution.py:473
  17.9 1.3 %copy-start.25 = (f32[3,9,17,512]{3,0,2,1:T(4,128)S(1)}, f32[3,9,17,512]{3,0,2,1:T(4,128)}, u32[]{:S(2)}) copy-start(f32[3,9,17,512]{3,0,2,1:T(4,128)} %param.14) | copy-start | bytes 2820100
  19.2 0.7 copy-start.19
  19.2 0.7 copy-start.20
  19.9 8.2 %copy-start = (f32[3,9,17,512]{3,2,1,0:T(8,128)}, f32[3,9,17,512]{3,2,1,0:T(8,128)S(1)}, u32[]{:S(2)}) copy-start(f32[3,9,17,512]{3,2,1,0:T(8,128)S(1)} %copy.15.u) | copy-start | bytes 2820100
  19.9 22.5 %copy-start.3 = (f32[3,4,32,256]{3,2,1,0:T(8,128)S(1)}, f32[3,4,32,256]{3,2,1,0:T(8,128)}, u32[]{:S(2)}) copy-start(f32[3,4,32,256]{3,2,1,0:T(8,128)} %momentum.5) | copy-start | bytes 1179652
  28.2 1.0 %copy-start.5 = (f32[3,5,5,4,8,128]{5,4,3,2,1,0:T(8,128)}, f32[3,5,5,4,8,128]{5,4,3,2,1,0:T(8,128)S(1)}, u32[]{:S(2)}) copy-start(f32[3,5,5,4,8,128]{5,4,3,2,1,0:T(8,128)S(1)} %get-tuple-element.40.b) | copy-start | bytes 3686404
  29.2 1.0 %copy-start.7 = (f32[3,5,5,4,8,128]{5,4,3,2,1,0:T(8,128)}, f32[3,5,5,4,8,128]{5,4,3,2,1,0:T(8,128)S(1)}, u32[]{:S(2)}) copy-start(f32[3,5,5,4,8,128]{5,4,3,2,1,0:T(8,128)S(1)} %get-tuple-element.41.f) | copy-start | bytes 3686404
  30.2 0.6 copy-start.16
  30.8 11.5 %collective-permute-start.3 = (f32[31,8,128]{2,1,0:T(8,128)}, f32[31,8,128]{2,1,0:T(8,128)}, u32[]{:S(2)}, u32[]{:S(2)}) collective-permute-start(f32[31,8,128]{2,1,0:T(8,128)} %get-tuple-element.35), channel_id=1, source_target_pairs={{2,4},{6,8},{10,12},{4,2},{8,6},{12,10},{3,5},{7,9},{11,13},{5,3},... | collective-permute-start | bytes 380936 | tf_op jit(solution)/shard_map/ppermute | solution.py:473
  32.2 10.2 %collective-permute-start.2 = (f32[31,8,128]{2,1,0:T(8,128)}, f32[31,8,128]{2,1,0:T(8,128)}, u32[]{:S(2)}, u32[]{:S(2)}) collective-permute-start(f32[31,8,128]{2,1,0:T(8,128)} %get-tuple-element.34.after), channel_id=1, source_target_pairs={{0,2},{2,0},{4,6},{6,4},{8,10},{10,8},{12,14},{14,12},{1,3},{3,1},... | collective-permute-start | bytes 380936 | tf_op jit(solution)/shard_map/ppermute | solution.py:472
  36.5 1.0 %copy-start.15 = (f32[6,128,128]{2,1,0:T(8,128)S(1)}, f32[6,128,128]{2,1,0:T(8,128)}, u32[]{:S(2)}) copy-start(f32[6,128,128]{2,1,0:T(8,128)} %constant.2.clone.tables) | copy-start | bytes 1179652
  37.5 10.3 %copy-start.6 = (f32[3,5,5,4,8,128]{5,4,3,2,1,0:T(8,128)S(1)}, f32[3,5,5,4,8,128]{5,4,3,2,1,0:T(8,128)}, u32[]{:S(2)}) copy-start(f32[3,5,5,4,8,128]{5,4,3,2,1,0:T(8,128)} %copy-done.5) | copy-start | bytes 3686404
  37.5 10.3 %copy-start.8 = (f32[3,5,5,4,8,128]{5,4,3,2,1,0:T(8,128)S(1)}, f32[3,5,5,4,8,128]{5,4,3,2,1,0:T(8,128)}, u32[]{:S(2)}) copy-start(f32[3,5,5,4,8,128]{5,4,3,2,1,0:T(8,128)} %copy-done.7) | copy-start | bytes 3686404
  42.4 0.9 %copy-start.10 = (f32[4,32,256]{2,1,0:T(8,128)S(1)}, f32[4,32,256]{2,1,0:T(8,128)}, u32[]{:S(2)}) copy-start(f32[4,32,256]{2,1,0:T(8,128)} %density.5) | copy-start | bytes 393220
  43.3 0.9 %copy-start.13 = (f32[4,32,256]{2,1,0:T(8,128)S(1)}, f32[4,32,256]{2,1,0:T(8,128)}, u32[]{:S(2)}) copy-start(f32[4,32,256]{2,1,0:T(8,128)} %energy.5) | copy-start | bytes 393220
  44.2 0.8 %copy-start.17 = (f32[15,8,128]{2,1,0:T(8,128)S(1)}, f32[15,8,128]{2,1,0:T(8,128)}, u32[]{:S(2)}) copy-start(f32[15,8,128]{2,1,0:T(8,128)} %copy-done.16) | copy-start | bytes 184324
  46.4 1.4 %collective-permute-start.4 = (f32[38,8,128]{2,1,0:T(8,128)S(1)}, f32[38,8,128]{2,1,0:T(8,128)S(1)}, u32[]{:S(2)}, u32[]{:S(2)}) collective-permute-start(f32[38,8,128]{2,1,0:T(8,128)S(1)} %get-tuple-element.38), channel_id=1, source_target_pairs={{0,1},{1,0},{16,17},{17,16},{2,3},{3,2},{18,19},{19,18},{4,5},{5,4... | collective-permute-start | bytes 466952 | tf_op jit(solution)/shard_map/ppermute | solution.py:472
  46.5 1.4 %collective-permute-start.5 = (f32[38,8,128]{2,1,0:T(8,128)S(1)}, f32[38,8,128]{2,1,0:T(8,128)S(1)}, u32[]{:S(2)}, u32[]{:S(2)}) collective-permute-start(f32[38,8,128]{2,1,0:T(8,128)S(1)} %get-tuple-element.39), channel_id=1, source_target_pairs={{1,16},{16,1},{3,18},{18,3},{5,20},{20,5},{7,22},{22,7},{9,24},{24... | collective-permute-start | bytes 466952 | tf_op jit(solution)/shard_map/ppermute | solution.py:473
  47.8 9.8 %copy-start.11 = (f32[4,32,256]{2,1,0:T(8,128)S(1)}, f32[4,32,256]{2,1,0:T(8,128)}, u32[]{:S(2)}) copy-start(f32[4,32,256]{2,1,0:T(8,128)} %density.5) | copy-start | bytes 393220
  47.8 9.8 %copy-start.14 = (f32[4,32,256]{2,1,0:T(8,128)S(1)}, f32[4,32,256]{2,1,0:T(8,128)}, u32[]{:S(2)}) copy-start(f32[4,32,256]{2,1,0:T(8,128)} %energy.5) | copy-start | bytes 393220
  52.4 11.2 %collective-permute-start.7 = (f32[30,8,128]{2,1,0:T(8,128)S(1)}, f32[30,8,128]{2,1,0:T(8,128)S(1)}, u32[]{:S(2)}, u32[]{:S(2)}) collective-permute-start(f32[30,8,128]{2,1,0:T(8,128)S(1)} %get-tuple-element.46), channel_id=1, source_target_pairs={{2,4},{6,8},{10,12},{4,2},{8,6},{12,10},{3,5},{7,9},{11,13},{5,3},... | collective-permute-start | bytes 368648 | tf_op jit(solution)/shard_map/ppermute | solution.py:473
  53.0 20.5 %copy-start.1 = (f32[3,9,17,512]{3,2,1,0:T(8,128)S(1)}, f32[3,9,17,512]{3,2,1,0:T(8,128)}, u32[]{:S(2)}) copy-start(f32[3,9,17,512]{3,2,1,0:T(8,128)} %copy-done) | copy-start | bytes 2820100
  53.1 10.5 %collective-permute-start.6 = (f32[30,8,128]{2,1,0:T(8,128)S(1)}, f32[30,8,128]{2,1,0:T(8,128)S(1)}, u32[]{:S(2)}, u32[]{:S(2)}) collective-permute-start(f32[30,8,128]{2,1,0:T(8,128)S(1)} %get-tuple-element.42.after), channel_id=1, source_target_pairs={{0,2},{2,0},{4,6},{6,4},{8,10},{10,8},{12,14},{14,12},{1,3},{3,1},... | collective-permute-start | bytes 368648 | tf_op jit(solution)/shard_map/ppermute | solution.py:472
  63.5 1.1 %copy-start.4 = (f32[5,4,32,256]{3,2,1,0:T(8,128)S(1)}, f32[5,4,32,256]{3,2,1,0:T(8,128)}, u32[]{:S(2)}) copy-start(f32[5,4,32,256]{3,2,1,0:T(8,128)} %shard_map.143.after) | copy-start | bytes 1966084
  64.7 12.3 %collective-permute-start.9 = (f32[15,8,128]{2,1,0:T(8,128)S(1)}, f32[15,8,128]{2,1,0:T(8,128)S(1)}, u32[]{:S(2)}, u32[]{:S(2)}) collective-permute-start(f32[15,8,128]{2,1,0:T(8,128)S(1)} %get-tuple-element.51), channel_id=1, source_target_pairs={{1,16},{16,1},{3,18},{18,3},{5,20},{20,5},{7,22},{22,7},{9,24},{24... | collective-permute-start | bytes 184328 | tf_op jit(solution)/shard_map/ppermute | solution.py:473
  65.5 11.5 %collective-permute-start.8 = (f32[15,8,128]{2,1,0:T(8,128)S(1)}, f32[15,8,128]{2,1,0:T(8,128)S(1)}, u32[]{:S(2)}, u32[]{:S(2)}) collective-permute-start(f32[15,8,128]{2,1,0:T(8,128)S(1)} %get-tuple-element.47.after), channel_id=1, source_target_pairs={{0,1},{1,0},{16,17},{17,16},{2,3},{3,2},{18,19},{19,18},{4,5},{5,4... | collective-permute-start | bytes 184328 | tf_op jit(solution)/shard_map/ppermute | solution.py:472

commit v5 on v4

--- a/solution.py
+++ b/solution.py
@@ -78,18 +78,22 @@
     return jnp.where(a == 4 * (b & 127) + (b >> 7), 1.0, 0.0).astype(jnp.bfloat16)
 
 
-def to_elements(nodes, table, tall, put):
+def rows_at(i, j, ex, c, count=4):
+    return pl.ds(((4 * ex + i) * 17 + j) * 8 + c, count, stride=32)
+
+
+def to_elements(nodes, c, table, tall, put):
     for i in range(5):
         for j in range(5):
             for ex in range(2):
                 for t in range(4):
-                    tall[i, j, 4 * ex : 4 * ex + 4, 128 * t : 128 * t + 128] = nodes[t, 4 * ex + i, pl.ds(j, 4, stride=4), :]
+                    tall[i, j, 4 * ex : 4 * ex + 4, 128 * t : 128 * t + 128] = nodes[t, rows_at(i, j, ex, c), :]
     out = one_hot_dot(tall[...].reshape(200, 512), table)
     for k in range(4):
         put(k, out[:, 128 * k : 128 * k + 128].reshape(5, 5, 8, 128))
 
 
-def to_nodes(get, table, tall, nodes):
+def to_nodes(get, c, table, tall, nodes):
     wide = jnp.concatenate([get(k).reshape(200, 128) for k in range(4)], axis=1)
     tall[...] = one_hot_dot(wide, table).reshape(5, 5, 8, 512)
     for i in range(5):
@@ -100,9 +104,18 @@
                 for t in range(4):
                     lanes = slice(128 * t, 128 * t + 128)
                     if j < 4:
-                        nodes[t, 4 * ex + i, pl.ds(j, 4, stride=4), :] = tall[i, j, 4 * ex : 4 * ex + 4, lanes]
+                        nodes[t, rows_at(i, j, ex, c), :] = tall[i, j, 4 * ex : 4 * ex + 4, lanes]
                     else:
-                        nodes[t, 4 * ex + i, 16:17, :] = tall[i, j, 4 * ex + 3 : 4 * ex + 4, lanes]
+                        at = ((4 * ex + i) * 17 + 16) * 8 + c
+                        nodes[t, at : at + 1, :] = tall[i, j, 4 * ex + 3 : 4 * ex + 4, lanes]
+
+
+def node_lanes(x, y, t):
+    return x, y, slice(None), slice(128 * t, 128 * t + 128)
+
+
+def node_rows(x, y, t):
+    return t, pl.ds(pl.multiple_of((x * 17 + y) * 8, 8), 3), slice(None)
 
 
 def lookup(material, row, region):
@@ -275,7 +288,7 @@
             first[c * 5 + i], second[c * 5 + i] = sort_out(odd_y, *rows)
 
 
-def first_edge_kernel(low, high, came1, came2, density, momentum, energy, crater1, crater2, after, first, second):
+def first_edge_kernel(low, high, came1, came2, rows_low, rows_high, crater1, crater2, after, first, second):
     edge_rows(low, high, came1, came2, first, second)
     odd, odd_y = parity_x(), parity_y()
     regions = sort_out(odd, came1[30], came2[30])
@@ -283,21 +296,20 @@
         first[15 + n] = value
         second[15 + n] = value
     for f in range(5):
-        field = field_of(f, density, momentum, energy)
         for t in range(2):
             lanes = slice(128 * t, 128 * t + 128)
+            at = 18 + f * 4 + t * 2
+            first[at], second[at] = sort_out(odd_y, rows_low[f * 2 + t], rows_high[f * 2 + t])
             ends = []
-            for near, far in ((0, 1), (31, 30)):
-                own = [field[x, r : r + 1, lanes] for r in (near, far) for x in range(4)]
+            for near in (0, 31):
                 sides = sort_out(odd, crater1[f, near : near + 1, lanes], crater2[f, near : near + 1, lanes])
-                ends.append((jnp.concatenate(own, axis=0), jnp.concatenate(list(sides) * 4, axis=0)))
-            for h in range(2):
-                at = 18 + f * 4 + t * 2 + h
-                first[at], second[at] = sort_out(odd_y, ends[0][h], ends[1][h])
-
-
-def second_edge_kernel(low, high, came1, came2, after, first, second):
+                ends.append(jnp.concatenate(list(sides) * 4, axis=0))
+            first[at + 1], second[at + 1] = sort_out(odd_y, *ends)
+
+
+def second_edge_kernel(low, high, came1, came2, after, first, second, token):
     edge_rows(low, high, came1, came2, first, second)
+    token[...] = after[...]
 
 
 def region_grid(own, x1, x2, y1, y2):
@@ -341,42 +353,45 @@
     return float(-1.0 / (half_size**3 * quad[i] * quad[j] * quad[k]))
 
 
-def first_kernel(u, v, a, region, material, b_out, f_out, x1, x2, y_low, y_high,
-                 elem, gx, gz, cross, planes, side, tall, nodes):
+def first_kernel(u, v, a, region, material, b_out, f_out, x1, x2, y_low, y_high, token,
+                 elem, gx, gz, cross, planes, side, tall, nodes, later):
     table = depth_table()
-    region_now = jnp.concatenate([region[0], region[1]], axis=0).astype(f32) + 1.0
-
-    def one(c, carry):
-        for t in range(4):
-            lanes = slice(128 * t, 128 * t + 128)
-            nodes[t] = u[c, :, :, lanes] + time_step * v[c, :, :, lanes] + 0.5 * time_step**2 * a[c, :, :, lanes]
+    region_now = region[...]
+
+    def column(x, carry):
+        for y in range(17):
+            for t in range(4):
+                at = node_lanes(x, y, t)
+                uu, vv, aa = u[at], v[at], a[at]
+                nodes[node_rows(x, y, t)] = uu + time_step * vv + 0.5 * time_step**2 * aa
+                later[node_rows(x, y, t)] = uu + 2.0 * time_step * vv + time_step**2 * aa
+        return carry
+
+    lax.fori_loop(0, 9, column, 0)
+    for c in range(3):
 
         def put_u(k, value):
             elem[c, :, :, k] = value
 
-        to_elements(nodes, table, tall, put_u)
-        for t in range(4):
-            lanes = slice(128 * t, 128 * t + 128)
-            nodes[t] = u[c, :, :, lanes] + 2.0 * time_step * v[c, :, :, lanes] + time_step**2 * a[c, :, :, lanes]
+        to_elements(nodes, c, table, tall, put_u)
 
         def put_b(k, value):
             b_out[c, :, :, k] = value
 
-        to_elements(nodes, table, tall, put_b)
-        return carry
-
-    lax.fori_loop(0, 3, one, 0)
+        to_elements(later, c, table, tall, put_b)
     internal(elem, f_out, lookup(material, 1, region_now), lookup(material, 2, region_now), gx, gz, cross, planes, side)
     pack_x(f_out, x1, x2)
     pack_y(f_out, y_low, y_high)
     x1[30] = region_now
     x2[30] = region_now
     y_low[15] = region_now
-
-
-def second_kernel(b, f, came_x1, came_x2, came_y1, came_y2, region, material, a_out, f_out, x1, x2, y_low, y_high, scales,
+    token[...] = region_now
+
+
+def second_kernel(b, f, came_x1, came_x2, came_y1, came_y2, region, material, a_out, f_out, x1, x2, y_low, y_high, scales, token,
                   elem, gx, gz, cross, planes, side):
-    region_now = jnp.concatenate([region[0], region[1]], axis=0).astype(f32) + 1.0
+    region_now = region[...]
+    token[...] = region_now
     a_out[...] = f[...]
     add_x(a_out, came_x1, came_x2)
     add_y(a_out, came_y1, came_y2)
@@ -406,16 +421,26 @@
     return jnp.where(lanes_of((17, 128)) < count, moved, 0.0)
 
 
+def surface_rows(x, c):
+    return 0, pl.ds(x * 136 + c, 17, stride=8), slice(None)
+
+
 def place_kernel(a1, surf1, u, v, a, after, u_out, first, tall, nodes):
     table = depth_table(back=True)
     for c in range(3):
-        to_nodes(lambda k: a1[c, :, :, k], table, tall, nodes)
+        to_nodes(lambda k: a1[c, :, :, k], c, table, tall, nodes)
         for x in range(9):
-            nodes[0, x] += add_surface(surf1, x, c, 1)
-        for t in range(4):
-            at = (c, slice(None), slice(None), slice(128 * t, 128 * t + 128))
-            first[c, t] = nodes[t]
-            u_out[at] = u[at] + 2.0 * time_step * v[at] + time_step**2 * (a[at] + nodes[t])
+            nodes[surface_rows(x, c)] += add_surface(surf1, x, c, 1)
+
+    def column(x, carry):
+        for y in range(17):
+            for t in range(4):
+                at, accel = node_lanes(x, y, t), nodes[node_rows(x, y, t)]
+                first[at] = accel
+                u_out[at] = u[at] + 2.0 * time_step * v[at] + time_step**2 * (a[at] + accel)
+        return carry
+
+    lax.fori_loop(0, 9, column, 0)
 
 
 def last_kernel(first, f, x1, x2, y1, y2, scales, surf1, surf2, v, a, v_out, a_out, tall, nodes, force):
@@ -430,13 +455,19 @@
                 for c in range(3):
                     force[c, i, j, k] = force[c, i, j, k] * scale
     for c in range(3):
-        to_nodes(lambda k: force[c, :, :, k], table, tall, nodes)
+        to_nodes(lambda k: force[c, :, :, k], c, table, tall, nodes)
         for x in range(9):
-            nodes[0, x] += add_surface(surf1, x, c, 1) + add_surface(surf2, x, c, 5)
-        for t in range(4):
-            at = (c, slice(None), slice(None), slice(128 * t, 128 * t + 128))
-            a_out[at] = nodes[t]
-            v_out[at] = v[at] + 0.5 * time_step * (a[at] + 2.0 * first[c, t] + nodes[t])
+            nodes[surface_rows(x, c)] += add_surface(surf1, x, c, 1) + add_surface(surf2, x, c, 5)
+
+    def column(x, carry):
+        for y in range(17):
+            for t in range(4):
+                at, accel = node_lanes(x, y, t), nodes[node_rows(x, y, t)]
+                a_out[at] = accel
+                v_out[at] = v[at] + 0.5 * time_step * (a[at] + 2.0 * first[at] + accel)
+        return carry
+
+    lax.fori_loop(0, 9, column, 0)
 
 
 def whole():
@@ -447,18 +478,26 @@
     return pl.BlockSpec(memory_space=pltpu.SMEM)
 
 
-def call(kernel, ins, outs, scratch, smem=(), away=(), mib=20):
+def call(kernel, ins, outs, scratch, smem=(), away=(), mib=10, copies=0):
     def spec(n):
-        return scalars() if n in smem else pl.BlockSpec(memory_space=pl.ANY) if n in away else whole()
-
+        return scalars() if n in smem else pl.BlockSpec(memory_space=pltpu.HBM) if n in away else whole()
+
+    scratch = [pltpu.VMEM(s, f32) if isinstance(s, tuple) else s for s in scratch]
     return pl.pallas_call(
         kernel,
         out_shape=[jax.ShapeDtypeStruct(s, f32) for s in outs],
         in_specs=[spec(n) for n in range(len(ins))],
         out_specs=[whole() for _ in outs],
-        scratch_shapes=[pltpu.VMEM(s, f32) for s in scratch],
+        scratch_shapes=scratch + ([pltpu.SemaphoreType.DMA((copies,))] if copies else []),
         compiler_params=pltpu.CompilerParams(vmem_limit_bytes=mib * 1024 * 1024),
     )(*ins)
+
+
+def fetch(pairs, semaphores):
+    copies = [pltpu.make_async_copy(source, target, semaphores.at[n]) for n, (source, target) in enumerate(pairs)]
+    for copy in copies:
+        copy.start()
+    return copies
 
 
 element_shape = (3, 5, 5, 4, 8, 128)
@@ -683,24 +722,31 @@
     return [g - jnp.where(ends[0], 2.0 * f, pltpu.roll(g, 1, axis)) for f, g in zip(fluxes, upper)]
 
 
-def field_of(f, density, momentum, energy):
-    return density if f == 0 else energy if f == 4 else momentum.at[f - 1]
-
-
-def start_kernel(nodes_y, density, momentum, energy, dest, slot, region, bottoms, first, second):
+def start_kernel(nodes_y, density, momentum, energy, dest, slot, region, bottoms, first, second, rows_low, rows_high,
+                 region_out, cells, dest_in, slot_in, region_in, semaphores):
+    copies = fetch(
+        [(dest, dest_in), (slot, slot_in), (region, region_in), (density, cells.at[0]),
+         (momentum, cells.at[pl.ds(1, 3)]), (energy, cells.at[4])],
+        semaphores,
+    )
+    for copy in copies:
+        copy.wait()
     sub, lane = rows_of(), lanes_of()
     pick = jnp.where(lane == 125 + sub, 1.0, 0.0)
     pieces = []
     odd = parity_x()
     for f in range(5):
-        field = field_of(f, density, momentum, energy)
-        columns = jnp.concatenate([field[x, :, 128:256] for x in range(4)], axis=0)
+        columns = jnp.concatenate([cells[f, x, :, 128:256] for x in range(4)], axis=0)
         pieces.append(full_dot(pick, columns, back=True)[0:3])
         for out, down in ((first, odd), (second, 1 - odd)):
-            out[f, 0:32, :] = field[3 - 3 * down]
-            out[f, 32:64, :] = field[2 - down]
+            out[f, 0:32, :] = cells[f, 3 - 3 * down]
+            out[f, 32:64, :] = cells[f, 2 - down]
+        for t in range(2):
+            lanes = slice(128 * t, 128 * t + 128)
+            for out, pair in ((rows_low, (0, 1)), (rows_high, (31, 30))):
+                out[f * 2 + t] = jnp.concatenate([cells[f, x, r : r + 1, lanes] for r in pair for x in range(4)], axis=0)
     count_gy, count_x = lax.axis_size("gy"), lax.axis_size("gx")
-    target, node = dest[...].astype(f32), slot[...].astype(f32)
+    target, node = dest_in[...].astype(f32), slot_in[...].astype(f32)
     grp = jnp.floor((target + 0.5) * (1.0 / (count_gy * count_x)))
     rest = target - grp * (count_gy * count_x)
     gx = jnp.floor((rest + 0.5) * (1.0 / count_gy))
@@ -708,7 +754,8 @@
     i = jnp.floor((node + 0.5) * (1.0 / 17.0))
     j = node - 17.0 * i
     pieces.append((8.0 * gx + i) * nodes_y + 16.0 * (grp * count_gy + gy) + j)
-    region_now = jnp.concatenate([region[0], region[1]], axis=0).astype(f32) + 1.0
+    region_now = jnp.concatenate([region_in[0], region_in[1]], axis=0).astype(f32) + 1.0
+    region_out[...] = region_now
     found = jnp.zeros((8, 128), f32)
     for z in range(2):
         found = jnp.where(lane == 8 * z + sub, jnp.broadcast_to(region_now[:, z : z + 1], (8, 128)), found)
@@ -718,19 +765,28 @@
         bottoms[n] = block
 
 
-def crater_kernel(density, momentum, energy, came1, came2, rows1, rows2, after, out, wide, mid, prims, face, fluxes):
+def crater_kernel(density, momentum, energy, came1, came2, rows1, rows2, after, out, token,
+                  wide, mid, prims, face, fluxes, semaphores):
+    planes, inner = pl.ds(2, 4), pl.ds(0, 32)
+    copies = fetch(
+        [(density, wide.at[0, planes, inner]), (momentum, wide.at[pl.ds(1, 3), planes, inner]),
+         (energy, wide.at[4, planes, inner])],
+        semaphores,
+    )
     place, last_y = along_y(), lax.axis_size("grp") * lax.axis_size("gy") - 1
     gx, last_x = position("gx"), lax.axis_size("gx") - 1
     odd, odd_y = parity_x(), parity_y()
     for f in range(5):
-        field = field_of(f, density, momentum, energy)
         low, high = sort_out(odd, came1[f], came2[f])
         for p, value in ((0, low[32:64]), (1, low[0:32]), (6, high[0:32]), (7, high[32:64])):
             wide[f, p, 0:32, :] = value
             wide[f, p, 32:40, :] = value[0:8]
+    token[...] = after[...]
+    for copy in copies:
+        copy.wait()
+    for f in range(5):
         for x in range(4):
-            wide[f, 2 + x, 0:32, :] = field[x]
-            wide[f, 2 + x, 32:40, :] = field[x, 24:32, :]
+            wide[f, 2 + x, 32:40, :] = wide[f, 2 + x, 24:32, :]
         for t in range(2):
             lanes = slice(128 * t, 128 * t + 128)
             at = 18 + f * 4 + t * 2
@@ -893,12 +949,14 @@
         faces[3, at, :] = ids[x]
 
 
-def surface_kernel(nodes_y, count_x, bottoms, material, tables, after, out1, out2, total, faces):
+def surface_kernel(nodes_y, count_x, bottoms, material, tables, after, out1, out2, total, faces, held, semaphores):
+    copies = fetch([(tables, held)], semaphores)
     base_x = (8 * position("gx") - 4).astype(f32)
     base_y = (16 * along_y() - 4).astype(f32)
     bottom_tractions(bottoms, count_x, faces)
     deposit(faces, nodes_y, base_x, base_y, total)
-    respond(total, region_rows(bottoms, count_x), material, tables, out1, out2)
+    copies[0].wait()
+    respond(total, region_rows(bottoms, count_x), material, held, out1, out2)
 
 
 def shards(density, momentum, energy, displacement, velocity_field, acceleration, material, element_region_index,
@@ -906,84 +964,78 @@
     along, rank = ("grp", "gy"), ("grp", "gx", "gy")
     nodes_y = 16 * lax.axis_size(along) + 1
     count_x, devices = lax.axis_size("gx"), lax.axis_size(rank)
-    crater, region = (density, momentum, energy), element_region_index
-    bottoms, crater1, crater2 = call(
+    crater = (density, momentum, energy)
+    u, v, a = [jnp.transpose(x, (1, 2, 0, 3)) for x in (displacement, velocity_field, acceleration)]
+    register = (8, 128)
+    bottoms, crater1, crater2, rows_low, rows_high, region = call(
         functools.partial(start_kernel, float(nodes_y)),
-        crater + (face_dest.reshape(1, -1), face_slot, region),
-        [(devices, 24, 128), (5, 64, 256), (5, 64, 256)],
-        [],
-        mib=12,
+        crater + (face_dest.reshape(1, -1), face_slot, element_region_index),
+        [(devices, 24, 128), (5, 64, 256), (5, 64, 256), (10, 8, 128), (10, 8, 128), register],
+        [(5, 4, 32, 256), pltpu.VMEM((1, 128), jnp.int32), pltpu.VMEM((1, 128), jnp.int32),
+         pltpu.VMEM((2, 4, 128), jnp.int32)],
+        away=(0, 1, 2, 3, 4, 5),
+        copies=6,
     )
     bottoms = lax.all_to_all(bottoms, rank, 0, 0, tiled=True)
     crater1, crater2 = exchange("gx", crater1, crater2)
-    b, f, x1, x2, y_low, y_high = call(
+    b, f, x1, x2, y_low, y_high, token = call(
         first_kernel,
-        (displacement, velocity_field, acceleration, region, material),
-        [element_shape, element_shape, (31, 8, 128), (31, 8, 128), (16, 8, 128), (15, 8, 128)],
-        internal_scratch + [(5, 5, 8, 512), (4, 9, 17, 128)],
+        (u, v, a, region, material),
+        [element_shape, element_shape, (31, 8, 128), (31, 8, 128), (16, 8, 128), (15, 8, 128), register],
+        internal_scratch + [(5, 5, 8, 512), (4, 1224, 128), (4, 1224, 128)],
         smem=(4,),
-        mib=24,
+        mib=14,
     )
     surf1, surf2 = call(
         functools.partial(surface_kernel, float(nodes_y), count_x),
-        (bottoms.reshape(devices * 24, 128), material, jnp.asarray(surface_tables()), x1),
+        (bottoms.reshape(devices * 24, 128), material, jnp.asarray(surface_tables()), token),
         [(24, 256), (24, 256)],
-        [(360, 128), (4, 4 * count_x, 128)],
+        [(360, 128), (4, 4 * count_x, 128), (6, 128, 128)],
         smem=(1,),
-        away=(3,),
-        mib=12,
+        away=(2,),
+        copies=1,
     )
     x1, x2 = exchange("gx", x1, x2)
     y1, y2 = call(
         first_edge_kernel,
-        (y_low, y_high, x1, x2) + crater + (crater1, crater2, surf1),
+        (y_low, y_high, x1, x2, rows_low, rows_high, crater1, crater2, surf1),
         [(38, 8, 128), (38, 8, 128)],
         [],
-        away=(9,),
-        mib=12,
     )
     y1, y2 = exchange(along, y1, y2)
-    a1, f2, p1, p2, y_low, y_high, scales = call(
+    a1, f2, p1, p2, y_low, y_high, scales, token = call(
         second_kernel,
         (b, f, x1, x2, y1, y2, region, material),
-        [element_shape, element_shape, (30, 8, 128), (30, 8, 128), (15, 8, 128), (15, 8, 128), (3, 3, 2, 8, 128)],
+        [element_shape, element_shape, (30, 8, 128), (30, 8, 128), (15, 8, 128), (15, 8, 128), (3, 3, 2, 8, 128), register],
         internal_scratch,
         smem=(7,),
-        mib=24,
-    )
-    (hydro_state,) = call(
+    )
+    hydro_state, token = call(
         crater_kernel,
-        crater + (crater1, crater2, y1, y2, p1),
-        [(5, 4, 32, 256)],
+        crater + (crater1, crater2, y1, y2, token),
+        [(5, 4, 32, 256), register],
         [(5, 8, 40, 256), (5, 8, 40, 256), (6, 40, 256), (5, 40, 256), (6, 40, 256)],
-        away=(7,),
-        mib=16,
+        away=(0, 1, 2),
+        copies=3,
     )
     p1, p2 = exchange("gx", p1, p2)
-    r1, r2 = call(
-        second_edge_kernel,
-        (y_low, y_high, p1, p2, hydro_state),
-        [(15, 8, 128), (15, 8, 128)],
-        [],
-        away=(4,),
-        mib=8,
+    r1, r2, token = call(
+        second_edge_kernel, (y_low, y_high, p1, p2, token), [(15, 8, 128), (15, 8, 128), register], []
     )
     u_out, first = call(
         place_kernel,
-        (a1, surf1, displacement, velocity_field, acceleration, r1),
-        [displacement.shape, (3, 4, 9, 17, 128)],
-        [(5, 5, 8, 512), (4, 9, 17, 128)],
-        away=(5,),
-        mib=20,
+        (a1, surf1, u, v, a, token),
+        [u.shape, u.shape],
+        [(5, 5, 8, 512), (4, 1224, 128)],
     )
     r1, r2 = exchange(along, r1, r2)
     v_out, a_out = call(
         last_kernel,
-        (first, f2, p1, p2, r1, r2, scales, surf1, surf2, velocity_field, acceleration),
-        [displacement.shape] * 2,
-        [(5, 5, 8, 512), (4, 9, 17, 128), element_shape],
-        mib=22,
-    )
+        (first, f2, p1, p2, r1, r2, scales, surf1, surf2, v, a),
+        [u.shape] * 2,
+        [(5, 5, 8, 512), (4, 1224, 128), element_shape],
+    )
+    u_out, v_out, a_out = [jnp.transpose(x, (2, 0, 1, 3)) for x in (u_out, v_out, a_out)]
     return hydro_state, u_out, v_out, a_out
 
 

time: 82.9 us -> 83.4 us (level)
  the two profiles are of different devices: /device:TPU:0 before, /device:TPU:3 now
where the time goes in v5:
time: 83.4 us; the launch traced here: 82.7 us
  Pallas kernels  35 us (42%)
  starting transfers between devices  27.8 us (33%)
  local copies, waits for them, and re-layouts  15.3 us (18%)
  waiting for transfers between devices  3.53 us (4%)
  between operations  0.95 us (1%)
    pallas_call x9, Pallas kernels, call(): pl.pallas_call(kernel, out_shape=[jax.ShapeDtypeStruct(s, f32) for s in o...  35 us
    ppermute x5, starting transfers between devices, exchange(): lax.ppermute(second, axis, pairs + [(j, i) for i, j in pairs])  19.6 us
    unnamed x52, local copies, waits for them, and re-layouts  15.3 us
    all_to_all x1, starting transfers between devices, shards(): bottoms = lax.all_to_all(bottoms, rank, 0, 0, tiled=True)  6.44 us
    ppermute x5, waiting for transfers between devices, exchange(): lax.ppermute(second, axis, pairs + [(j, i) for i, j in pairs])  3.51 us
    ppermute x5, starting transfers between devices, exchange(): first = lax.ppermute(first, axis, [(i, i ^ 1) for i in range(count)])  1.84 us
  transfers between devices with their start and end apart: 11, of which 1 were waited for; matrix products, arithmetic and copies ran while one was open for 0% of the time, Pallas kernels for 28%

profile of v5, /device:TPU:3, one launch (start us, length us, event | category | flops | bytes accessed | tf_op | source)
XLA Modules:
  0.0 82.7 jit_solution(17874713620619666756)
XLA Ops:
  0.6 0.0 copy-start.5
  0.7 1.1 %copy-done.5 = f32[3,4,32,256]{3,2,1,0:T(8,128)S(1)} copy-done((f32[3,4,32,256]{3,2,1,0:T(8,128)S(1)}, f32[3,4,32,256]{3,2,1,0:T(8,128)}, u32[]{:S(2)}) %copy-start.5) | copy-done | bytes 393240
  1.7 0.9 %copy-done.9 = f32[4,32,256]{2,1,0:T(8,128)S(1)} copy-done((f32[4,32,256]{2,1,0:T(8,128)S(1)}, f32[4,32,256]{2,1,0:T(8,128)}, u32[]{:S(2)}) %copy-start.9) | copy-done | bytes 131096
  2.6 0.9 %copy-done.11 = f32[4,32,256]{2,1,0:T(8,128)S(1)} copy-done((f32[4,32,256]{2,1,0:T(8,128)S(1)}, f32[4,32,256]{2,1,0:T(8,128)}, u32[]{:S(2)}) %copy-start.11) | copy-done | bytes 131096
  3.6 0.7 copy-done.23
  4.2 0.7 copy-done.24
  4.9 0.7 copy-done.25
  5.6 2.1 %shard_map.138 = (f32[32,24,128]{2,1,0:T(8,128)}, f32[5,64,256]{2,1,0:T(8,128)}, f32[5,64,256]{2,1,0:T(8,128)}, f32[10,8,128]{2,1,0:T(8,128)S(1)}, f32[10,8,128]{2,1,0:T(8,128)S(1)}, /*index=5*/f32[8,128]{1,0:T(8,128)S(1)}) custom-call(f32[4,32,256]{2,1,0:T(8,128)S(1)} %copy-done.9, f32[3,4,32,256]{3,2,1,0:T(8,128)S(1)} %copy-done.5, ...), custom_call_target="tpu_custom_call" | custom-call | tf_op jit(solution)/shard_map/pallas_call | solution.py:486
  7.7 0.6 copy-done.18
  8.3 0.6 copy-done.20
  8.9 6.4 %all-to-all-start = ((f32[32,24,128]{2,1,0:T(8,128)}), f32[32,24,128]{2,1,0:T(8,128)S(1)}, u32[]{:S(2)}, u32[]{:S(2)}) async-start(f32[32,24,128]{2,1,0:T(8,128)} %get-tuple-element.47), calls=%async_computation | async-start | bytes 786432 | tf_op jit(solution)/shard_map/all_to_all | solution.py:979
  15.3 0.1 collective-permute-start
  15.5 4.2 %collective-permute-start.1 = (f32[5,64,256]{2,1,0:T(8,128)}, f32[5,64,256]{2,1,0:T(8,128)S(1)}, u32[]{:S(2)}, u32[]{:S(2)}) collective-permute-start(f32[5,64,256]{2,1,0:T(8,128)} %get-tuple-element.39), channel_id=1, source_target_pairs={{2,4},{6,8},{10,12},{4,2},{8,6},{12,10},{3,5},{7,9},{11,13},{5,3},... | collective-permute-start | bytes 983048 | tf_op jit(solution)/shard_map/ppermute | solution.py:512
  19.7 0.0 copy-start.1
  19.7 1.3 %copy-done.1 = f32[3,9,17,512]{3,0,2,1:T(4,128)S(1)} copy-done((f32[3,9,17,512]{3,0,2,1:T(4,128)S(1)}, f32[3,9,17,512]{3,0,2,1:T(4,128)}, u32[]{:S(2)}) %copy-start.1) | copy-done | bytes 940056
  21.0 1.3 %copy-done.3 = f32[3,9,17,512]{3,0,2,1:T(4,128)S(1)} copy-done((f32[3,9,17,512]{3,0,2,1:T(4,128)S(1)}, f32[3,9,17,512]{3,0,2,1:T(4,128)}, u32[]{:S(2)}) %copy-start.3) | copy-done | bytes 940056
  22.3 8.9 %shard_map.139 = (f32[3,5,5,4,8,128]{5,4,3,2,1,0:T(8,128)S(1)}, f32[3,5,5,4,8,128]{5,4,3,2,1,0:T(8,128)S(1)}, f32[31,8,128]{2,1,0:T(8,128)}, f32[31,8,128]{2,1,0...) custom-call(f32[9,17,3,512]{3,2,1,0:T(4,128)S(1)} %bitcast.14, ...), custom_call_target="tpu_custom_call" | custom-call | tf_op jit(solution)/shard_map/pallas_call | solution.py:486
  31.2 1.0 %copy-done.7 = f32[3,5,5,4,8,128]{5,4,3,2,1,0:T(8,128)} copy-done((f32[3,5,5,4,8,128]{5,4,3,2,1,0:T(8,128)}, f32[3,5,5,4,8,128]{5,4,3,2,1,0:T(8,128)S(1)}, u32[]{:S(2)}) %copy-start.7) | copy-done | bytes 1228824
  32.2 0.6 copy-done.14
  32.8 0.6 copy-done.16
  33.5 4.3 %collective-permute-start.3 = (f32[31,8,128]{2,1,0:T(8,128)}, f32[31,8,128]{2,1,0:T(8,128)}, u32[]{:S(2)}, u32[]{:S(2)}) collective-permute-start(f32[31,8,128]{2,1,0:T(8,128)} %get-tuple-element.44), channel_id=1, source_target_pairs={{2,4},{6,8},{10,12},{4,2},{8,6},{12,10},{3,5},{7,9},{11,13},{5,3},... | collective-permute-start | bytes 380936 | tf_op jit(solution)/shard_map/ppermute | solution.py:512
  37.8 0.0 all-to-all-done
  37.8 0.0 copy-start.8
  37.8 0.0 copy-start.13
  37.8 1.1 %copy-done.13 = f32[6,128,128]{2,1,0:T(8,128)S(1)} copy-done((f32[6,128,128]{2,1,0:T(8,128)S(1)}, f32[6,128,128]{2,1,0:T(8,128)}, u32[]{:S(2)}) %copy-start.13) | copy-done | bytes 393240
  38.9 5.0 %shard_map.140 = (f32[24,256]{1,0:T(8,128)S(1)}, f32[24,256]{1,0:T(8,128)S(1)}) custom-call(f32[768,128]{1,0:T(8,128)S(1)} %bitcast.16, f32[3,8]{1,0:T(4,128)S(1)} %copy-done.22, f32[6,128,128]{2,1,0:T(8,128)S(1)} %copy-done.13, f32[8,128]{1,0:T(8,128)S(1)} %get-tuple-element.48.after), custom_call_target="tpu_custom_call" | custom-call | tf_op jit(solution)/shard_map/pallas_call | solution.py:486
  43.9 0.0 collective-permute-done.2.came1.came_x1
  44.0 0.0 collective-permute-done.crater1.came1
  44.0 0.0 collective-permute-done.1.crater2.came2
  44.0 0.8 %copy-done.15 = f32[16,8,128]{2,1,0:T(8,128)S(1)} copy-done((f32[16,8,128]{2,1,0:T(8,128)S(1)}, f32[16,8,128]{2,1,0:T(8,128)}, u32[]{:S(2)}) %copy-start.15) | copy-done | bytes 65560
  44.8 0.8 %copy-done.17 = f32[15,8,128]{2,1,0:T(8,128)S(1)} copy-done((f32[15,8,128]{2,1,0:T(8,128)S(1)}, f32[15,8,128]{2,1,0:T(8,128)}, u32[]{:S(2)}) %copy-start.17) | copy-done | bytes 61464
  45.7 0.8 copy-done.19
  46.4 0.8 copy-done.21
  47.2 1.0 %shard_map.141 = (f32[38,8,128]{2,1,0:T(8,128)S(1)}, f32[38,8,128]{2,1,0:T(8,128)S(1)}) custom-call(f32[16,8,128]{2,1,0:T(8,128)S(1)} %copy-done.15, f32[15,8,128]{2,1,0:T(8,128)S(1)} %copy-done.17, f32[31,8,128]{2,1,0:T(8,128)} %collective-permute-done.2.came1.came_x1, f32[31,8,128]{2,1,0:T(8,128)} %collective-permute-done.3.came2.came_x2, ...), custom_call_target="tpu_custom_call" | custom-call | tf_op jit(solution)/shard_map/pallas_call | solution.py:486
  48.2 1.5 %collective-permute-start.4 = (f32[38,8,128]{2,1,0:T(8,128)S(1)}, f32[38,8,128]{2,1,0:T(8,128)S(1)}, u32[]{:S(2)}, u32[]{:S(2)}) collective-permute-start(f32[38,8,128]{2,1,0:T(8,128)S(1)} %get-tuple-element.50), channel_id=1, source_target_pairs={{0,1},{1,0},{16,17},{17,16},{2,3},{3,2},{18,19},{19,18},{4,5},{5,4... | collective-permute-start | bytes 466952 | tf_op jit(solution)/shard_map/ppermute | solution.py:511
  49.8 3.0 %collective-permute-start.5 = (f32[38,8,128]{2,1,0:T(8,128)S(1)}, f32[38,8,128]{2,1,0:T(8,128)S(1)}, u32[]{:S(2)}, u32[]{:S(2)}) collective-permute-start(f32[38,8,128]{2,1,0:T(8,128)S(1)} %get-tuple-element.51), channel_id=1, source_target_pairs={{1,16},{16,1},{3,18},{18,3},{5,20},{20,5},{7,22},{22,7},{9,24},{24... | collective-permute-start | bytes 466952 | tf_op jit(solution)/shard_map/ppermute | solution.py:512
  52.8 3.5 %collective-permute-done.5.came_y2.rows2 = f32[38,8,128]{2,1,0:T(8,128)S(1)} collective-permute-done((f32[38,8,128]{2,1,0:T(8,128)S(1)}, f32[38,8,128]{2,1,0:T(8,128)S(1)}, u32[]{:S(2)}, u32[]{:S(2)}) %collective-permute-start.5) | collective-permute-done | bytes 155680 | tf_op jit(solution)/shard_map/ppermute | solution.py:512
  56.3 0.0 copy-start.4
  56.4 4.6 %shard_map.142 = (f32[3,5,5,4,8,128]{5,4,3,2,1,0:T(8,128)S(1)}, f32[3,5,5,4,8,128]{5,4,3,2,1,0:T(8,128)S(1)}, f32[30,8,128]{2,1,0:T(8,128)S(1)}, f32[30,8,128]{2...) custom-call(f32[3,5,5,4,8,128]{5,4,3,2,1,0:T(8,128)S(1)} %get-tuple-, ...), custom_call_target="tpu_custom_call" | custom-call | tf_op jit(solution)/shard_map/pallas_call | solution.py:486
  61.0 0.0 copy-start.2
  61.0 0.1 collective-permute-start.6
  61.1 4.3 %collective-permute-start.7 = (f32[30,8,128]{2,1,0:T(8,128)S(1)}, f32[30,8,128]{2,1,0:T(8,128)S(1)}, u32[]{:S(2)}, u32[]{:S(2)}) collective-permute-start(f32[30,8,128]{2,1,0:T(8,128)S(1)} %get-tuple-element.60), channel_id=1, source_target_pairs={{2,4},{6,8},{10,12},{4,2},{8,6},{12,10},{3,5},{7,9},{11,13},{5,3},... | collective-permute-start | bytes 368648 | tf_op jit(solution)/shard_map/ppermute | solution.py:512
  65.4 4.9 %shard_map.143 = (f32[5,4,32,256]{3,2,1,0:T(8,128)}, f32[8,128]{1,0:T(8,128)S(1)}) custom-call(f32[4,32,256]{2,1,0:T(8,128)S(1)} %copy-done.10, f32[3,4,32,256]{3,2,1,0:T(8,128)S(1)} %copy-done.6, f32[4,32,256]{2,1,0:T(8,128)S(1)} %copy-done.12, f32[5,64,256]{2,1,0:T(8,128)S(1)} %collective-permute-done.crater1.came1, ...), custom_call_target="tpu_custom_call" | custom-call | tf_op jit(solution)/shard_map/pallas_call | solution.py:486
  70.4 0.1 shard_map.144
  70.4 0.1 collective-permute-start.8
  70.5 3.8 %collective-permute-start.9 = (f32[15,8,128]{2,1,0:T(8,128)S(1)}, f32[15,8,128]{2,1,0:T(8,128)S(1)}, u32[]{:S(2)}, u32[]{:S(2)}) collective-permute-start(f32[15,8,128]{2,1,0:T(8,128)S(1)} %get-tuple-element.67), channel_id=1, source_target_pairs={{1,16},{16,1},{3,18},{18,3},{5,20},{20,5},{7,22},{22,7},{9,24},{24... | collective-permute-start | bytes 184328 | tf_op jit(solution)/shard_map/ppermute | solution.py:512
  74.3 3.9 %shard_map.145 = (f32[9,17,3,512]{3,2,1,0:T(4,128)}, f32[9,17,3,512]{3,2,1,0:T(4,128)S(1)}) custom-call(f32[3,5,5,4,8,128]{5,4,3,2,1,0:T(8,128)S(1)} %get-tuple-element.56.a1, f32[24,256]{1,0:T(8,128)S(1)} %get-tuple-element.49.after.surf1, f32[9,17,3,512]{3,2,1,0:T(4,128)S(1)} %bitcast.15, f32[9,17,3,512]{3,2,1,0:T(4,128)S(1)} %bitcast.9, ...), custom_call_target="tpu_custom_call" | custom-call | tf_op jit(solution)/shard_map/pallas_call | solution.py:486
  78.2 4.4 %shard_map.146 = (f32[9,17,3,512]{3,2,1,0:T(4,128)}, f32[9,17,3,512]{3,2,1,0:T(4,128)}) custom-call(f32[9,17,3,512]{3,2,1,0:T(4,128)S(1)} %get-tuple-element.64.first, f32[3,5,5,4,8,128]{5,4,3,2,1,0:T(8,128)S(1)} %get-tuple-element.65.f, f32[30,8,128]{2,1,0:T(8,128)S(1)} %collective-permute-done.6.came1.x1, ...), custom_call_target="tpu_custom_call" | custom-call | tf_op jit(solution)/shard_map/pallas_call | solution.py:486
  (35 shorter events, 0.1 us)
Async XLA Ops:
  0.6 19.0 %copy-start = (f32[3,9,17,512]{3,0,2,1:T(4,128)S(1)}, f32[3,9,17,512]{3,0,2,1:T(4,128)}, u32[]{:S(2)}) copy-start(f32[3,9,17,512]{3,0,2,1:T(4,128)} %param.15) | copy-start | bytes 2820100
  0.6 1.1 %copy-start.5 = (f32[3,4,32,256]{3,2,1,0:T(8,128)S(1)}, f32[3,4,32,256]{3,2,1,0:T(8,128)}, u32[]{:S(2)}) copy-start(f32[3,4,32,256]{3,2,1,0:T(8,128)} %momentum.3) | copy-start | bytes 1179652
  1.7 0.9 %copy-start.9 = (f32[4,32,256]{2,1,0:T(8,128)S(1)}, f32[4,32,256]{2,1,0:T(8,128)}, u32[]{:S(2)}) copy-start(f32[4,32,256]{2,1,0:T(8,128)} %density.3) | copy-start | bytes 393220
  2.6 0.9 %copy-start.11 = (f32[4,32,256]{2,1,0:T(8,128)S(1)}, f32[4,32,256]{2,1,0:T(8,128)}, u32[]{:S(2)}) copy-start(f32[4,32,256]{2,1,0:T(8,128)} %energy.3) | copy-start | bytes 393220
  3.5 0.7 copy-start.23
  4.2 0.7 copy-start.24
  4.9 0.7 copy-start.25
  5.5 14.1 %copy-start.22 = (f32[3,8]{1,0:T(4,128)S(1)}, f32[3,8]{1,0:T(4,128)}, u32[]{:S(2)}) copy-start(f32[3,8]{1,0:T(4,128)} %material.5) | copy-start | bytes 292
  7.6 0.6 copy-start.18
  8.2 0.6 copy-start.20
  8.9 28.9 %all-to-all-start = ((f32[32,24,128]{2,1,0:T(8,128)}), f32[32,24,128]{2,1,0:T(8,128)S(1)}, u32[]{:S(2)}, u32[]{:S(2)}) async-start(f32[32,24,128]{2,1,0:T(8,128)} %get-tuple-element.47), calls=%async_computation | async-start | bytes 786432 | tf_op jit(solution)/shard_map/all_to_all | solution.py:979
  15.3 28.7 %collective-permute-start = (f32[5,64,256]{2,1,0:T(8,128)}, f32[5,64,256]{2,1,0:T(8,128)S(1)}, u32[]{:S(2)}, u32[]{:S(2)}) collective-permute-start(f32[5,64,256]{2,1,0:T(8,128)} %get-tuple-element.38), channel_id=1, source_target_pairs={{0,2},{2,0},{4,6},{6,4},{8,10},{10,8},{12,14},{14,12},{1,3},{3,1},... | collective-permute-start | bytes 983048 | tf_op jit(solution)/shard_map/ppermute | solution.py:511
  15.5 28.5 %collective-permute-start.1 = (f32[5,64,256]{2,1,0:T(8,128)}, f32[5,64,256]{2,1,0:T(8,128)S(1)}, u32[]{:S(2)}, u32[]{:S(2)}) collective-permute-start(f32[5,64,256]{2,1,0:T(8,128)} %get-tuple-element.39), channel_id=1, source_target_pairs={{2,4},{6,8},{10,12},{4,2},{8,6},{12,10},{3,5},{7,9},{11,13},{5,3},... | collective-permute-start | bytes 983048 | tf_op jit(solution)/shard_map/ppermute | solution.py:512
  19.7 1.3 %copy-start.1 = (f32[3,9,17,512]{3,0,2,1:T(4,128)S(1)}, f32[3,9,17,512]{3,0,2,1:T(4,128)}, u32[]{:S(2)}) copy-start(f32[3,9,17,512]{3,0,2,1:T(4,128)} %param.16) | copy-start | bytes 2820100
  21.0 1.3 %copy-start.3 = (f32[3,9,17,512]{3,0,2,1:T(4,128)S(1)}, f32[3,9,17,512]{3,0,2,1:T(4,128)}, u32[]{:S(2)}) copy-start(f32[3,9,17,512]{3,0,2,1:T(4,128)} %param.14) | copy-start | bytes 2820100
  31.2 1.0 %copy-start.7 = (f32[3,5,5,4,8,128]{5,4,3,2,1,0:T(8,128)}, f32[3,5,5,4,8,128]{5,4,3,2,1,0:T(8,128)S(1)}, u32[]{:S(2)}) copy-start(f32[3,5,5,4,8,128]{5,4,3,2,1,0:T(8,128)S(1)} %get-tuple-element.53.f) | copy-start | bytes 3686404
  32.2 0.6 copy-start.14
  32.8 0.6 copy-start.16
  33.5 10.5 %collective-permute-start.2 = (f32[31,8,128]{2,1,0:T(8,128)}, f32[31,8,128]{2,1,0:T(8,128)}, u32[]{:S(2)}, u32[]{:S(2)}) collective-permute-start(f32[31,8,128]{2,1,0:T(8,128)} %get-tuple-element.43), channel_id=1, source_target_pairs={{0,2},{2,0},{4,6},{6,4},{8,10},{10,8},{12,14},{14,12},{1,3},{3,1},... | collective-permute-start | bytes 380936 | tf_op jit(solution)/shard_map/ppermute | solution.py:511
  33.5 10.5 %collective-permute-start.3 = (f32[31,8,128]{2,1,0:T(8,128)}, f32[31,8,128]{2,1,0:T(8,128)}, u32[]{:S(2)}, u32[]{:S(2)}) collective-permute-start(f32[31,8,128]{2,1,0:T(8,128)} %get-tuple-element.44), channel_id=1, source_target_pairs={{2,4},{6,8},{10,12},{4,2},{8,6},{12,10},{3,5},{7,9},{11,13},{5,3},... | collective-permute-start | bytes 380936 | tf_op jit(solution)/shard_map/ppermute | solution.py:512
  37.8 18.6 %copy-start.8 = (f32[3,5,5,4,8,128]{5,4,3,2,1,0:T(8,128)S(1)}, f32[3,5,5,4,8,128]{5,4,3,2,1,0:T(8,128)}, u32[]{:S(2)}) copy-start(f32[3,5,5,4,8,128]{5,4,3,2,1,0:T(8,128)} %copy-done.7) | copy-start | bytes 3686404
  37.8 1.1 %copy-start.13 = (f32[6,128,128]{2,1,0:T(8,128)S(1)}, f32[6,128,128]{2,1,0:T(8,128)}, u32[]{:S(2)}) copy-start(f32[6,128,128]{2,1,0:T(8,128)} %constant.2.clone.tables) | copy-start | bytes 1179652
  44.0 0.8 %copy-start.15 = (f32[16,8,128]{2,1,0:T(8,128)S(1)}, f32[16,8,128]{2,1,0:T(8,128)}, u32[]{:S(2)}) copy-start(f32[16,8,128]{2,1,0:T(8,128)} %copy-done.14) | copy-start | bytes 196612
  44.8 0.8 %copy-start.17 = (f32[15,8,128]{2,1,0:T(8,128)S(1)}, f32[15,8,128]{2,1,0:T(8,128)}, u32[]{:S(2)}) copy-start(f32[15,8,128]{2,1,0:T(8,128)} %copy-done.16) | copy-start | bytes 184324
  45.7 0.8 copy-start.19
  46.4 0.8 copy-start.21
  48.2 4.6 %collective-permute-start.4 = (f32[38,8,128]{2,1,0:T(8,128)S(1)}, f32[38,8,128]{2,1,0:T(8,128)S(1)}, u32[]{:S(2)}, u32[]{:S(2)}) collective-permute-start(f32[38,8,128]{2,1,0:T(8,128)S(1)} %get-tuple-element.50), channel_id=1, source_target_pairs={{0,1},{1,0},{16,17},{17,16},{2,3},{3,2},{18,19},{19,18},{4,5},{5,4... | collective-permute-start | bytes 466952 | tf_op jit(solution)/shard_map/ppermute | solution.py:511
  49.8 6.5 %collective-permute-start.5 = (f32[38,8,128]{2,1,0:T(8,128)S(1)}, f32[38,8,128]{2,1,0:T(8,128)S(1)}, u32[]{:S(2)}, u32[]{:S(2)}) collective-permute-start(f32[38,8,128]{2,1,0:T(8,128)S(1)} %get-tuple-element.51), channel_id=1, source_target_pairs={{1,16},{16,1},{3,18},{18,3},{5,20},{20,5},{7,22},{22,7},{9,24},{24... | collective-permute-start | bytes 466952 | tf_op jit(solution)/shard_map/ppermute | solution.py:512
  56.3 9.0 %copy-start.6 = (f32[3,4,32,256]{3,2,1,0:T(8,128)S(1)}, f32[3,4,32,256]{3,2,1,0:T(8,128)}, u32[]{:S(2)}) copy-start(f32[3,4,32,256]{3,2,1,0:T(8,128)} %momentum.3) | copy-start | bytes 1179652
  56.3 9.1 %copy-start.10 = (f32[4,32,256]{2,1,0:T(8,128)S(1)}, f32[4,32,256]{2,1,0:T(8,128)}, u32[]{:S(2)}) copy-start(f32[4,32,256]{2,1,0:T(8,128)} %density.3) | copy-start | bytes 393220
  56.3 9.1 %copy-start.12 = (f32[4,32,256]{2,1,0:T(8,128)S(1)}, f32[4,32,256]{2,1,0:T(8,128)}, u32[]{:S(2)}) copy-start(f32[4,32,256]{2,1,0:T(8,128)} %energy.3) | copy-start | bytes 393220
  56.3 17.9 %copy-start.4 = (f32[3,9,17,512]{3,0,2,1:T(4,128)S(1)}, f32[3,9,17,512]{3,0,2,1:T(4,128)}, u32[]{:S(2)}) copy-start(f32[3,9,17,512]{3,0,2,1:T(4,128)} %param.14) | copy-start | bytes 2820100
  61.0 13.3 %copy-start.2 = (f32[3,9,17,512]{3,0,2,1:T(4,128)S(1)}, f32[3,9,17,512]{3,0,2,1:T(4,128)}, u32[]{:S(2)}) copy-start(f32[3,9,17,512]{3,0,2,1:T(4,128)} %param.16) | copy-start | bytes 2820100
  61.0 9.4 %collective-permute-start.6 = (f32[30,8,128]{2,1,0:T(8,128)S(1)}, f32[30,8,128]{2,1,0:T(8,128)S(1)}, u32[]{:S(2)}, u32[]{:S(2)}) collective-permute-start(f32[30,8,128]{2,1,0:T(8,128)S(1)} %get-tuple-element.59), channel_id=1, source_target_pairs={{0,2},{2,0},{4,6},{6,4},{8,10},{10,8},{12,14},{14,12},{1,3},{3,1},... | collective-permute-start | bytes 368648 | tf_op jit(solution)/shard_map/ppermute | solution.py:511
  61.1 9.3 %collective-permute-start.7 = (f32[30,8,128]{2,1,0:T(8,128)S(1)}, f32[30,8,128]{2,1,0:T(8,128)S(1)}, u32[]{:S(2)}, u32[]{:S(2)}) collective-permute-start(f32[30,8,128]{2,1,0:T(8,128)S(1)} %get-tuple-element.60), channel_id=1, source_target_pairs={{2,4},{6,8},{10,12},{4,2},{8,6},{12,10},{3,5},{7,9},{11,13},{5,3},... | collective-permute-start | bytes 368648 | tf_op jit(solution)/shard_map/ppermute | solution.py:512
  70.4 7.8 %collective-permute-start.8 = (f32[15,8,128]{2,1,0:T(8,128)S(1)}, f32[15,8,128]{2,1,0:T(8,128)S(1)}, u32[]{:S(2)}, u32[]{:S(2)}) collective-permute-start(f32[15,8,128]{2,1,0:T(8,128)S(1)} %get-tuple-element.66), channel_id=1, source_target_pairs={{0,1},{1,0},{16,17},{17,16},{2,3},{3,2},{18,19},{19,18},{4,5},{5,4... | collective-permute-start | bytes 184328 | tf_op jit(solution)/shard_map/ppermute | solution.py:511
  70.5 7.7 %collective-permute-start.9 = (f32[15,8,128]{2,1,0:T(8,128)S(1)}, f32[15,8,128]{2,1,0:T(8,128)S(1)}, u32[]{:S(2)}, u32[]{:S(2)}) collective-permute-start(f32[15,8,128]{2,1,0:T(8,128)S(1)} %get-tuple-element.67), channel_id=1, source_target_pairs={{1,16},{16,1},{3,18},{18,3},{5,20},{20,5},{7,22},{22,7},{9,24},{24... | collective-permute-start | bytes 184328 | tf_op jit(solution)/shard_map/ppermute | solution.py:512

commit v6 on v5

--- a/solution.py
+++ b/solution.py
@@ -68,54 +68,65 @@
     return high, middle, (rest - middle.astype(f32)).astype(jnp.bfloat16)
 
 
-def one_hot_dot(x, table, dims=(((1,), (0,)), ((), ()))):
-    return sum(lax.dot_general(part, table, dims, preferred_element_type=f32) for part in split_three(x))
-
-
 def depth_table(back=False):
-    a = lax.broadcasted_iota(jnp.int32, (512, 512), 1 if back else 0)
-    b = lax.broadcasted_iota(jnp.int32, (512, 512), 0 if back else 1)
-    return jnp.where(a == 4 * (b & 127) + (b >> 7), 1.0, 0.0).astype(jnp.bfloat16)
+    a = lax.broadcasted_iota(jnp.int32, (256, 256), 1 if back else 0)
+    b = lax.broadcasted_iota(jnp.int32, (256, 256), 0 if back else 1)
+    table = jnp.where(a == 4 * (b & 63) + (b >> 6), 1.0, 0.0).astype(jnp.bfloat16)
+    return jnp.concatenate([table] * 3, axis=0)
+
+
+def moved_lanes(x, table):
+    return jnp.dot(jnp.concatenate(split_three(x), axis=1), table, preferred_element_type=f32)
+
+
+def interleave(x, y):
+    front = lanes_of(x.shape) < 64
+    return jnp.where(front, x, pltpu.roll(y, 64, 1)), jnp.where(front, pltpu.roll(x, 64, 1), y)
 
 
 def rows_at(i, j, ex, c, count=4):
     return pl.ds(((4 * ex + i) * 17 + j) * 8 + c, count, stride=32)
 
 
-def to_elements(nodes, c, table, tall, put):
-    for i in range(5):
-        for j in range(5):
-            for ex in range(2):
-                for t in range(4):
-                    tall[i, j, 4 * ex : 4 * ex + 4, 128 * t : 128 * t + 128] = nodes[t, rows_at(i, j, ex, c), :]
-    out = one_hot_dot(tall[...].reshape(200, 512), table)
-    for k in range(4):
-        put(k, out[:, 128 * k : 128 * k + 128].reshape(5, 5, 8, 128))
-
-
-def to_nodes(get, c, table, tall, nodes):
-    wide = jnp.concatenate([get(k).reshape(200, 128) for k in range(4)], axis=1)
-    tall[...] = one_hot_dot(wide, table).reshape(5, 5, 8, 512)
-    for i in range(5):
-        for j in range(5):
+def tile_copies(field, held, semaphores, first, out=False):
+    copies = []
+    for t in range(4):
+        outside = field.at[:, :, :, pl.ds(128 * t, 128)]
+        inside = held.reshape(4, 9, 17, 8, 128).at[t, :, :, pl.ds(0, 3), :]
+        ends = (inside, outside) if out else (outside, inside)
+        copies.append(pltpu.make_async_copy(*ends, semaphores.at[first + t]))
+    return copies
+
+
+def to_elements(half, wide, table, kept, puts):
+    moved = moved_lanes(wide[...].reshape(600, 256), table)
+    if half == 0:
+        kept[...] = moved
+        return
+    for pair in range(2):
+        lanes = slice(128 * pair, 128 * pair + 128)
+        for l, value in enumerate(interleave(kept[:, lanes], moved[:, lanes])):
+            puts(2 * pair + l, value.reshape(3, 5, 5, 8, 128))
+
+
+def to_nodes(get, table, tall):
+    pairs = [interleave(get(2 * p).reshape(600, 128), get(2 * p + 1).reshape(600, 128)) for p in range(2)]
+    for half in range(2):
+        wide = jnp.concatenate([pairs[0][half], pairs[1][half]], axis=1)
+        tall[half] = moved_lanes(wide, table).reshape(3, 5, 5, 8, 256)
+
+
+def node_pieces(tall, t):
+    lanes = slice(128 * (t % 2), 128 * (t % 2) + 128)
+    for c in range(3):
+        for i in range(5):
             for ex in range(2):
                 if i == 4 and ex == 0:
                     continue
-                for t in range(4):
-                    lanes = slice(128 * t, 128 * t + 128)
-                    if j < 4:
-                        nodes[t, rows_at(i, j, ex, c), :] = tall[i, j, 4 * ex : 4 * ex + 4, lanes]
-                    else:
-                        at = ((4 * ex + i) * 17 + 16) * 8 + c
-                        nodes[t, at : at + 1, :] = tall[i, j, 4 * ex + 3 : 4 * ex + 4, lanes]
-
-
-def node_lanes(x, y, t):
-    return x, y, slice(None), slice(128 * t, 128 * t + 128)
-
-
-def node_rows(x, y, t):
-    return t, pl.ds(pl.multiple_of((x * 17 + y) * 8, 8), 3), slice(None)
+                for j in range(4):
+                    yield rows_at(i, j, ex, c), j, 4 * ex + i, c, tall[t // 2, c, i, j, 4 * ex : 4 * ex + 4, lanes]
+                at = ((4 * ex + i) * 17 + 16) * 8 + c
+                yield pl.ds(at, 1), 16, 4 * ex + i, c, tall[t // 2, c, i, 4, 4 * ex + 3 : 4 * ex + 4, lanes]
 
 
 def lookup(material, row, region):
@@ -288,23 +299,29 @@
             first[c * 5 + i], second[c * 5 + i] = sort_out(odd_y, *rows)
 
 
-def first_edge_kernel(low, high, came1, came2, rows_low, rows_high, crater1, crater2, after, first, second):
+def first_edge_kernel(low, high, came1, came2, rows_low, rows_high, crater1, crater2, after, first, second, ends, semaphores):
+    copies = fetch(
+        [(c.at[:, pl.ds(24 * h, 8), :], ends.at[n, :, pl.ds(8 * h, 8), :]) for n, c in enumerate((crater1, crater2)) for h in range(2)],
+        semaphores,
+    )
     edge_rows(low, high, came1, came2, first, second)
     odd, odd_y = parity_x(), parity_y()
     regions = sort_out(odd, came1[30], came2[30])
     for n, value in enumerate((low[15], regions[0], regions[1])):
         first[15 + n] = value
         second[15 + n] = value
+    for copy in copies:
+        copy.wait()
     for f in range(5):
         for t in range(2):
             lanes = slice(128 * t, 128 * t + 128)
             at = 18 + f * 4 + t * 2
             first[at], second[at] = sort_out(odd_y, rows_low[f * 2 + t], rows_high[f * 2 + t])
-            ends = []
-            for near in (0, 31):
-                sides = sort_out(odd, crater1[f, near : near + 1, lanes], crater2[f, near : near + 1, lanes])
-                ends.append(jnp.concatenate(list(sides) * 4, axis=0))
-            first[at + 1], second[at + 1] = sort_out(odd_y, *ends)
+            found = []
+            for row in (0, 15):
+                sides = sort_out(odd, ends[0, f, row : row + 1, lanes], ends[1, f, row : row + 1, lanes])
+                found.append(jnp.concatenate(list(sides) * 4, axis=0))
+            first[at + 1], second[at + 1] = sort_out(odd_y, *found)
 
 
 def second_edge_kernel(low, high, came1, came2, after, first, second, token):
@@ -354,31 +371,40 @@
 
 
 def first_kernel(u, v, a, region, material, b_out, f_out, x1, x2, y_low, y_high, token,
-                 elem, gx, gz, cross, planes, side, tall, nodes, later):
+                 elem, gx, gz, cross, planes, side, u_in, v_in, a_in, wide_u, wide_b, kept_u, kept_b, b_held, semaphores):
+    copies = [tile_copies(f, h, semaphores, 4 * n) for n, (f, h) in enumerate(((u, u_in), (v, v_in), (a, a_in)))]
+    for t in range(4):
+        for copy in copies:
+            copy[t].start()
     table = depth_table()
     region_now = region[...]
 
-    def column(x, carry):
-        for y in range(17):
-            for t in range(4):
-                at = node_lanes(x, y, t)
-                uu, vv, aa = u[at], v[at], a[at]
-                nodes[node_rows(x, y, t)] = uu + time_step * vv + 0.5 * time_step**2 * aa
-                later[node_rows(x, y, t)] = uu + 2.0 * time_step * vv + time_step**2 * aa
-        return carry
-
-    lax.fori_loop(0, 9, column, 0)
-    for c in range(3):
-
-        def put_u(k, value):
-            elem[c, :, :, k] = value
-
-        to_elements(nodes, c, table, tall, put_u)
-
-        def put_b(k, value):
-            b_out[c, :, :, k] = value
-
-        to_elements(later, c, table, tall, put_b)
+    def put_u(l, value):
+        elem[:, :, :, l] = value
+
+    def put_b(l, value):
+        b_held[:, :, :, l] = value
+
+    for half in range(2):
+        for t in (2 * half, 2 * half + 1):
+            for copy in copies:
+                copy[t].wait()
+        for t in (2 * half, 2 * half + 1):
+            lanes = slice(128 * (t % 2), 128 * (t % 2) + 128)
+            for c in range(3):
+                for i in range(5):
+                    for j in range(5):
+                        for ex in range(2):
+                            at = (t, rows_at(i, j, ex, c), slice(None))
+                            to = (c, i, j, slice(4 * ex, 4 * ex + 4), lanes)
+                            step = time_step * v_in[at] + (0.5 * time_step**2) * a_in[at]
+                            uu = u_in[at] + step
+                            wide_u[to] = uu
+                            wide_b[to] = uu + step
+        to_elements(half, wide_u, table, kept_u, put_u)
+        to_elements(half, wide_b, table, kept_b, put_b)
+    save_b = pltpu.make_async_copy(b_held, b_out, semaphores.at[12])
+    save_b.start()
     internal(elem, f_out, lookup(material, 1, region_now), lookup(material, 2, region_now), gx, gz, cross, planes, side)
     pack_x(f_out, x1, x2)
     pack_y(f_out, y_low, y_high)
@@ -386,6 +412,7 @@
     x2[30] = region_now
     y_low[15] = region_now
     token[...] = region_now
+    save_b.wait()
 
 
 def second_kernel(b, f, came_x1, came_x2, came_y1, came_y2, region, material, a_out, f_out, x1, x2, y_low, y_high, scales, token,
@@ -414,37 +441,43 @@
     pack_y(f_out, y_low, y_high)
 
 
-def add_surface(source, x, c, count):
-    at = 8 * (c * 9 + x)
-    tile, shift = at // 128, (128 - at % 128) % 128
-    moved = rolled(source[0:17, 128 * tile : 128 * tile + 128], shift, 1)
-    return jnp.where(lanes_of((17, 128)) < count, moved, 0.0)
-
-
-def surface_rows(x, c):
-    return 0, pl.ds(x * 136 + c, 17, stride=8), slice(None)
-
-
-def place_kernel(a1, surf1, u, v, a, after, u_out, first, tall, nodes):
-    table = depth_table(back=True)
-    for c in range(3):
-        to_nodes(lambda k: a1[c, :, :, k], c, table, tall, nodes)
-        for x in range(9):
-            nodes[surface_rows(x, c)] += add_surface(surf1, x, c, 1)
-
-    def column(x, carry):
-        for y in range(17):
-            for t in range(4):
-                at, accel = node_lanes(x, y, t), nodes[node_rows(x, y, t)]
-                first[at] = accel
-                u_out[at] = u[at] + 2.0 * time_step * v[at] + time_step**2 * (a[at] + accel)
-        return carry
-
-    lax.fori_loop(0, 9, column, 0)
-
-
-def last_kernel(first, f, x1, x2, y1, y2, scales, surf1, surf2, v, a, v_out, a_out, tall, nodes, force):
-    table = depth_table(back=True)
+def spread_surface(source, held, count):
+    lane = lanes_of((24, 128))
+    for n in range(27):
+        at = 8 * n
+        tile, shift = at // 128, (128 - at % 128) % 128
+        moved = rolled(source[:, 128 * tile : 128 * tile + 128], shift, 1)
+        held[n] = jnp.where(lane < count, moved, 0.0)
+
+
+def surface_piece(held, y, x, c):
+    return held[c * 9 + x, pl.ds(y, 4, stride=4), :] if y < 16 else held[c * 9 + x, 16:17, :]
+
+
+def place_kernel(a1, surf1, u, v, a, after, u_out, v_part, u_in, v_in, a_in, tall, surface, semaphores):
+    copies = [tile_copies(f, h, semaphores, 4 * n) for n, (f, h) in enumerate(((u, u_in), (v, v_in), (a, a_in)))]
+    for t in range(4):
+        for copy in copies:
+            copy[t].start()
+    spread_surface(surf1, surface, 1)
+    to_nodes(lambda l: a1[:, :, :, l], depth_table(back=True), tall)
+    saves = tile_copies(u_out, u_in, semaphores, 12, out=True)
+    for t in range(4):
+        for copy in copies:
+            copy[t].wait()
+        for rows, y, x, c, accel in node_pieces(tall, t):
+            at = (t, rows, slice(None))
+            if t == 0:
+                accel = accel + surface_piece(surface, y, x, c)
+            vv, aa = v_in[at], a_in[at]
+            u_in[at] = u_in[at] + 2.0 * time_step * vv + time_step**2 * (aa + accel)
+            v_part[at] = vv + (0.5 * time_step) * (aa + 2.0 * accel)
+        saves[t].start()
+    for save in saves:
+        save.wait()
+
+
+def last_kernel(v_part, f, x1, x2, y1, y2, scales, surf1, surf2, v_out, a_out, v_held, a_held, tall, surface, force, semaphores):
     force[...] = f[...]
     add_x(force, x1, x2)
     add_y(force, y1, y2)
@@ -454,20 +487,21 @@
                 scale = scales[edge_kind(i), edge_kind(j), min(k, 1)] * accel_scale(i, j, k)
                 for c in range(3):
                     force[c, i, j, k] = force[c, i, j, k] * scale
-    for c in range(3):
-        to_nodes(lambda k: force[c, :, :, k], c, table, tall, nodes)
-        for x in range(9):
-            nodes[surface_rows(x, c)] += add_surface(surf1, x, c, 1) + add_surface(surf2, x, c, 5)
-
-    def column(x, carry):
-        for y in range(17):
-            for t in range(4):
-                at, accel = node_lanes(x, y, t), nodes[node_rows(x, y, t)]
-                a_out[at] = accel
-                v_out[at] = v[at] + 0.5 * time_step * (a[at] + 2.0 * first[at] + accel)
-        return carry
-
-    lax.fori_loop(0, 9, column, 0)
+    spread_surface(surf1, surface.at[0], 1)
+    spread_surface(surf2, surface.at[1], 5)
+    to_nodes(lambda l: force[:, :, :, l], depth_table(back=True), tall)
+    saves = tile_copies(v_out, v_held, semaphores, 0, out=True) + tile_copies(a_out, a_held, semaphores, 4, out=True)
+    for t in range(4):
+        for rows, y, x, c, accel in node_pieces(tall, t):
+            at = (t, rows, slice(None))
+            if t == 0:
+                accel = accel + surface_piece(surface.at[0], y, x, c) + surface_piece(surface.at[1], y, x, c)
+            a_held[at] = accel
+            v_held[at] = v_part[at] + (0.5 * time_step) * accel
+        saves[t].start()
+        saves[4 + t].start()
+    for save in saves:
+        save.wait()
 
 
 def whole():
@@ -478,7 +512,7 @@
     return pl.BlockSpec(memory_space=pltpu.SMEM)
 
 
-def call(kernel, ins, outs, scratch, smem=(), away=(), mib=10, copies=0):
+def call(kernel, ins, outs, scratch, smem=(), away=(), out_away=(), mib=10, copies=0):
     def spec(n):
         return scalars() if n in smem else pl.BlockSpec(memory_space=pltpu.HBM) if n in away else whole()
 
@@ -487,7 +521,7 @@
         kernel,
         out_shape=[jax.ShapeDtypeStruct(s, f32) for s in outs],
         in_specs=[spec(n) for n in range(len(ins))],
-        out_specs=[whole() for _ in outs],
+        out_specs=[pl.BlockSpec(memory_space=pltpu.HBM) if n in out_away else whole() for n in range(len(outs))],
         scratch_shapes=scratch + ([pltpu.SemaphoreType.DMA((copies,))] if copies else []),
         compiler_params=pltpu.CompilerParams(vmem_limit_bytes=mib * 1024 * 1024),
     )(*ins)
@@ -966,7 +1000,7 @@
     count_x, devices = lax.axis_size("gx"), lax.axis_size(rank)
     crater = (density, momentum, energy)
     u, v, a = [jnp.transpose(x, (1, 2, 0, 3)) for x in (displacement, velocity_field, acceleration)]
-    register = (8, 128)
+    register, held_shape = (8, 128), (4, 1224, 128)
     bottoms, crater1, crater2, rows_low, rows_high, region = call(
         functools.partial(start_kernel, float(nodes_y)),
         crater + (face_dest.reshape(1, -1), face_slot, element_region_index),
@@ -974,6 +1008,7 @@
         [(5, 4, 32, 256), pltpu.VMEM((1, 128), jnp.int32), pltpu.VMEM((1, 128), jnp.int32),
          pltpu.VMEM((2, 4, 128), jnp.int32)],
         away=(0, 1, 2, 3, 4, 5),
+        mib=56,
         copies=6,
     )
     bottoms = lax.all_to_all(bottoms, rank, 0, 0, tiled=True)
@@ -982,9 +1017,14 @@
         first_kernel,
         (u, v, a, region, material),
         [element_shape, element_shape, (31, 8, 128), (31, 8, 128), (16, 8, 128), (15, 8, 128), register],
-        internal_scratch + [(5, 5, 8, 512), (4, 1224, 128), (4, 1224, 128)],
+        internal_scratch
+        + [held_shape] * 3
+        + [(3, 5, 5, 8, 256), (3, 5, 5, 8, 256), (600, 256), (600, 256), element_shape],
         smem=(4,),
-        mib=14,
+        away=(0, 1, 2),
+        out_away=(0,),
+        mib=56,
+        copies=13,
     )
     surf1, surf2 = call(
         functools.partial(surface_kernel, float(nodes_y), count_x),
@@ -993,6 +1033,7 @@
         [(360, 128), (4, 4 * count_x, 128), (6, 128, 128)],
         smem=(1,),
         away=(2,),
+        mib=56,
         copies=1,
     )
     x1, x2 = exchange("gx", x1, x2)
@@ -1000,7 +1041,10 @@
         first_edge_kernel,
         (y_low, y_high, x1, x2, rows_low, rows_high, crater1, crater2, surf1),
         [(38, 8, 128), (38, 8, 128)],
-        [],
+        [(2, 5, 16, 256)],
+        away=(6, 7),
+        mib=56,
+        copies=4,
     )
     y1, y2 = exchange(along, y1, y2)
     a1, f2, p1, p2, y_low, y_high, scales, token = call(
@@ -1022,18 +1066,25 @@
     r1, r2, token = call(
         second_edge_kernel, (y_low, y_high, p1, p2, token), [(15, 8, 128), (15, 8, 128), register], []
     )
-    u_out, first = call(
+    u_out, v_part = call(
         place_kernel,
         (a1, surf1, u, v, a, token),
-        [u.shape, u.shape],
-        [(5, 5, 8, 512), (4, 1224, 128)],
+        [u.shape, held_shape],
+        [held_shape] * 3 + [(2, 3, 5, 5, 8, 256), (27, 24, 128)],
+        away=(2, 3, 4),
+        out_away=(0,),
+        mib=20,
+        copies=16,
     )
     r1, r2 = exchange(along, r1, r2)
     v_out, a_out = call(
         last_kernel,
-        (first, f2, p1, p2, r1, r2, scales, surf1, surf2, v, a),
+        (v_part, f2, p1, p2, r1, r2, scales, surf1, surf2),
         [u.shape] * 2,
-        [(5, 5, 8, 512), (4, 1224, 128), element_shape],
+        [held_shape] * 2 + [(2, 3, 5, 5, 8, 256), (2, 27, 24, 128), element_shape],
+        out_away=(0, 1),
+        mib=16,
+        copies=8,
     )
     u_out, v_out, a_out = [jnp.transpose(x, (2, 0, 1, 3)) for x in (u_out, v_out, a_out)]
     return hydro_state, u_out, v_out, a_out

time: 83.4 us -> 80.2 us (0.962)
  local copies, waits for them, and re-layouts: 15.3 us -> 6.67 us
  Pallas kernels: 35 us -> 40.1 us
    unnamed x52 -> x42, local copies, waits for them, and re-layouts: 15.3 us -> 6.67 us
    pallas_call x9, Pallas kernels: 35 us -> 40.1 us  [call(): pl.pallas_call(kernel, out_shape=[jax.ShapeDtypeStruct(s, f32) for s in o...]
  transfers between devices with their start and end apart: 11 -> 11, of which waited for: 1 -> 1; matrix products, arithmetic and copies ran while one was open for 0% -> 0% of each run, Pallas kernels for 28% -> 34%
where the time goes in v6:
time: 80.2 us; the launch traced here: 79.6 us
  Pallas kernels  40.1 us (50%)
  starting transfers between devices  27.9 us (35%)
  local copies, waits for them, and re-layouts  6.67 us (8%)
  waiting for transfers between devices  3.74 us (5%)
  between operations  1.18 us (1%)
    pallas_call x9, Pallas kernels, call(): pl.pallas_call(kernel, out_shape=[jax.ShapeDtypeStruct(s, f32) for s in o...  40.1 us
    ppermute x5, starting transfers between devices, exchange(): lax.ppermute(second, axis, pairs + [(j, i) for i, j in pairs])  19.5 us
    unnamed x42, local copies, waits for them, and re-layouts  6.67 us
    all_to_all x1, starting transfers between devices, shards(): bottoms = lax.all_to_all(bottoms, rank, 0, 0, tiled=True)  6.45 us
    ppermute x5, waiting for transfers between devices, exchange(): lax.ppermute(second, axis, pairs + [(j, i) for i, j in pairs])  3.73 us
    ppermute x5, starting transfers between devices, exchange(): first = lax.ppermute(first, axis, [(i, i ^ 1) for i in range(count)])  1.91 us
  transfers between devices with their start and end apart: 11, of which 1 were waited for; matrix products, arithmetic and copies ran while one was open for 0% of the time, Pallas kernels for 34%

profile of v6, /device:TPU:3, one launch (start us, length us, event | category | flops | bytes accessed | tf_op | source)
XLA Modules:
  0.0 79.6 jit_solution(12855224407247468551)
XLA Ops:
  0.6 2.7 %shard_map.138 = (f32[32,24,128]{2,1,0:T(8,128)}, f32[5,64,256]{2,1,0:T(8,128)}, f32[5,64,256]{2,1,0:T(8,128)}, f32[10,8,128]{2,1,0:T(8,128)}, f32[10,8,128]{2,1,0:T(8,128)}, /*index=5*/f32[8,128]{1,0:T(8,128)}) custom-call(f32[4,32,256]{2,1,0:T(8,128)} %density.3, f32[3,4,32,256]{3,2,1,0:T(8,128)} %momentum.3, f32[4,32,256]{2,1,0:T(8,128)} %energy.3, ...), custom_call_target="tpu_custom_call" | custom-call | tf_op jit(solution)/shard_map/pallas_call | solution.py:520
  3.3 6.4 %all-to-all-start = ((f32[32,24,128]{2,1,0:T(8,128)}), f32[32,24,128]{2,1,0:T(8,128)S(1)}, u32[]{:S(2)}, u32[]{:S(2)}) async-start(f32[32,24,128]{2,1,0:T(8,128)} %get-tuple-element.47), calls=%async_computation | async-start | bytes 786432 | tf_op jit(solution)/shard_map/all_to_all | solution.py:1014
  9.8 0.1 collective-permute-start
  9.9 4.2 %collective-permute-start.1 = (f32[5,64,256]{2,1,0:T(8,128)}, f32[5,64,256]{2,1,0:T(8,128)S(1)}, u32[]{:S(2)}, u32[]{:S(2)}) collective-permute-start(f32[5,64,256]{2,1,0:T(8,128)} %get-tuple-element.39), channel_id=1, source_target_pairs={{2,4},{6,8},{10,12},{4,2},{8,6},{12,10},{3,5},{7,9},{11,13},{5,3},... | collective-permute-start | bytes 983048 | tf_op jit(solution)/shard_map/ppermute | solution.py:546
  14.1 10.9 %shard_map.139 = (f32[3,5,5,4,8,128]{5,4,3,2,1,0:T(8,128)}, f32[3,5,5,4,8,128]{5,4,3,2,1,0:T(8,128)}, f32[31,8,128]{2,1,0:T(8,128)}, f32[31,8,128]{2,1,0:T(8,128...) custom-call(f32[9,17,3,512]{3,2,1,0:T(4,128)} %bitcast.8, f32[9,17,3,512]{3,2,1,0:T(4,128)} %bitcast.10, ...), custom_call_target="tpu_custom_call" | custom-call | tf_op jit(solution)/shard_map/pallas_call | solution.py:520
  25.1 0.0 copy-start.8
  25.1 0.0 copy-start.18
  25.1 0.1 collective-permute-start.2
  25.2 4.2 %collective-permute-start.3 = (f32[31,8,128]{2,1,0:T(8,128)}, f32[31,8,128]{2,1,0:T(8,128)S(1)}, u32[]{:S(2)}, u32[]{:S(2)}) collective-permute-start(f32[31,8,128]{2,1,0:T(8,128)} %get-tuple-element.44), channel_id=1, source_target_pairs={{2,4},{6,8},{10,12},{4,2},{8,6},{12,10},{3,5},{7,9},{11,13},{5,3},... | collective-permute-start | bytes 380936 | tf_op jit(solution)/shard_map/ppermute | solution.py:546
  29.4 0.0 all-to-all-done
  29.4 0.0 copy-start.20
  29.5 0.7 copy-done.20
  30.2 5.9 %shard_map.140 = (f32[24,256]{1,0:T(8,128)}, f32[24,256]{1,0:T(8,128)}) custom-call(f32[768,128]{1,0:T(8,128)} %bitcast.14, f32[3,8]{1,0:T(4,128)} %material.5, f32[6,128,128]{2,1,0:T(8,128)} %constant.2.clone.tables, f32[8,128]{1,0:T(8,128)} %get-tuple-element.48.after), custom_call_target="tpu_custom_call" | custom-call | tf_op jit(solution)/shard_map/pallas_call | solution.py:520
  36.1 0.0 collective-permute-done.2.came1.came_x1
  36.1 0.0 collective-permute-done.3.came2.came_x2
  36.2 0.0 collective-permute-done.crater1.came1
  36.2 0.0 copy-start.4
  36.2 0.0 collective-permute-done.1.crater2.came2
  36.2 0.0 copy-start.6
  36.2 0.6 copy-done.12
  36.8 0.1 copy-done.14
  36.8 0.1 copy-done.4
  36.9 0.1 copy-done.6
  37.0 2.7 %shard_map.141 = (f32[38,8,128]{2,1,0:T(8,128)}, f32[38,8,128]{2,1,0:T(8,128)}) custom-call(f32[16,8,128]{2,1,0:T(8,128)} %get-tuple-element.41.low, f32[15,8,128]{2,1,0:T(8,128)} %get-tuple-element.42.high, f32[31,8,128]{2,1,0:T(8,128)} %copy-done.12, f32[31,8,128]{2,1,0:T(8,128)} %copy-done.14, f32[10,8,128]{2,1,0:T(8,128)} %get-tuple-element.45.rows_low, ...), custom_call_target="tpu_custom_call" | custom-call | tf_op jit(solution)/shard_map/pallas_call | solution.py:520
  39.8 1.5 %collective-permute-start.4 = (f32[38,8,128]{2,1,0:T(8,128)}, f32[38,8,128]{2,1,0:T(8,128)S(1)}, u32[]{:S(2)}, u32[]{:S(2)}) collective-permute-start(f32[38,8,128]{2,1,0:T(8,128)} %get-tuple-element.50), channel_id=1, source_target_pairs={{0,1},{1,0},{16,17},{17,16},{2,3},{3,2},{18,19},{19,18},{4,5},{5,4... | collective-permute-start | bytes 466952 | tf_op jit(solution)/shard_map/ppermute | solution.py:545
  41.3 3.0 %collective-permute-start.5 = (f32[38,8,128]{2,1,0:T(8,128)}, f32[38,8,128]{2,1,0:T(8,128)S(1)}, u32[]{:S(2)}, u32[]{:S(2)}) collective-permute-start(f32[38,8,128]{2,1,0:T(8,128)} %get-tuple-element.51), channel_id=1, source_target_pairs={{1,16},{16,1},{3,18},{18,3},{5,20},{20,5},{7,22},{22,7},{9,24},{24... | collective-permute-start | bytes 466952 | tf_op jit(solution)/shard_map/ppermute | solution.py:546
  44.3 0.0 collective-permute-done.4.came_y1.rows1
  44.4 3.7 %collective-permute-done.5.came_y2.rows2 = f32[38,8,128]{2,1,0:T(8,128)S(1)} collective-permute-done((f32[38,8,128]{2,1,0:T(8,128)}, f32[38,8,128]{2,1,0:T(8,128)S(1)}, u32[]{:S(2)}, u32[]{:S(2)}) %collective-permute-start.5) | collective-permute-done | bytes 155680 | tf_op jit(solution)/shard_map/ppermute | solution.py:546
  48.1 0.0 copy-start.9
  48.1 1.3 %copy-done.9 = f32[3,5,5,4,8,128]{5,4,3,2,1,0:T(8,128)S(1)} copy-done((f32[3,5,5,4,8,128]{5,4,3,2,1,0:T(8,128)S(1)}, f32[3,5,5,4,8,128]{5,4,3,2,1,0:T(8,128)}, u32[]{:S(2)}) %copy-start.9) | copy-done | bytes 1228824
  49.4 0.9 %copy-done.13 = f32[31,8,128]{2,1,0:T(8,128)S(1)} copy-done((f32[31,8,128]{2,1,0:T(8,128)S(1)}, f32[31,8,128]{2,1,0:T(8,128)}, u32[]{:S(2)}) %copy-start.13) | copy-done | bytes 127000
  50.3 0.9 %copy-done.15 = f32[31,8,128]{2,1,0:T(8,128)S(1)} copy-done((f32[31,8,128]{2,1,0:T(8,128)S(1)}, f32[31,8,128]{2,1,0:T(8,128)}, u32[]{:S(2)}) %copy-start.15) | copy-done | bytes 127000
  51.2 4.0 %shard_map.142 = (f32[3,5,5,4,8,128]{5,4,3,2,1,0:T(8,128)S(1)}, f32[3,5,5,4,8,128]{5,4,3,2,1,0:T(8,128)S(1)}, f32[30,8,128]{2,1,0:T(8,128)S(1)}, f32[30,8,128]{2...) custom-call(f32[3,5,5,4,8,128]{5,4,3,2,1,0:T(8,128)S(1)} %copy-done., ...), custom_call_target="tpu_custom_call" | custom-call | tf_op jit(solution)/shard_map/pallas_call | solution.py:520
  55.2 0.0 copy-start
  55.2 0.1 collective-permute-start.6
  55.3 4.3 %collective-permute-start.7 = (f32[30,8,128]{2,1,0:T(8,128)S(1)}, f32[30,8,128]{2,1,0:T(8,128)S(1)}, u32[]{:S(2)}, u32[]{:S(2)}) collective-permute-start(f32[30,8,128]{2,1,0:T(8,128)S(1)} %get-tuple-element.60), channel_id=1, source_target_pairs={{2,4},{6,8},{10,12},{4,2},{8,6},{12,10},{3,5},{7,9},{11,13},{5,3},... | collective-permute-start | bytes 368648 | tf_op jit(solution)/shard_map/ppermute | solution.py:546
  59.7 0.0 copy-start.5
  59.7 1.0 %copy-done.5 = f32[5,64,256]{2,1,0:T(8,128)S(1)} copy-done((f32[5,64,256]{2,1,0:T(8,128)S(1)}, f32[5,64,256]{2,1,0:T(8,128)}, u32[]{:S(2)}) %copy-start.5) | copy-done | bytes 327704
  60.6 1.0 %copy-done.7 = f32[5,64,256]{2,1,0:T(8,128)S(1)} copy-done((f32[5,64,256]{2,1,0:T(8,128)S(1)}, f32[5,64,256]{2,1,0:T(8,128)}, u32[]{:S(2)}) %copy-start.7) | copy-done | bytes 327704
  61.6 4.9 %shard_map.143 = (f32[5,4,32,256]{3,2,1,0:T(8,128)}, f32[8,128]{1,0:T(8,128)S(1)}) custom-call(f32[4,32,256]{2,1,0:T(8,128)S(1)} %copy-done.10, f32[3,4,32,256]{3,2,1,0:T(8,128)S(1)} %copy-done.3, f32[4,32,256]{2,1,0:T(8,128)S(1)} %copy-done.11, f32[5,64,256]{2,1,0:T(8,128)S(1)} %copy-done.5, f32[5,64,256]{2,1,0:T(8,128)S(1)} %copy-done.7, ...), custom_call_target="tpu_custom_call" | custom-call | tf_op jit(solution)/shard_map/pallas_call | solution.py:520
  66.5 0.0 collective-permute-done.6.came1.x1
  66.6 0.0 collective-permute-done.7.came2.x2
  66.6 0.1 shard_map.144
  66.6 0.1 collective-permute-start.8
  66.7 3.8 %collective-permute-start.9 = (f32[15,8,128]{2,1,0:T(8,128)S(1)}, f32[15,8,128]{2,1,0:T(8,128)S(1)}, u32[]{:S(2)}, u32[]{:S(2)}) collective-permute-start(f32[15,8,128]{2,1,0:T(8,128)S(1)} %get-tuple-element.67), channel_id=1, source_target_pairs={{1,16},{16,1},{3,18},{18,3},{5,20},{20,5},{7,22},{22,7},{9,24},{24... | collective-permute-start | bytes 184328 | tf_op jit(solution)/shard_map/ppermute | solution.py:546
  70.5 5.3 %shard_map.145 = (f32[9,17,3,512]{3,2,1,0:T(4,128)}, f32[4,1224,128]{2,1,0:T(8,128)S(1)}) custom-call(f32[3,5,5,4,8,128]{5,4,3,2,1,0:T(8,128)S(1)} %get-tuple-element.56.a1, f32[24,256]{1,0:T(8,128)S(1)} %copy-done.16, f32[9,17,3,512]{3,2,1,0:T(4,128)S(1)} %bitcast.9, f32[9,17,3,512]{3,2,1,0:T(4,128)S(1)} %bitcast.11, f32[9,17,3,512]{3,2,1,0:T(4,128)S(1)} %bitcast.13, ...), custom_call_target="tpu_custom_call" | custom-call | tf_op jit(solution)/shard_map/pallas_call | solution.py:520
  75.9 0.0 collective-permute-done.9.y2
  75.9 3.5 %shard_map.146 = (f32[9,17,3,512]{3,2,1,0:T(4,128)}, f32[9,17,3,512]{3,2,1,0:T(4,128)}) custom-call(f32[4,1224,128]{2,1,0:T(8,128)S(1)} %get-tuple-element.64.v_part, f32[3,5,5,4,8,128]{5,4,3,2,1,0:T(8,128)S(1)} %get-tuple-element.65.f, f32[30,8,128]{2,1,0:T(8,128)S(1)} %collective-permute-done.6.came1.x1, ...), custom_call_target="tpu_custom_call" | custom-call | tf_op jit(solution)/shard_map/pallas_call | solution.py:520
  (25 shorter events, 0.0 us)
Async XLA Ops:
  3.3 26.1 %all-to-all-start = ((f32[32,24,128]{2,1,0:T(8,128)}), f32[32,24,128]{2,1,0:T(8,128)S(1)}, u32[]{:S(2)}, u32[]{:S(2)}) async-start(f32[32,24,128]{2,1,0:T(8,128)} %get-tuple-element.47), calls=%async_computation | async-start | bytes 786432 | tf_op jit(solution)/shard_map/all_to_all | solution.py:1014
  9.8 26.4 %collective-permute-start = (f32[5,64,256]{2,1,0:T(8,128)}, f32[5,64,256]{2,1,0:T(8,128)S(1)}, u32[]{:S(2)}, u32[]{:S(2)}) collective-permute-start(f32[5,64,256]{2,1,0:T(8,128)} %get-tuple-element.38), channel_id=1, source_target_pairs={{0,2},{2,0},{4,6},{6,4},{8,10},{10,8},{12,14},{14,12},{1,3},{3,1},... | collective-permute-start | bytes 983048 | tf_op jit(solution)/shard_map/ppermute | solution.py:545
  9.9 26.2 %collective-permute-start.1 = (f32[5,64,256]{2,1,0:T(8,128)}, f32[5,64,256]{2,1,0:T(8,128)S(1)}, u32[]{:S(2)}, u32[]{:S(2)}) collective-permute-start(f32[5,64,256]{2,1,0:T(8,128)} %get-tuple-element.39), channel_id=1, source_target_pairs={{2,4},{6,8},{10,12},{4,2},{8,6},{12,10},{3,5},{7,9},{11,13},{5,3},... | collective-permute-start | bytes 983048 | tf_op jit(solution)/shard_map/ppermute | solution.py:546
  25.1 23.0 %copy-start.8 = (f32[3,5,5,4,8,128]{5,4,3,2,1,0:T(8,128)S(1)}, f32[3,5,5,4,8,128]{5,4,3,2,1,0:T(8,128)}, u32[]{:S(2)}) copy-start(f32[3,5,5,4,8,128]{5,4,3,2,1,0:T(8,128)} %get-tuple-element.52.b) | copy-start | bytes 3686404
  25.1 23.0 %copy-start.18 = (f32[3,8]{1,0:T(4,128)S(1)}, f32[3,8]{1,0:T(4,128)}, u32[]{:S(2)}) copy-start(f32[3,8]{1,0:T(4,128)} %material.5) | copy-start | bytes 292
  25.1 23.0 %copy-start.19 = (f32[8,128]{1,0:T(8,128)S(1)}, f32[8,128]{1,0:T(8,128)}, u32[]{:S(2)}) copy-start(f32[8,128]{1,0:T(8,128)} %get-tuple-element.40.region) | copy-start | bytes 12292
  25.1 11.0 %collective-permute-start.2 = (f32[31,8,128]{2,1,0:T(8,128)}, f32[31,8,128]{2,1,0:T(8,128)S(1)}, u32[]{:S(2)}, u32[]{:S(2)}) collective-permute-start(f32[31,8,128]{2,1,0:T(8,128)} %get-tuple-element.43), channel_id=1, source_target_pairs={{0,2},{2,0},{4,6},{6,4},{8,10},{10,8},{12,14},{14,12},{1,3},{3,1},... | collective-permute-start | bytes 380936 | tf_op jit(solution)/shard_map/ppermute | solution.py:545
  25.2 11.0 %collective-permute-start.3 = (f32[31,8,128]{2,1,0:T(8,128)}, f32[31,8,128]{2,1,0:T(8,128)S(1)}, u32[]{:S(2)}, u32[]{:S(2)}) collective-permute-start(f32[31,8,128]{2,1,0:T(8,128)} %get-tuple-element.44), channel_id=1, source_target_pairs={{2,4},{6,8},{10,12},{4,2},{8,6},{12,10},{3,5},{7,9},{11,13},{5,3},... | collective-permute-start | bytes 380936 | tf_op jit(solution)/shard_map/ppermute | solution.py:546
  29.4 0.7 copy-start.20
  36.1 0.7 copy-start.12
  36.1 0.7 copy-start.14
  36.2 0.8 copy-start.4
  36.2 0.9 %copy-start.6 = (f32[5,64,256]{2,1,0:T(8,128)}, f32[5,64,256]{2,1,0:T(8,128)S(1)}, u32[]{:S(2)}) copy-start(f32[5,64,256]{2,1,0:T(8,128)S(1)} %collective-permute-done.1.crater2.came2) | copy-start | bytes 983044
  37.0 22.6 %copy-start.10 = (f32[4,32,256]{2,1,0:T(8,128)S(1)}, f32[4,32,256]{2,1,0:T(8,128)}, u32[]{:S(2)}) copy-start(f32[4,32,256]{2,1,0:T(8,128)} %density.3) | copy-start | bytes 393220
  37.0 22.6 %copy-start.11 = (f32[4,32,256]{2,1,0:T(8,128)S(1)}, f32[4,32,256]{2,1,0:T(8,128)}, u32[]{:S(2)}) copy-start(f32[4,32,256]{2,1,0:T(8,128)} %energy.3) | copy-start | bytes 393220
  39.8 4.6 %collective-permute-start.4 = (f32[38,8,128]{2,1,0:T(8,128)}, f32[38,8,128]{2,1,0:T(8,128)S(1)}, u32[]{:S(2)}, u32[]{:S(2)}) collective-permute-start(f32[38,8,128]{2,1,0:T(8,128)} %get-tuple-element.50), channel_id=1, source_target_pairs={{0,1},{1,0},{16,17},{17,16},{2,3},{3,2},{18,19},{19,18},{4,5},{5,4... | collective-permute-start | bytes 466952 | tf_op jit(solution)/shard_map/ppermute | solution.py:545
  41.3 6.7 %collective-permute-start.5 = (f32[38,8,128]{2,1,0:T(8,128)}, f32[38,8,128]{2,1,0:T(8,128)S(1)}, u32[]{:S(2)}, u32[]{:S(2)}) collective-permute-start(f32[38,8,128]{2,1,0:T(8,128)} %get-tuple-element.51), channel_id=1, source_target_pairs={{1,16},{16,1},{3,18},{18,3},{5,20},{20,5},{7,22},{22,7},{9,24},{24... | collective-permute-start | bytes 466952 | tf_op jit(solution)/shard_map/ppermute | solution.py:546
  48.1 1.3 %copy-start.9 = (f32[3,5,5,4,8,128]{5,4,3,2,1,0:T(8,128)S(1)}, f32[3,5,5,4,8,128]{5,4,3,2,1,0:T(8,128)}, u32[]{:S(2)}) copy-start(f32[3,5,5,4,8,128]{5,4,3,2,1,0:T(8,128)} %get-tuple-element.53.f) | copy-start | bytes 3686404
  49.4 0.9 %copy-start.13 = (f32[31,8,128]{2,1,0:T(8,128)S(1)}, f32[31,8,128]{2,1,0:T(8,128)}, u32[]{:S(2)}) copy-start(f32[31,8,128]{2,1,0:T(8,128)} %copy-done.12) | copy-start | bytes 380932
  50.3 0.9 %copy-start.15 = (f32[31,8,128]{2,1,0:T(8,128)S(1)}, f32[31,8,128]{2,1,0:T(8,128)}, u32[]{:S(2)}) copy-start(f32[31,8,128]{2,1,0:T(8,128)} %copy-done.14) | copy-start | bytes 380932
  51.2 8.5 %copy-start.3 = (f32[3,4,32,256]{3,2,1,0:T(8,128)S(1)}, f32[3,4,32,256]{3,2,1,0:T(8,128)}, u32[]{:S(2)}) copy-start(f32[3,4,32,256]{3,2,1,0:T(8,128)} %momentum.3) | copy-start | bytes 1179652
  51.2 19.3 %copy-start.1 = (f32[3,9,17,512]{3,0,2,1:T(4,128)S(1)}, f32[3,9,17,512]{3,0,2,1:T(4,128)}, u32[]{:S(2)}) copy-start(f32[3,9,17,512]{3,0,2,1:T(4,128)} %param.15) | copy-start | bytes 2820100
  51.2 19.3 %copy-start.2 = (f32[3,9,17,512]{3,0,2,1:T(4,128)S(1)}, f32[3,9,17,512]{3,0,2,1:T(4,128)}, u32[]{:S(2)}) copy-start(f32[3,9,17,512]{3,0,2,1:T(4,128)} %param.16) | copy-start | bytes 2820100
  51.2 19.3 %copy-start.16 = (f32[24,256]{1,0:T(8,128)S(1)}, f32[24,256]{1,0:T(8,128)}, u32[]{:S(2)}) copy-start(f32[24,256]{1,0:T(8,128)} %get-tuple-element.49.after.surf1) | copy-start | bytes 73732
  55.2 15.3 %copy-start = (f32[3,9,17,512]{3,0,2,1:T(4,128)S(1)}, f32[3,9,17,512]{3,0,2,1:T(4,128)}, u32[]{:S(2)}) copy-start(f32[3,9,17,512]{3,0,2,1:T(4,128)} %param.14) | copy-start | bytes 2820100
  55.2 11.3 %collective-permute-start.6 = (f32[30,8,128]{2,1,0:T(8,128)S(1)}, f32[30,8,128]{2,1,0:T(8,128)S(1)}, u32[]{:S(2)}, u32[]{:S(2)}) collective-permute-start(f32[30,8,128]{2,1,0:T(8,128)S(1)} %get-tuple-element.59), channel_id=1, source_target_pairs={{0,2},{2,0},{4,6},{6,4},{8,10},{10,8},{12,14},{14,12},{1,3},{3,1},... | collective-permute-start | bytes 368648 | tf_op jit(solution)/shard_map/ppermute | solution.py:545
  55.3 11.2 %collective-permute-start.7 = (f32[30,8,128]{2,1,0:T(8,128)S(1)}, f32[30,8,128]{2,1,0:T(8,128)S(1)}, u32[]{:S(2)}, u32[]{:S(2)}) collective-permute-start(f32[30,8,128]{2,1,0:T(8,128)S(1)} %get-tuple-element.60), channel_id=1, source_target_pairs={{2,4},{6,8},{10,12},{4,2},{8,6},{12,10},{3,5},{7,9},{11,13},{5,3},... | collective-permute-start | bytes 368648 | tf_op jit(solution)/shard_map/ppermute | solution.py:546
  59.7 1.0 %copy-start.5 = (f32[5,64,256]{2,1,0:T(8,128)S(1)}, f32[5,64,256]{2,1,0:T(8,128)}, u32[]{:S(2)}) copy-start(f32[5,64,256]{2,1,0:T(8,128)} %copy-done.4) | copy-start | bytes 983044
  60.6 1.0 %copy-start.7 = (f32[5,64,256]{2,1,0:T(8,128)S(1)}, f32[5,64,256]{2,1,0:T(8,128)}, u32[]{:S(2)}) copy-start(f32[5,64,256]{2,1,0:T(8,128)} %copy-done.6) | copy-start | bytes 983044
  66.6 9.3 %collective-permute-start.8 = (f32[15,8,128]{2,1,0:T(8,128)S(1)}, f32[15,8,128]{2,1,0:T(8,128)S(1)}, u32[]{:S(2)}, u32[]{:S(2)}) collective-permute-start(f32[15,8,128]{2,1,0:T(8,128)S(1)} %get-tuple-element.66), channel_id=1, source_target_pairs={{0,1},{1,0},{16,17},{17,16},{2,3},{3,2},{18,19},{19,18},{4,5},{5,4... | collective-permute-start | bytes 184328 | tf_op jit(solution)/shard_map/ppermute | solution.py:545
  66.7 9.2 %collective-permute-start.9 = (f32[15,8,128]{2,1,0:T(8,128)S(1)}, f32[15,8,128]{2,1,0:T(8,128)S(1)}, u32[]{:S(2)}, u32[]{:S(2)}) collective-permute-start(f32[15,8,128]{2,1,0:T(8,128)S(1)} %get-tuple-element.67), channel_id=1, source_target_pairs={{1,16},{16,1},{3,18},{18,3},{5,20},{20,5},{7,22},{22,7},{9,24},{24... | collective-permute-start | bytes 184328 | tf_op jit(solution)/shard_map/ppermute | solution.py:546
  70.5 5.4 %copy-start.17 = (f32[24,256]{1,0:T(8,128)S(1)}, f32[24,256]{1,0:T(8,128)}, u32[]{:S(2)}) copy-start(f32[24,256]{1,0:T(8,128)} %get-tuple-element.69.surf2) | copy-start | bytes 73732

commit v7 on v6

--- a/solution.py
+++ b/solution.py
@@ -84,8 +84,42 @@
     return jnp.where(front, x, pltpu.roll(y, 64, 1)), jnp.where(front, pltpu.roll(x, 64, 1), y)
 
 
-def rows_at(i, j, ex, c, count=4):
-    return pl.ds(((4 * ex + i) * 17 + j) * 8 + c, count, stride=32)
+def node_at(i, j, r):
+    start = ((4 * (r // 4) + i) * 17 + 4 * (r % 4) + j) * 8
+    return pl.ds(start if isinstance(i, int) else pl.multiple_of(start, 8), 8)
+
+
+def gather_rows(nodes):
+    sub = rows_of()
+    turned = [rolled(v, r) for r, v in enumerate(nodes)]
+    out = []
+    for c in range(3):
+        total = turned[0]
+        for r in range(1, 8):
+            total = jnp.where(sub == (r + c) % 8, turned[r], total)
+        out.append(rolled(total, -c))
+    return out
+
+
+def scatter_rows(parts, wanted):
+    sub = rows_of()
+    turned = [rolled(v, c) for c, v in enumerate(parts)]
+    out = []
+    for r in wanted:
+        total = jnp.where(sub == r, turned[0], jnp.where(sub == (r + 1) % 8, turned[1], turned[2]))
+        out.append((r, rolled(total, -r)))
+    return out
+
+
+def every_node(body):
+    def column(i, carry):
+        for j in range(5):
+            body(i, j, range(8) if j < 4 else (3, 7))
+        return carry
+
+    lax.fori_loop(0, 4, column, 0)
+    for j in range(5):
+        body(4, j, range(4, 8) if j < 4 else (7,))
 
 
 def tile_copies(field, held, semaphores, first, out=False):
@@ -114,19 +148,6 @@
     for half in range(2):
         wide = jnp.concatenate([pairs[0][half], pairs[1][half]], axis=1)
         tall[half] = moved_lanes(wide, table).reshape(3, 5, 5, 8, 256)
-
-
-def node_pieces(tall, t):
-    lanes = slice(128 * (t % 2), 128 * (t % 2) + 128)
-    for c in range(3):
-        for i in range(5):
-            for ex in range(2):
-                if i == 4 and ex == 0:
-                    continue
-                for j in range(4):
-                    yield rows_at(i, j, ex, c), j, 4 * ex + i, c, tall[t // 2, c, i, j, 4 * ex : 4 * ex + 4, lanes]
-                at = ((4 * ex + i) * 17 + 16) * 8 + c
-                yield pl.ds(at, 1), 16, 4 * ex + i, c, tall[t // 2, c, i, 4, 4 * ex + 3 : 4 * ex + 4, lanes]
 
 
 def lookup(material, row, region):
@@ -299,7 +320,8 @@
             first[c * 5 + i], second[c * 5 + i] = sort_out(odd_y, *rows)
 
 
-def first_edge_kernel(low, high, came1, came2, rows_low, rows_high, crater1, crater2, after, first, second, ends, semaphores):
+def first_edge_kernel(low, high, came1, came2, rows_low, rows_high, crater1, crater2, after, first, second, token, ends, semaphores):
+    token[...] = after[0:8]
     copies = fetch(
         [(c.at[:, pl.ds(24 * h, 8), :], ends.at[n, :, pl.ds(8 * h, 8), :]) for n, c in enumerate((crater1, crater2)) for h in range(2)],
         semaphores,
@@ -389,18 +411,24 @@
         for t in (2 * half, 2 * half + 1):
             for copy in copies:
                 copy[t].wait()
-        for t in (2 * half, 2 * half + 1):
-            lanes = slice(128 * (t % 2), 128 * (t % 2) + 128)
-            for c in range(3):
-                for i in range(5):
-                    for j in range(5):
-                        for ex in range(2):
-                            at = (t, rows_at(i, j, ex, c), slice(None))
-                            to = (c, i, j, slice(4 * ex, 4 * ex + 4), lanes)
-                            step = time_step * v_in[at] + (0.5 * time_step**2) * a_in[at]
-                            uu = u_in[at] + step
-                            wide_u[to] = uu
-                            wide_b[to] = uu + step
+
+        def column(i, carry):
+            for t in (2 * half, 2 * half + 1):
+                lanes = slice(128 * (t % 2), 128 * (t % 2) + 128)
+                for j in range(5):
+                    now, later = [], []
+                    for r in range(8):
+                        at = (t, node_at(i, j, r), slice(None))
+                        step = time_step * v_in[at] + (0.5 * time_step**2) * a_in[at]
+                        now.append(u_in[at] + step)
+                        later.append(now[-1] + step)
+                    for c, value in enumerate(gather_rows(now)):
+                        wide_u[c, i, j, :, lanes] = value
+                    for c, value in enumerate(gather_rows(later)):
+                        wide_b[c, i, j, :, lanes] = value
+            return carry
+
+        lax.fori_loop(0, 5, column, 0)
         to_elements(half, wide_u, table, kept_u, put_u)
         to_elements(half, wide_b, table, kept_b, put_b)
     save_b = pltpu.make_async_copy(b_held, b_out, semaphores.at[12])
@@ -415,10 +443,10 @@
     save_b.wait()
 
 
-def second_kernel(b, f, came_x1, came_x2, came_y1, came_y2, region, material, a_out, f_out, x1, x2, y_low, y_high, scales, token,
+def second_kernel(b, f, came_x1, came_x2, came_y1, came_y2, region, material, after, a_out, f_out, x1, x2, y_low, y_high, scales, token,
                   elem, gx, gz, cross, planes, side):
     region_now = region[...]
-    token[...] = region_now
+    token[...] = after[...]
     a_out[...] = f[...]
     add_x(a_out, came_x1, came_x2)
     add_y(a_out, came_y1, came_y2)
@@ -450,28 +478,37 @@
         held[n] = jnp.where(lane < count, moved, 0.0)
 
 
-def surface_piece(held, y, x, c):
-    return held[c * 9 + x, pl.ds(y, 4, stride=4), :] if y < 16 else held[c * 9 + x, 16:17, :]
-
-
-def place_kernel(a1, surf1, u, v, a, after, u_out, v_part, u_in, v_in, a_in, tall, surface, semaphores):
+def add_surface(held, tall):
+    for c in range(3):
+        for i in range(5):
+            for j in range(5):
+                for ex in range(2):
+                    value = held[c * 9 + 4 * ex + i, pl.ds(j, 4, stride=4), :]
+                    tall[0, c, i, j, 4 * ex : 4 * ex + 4, 0:128] += value
+
+
+def place_kernel(a1, surf1, u, v, a, after, u_out, v_part, u_in, v_in, a_in, tall, surface, u_held, semaphores):
     copies = [tile_copies(f, h, semaphores, 4 * n) for n, (f, h) in enumerate(((u, u_in), (v, v_in), (a, a_in)))]
     for t in range(4):
         for copy in copies:
             copy[t].start()
     spread_surface(surf1, surface, 1)
     to_nodes(lambda l: a1[:, :, :, l], depth_table(back=True), tall)
-    saves = tile_copies(u_out, u_in, semaphores, 12, out=True)
+    add_surface(surface, tall)
+    saves = tile_copies(u_out, u_held, semaphores, 12, out=True)
     for t in range(4):
         for copy in copies:
             copy[t].wait()
-        for rows, y, x, c, accel in node_pieces(tall, t):
-            at = (t, rows, slice(None))
-            if t == 0:
-                accel = accel + surface_piece(surface, y, x, c)
-            vv, aa = v_in[at], a_in[at]
-            u_in[at] = u_in[at] + 2.0 * time_step * vv + time_step**2 * (aa + accel)
-            v_part[at] = vv + (0.5 * time_step) * (aa + 2.0 * accel)
+        lanes = slice(128 * (t % 2), 128 * (t % 2) + 128)
+
+        def body(i, j, wanted):
+            for r, accel in scatter_rows([tall[t // 2, c, i, j, :, lanes] for c in range(3)], wanted):
+                at = (t, node_at(i, j, r), slice(None))
+                vv, aa = v_in[at], a_in[at]
+                u_held[at] = u_in[at] + 2.0 * time_step * vv + time_step**2 * (aa + accel)
+                v_part[at] = vv + (0.5 * time_step) * (aa + 2.0 * accel)
+
+        every_node(body)
         saves[t].start()
     for save in saves:
         save.wait()
@@ -489,15 +526,20 @@
                     force[c, i, j, k] = force[c, i, j, k] * scale
     spread_surface(surf1, surface.at[0], 1)
     spread_surface(surf2, surface.at[1], 5)
+    surface[0] = surface[0] + surface[1]
     to_nodes(lambda l: force[:, :, :, l], depth_table(back=True), tall)
+    add_surface(surface.at[0], tall)
     saves = tile_copies(v_out, v_held, semaphores, 0, out=True) + tile_copies(a_out, a_held, semaphores, 4, out=True)
     for t in range(4):
-        for rows, y, x, c, accel in node_pieces(tall, t):
-            at = (t, rows, slice(None))
-            if t == 0:
-                accel = accel + surface_piece(surface.at[0], y, x, c) + surface_piece(surface.at[1], y, x, c)
-            a_held[at] = accel
-            v_held[at] = v_part[at] + (0.5 * time_step) * accel
+        lanes = slice(128 * (t % 2), 128 * (t % 2) + 128)
+
+        def body(i, j, wanted):
+            for r, accel in scatter_rows([tall[t // 2, c, i, j, :, lanes] for c in range(3)], wanted):
+                at = (t, node_at(i, j, r), slice(None))
+                a_held[at] = accel
+                v_held[at] = v_part[at] + (0.5 * time_step) * accel
+
+        every_node(body)
         saves[t].start()
         saves[4 + t].start()
     for save in saves:
@@ -612,22 +654,6 @@
                 here = (sub == 2 * x + ex) & (lane >= 4 * y - 2) & (lane < 4 * y + 2) & (lane < 8)
                 out = jnp.where(here, rolled(row, 4 * y - 2 - 8 * z - 4 * ex, 1), out)
     return out
-
-
-def region_rows(bottoms, count_x):
-    gx, place, count_gy = position("gx"), along_y(), lax.axis_size("gy")
-    last_y = lax.axis_size("grp") * count_gy - 1
-    found = []
-    for x in range(3):
-        found.append([])
-        for y in range(3):
-            px, py = gx + x - 1, place + y - 1
-            inside = (px >= 0) & (px < count_x) & (py >= 0) & (py <= last_y)
-            cx, cy = jnp.clip(px, 0, count_x - 1), jnp.clip(py, 0, last_y)
-            rank = (cy // count_gy) * (count_x * count_gy) + cx * count_gy + cy % count_gy
-            row = bottoms[pl.ds(pl.multiple_of(rank * 24 + 16, 8), 1), :]
-            found[x].append(jnp.where(inside, row, 0.0))
-    return found
 
 
 def respond(total, grid, material, tables, out1, out2):
@@ -983,14 +1009,34 @@
         faces[3, at, :] = ids[x]
 
 
-def surface_kernel(nodes_y, count_x, bottoms, material, tables, after, out1, out2, total, faces, held, semaphores):
-    copies = fetch([(tables, held)], semaphores)
+def deposit_kernel(nodes_y, count_x, bottoms, after, total, faces):
     base_x = (8 * position("gx") - 4).astype(f32)
     base_y = (16 * along_y() - 4).astype(f32)
     bottom_tractions(bottoms, count_x, faces)
     deposit(faces, nodes_y, base_x, base_y, total)
-    copies[0].wait()
-    respond(total, region_rows(bottoms, count_x), material, held, out1, out2)
+
+
+def respond_kernel(count_x, total, bottoms, material, tables, after, out1, out2, token, held, rows, semaphores):
+    gx, place, count_gy = position("gx"), along_y(), lax.axis_size("gy")
+    last_y = lax.axis_size("grp") * count_gy - 1
+    pairs = [(tables, held)]
+    for x in range(3):
+        for y in range(3):
+            cx, cy = jnp.clip(gx + x - 1, 0, count_x - 1), jnp.clip(place + y - 1, 0, last_y)
+            rank = (cy // count_gy) * (count_x * count_gy) + cx * count_gy + cy % count_gy
+            pairs.append((bottoms.at[rank, pl.ds(16, 8), :], rows.at[3 * x + y]))
+    copies = fetch(pairs, semaphores)
+    for copy in copies:
+        copy.wait()
+    found = []
+    for x in range(3):
+        found.append([])
+        for y in range(3):
+            px, py = gx + x - 1, place + y - 1
+            inside = (px >= 0) & (px < count_x) & (py >= 0) & (py <= last_y)
+            found[x].append(jnp.where(inside, rows[3 * x + y, 0:1, :], 0.0))
+    respond(total, found, material, held, out1, out2)
+    token[...] = after[...]
 
 
 def shards(density, momentum, energy, displacement, velocity_field, acceleration, material, element_region_index,
@@ -1026,30 +1072,34 @@
         mib=56,
         copies=13,
     )
-    surf1, surf2 = call(
-        functools.partial(surface_kernel, float(nodes_y), count_x),
-        (bottoms.reshape(devices * 24, 128), material, jnp.asarray(surface_tables()), token),
-        [(24, 256), (24, 256)],
-        [(360, 128), (4, 4 * count_x, 128), (6, 128, 128)],
-        smem=(1,),
-        away=(2,),
-        mib=56,
-        copies=1,
+    (total,) = call(
+        functools.partial(deposit_kernel, float(nodes_y), count_x),
+        (bottoms.reshape(devices * 24, 128), token),
+        [(360, 128)],
+        [(4, 4 * count_x, 128)],
     )
     x1, x2 = exchange("gx", x1, x2)
-    y1, y2 = call(
+    y1, y2, token = call(
         first_edge_kernel,
-        (y_low, y_high, x1, x2, rows_low, rows_high, crater1, crater2, surf1),
-        [(38, 8, 128), (38, 8, 128)],
+        (y_low, y_high, x1, x2, rows_low, rows_high, crater1, crater2, total),
+        [(38, 8, 128), (38, 8, 128), register],
         [(2, 5, 16, 256)],
         away=(6, 7),
-        mib=56,
         copies=4,
+    )
+    surf1, surf2, token = call(
+        functools.partial(respond_kernel, count_x),
+        (total, bottoms, material, jnp.asarray(surface_tables()), token),
+        [(24, 256), (24, 256), register],
+        [(6, 128, 128), (9, 8, 128)],
+        smem=(2,),
+        away=(1, 3),
+        copies=10,
     )
     y1, y2 = exchange(along, y1, y2)
     a1, f2, p1, p2, y_low, y_high, scales, token = call(
         second_kernel,
-        (b, f, x1, x2, y1, y2, region, material),
+        (b, f, x1, x2, y1, y2, region, material, token),
         [element_shape, element_shape, (30, 8, 128), (30, 8, 128), (15, 8, 128), (15, 8, 128), (3, 3, 2, 8, 128), register],
         internal_scratch,
         smem=(7,),
@@ -1070,7 +1120,7 @@
         place_kernel,
         (a1, surf1, u, v, a, token),
         [u.shape, held_shape],
-        [held_shape] * 3 + [(2, 3, 5, 5, 8, 256), (27, 24, 128)],
+        [held_shape] * 3 + [(2, 3, 5, 5, 8, 256), (27, 24, 128), held_shape],
         away=(2, 3, 4),
         out_away=(0,),
         mib=20,

time: 80.2 us -> 67.7 us (0.84)
  Pallas kernels: 40.1 us -> 32.9 us
  local copies, waits for them, and re-layouts: 6.67 us -> 2.4 us
  starting transfers between devices: 27.9 us -> 27 us
    pallas_call x9 -> x10, Pallas kernels: 40.1 us -> 32.9 us  [call(): pl.pallas_call(kernel, out_shape=[jax.ShapeDtypeStruct(s, f32) for s in o...]
    unnamed x42 -> x32, local copies, waits for them, and re-layouts: 6.67 us -> 2.4 us
    ppermute x5, waiting for transfers between devices: 0.01 us -> 2.8 us  [exchange(): first = lax.ppermute(first, axis, [(i, i ^ 1) for i in range(count)])]
    ppermute x5, waiting for transfers between devices: 3.73 us -> 1.04 us  [exchange(): lax.ppermute(second, axis, pairs + [(j, i) for i, j in pairs])]
  transfers between devices with their start and end apart: 11 -> 11, of which waited for: 1 -> 2; matrix products, arithmetic and copies ran while one was open for 0% -> 0% of each run, Pallas kernels for 34% -> 35%
where the time goes in v7:
time: 67.7 us; the launch traced here: 67.2 us
  Pallas kernels  32.9 us (49%)
  starting transfers between devices  27 us (40%)
  waiting for transfers between devices  3.84 us (6%)
  local copies, waits for them, and re-layouts  2.4 us (4%)
  between operations  1.02 us (2%)
    pallas_call x10, Pallas kernels, call(): pl.pallas_call(kernel, out_shape=[jax.ShapeDtypeStruct(s, f32) for s in o...  32.9 us
    ppermute x5, starting transfers between devices, exchange(): lax.ppermute(second, axis, pairs + [(j, i) for i, j in pairs])  19.3 us
    all_to_all x1, starting transfers between devices, shards(): bottoms = lax.all_to_all(bottoms, rank, 0, 0, tiled=True)  6.45 us
    ppermute x5, waiting for transfers between devices, exchange(): first = lax.ppermute(first, axis, [(i, i ^ 1) for i in range(count)])  2.8 us
    unnamed x32, local copies, waits for them, and re-layouts  2.4 us
  transfers between devices with their start and end apart: 11, of which 2 were waited for; matrix products, arithmetic and copies ran while one was open for 0% of the time, Pallas kernels for 35%

profile of v7, /device:TPU:3, one launch (start us, length us, event | category | flops | bytes accessed | tf_op | source)
XLA Modules:
  0.0 67.2 jit_solution(7286510120838278978)
XLA Ops:
  0.6 2.7 %shard_map.138 = (f32[32,24,128]{2,1,0:T(8,128)}, f32[5,64,256]{2,1,0:T(8,128)}, f32[5,64,256]{2,1,0:T(8,128)}, f32[10,8,128]{2,1,0:T(8,128)}, f32[10,8,128]{2,1,0:T(8,128)}, /*index=5*/f32[8,128]{1,0:T(8,128)}) custom-call(f32[4,32,256]{2,1,0:T(8,128)} %density.3, f32[3,4,32,256]{3,2,1,0:T(8,128)} %momentum.3, f32[4,32,256]{2,1,0:T(8,128)} %energy.3, ...), custom_call_target="tpu_custom_call" | custom-call | tf_op jit(solution)/shard_map/pallas_call | solution.py:562
  3.3 6.4 %all-to-all-start = ((f32[32,24,128]{2,1,0:T(8,128)}), f32[32,24,128]{2,1,0:T(8,128)S(1)}, u32[]{:S(2)}, u32[]{:S(2)}) async-start(f32[32,24,128]{2,1,0:T(8,128)} %get-tuple-element.49), calls=%async_computation | async-start | bytes 786432 | tf_op jit(solution)/shard_map/all_to_all | solution.py:1060
  9.8 0.1 collective-permute-start
  9.9 4.2 %collective-permute-start.1 = (f32[5,64,256]{2,1,0:T(8,128)}, f32[5,64,256]{2,1,0:T(8,128)S(1)}, u32[]{:S(2)}, u32[]{:S(2)}) collective-permute-start(f32[5,64,256]{2,1,0:T(8,128)} %get-tuple-element.41), channel_id=1, source_target_pairs={{2,4},{6,8},{10,12},{4,2},{8,6},{12,10},{3,5},{7,9},{11,13},{5,3},... | collective-permute-start | bytes 983048 | tf_op jit(solution)/shard_map/ppermute | solution.py:588
  14.2 0.0 copy-start.8
  14.2 9.8 %shard_map.139 = (f32[3,5,5,4,8,128]{5,4,3,2,1,0:T(8,128)}, f32[3,5,5,4,8,128]{5,4,3,2,1,0:T(8,128)}, f32[31,8,128]{2,1,0:T(8,128)}, f32[31,8,128]{2,1,0:T(8,128...) custom-call(f32[9,17,3,512]{3,2,1,0:T(4,128)} %bitcast.8, f32[9,17,3,512]{3,2,1,0:T(4,128)} %bitcast.10, ...), custom_call_target="tpu_custom_call" | custom-call | tf_op jit(solution)/shard_map/pallas_call | solution.py:562
  24.0 0.0 copy-start.13
  24.0 0.1 collective-permute-start.2
  24.1 0.0 copy-start.14
  24.1 4.4 %collective-permute-start.3 = (f32[31,8,128]{2,1,0:T(8,128)}, f32[31,8,128]{2,1,0:T(8,128)S(1)}, u32[]{:S(2)}, u32[]{:S(2)}) collective-permute-start(f32[31,8,128]{2,1,0:T(8,128)} %get-tuple-element.46), channel_id=1, source_target_pairs={{2,4},{6,8},{10,12},{4,2},{8,6},{12,10},{3,5},{7,9},{11,13},{5,3},... | collective-permute-start | bytes 380936 | tf_op jit(solution)/shard_map/ppermute | solution.py:588
  28.5 0.0 all-to-all-done.bottoms
  28.5 0.7 copy-done.15
  29.2 2.8 %shard_map.140.after.total = f32[360,128]{1,0:T(8,128)S(1)} custom-call(f32[768,128]{1,0:T(8,128)S(1)} %bitcast.14, f32[8,128]{1,0:T(8,128)S(1)} %copy-done.15), custom_call_target="tpu_custom_call" | custom-call | tf_op jit(solution)/shard_map/pallas_call | solution.py:562
  32.0 0.0 copy-start.4
  32.0 2.8 %collective-permute-done.2.came1.came_x1 = f32[31,8,128]{2,1,0:T(8,128)S(1)} collective-permute-done((f32[31,8,128]{2,1,0:T(8,128)}, f32[31,8,128]{2,1,0:T(8,128)S(1)}, u32[]{:S(2)}, u32[]{:S(2)}) %collective-permute-start.2) | collective-permute-done | bytes 127008 | tf_op jit(solution)/shard_map/ppermute | solution.py:587
  34.8 0.0 collective-permute-done.3.came2.came_x2
  34.8 0.0 collective-permute-done.crater1.came1
  34.8 0.0 collective-permute-done.1.crater2.came2
  34.8 0.0 copy-done.11
  34.8 0.0 copy-done.12
  34.8 0.0 copy-start.9
  34.8 0.8 %copy-done.9 = f32[16,8,128]{2,1,0:T(8,128)S(1)} copy-done((f32[16,8,128]{2,1,0:T(8,128)S(1)}, f32[16,8,128]{2,1,0:T(8,128)}, u32[]{:S(2)}) %copy-start.9) | copy-done | bytes 65560
  35.6 0.8 %copy-done.10 = f32[15,8,128]{2,1,0:T(8,128)S(1)} copy-done((f32[15,8,128]{2,1,0:T(8,128)S(1)}, f32[15,8,128]{2,1,0:T(8,128)}, u32[]{:S(2)}) %copy-start.10) | copy-done | bytes 61464
  36.5 0.2 shard_map.141
  36.6 0.9 %collective-permute-start.4 = (f32[38,8,128]{2,1,0:T(8,128)S(1)}, f32[38,8,128]{2,1,0:T(8,128)S(1)}, u32[]{:S(2)}, u32[]{:S(2)}) collective-permute-start(f32[38,8,128]{2,1,0:T(8,128)S(1)} %get-tuple-element.51), channel_id=1, source_target_pairs={{0,1},{1,0},{16,17},{17,16},{2,3},{3,2},{18,19},{19,18},{4,5},{5,4... | collective-permute-start | bytes 466952 | tf_op jit(solution)/shard_map/ppermute | solution.py:587
  37.5 3.0 %collective-permute-start.5 = (f32[38,8,128]{2,1,0:T(8,128)S(1)}, f32[38,8,128]{2,1,0:T(8,128)S(1)}, u32[]{:S(2)}, u32[]{:S(2)}) collective-permute-start(f32[38,8,128]{2,1,0:T(8,128)S(1)} %get-tuple-element.52), channel_id=1, source_target_pairs={{1,16},{16,1},{3,18},{18,3},{5,20},{20,5},{7,22},{22,7},{9,24},{24... | collective-permute-start | bytes 466952 | tf_op jit(solution)/shard_map/ppermute | solution.py:588
  40.5 0.0 copy-start.7
  40.5 2.5 %shard_map.142 = (f32[24,256]{1,0:T(8,128)S(1)}, f32[24,256]{1,0:T(8,128)S(1)}, f32[8,128]{1,0:T(8,128)S(1)}) custom-call(f32[360,128]{1,0:T(8,128)S(1)} %shard_map.140.after.total, f32[32,24,128]{2,1,0:T(8,128)S(1)} %all-to-all-done.bottoms, f32[3,8]{1,0:T(4,128)S(1)} %copy-done.13, f32[6,128,128]{2,1,0:T(8,128)S(1)} %copy-done.8, ...), custom_call_target="tpu_custom_call" | custom-call | tf_op jit(solution)/shard_map/pallas_call | solution.py:562
  43.0 0.0 collective-permute-done.4.came_y1.rows1
  43.0 1.0 %collective-permute-done.5.came_y2.rows2 = f32[38,8,128]{2,1,0:T(8,128)S(1)} collective-permute-done((f32[38,8,128]{2,1,0:T(8,128)S(1)}, f32[38,8,128]{2,1,0:T(8,128)S(1)}, u32[]{:S(2)}, u32[]{:S(2)}) %collective-permute-start.5) | collective-permute-done | bytes 155680 | tf_op jit(solution)/shard_map/ppermute | solution.py:588
  44.0 0.0 copy-start.3
  44.1 0.0 copy-start.6
  44.1 0.0 copy-start.1
  44.1 0.0 copy-start.2
  44.1 4.1 %shard_map.143 = (f32[3,5,5,4,8,128]{5,4,3,2,1,0:T(8,128)S(1)}, f32[3,5,5,4,8,128]{5,4,3,2,1,0:T(8,128)S(1)}, f32[30,8,128]{2,1,0:T(8,128)S(1)}, f32[30,8,128]{2...) custom-call(f32[3,5,5,4,8,128]{5,4,3,2,1,0:T(8,128)S(1)} %copy-done., ...), custom_call_target="tpu_custom_call" | custom-call | tf_op jit(solution)/shard_map/pallas_call | solution.py:562
  48.2 0.0 copy-start
  48.2 0.1 collective-permute-start.6
  48.3 4.3 %collective-permute-start.7 = (f32[30,8,128]{2,1,0:T(8,128)S(1)}, f32[30,8,128]{2,1,0:T(8,128)S(1)}, u32[]{:S(2)}, u32[]{:S(2)}) collective-permute-start(f32[30,8,128]{2,1,0:T(8,128)S(1)} %get-tuple-element.64), channel_id=1, source_target_pairs={{2,4},{6,8},{10,12},{4,2},{8,6},{12,10},{3,5},{7,9},{11,13},{5,3},... | collective-permute-start | bytes 368648 | tf_op jit(solution)/shard_map/ppermute | solution.py:588
  52.6 4.9 %shard_map.144 = (f32[5,4,32,256]{3,2,1,0:T(8,128)}, f32[8,128]{1,0:T(8,128)S(1)}) custom-call(f32[4,32,256]{2,1,0:T(8,128)S(1)} %copy-done.6, f32[3,4,32,256]{3,2,1,0:T(8,128)S(1)} %copy-done.3, f32[4,32,256]{2,1,0:T(8,128)S(1)} %copy-done.7, f32[5,64,256]{2,1,0:T(8,128)S(1)} %collective-permute-done.crater1.came1, ...), custom_call_target="tpu_custom_call" | custom-call | tf_op jit(solution)/shard_map/pallas_call | solution.py:562
  57.6 0.0 collective-permute-done.6.came1.x1
  57.6 0.0 collective-permute-done.7.came2.x2
  57.6 0.1 shard_map.145
  57.6 0.1 collective-permute-start.8
  57.7 3.4 %collective-permute-start.9 = (f32[15,8,128]{2,1,0:T(8,128)S(1)}, f32[15,8,128]{2,1,0:T(8,128)S(1)}, u32[]{:S(2)}, u32[]{:S(2)}) collective-permute-start(f32[15,8,128]{2,1,0:T(8,128)S(1)} %get-tuple-element.71), channel_id=1, source_target_pairs={{1,16},{16,1},{3,18},{18,3},{5,20},{20,5},{7,22},{22,7},{9,24},{24... | collective-permute-start | bytes 184328 | tf_op jit(solution)/shard_map/ppermute | solution.py:588
  61.2 3.5 %shard_map.146 = (f32[9,17,3,512]{3,2,1,0:T(4,128)}, f32[4,1224,128]{2,1,0:T(8,128)S(1)}) custom-call(f32[3,5,5,4,8,128]{5,4,3,2,1,0:T(8,128)S(1)} %get-tuple-element.59.a1, f32[24,256]{1,0:T(8,128)S(1)} %get-tuple-element.60.surf1, f32[9,17,3,512]{3,2,1,0:T(4,128)S(1)} %bitcast.9, f32[9,17,3,512]{3,2,1,0:T(4,128)S(1)} %bitcast.11, ...), custom_call_target="tpu_custom_call" | custom-call | tf_op jit(solution)/shard_map/pallas_call | solution.py:562
  64.7 0.0 collective-permute-done.8.y1
  64.7 0.0 collective-permute-done.9.y2
  64.7 2.4 %shard_map.147 = (f32[9,17,3,512]{3,2,1,0:T(4,128)}, f32[9,17,3,512]{3,2,1,0:T(4,128)}) custom-call(f32[4,1224,128]{2,1,0:T(8,128)S(1)} %get-tuple-element.68.v_part, f32[3,5,5,4,8,128]{5,4,3,2,1,0:T(8,128)S(1)} %get-tuple-element.69.f, f32[30,8,128]{2,1,0:T(8,128)S(1)} %collective-permute-done.6.came1.x1, ...), custom_call_target="tpu_custom_call" | custom-call | tf_op jit(solution)/shard_map/pallas_call | solution.py:562
  (16 shorter events, 0.0 us)
Async XLA Ops:
  3.3 25.1 %all-to-all-start = ((f32[32,24,128]{2,1,0:T(8,128)}), f32[32,24,128]{2,1,0:T(8,128)S(1)}, u32[]{:S(2)}, u32[]{:S(2)}) async-start(f32[32,24,128]{2,1,0:T(8,128)} %get-tuple-element.49), calls=%async_computation | async-start | bytes 786432 | tf_op jit(solution)/shard_map/all_to_all | solution.py:1060
  9.8 25.0 %collective-permute-start = (f32[5,64,256]{2,1,0:T(8,128)}, f32[5,64,256]{2,1,0:T(8,128)S(1)}, u32[]{:S(2)}, u32[]{:S(2)}) collective-permute-start(f32[5,64,256]{2,1,0:T(8,128)} %get-tuple-element.40), channel_id=1, source_target_pairs={{0,2},{2,0},{4,6},{6,4},{8,10},{10,8},{12,14},{14,12},{1,3},{3,1},... | collective-permute-start | bytes 983048 | tf_op jit(solution)/shard_map/ppermute | solution.py:587
  9.9 24.8 %collective-permute-start.1 = (f32[5,64,256]{2,1,0:T(8,128)}, f32[5,64,256]{2,1,0:T(8,128)S(1)}, u32[]{:S(2)}, u32[]{:S(2)}) collective-permute-start(f32[5,64,256]{2,1,0:T(8,128)} %get-tuple-element.41), channel_id=1, source_target_pairs={{2,4},{6,8},{10,12},{4,2},{8,6},{12,10},{3,5},{7,9},{11,13},{5,3},... | collective-permute-start | bytes 983048 | tf_op jit(solution)/shard_map/ppermute | solution.py:588
  14.1 20.6 %copy-start.11 = (f32[10,8,128]{2,1,0:T(8,128)S(1)}, f32[10,8,128]{2,1,0:T(8,128)}, u32[]{:S(2)}) copy-start(f32[10,8,128]{2,1,0:T(8,128)} %get-tuple-element.47.rows_low) | copy-start | bytes 122884
  14.1 20.6 %copy-start.12 = (f32[10,8,128]{2,1,0:T(8,128)S(1)}, f32[10,8,128]{2,1,0:T(8,128)}, u32[]{:S(2)}) copy-start(f32[10,8,128]{2,1,0:T(8,128)} %get-tuple-element.48.rows_high) | copy-start | bytes 122884
  14.2 26.3 %copy-start.8 = (f32[6,128,128]{2,1,0:T(8,128)S(1)}, f32[6,128,128]{2,1,0:T(8,128)}, u32[]{:S(2)}) copy-start(f32[6,128,128]{2,1,0:T(8,128)} %constant.2.clone.tables) | copy-start | bytes 1179652
  24.0 16.5 %copy-start.13 = (f32[3,8]{1,0:T(4,128)S(1)}, f32[3,8]{1,0:T(4,128)}, u32[]{:S(2)}) copy-start(f32[3,8]{1,0:T(4,128)} %material.5) | copy-start | bytes 292
  24.0 10.7 %collective-permute-start.2 = (f32[31,8,128]{2,1,0:T(8,128)}, f32[31,8,128]{2,1,0:T(8,128)S(1)}, u32[]{:S(2)}, u32[]{:S(2)}) collective-permute-start(f32[31,8,128]{2,1,0:T(8,128)} %get-tuple-element.45), channel_id=1, source_target_pairs={{0,2},{2,0},{4,6},{6,4},{8,10},{10,8},{12,14},{14,12},{1,3},{3,1},... | collective-permute-start | bytes 380936 | tf_op jit(solution)/shard_map/ppermute | solution.py:587
  24.1 19.9 %copy-start.14 = (f32[8,128]{1,0:T(8,128)S(1)}, f32[8,128]{1,0:T(8,128)}, u32[]{:S(2)}) copy-start(f32[8,128]{1,0:T(8,128)} %get-tuple-element.42.region) | copy-start | bytes 12292
  24.1 10.7 %collective-permute-start.3 = (f32[31,8,128]{2,1,0:T(8,128)}, f32[31,8,128]{2,1,0:T(8,128)S(1)}, u32[]{:S(2)}, u32[]{:S(2)}) collective-permute-start(f32[31,8,128]{2,1,0:T(8,128)} %get-tuple-element.46), channel_id=1, source_target_pairs={{2,4},{6,8},{10,12},{4,2},{8,6},{12,10},{3,5},{7,9},{11,13},{5,3},... | collective-permute-start | bytes 380936 | tf_op jit(solution)/shard_map/ppermute | solution.py:588
  28.5 0.7 %copy-start.15 = (f32[8,128]{1,0:T(8,128)S(1)}, f32[8,128]{1,0:T(8,128)}, u32[]{:S(2)}) copy-start(f32[8,128]{1,0:T(8,128)} %get-tuple-element.50.after) | copy-start | bytes 12292
  29.2 14.9 %copy-start.5 = (f32[3,5,5,4,8,128]{5,4,3,2,1,0:T(8,128)S(1)}, f32[3,5,5,4,8,128]{5,4,3,2,1,0:T(8,128)}, u32[]{:S(2)}) copy-start(f32[3,5,5,4,8,128]{5,4,3,2,1,0:T(8,128)} %get-tuple-element.54.f) | copy-start | bytes 3686404
  32.0 12.1 %copy-start.4 = (f32[3,5,5,4,8,128]{5,4,3,2,1,0:T(8,128)S(1)}, f32[3,5,5,4,8,128]{5,4,3,2,1,0:T(8,128)}, u32[]{:S(2)}) copy-start(f32[3,5,5,4,8,128]{5,4,3,2,1,0:T(8,128)} %get-tuple-element.53.b) | copy-start | bytes 3686404
  34.8 0.8 %copy-start.9 = (f32[16,8,128]{2,1,0:T(8,128)S(1)}, f32[16,8,128]{2,1,0:T(8,128)}, u32[]{:S(2)}) copy-start(f32[16,8,128]{2,1,0:T(8,128)} %get-tuple-element.43.low) | copy-start | bytes 196612
  35.6 0.8 %copy-start.10 = (f32[15,8,128]{2,1,0:T(8,128)S(1)}, f32[15,8,128]{2,1,0:T(8,128)}, u32[]{:S(2)}) copy-start(f32[15,8,128]{2,1,0:T(8,128)} %get-tuple-element.44.high) | copy-start | bytes 184324
  36.6 6.4 %collective-permute-start.4 = (f32[38,8,128]{2,1,0:T(8,128)S(1)}, f32[38,8,128]{2,1,0:T(8,128)S(1)}, u32[]{:S(2)}, u32[]{:S(2)}) collective-permute-start(f32[38,8,128]{2,1,0:T(8,128)S(1)} %get-tuple-element.51), channel_id=1, source_target_pairs={{0,1},{1,0},{16,17},{17,16},{2,3},{3,2},{18,19},{19,18},{4,5},{5,4... | collective-permute-start | bytes 466952 | tf_op jit(solution)/shard_map/ppermute | solution.py:587
  37.5 6.5 %collective-permute-start.5 = (f32[38,8,128]{2,1,0:T(8,128)S(1)}, f32[38,8,128]{2,1,0:T(8,128)S(1)}, u32[]{:S(2)}, u32[]{:S(2)}) collective-permute-start(f32[38,8,128]{2,1,0:T(8,128)S(1)} %get-tuple-element.52), channel_id=1, source_target_pairs={{1,16},{16,1},{3,18},{18,3},{5,20},{20,5},{7,22},{22,7},{9,24},{24... | collective-permute-start | bytes 466952 | tf_op jit(solution)/shard_map/ppermute | solution.py:588
  40.5 12.1 %copy-start.7 = (f32[4,32,256]{2,1,0:T(8,128)S(1)}, f32[4,32,256]{2,1,0:T(8,128)}, u32[]{:S(2)}) copy-start(f32[4,32,256]{2,1,0:T(8,128)} %energy.3) | copy-start | bytes 393220
  44.0 8.6 %copy-start.3 = (f32[3,4,32,256]{3,2,1,0:T(8,128)S(1)}, f32[3,4,32,256]{3,2,1,0:T(8,128)}, u32[]{:S(2)}) copy-start(f32[3,4,32,256]{3,2,1,0:T(8,128)} %momentum.3) | copy-start | bytes 1179652
  44.1 8.6 %copy-start.6 = (f32[4,32,256]{2,1,0:T(8,128)S(1)}, f32[4,32,256]{2,1,0:T(8,128)}, u32[]{:S(2)}) copy-start(f32[4,32,256]{2,1,0:T(8,128)} %density.3) | copy-start | bytes 393220
  44.1 17.1 %copy-start.1 = (f32[3,9,17,512]{3,0,2,1:T(4,128)S(1)}, f32[3,9,17,512]{3,0,2,1:T(4,128)}, u32[]{:S(2)}) copy-start(f32[3,9,17,512]{3,0,2,1:T(4,128)} %param.15) | copy-start | bytes 2820100
  44.1 17.1 %copy-start.2 = (f32[3,9,17,512]{3,0,2,1:T(4,128)S(1)}, f32[3,9,17,512]{3,0,2,1:T(4,128)}, u32[]{:S(2)}) copy-start(f32[3,9,17,512]{3,0,2,1:T(4,128)} %param.16) | copy-start | bytes 2820100
  48.2 13.0 %copy-start = (f32[3,9,17,512]{3,0,2,1:T(4,128)S(1)}, f32[3,9,17,512]{3,0,2,1:T(4,128)}, u32[]{:S(2)}) copy-start(f32[3,9,17,512]{3,0,2,1:T(4,128)} %param.14) | copy-start | bytes 2820100
  48.2 9.4 %collective-permute-start.6 = (f32[30,8,128]{2,1,0:T(8,128)S(1)}, f32[30,8,128]{2,1,0:T(8,128)S(1)}, u32[]{:S(2)}, u32[]{:S(2)}) collective-permute-start(f32[30,8,128]{2,1,0:T(8,128)S(1)} %get-tuple-element.63), channel_id=1, source_target_pairs={{0,2},{2,0},{4,6},{6,4},{8,10},{10,8},{12,14},{14,12},{1,3},{3,1},... | collective-permute-start | bytes 368648 | tf_op jit(solution)/shard_map/ppermute | solution.py:587
  48.3 9.3 %collective-permute-start.7 = (f32[30,8,128]{2,1,0:T(8,128)S(1)}, f32[30,8,128]{2,1,0:T(8,128)S(1)}, u32[]{:S(2)}, u32[]{:S(2)}) collective-permute-start(f32[30,8,128]{2,1,0:T(8,128)S(1)} %get-tuple-element.64), channel_id=1, source_target_pairs={{2,4},{6,8},{10,12},{4,2},{8,6},{12,10},{3,5},{7,9},{11,13},{5,3},... | collective-permute-start | bytes 368648 | tf_op jit(solution)/shard_map/ppermute | solution.py:588
  57.6 7.1 %collective-permute-start.8 = (f32[15,8,128]{2,1,0:T(8,128)S(1)}, f32[15,8,128]{2,1,0:T(8,128)S(1)}, u32[]{:S(2)}, u32[]{:S(2)}) collective-permute-start(f32[15,8,128]{2,1,0:T(8,128)S(1)} %get-tuple-element.70), channel_id=1, source_target_pairs={{0,1},{1,0},{16,17},{17,16},{2,3},{3,2},{18,19},{19,18},{4,5},{5,4... | collective-permute-start | bytes 184328 | tf_op jit(solution)/shard_map/ppermute | solution.py:587
  57.7 7.0 %collective-permute-start.9 = (f32[15,8,128]{2,1,0:T(8,128)S(1)}, f32[15,8,128]{2,1,0:T(8,128)S(1)}, u32[]{:S(2)}, u32[]{:S(2)}) collective-permute-start(f32[15,8,128]{2,1,0:T(8,128)S(1)} %get-tuple-element.71), channel_id=1, source_target_pairs={{1,16},{16,1},{3,18},{18,3},{5,20},{20,5},{7,22},{22,7},{9,24},{24... | collective-permute-start | bytes 184328 | tf_op jit(solution)/shard_map/ppermute | solution.py:588

commit v8 on v7

--- a/solution.py
+++ b/solution.py
@@ -392,14 +392,29 @@
     return float(-1.0 / (half_size**3 * quad[i] * quad[j] * quad[k]))
 
 
-def first_kernel(u, v, a, region, material, b_out, f_out, x1, x2, y_low, y_high, token,
-                 elem, gx, gz, cross, planes, side, u_in, v_in, a_in, wide_u, wide_b, kept_u, kept_b, b_held, semaphores):
+def first_kernel(nodes_y, u, v, a, density, momentum, energy, dest, slot, region, material,
+                 b_out, bottoms, f_out, x1, x2, y_low, y_high, rows_low, rows_high, region_out,
+                 elem, gx, gz, cross, planes, side, u_in, v_in, a_in, wide_u, wide_b, kept_u, kept_b, b_held,
+                 cells, copies_held, dest_in, slot_in, region_in, semaphores):
+    early = fetch(
+        [(region, region_in), (dest, dest_in), (slot, slot_in), (density, cells.at[0]),
+         (momentum, cells.at[pl.ds(1, 3)]), (energy, cells.at[4])],
+        semaphores.at[pl.ds(14, 6)],
+    )
     copies = [tile_copies(f, h, semaphores, 4 * n) for n, (f, h) in enumerate(((u, u_in), (v, v_in), (a, a_in)))]
     for t in range(4):
         for copy in copies:
             copy[t].start()
     table = depth_table()
-    region_now = region[...]
+    for copy in early:
+        copy.wait()
+    region_now = jnp.concatenate([region_in[0], region_in[1]], axis=0).astype(f32) + 1.0
+    region_out[...] = region_now
+    block = deepest_block(nodes_y, cells, dest_in, slot_in, region_now, rows_low, rows_high)
+    for n in range(bottoms.shape[0]):
+        copies_held[n] = block
+    save_bottoms = pltpu.make_async_copy(copies_held, bottoms, semaphores.at[13])
+    save_bottoms.start()
 
     def put_u(l, value):
         elem[:, :, :, l] = value
@@ -439,8 +454,8 @@
     x1[30] = region_now
     x2[30] = region_now
     y_low[15] = region_now
-    token[...] = region_now
     save_b.wait()
+    save_bottoms.wait()
 
 
 def second_kernel(b, f, came_x1, came_x2, came_y1, came_y2, region, material, after, a_out, f_out, x1, x2, y_low, y_high, scales, token,
@@ -782,31 +797,32 @@
     return [g - jnp.where(ends[0], 2.0 * f, pltpu.roll(g, 1, axis)) for f, g in zip(fluxes, upper)]
 
 
-def start_kernel(nodes_y, density, momentum, energy, dest, slot, region, bottoms, first, second, rows_low, rows_high,
-                 region_out, cells, dest_in, slot_in, region_in, semaphores):
-    copies = fetch(
-        [(dest, dest_in), (slot, slot_in), (region, region_in), (density, cells.at[0]),
-         (momentum, cells.at[pl.ds(1, 3)]), (energy, cells.at[4])],
-        semaphores,
-    )
-    for copy in copies:
+def planes_kernel(density, momentum, energy, first, second, semaphores):
+    odd = parity_x()
+    pairs = []
+    for out, down in ((first, odd), (second, 1 - odd)):
+        for n, plane in enumerate((3 - 3 * down, 2 - down)):
+            rows = pl.ds(32 * n, 32)
+            pairs.append((density.at[plane], out.at[0, rows]))
+            pairs.append((momentum.at[:, plane], out.at[pl.ds(1, 3), rows]))
+            pairs.append((energy.at[plane], out.at[4, rows]))
+    for copy in fetch(pairs, semaphores):
         copy.wait()
+
+
+def deepest_block(nodes_y, cells, dest, slot, region_now, rows_low, rows_high):
     sub, lane = rows_of(), lanes_of()
     pick = jnp.where(lane == 125 + sub, 1.0, 0.0)
     pieces = []
-    odd = parity_x()
     for f in range(5):
         columns = jnp.concatenate([cells[f, x, :, 128:256] for x in range(4)], axis=0)
         pieces.append(full_dot(pick, columns, back=True)[0:3])
-        for out, down in ((first, odd), (second, 1 - odd)):
-            out[f, 0:32, :] = cells[f, 3 - 3 * down]
-            out[f, 32:64, :] = cells[f, 2 - down]
         for t in range(2):
             lanes = slice(128 * t, 128 * t + 128)
             for out, pair in ((rows_low, (0, 1)), (rows_high, (31, 30))):
                 out[f * 2 + t] = jnp.concatenate([cells[f, x, r : r + 1, lanes] for r in pair for x in range(4)], axis=0)
     count_gy, count_x = lax.axis_size("gy"), lax.axis_size("gx")
-    target, node = dest_in[...].astype(f32), slot_in[...].astype(f32)
+    target, node = dest[...].astype(f32), slot[...].astype(f32)
     grp = jnp.floor((target + 0.5) * (1.0 / (count_gy * count_x)))
     rest = target - grp * (count_gy * count_x)
     gx = jnp.floor((rest + 0.5) * (1.0 / count_gy))
@@ -814,15 +830,11 @@
     i = jnp.floor((node + 0.5) * (1.0 / 17.0))
     j = node - 17.0 * i
     pieces.append((8.0 * gx + i) * nodes_y + 16.0 * (grp * count_gy + gy) + j)
-    region_now = jnp.concatenate([region_in[0], region_in[1]], axis=0).astype(f32) + 1.0
-    region_out[...] = region_now
     found = jnp.zeros((8, 128), f32)
     for z in range(2):
         found = jnp.where(lane == 8 * z + sub, jnp.broadcast_to(region_now[:, z : z + 1], (8, 128)), found)
     pieces.append(jnp.broadcast_to(jnp.sum(found, axis=0, keepdims=True), (8, 128)))
-    block = jnp.concatenate(pieces, axis=0)
-    for n in range(bottoms.shape[0]):
-        bottoms[n] = block
+    return jnp.concatenate(pieces, axis=0)
 
 
 def crater_kernel(density, momentum, energy, came1, came2, rows1, rows2, after, out, token,
@@ -1047,34 +1059,30 @@
     crater = (density, momentum, energy)
     u, v, a = [jnp.transpose(x, (1, 2, 0, 3)) for x in (displacement, velocity_field, acceleration)]
     register, held_shape = (8, 128), (4, 1224, 128)
-    bottoms, crater1, crater2, rows_low, rows_high, region = call(
-        functools.partial(start_kernel, float(nodes_y)),
-        crater + (face_dest.reshape(1, -1), face_slot, element_region_index),
-        [(devices, 24, 128), (5, 64, 256), (5, 64, 256), (10, 8, 128), (10, 8, 128), register],
-        [(5, 4, 32, 256), pltpu.VMEM((1, 128), jnp.int32), pltpu.VMEM((1, 128), jnp.int32),
-         pltpu.VMEM((2, 4, 128), jnp.int32)],
-        away=(0, 1, 2, 3, 4, 5),
-        mib=56,
-        copies=6,
-    )
-    bottoms = lax.all_to_all(bottoms, rank, 0, 0, tiled=True)
+    crater1, crater2 = call(
+        planes_kernel, crater, [(5, 64, 256), (5, 64, 256)], [], away=(0, 1, 2), out_away=(0, 1), mib=56, copies=12
+    )
     crater1, crater2 = exchange("gx", crater1, crater2)
-    b, f, x1, x2, y_low, y_high, token = call(
-        first_kernel,
-        (u, v, a, region, material),
-        [element_shape, element_shape, (31, 8, 128), (31, 8, 128), (16, 8, 128), (15, 8, 128), register],
+    vectors = pltpu.VMEM((1, 128), jnp.int32)
+    b, bottoms, f, x1, x2, y_low, y_high, rows_low, rows_high, region = call(
+        functools.partial(first_kernel, float(nodes_y)),
+        (u, v, a) + crater + (face_dest.reshape(1, -1), face_slot, element_region_index, material),
+        [element_shape, (devices, 24, 128), element_shape, (31, 8, 128), (31, 8, 128), (16, 8, 128), (15, 8, 128),
+         (10, 8, 128), (10, 8, 128), register],
         internal_scratch
         + [held_shape] * 3
-        + [(3, 5, 5, 8, 256), (3, 5, 5, 8, 256), (600, 256), (600, 256), element_shape],
-        smem=(4,),
-        away=(0, 1, 2),
-        out_away=(0,),
+        + [(3, 5, 5, 8, 256), (3, 5, 5, 8, 256), (600, 256), (600, 256), element_shape]
+        + [(5, 4, 32, 256), (devices, 24, 128), vectors, vectors, pltpu.VMEM((2, 4, 128), jnp.int32)],
+        smem=(9,),
+        away=(0, 1, 2, 3, 4, 5, 6, 7, 8),
+        out_away=(0, 1),
         mib=56,
-        copies=13,
-    )
+        copies=20,
+    )
+    bottoms = lax.all_to_all(bottoms, rank, 0, 0, tiled=True)
     (total,) = call(
         functools.partial(deposit_kernel, float(nodes_y), count_x),
-        (bottoms.reshape(devices * 24, 128), token),
+        (bottoms.reshape(devices * 24, 128), region),
         [(360, 128)],
         [(4, 4 * count_x, 128)],
     )

time: 67.7 us -> 92 us (1.36)
  Pallas kernels: 32.9 us -> 51.6 us
  waiting for transfers between devices: 3.84 us -> 11.2 us
  local copies, waits for them, and re-layouts: 2.4 us -> 0.09 us
    pallas_call x10, Pallas kernels: 32.9 us -> 51.6 us  [call(): pl.pallas_call(kernel, out_shape=[jax.ShapeDtypeStruct(s, f32) for s in o...]
    ppermute x5, waiting for transfers between devices: 2.8 us -> 10.2 us  [exchange(): first = lax.ppermute(first, axis, [(i, i ^ 1) for i in range(count)])]
    unnamed x32 -> x34, local copies, waits for them, and re-layouts: 2.4 us -> 0.09 us
  transfers between devices with their start and end apart: 11 -> 11, of which waited for: 2 -> 2; matrix products, arithmetic and copies ran while one was open for 0% -> 0% of each run, Pallas kernels for 35% -> 38%
where the time goes in v8:
time: 92 us; the launch traced here: 91.6 us
  Pallas kernels  51.6 us (56%)
  starting transfers between devices  27.5 us (30%)
  waiting for transfers between devices  11.2 us (12%)
  between operations  1.23 us (1%)
    pallas_call x10, Pallas kernels, call(): pl.pallas_call(kernel, out_shape=[jax.ShapeDtypeStruct(s, f32) for s in o...  51.6 us
    ppermute x5, starting transfers between devices, exchange(): lax.ppermute(second, axis, pairs + [(j, i) for i, j in pairs])  19.4 us
    ppermute x5, waiting for transfers between devices, exchange(): first = lax.ppermute(first, axis, [(i, i ^ 1) for i in range(count)])  10.2 us
    all_to_all x1, starting transfers between devices, shards(): bottoms = lax.all_to_all(bottoms, rank, 0, 0, tiled=True)  6.46 us
  transfers between devices with their start and end apart: 11, of which 2 were waited for; matrix products, arithmetic and copies ran while one was open for 0% of the time, Pallas kernels for 38%

profile of v8, /device:TPU:3, one launch (start us, length us, event | category | flops | bytes accessed | tf_op | source)
XLA Modules:
  0.0 91.6 jit_solution(7850774169985864819)
XLA Ops:
  0.6 10.2 %shard_map.139 = (f32[3,5,5,4,8,128]{5,4,3,2,1,0:T(8,128)}, f32[32,24,128]{2,1,0:T(8,128)}, f32[3,5,5,4,8,128]{5,4,3,2,1,0:T(8,128)}, f32[31,8,128]{2,1,0:T(8,12...) custom-call(f32[9,17,3,512]{3,2,1,0:T(4,128)} %bitcast.8, ...), custom_call_target="tpu_custom_call" | custom-call | tf_op jit(solution)/shard_map/pallas_call | solution.py:577
  10.8 0.0 copy-start.16
  10.8 0.0 copy-start.15
  10.8 0.0 copy-start.14
  10.8 0.0 copy-start.9
  10.9 6.5 %all-to-all-start = ((f32[32,24,128]{2,1,0:T(8,128)}), f32[32,24,128]{2,1,0:T(8,128)S(1)}, u32[]{:S(2)}, u32[]{:S(2)}) async-start(f32[32,24,128]{2,1,0:T(8,128)} %get-tuple-element.47), calls=%async_computation | async-start | bytes 786432 | tf_op jit(solution)/shard_map/all_to_all | solution.py:1082
  17.3 0.0 copy-start.8
  17.3 0.0 copy-start.13
  17.4 21.1 %shard_map.138 = (f32[5,64,256]{2,1,0:T(8,128)}, f32[5,64,256]{2,1,0:T(8,128)}) custom-call(f32[4,32,256]{2,1,0:T(8,128)} %density.5, f32[3,4,32,256]{3,2,1,0:T(8,128)} %momentum.5, f32[4,32,256]{2,1,0:T(8,128)} %energy.5), custom_call_target="tpu_custom_call" | custom-call | tf_op jit(solution)/shard_map/pallas_call | solution.py:577
  38.4 0.1 collective-permute-start
  38.6 4.2 %collective-permute-start.1 = (f32[5,64,256]{2,1,0:T(8,128)}, f32[5,64,256]{2,1,0:T(8,128)S(1)}, u32[]{:S(2)}, u32[]{:S(2)}) collective-permute-start(f32[5,64,256]{2,1,0:T(8,128)} %get-tuple-element.40), channel_id=1, source_target_pairs={{2,4},{6,8},{10,12},{4,2},{8,6},{12,10},{3,5},{7,9},{11,13},{5,3},... | collective-permute-start | bytes 983048 | tf_op jit(solution)/shard_map/ppermute | solution.py:603
  42.8 0.0 copy-done.16
  42.8 0.1 collective-permute-start.2
  42.9 4.2 %collective-permute-start.3 = (f32[31,8,128]{2,1,0:T(8,128)S(1)}, f32[31,8,128]{2,1,0:T(8,128)S(1)}, u32[]{:S(2)}, u32[]{:S(2)}) collective-permute-start(f32[31,8,128]{2,1,0:T(8,128)S(1)} %copy-done.15), channel_id=1, source_target_pairs={{2,4},{6,8},{10,12},{4,2},{8,6},{12,10},{3,5},{7,9},{11,13},{5,3},... | collective-permute-start | bytes 380936 | tf_op jit(solution)/shard_map/ppermute | solution.py:603
  47.1 0.0 all-to-all-done.bottoms
  47.2 0.0 copy-start.5
  47.2 2.8 %shard_map.140.after.total = f32[360,128]{1,0:T(8,128)S(1)} custom-call(f32[768,128]{1,0:T(8,128)S(1)} %bitcast.14, f32[8,128]{1,0:T(8,128)S(1)} %copy-done.14), custom_call_target="tpu_custom_call" | custom-call | tf_op jit(solution)/shard_map/pallas_call | solution.py:577
  50.0 0.0 copy-start.4
  50.0 10.2 %collective-permute-done.2.came1.came_x1 = f32[31,8,128]{2,1,0:T(8,128)S(1)} collective-permute-done((f32[31,8,128]{2,1,0:T(8,128)S(1)}, f32[31,8,128]{2,1,0:T(8,128)S(1)}, u32[]{:S(2)}, u32[]{:S(2)}) %collective-permute-start.2) | collective-permute-done | bytes 127008 | tf_op jit(solution)/shard_map/ppermute | solution.py:602
  60.1 0.0 collective-permute-done.3.came2.came_x2
  60.1 0.0 collective-permute-done.crater1.came1
  60.1 0.0 collective-permute-done.1.crater2.came2
  60.2 0.2 shard_map.141
  60.3 1.3 %collective-permute-start.4 = (f32[38,8,128]{2,1,0:T(8,128)S(1)}, f32[38,8,128]{2,1,0:T(8,128)S(1)}, u32[]{:S(2)}, u32[]{:S(2)}) collective-permute-start(f32[38,8,128]{2,1,0:T(8,128)S(1)} %get-tuple-element.49), channel_id=1, source_target_pairs={{0,1},{1,0},{16,17},{17,16},{2,3},{3,2},{18,19},{19,18},{4,5},{5,4... | collective-permute-start | bytes 466952 | tf_op jit(solution)/shard_map/ppermute | solution.py:602
  61.6 3.0 %collective-permute-start.5 = (f32[38,8,128]{2,1,0:T(8,128)S(1)}, f32[38,8,128]{2,1,0:T(8,128)S(1)}, u32[]{:S(2)}, u32[]{:S(2)}) collective-permute-start(f32[38,8,128]{2,1,0:T(8,128)S(1)} %get-tuple-element.50), channel_id=1, source_target_pairs={{1,16},{16,1},{3,18},{18,3},{5,20},{20,5},{7,22},{22,7},{9,24},{24... | collective-permute-start | bytes 466952 | tf_op jit(solution)/shard_map/ppermute | solution.py:603
  64.6 0.0 copy-start.7
  64.6 2.5 %shard_map.142 = (f32[24,256]{1,0:T(8,128)S(1)}, f32[24,256]{1,0:T(8,128)S(1)}, f32[8,128]{1,0:T(8,128)S(1)}) custom-call(f32[360,128]{1,0:T(8,128)S(1)} %shard_map.140.after.total, f32[32,24,128]{2,1,0:T(8,128)S(1)} %all-to-all-done.bottoms, f32[3,8]{1,0:T(4,128)S(1)} %copy-done.13, f32[6,128,128]{2,1,0:T(8,128)S(1)} %copy-done.8, ...), custom_call_target="tpu_custom_call" | custom-call | tf_op jit(solution)/shard_map/pallas_call | solution.py:577
  67.1 0.0 collective-permute-done.4.came_y1.rows1
  67.1 1.0 %collective-permute-done.5.came_y2.rows2 = f32[38,8,128]{2,1,0:T(8,128)S(1)} collective-permute-done((f32[38,8,128]{2,1,0:T(8,128)S(1)}, f32[38,8,128]{2,1,0:T(8,128)S(1)}, u32[]{:S(2)}, u32[]{:S(2)}) %collective-permute-start.5) | collective-permute-done | bytes 155680 | tf_op jit(solution)/shard_map/ppermute | solution.py:603
  68.2 0.0 copy-start.1
  68.2 0.0 copy-start.2
  68.2 4.0 %shard_map.143 = (f32[3,5,5,4,8,128]{5,4,3,2,1,0:T(8,128)S(1)}, f32[3,5,5,4,8,128]{5,4,3,2,1,0:T(8,128)S(1)}, f32[30,8,128]{2,1,0:T(8,128)S(1)}, f32[30,8,128]{2...) custom-call(f32[3,5,5,4,8,128]{5,4,3,2,1,0:T(8,128)S(1)} %copy-done., ...), custom_call_target="tpu_custom_call" | custom-call | tf_op jit(solution)/shard_map/pallas_call | solution.py:577
  72.2 0.0 copy-start
  72.2 0.1 collective-permute-start.6
  72.3 4.3 %collective-permute-start.7 = (f32[30,8,128]{2,1,0:T(8,128)S(1)}, f32[30,8,128]{2,1,0:T(8,128)S(1)}, u32[]{:S(2)}, u32[]{:S(2)}) collective-permute-start(f32[30,8,128]{2,1,0:T(8,128)S(1)} %get-tuple-element.62), channel_id=1, source_target_pairs={{2,4},{6,8},{10,12},{4,2},{8,6},{12,10},{3,5},{7,9},{11,13},{5,3},... | collective-permute-start | bytes 368648 | tf_op jit(solution)/shard_map/ppermute | solution.py:603
  76.6 0.0 copy-done.7
  76.6 0.0 copy-done.3
  76.6 0.0 copy-done.6
  76.6 4.9 %shard_map.144 = (f32[5,4,32,256]{3,2,1,0:T(8,128)}, f32[8,128]{1,0:T(8,128)S(1)}) custom-call(f32[4,32,256]{2,1,0:T(8,128)S(1)} %copy-done.6, f32[3,4,32,256]{3,2,1,0:T(8,128)S(1)} %copy-done.3, f32[4,32,256]{2,1,0:T(8,128)S(1)} %copy-done.7, f32[5,64,256]{2,1,0:T(8,128)S(1)} %collective-permute-done.crater1.came1, ...), custom_call_target="tpu_custom_call" | custom-call | tf_op jit(solution)/shard_map/pallas_call | solution.py:577
  81.6 0.0 collective-permute-done.6.came1.x1
  81.6 0.0 collective-permute-done.7.came2.x2
  81.6 0.1 shard_map.145
  81.6 0.1 collective-permute-start.8
  81.7 3.7 %collective-permute-start.9 = (f32[15,8,128]{2,1,0:T(8,128)S(1)}, f32[15,8,128]{2,1,0:T(8,128)S(1)}, u32[]{:S(2)}, u32[]{:S(2)}) collective-permute-start(f32[15,8,128]{2,1,0:T(8,128)S(1)} %get-tuple-element.69), channel_id=1, source_target_pairs={{1,16},{16,1},{3,18},{18,3},{5,20},{20,5},{7,22},{22,7},{9,24},{24... | collective-permute-start | bytes 184328 | tf_op jit(solution)/shard_map/ppermute | solution.py:603
  85.5 3.5 %shard_map.146 = (f32[9,17,3,512]{3,2,1,0:T(4,128)}, f32[4,1224,128]{2,1,0:T(8,128)S(1)}) custom-call(f32[3,5,5,4,8,128]{5,4,3,2,1,0:T(8,128)S(1)} %get-tuple-element.57.a1, f32[24,256]{1,0:T(8,128)S(1)} %get-tuple-element.58.surf1, f32[9,17,3,512]{3,2,1,0:T(4,128)S(1)} %bitcast.9, f32[9,17,3,512]{3,2,1,0:T(4,128)S(1)} %bitcast.11, ...), custom_call_target="tpu_custom_call" | custom-call | tf_op jit(solution)/shard_map/pallas_call | solution.py:577
  89.0 0.0 collective-permute-done.8.y1
  89.0 0.0 collective-permute-done.9.y2
  89.0 2.4 %shard_map.147 = (f32[9,17,3,512]{3,2,1,0:T(4,128)}, f32[9,17,3,512]{3,2,1,0:T(4,128)}) custom-call(f32[4,1224,128]{2,1,0:T(8,128)S(1)} %get-tuple-element.66.v_part, f32[3,5,5,4,8,128]{5,4,3,2,1,0:T(8,128)S(1)} %get-tuple-element.67.f, f32[30,8,128]{2,1,0:T(8,128)S(1)} %collective-permute-done.6.came1.x1, ...), custom_call_target="tpu_custom_call" | custom-call | tf_op jit(solution)/shard_map/pallas_call | solution.py:577
  (18 shorter events, 0.0 us)
Async XLA Ops:
  10.8 32.0 %copy-start.16 = (f32[31,8,128]{2,1,0:T(8,128)S(1)}, f32[31,8,128]{2,1,0:T(8,128)}, u32[]{:S(2)}) copy-start(f32[31,8,128]{2,1,0:T(8,128)} %get-tuple-element.43) | copy-start | bytes 380932
  10.8 32.1 %copy-start.15 = (f32[31,8,128]{2,1,0:T(8,128)S(1)}, f32[31,8,128]{2,1,0:T(8,128)}, u32[]{:S(2)}) copy-start(f32[31,8,128]{2,1,0:T(8,128)} %get-tuple-element.44) | copy-start | bytes 380932
  10.8 36.3 %copy-start.14 = (f32[8,128]{1,0:T(8,128)S(1)}, f32[8,128]{1,0:T(8,128)}, u32[]{:S(2)}) copy-start(f32[8,128]{1,0:T(8,128)} %get-tuple-element.48.after.region) | copy-start | bytes 12292
  10.8 49.3 %copy-start.9 = (f32[16,8,128]{2,1,0:T(8,128)S(1)}, f32[16,8,128]{2,1,0:T(8,128)}, u32[]{:S(2)}) copy-start(f32[16,8,128]{2,1,0:T(8,128)} %get-tuple-element.41.low) | copy-start | bytes 196612
  10.8 49.3 %copy-start.10 = (f32[15,8,128]{2,1,0:T(8,128)S(1)}, f32[15,8,128]{2,1,0:T(8,128)}, u32[]{:S(2)}) copy-start(f32[15,8,128]{2,1,0:T(8,128)} %get-tuple-element.42.high) | copy-start | bytes 184324
  10.8 49.3 %copy-start.11 = (f32[10,8,128]{2,1,0:T(8,128)S(1)}, f32[10,8,128]{2,1,0:T(8,128)}, u32[]{:S(2)}) copy-start(f32[10,8,128]{2,1,0:T(8,128)} %get-tuple-element.45.rows_low) | copy-start | bytes 122884
  10.9 49.3 %copy-start.12 = (f32[10,8,128]{2,1,0:T(8,128)S(1)}, f32[10,8,128]{2,1,0:T(8,128)}, u32[]{:S(2)}) copy-start(f32[10,8,128]{2,1,0:T(8,128)} %get-tuple-element.46.rows_high) | copy-start | bytes 122884
  10.9 36.3 %all-to-all-start = ((f32[32,24,128]{2,1,0:T(8,128)}), f32[32,24,128]{2,1,0:T(8,128)S(1)}, u32[]{:S(2)}, u32[]{:S(2)}) async-start(f32[32,24,128]{2,1,0:T(8,128)} %get-tuple-element.47), calls=%async_computation | async-start | bytes 786432 | tf_op jit(solution)/shard_map/all_to_all | solution.py:1082
  17.3 47.3 %copy-start.8 = (f32[6,128,128]{2,1,0:T(8,128)S(1)}, f32[6,128,128]{2,1,0:T(8,128)}, u32[]{:S(2)}) copy-start(f32[6,128,128]{2,1,0:T(8,128)} %constant.2.clone.tables) | copy-start | bytes 1179652
  17.3 47.3 %copy-start.13 = (f32[3,8]{1,0:T(4,128)S(1)}, f32[3,8]{1,0:T(4,128)}, u32[]{:S(2)}) copy-start(f32[3,8]{1,0:T(4,128)} %material.5) | copy-start | bytes 292
  38.4 21.7 %collective-permute-start = (f32[5,64,256]{2,1,0:T(8,128)}, f32[5,64,256]{2,1,0:T(8,128)S(1)}, u32[]{:S(2)}, u32[]{:S(2)}) collective-permute-start(f32[5,64,256]{2,1,0:T(8,128)} %get-tuple-element.39), channel_id=1, source_target_pairs={{0,2},{2,0},{4,6},{6,4},{8,10},{10,8},{12,14},{14,12},{1,3},{3,1},... | collective-permute-start | bytes 983048 | tf_op jit(solution)/shard_map/ppermute | solution.py:602
  38.6 21.5 %collective-permute-start.1 = (f32[5,64,256]{2,1,0:T(8,128)}, f32[5,64,256]{2,1,0:T(8,128)S(1)}, u32[]{:S(2)}, u32[]{:S(2)}) collective-permute-start(f32[5,64,256]{2,1,0:T(8,128)} %get-tuple-element.40), channel_id=1, source_target_pairs={{2,4},{6,8},{10,12},{4,2},{8,6},{12,10},{3,5},{7,9},{11,13},{5,3},... | collective-permute-start | bytes 983048 | tf_op jit(solution)/shard_map/ppermute | solution.py:603
  42.8 17.3 %collective-permute-start.2 = (f32[31,8,128]{2,1,0:T(8,128)S(1)}, f32[31,8,128]{2,1,0:T(8,128)S(1)}, u32[]{:S(2)}, u32[]{:S(2)}) collective-permute-start(f32[31,8,128]{2,1,0:T(8,128)S(1)} %copy-done.16), channel_id=1, source_target_pairs={{0,2},{2,0},{4,6},{6,4},{8,10},{10,8},{12,14},{14,12},{1,3},{3,1},... | collective-permute-start | bytes 380936 | tf_op jit(solution)/shard_map/ppermute | solution.py:602
  42.9 17.2 %collective-permute-start.3 = (f32[31,8,128]{2,1,0:T(8,128)S(1)}, f32[31,8,128]{2,1,0:T(8,128)S(1)}, u32[]{:S(2)}, u32[]{:S(2)}) collective-permute-start(f32[31,8,128]{2,1,0:T(8,128)S(1)} %copy-done.15), channel_id=1, source_target_pairs={{2,4},{6,8},{10,12},{4,2},{8,6},{12,10},{3,5},{7,9},{11,13},{5,3},... | collective-permute-start | bytes 380936 | tf_op jit(solution)/shard_map/ppermute | solution.py:603
  47.2 21.0 %copy-start.5 = (f32[3,5,5,4,8,128]{5,4,3,2,1,0:T(8,128)S(1)}, f32[3,5,5,4,8,128]{5,4,3,2,1,0:T(8,128)}, u32[]{:S(2)}) copy-start(f32[3,5,5,4,8,128]{5,4,3,2,1,0:T(8,128)} %get-tuple-element.52.f) | copy-start | bytes 3686404
  50.0 18.2 %copy-start.4 = (f32[3,5,5,4,8,128]{5,4,3,2,1,0:T(8,128)S(1)}, f32[3,5,5,4,8,128]{5,4,3,2,1,0:T(8,128)}, u32[]{:S(2)}) copy-start(f32[3,5,5,4,8,128]{5,4,3,2,1,0:T(8,128)} %get-tuple-element.51.b) | copy-start | bytes 3686404
  60.3 6.8 %collective-permute-start.4 = (f32[38,8,128]{2,1,0:T(8,128)S(1)}, f32[38,8,128]{2,1,0:T(8,128)S(1)}, u32[]{:S(2)}, u32[]{:S(2)}) collective-permute-start(f32[38,8,128]{2,1,0:T(8,128)S(1)} %get-tuple-element.49), channel_id=1, source_target_pairs={{0,1},{1,0},{16,17},{17,16},{2,3},{3,2},{18,19},{19,18},{4,5},{5,4... | collective-permute-start | bytes 466952 | tf_op jit(solution)/shard_map/ppermute | solution.py:602
  61.6 6.5 %collective-permute-start.5 = (f32[38,8,128]{2,1,0:T(8,128)S(1)}, f32[38,8,128]{2,1,0:T(8,128)S(1)}, u32[]{:S(2)}, u32[]{:S(2)}) collective-permute-start(f32[38,8,128]{2,1,0:T(8,128)S(1)} %get-tuple-element.50), channel_id=1, source_target_pairs={{1,16},{16,1},{3,18},{18,3},{5,20},{20,5},{7,22},{22,7},{9,24},{24... | collective-permute-start | bytes 466952 | tf_op jit(solution)/shard_map/ppermute | solution.py:603
  64.6 12.0 %copy-start.7 = (f32[4,32,256]{2,1,0:T(8,128)S(1)}, f32[4,32,256]{2,1,0:T(8,128)}, u32[]{:S(2)}) copy-start(f32[4,32,256]{2,1,0:T(8,128)} %energy.5) | copy-start | bytes 393220
  68.1 8.4 %copy-start.3 = (f32[3,4,32,256]{3,2,1,0:T(8,128)S(1)}, f32[3,4,32,256]{3,2,1,0:T(8,128)}, u32[]{:S(2)}) copy-start(f32[3,4,32,256]{3,2,1,0:T(8,128)} %momentum.5) | copy-start | bytes 1179652
  68.1 8.5 %copy-start.6 = (f32[4,32,256]{2,1,0:T(8,128)S(1)}, f32[4,32,256]{2,1,0:T(8,128)}, u32[]{:S(2)}) copy-start(f32[4,32,256]{2,1,0:T(8,128)} %density.5) | copy-start | bytes 393220
  68.2 17.3 %copy-start.1 = (f32[3,9,17,512]{3,0,2,1:T(4,128)S(1)}, f32[3,9,17,512]{3,0,2,1:T(4,128)}, u32[]{:S(2)}) copy-start(f32[3,9,17,512]{3,0,2,1:T(4,128)} %param.15) | copy-start | bytes 2820100
  68.2 17.3 %copy-start.2 = (f32[3,9,17,512]{3,0,2,1:T(4,128)S(1)}, f32[3,9,17,512]{3,0,2,1:T(4,128)}, u32[]{:S(2)}) copy-start(f32[3,9,17,512]{3,0,2,1:T(4,128)} %param.16) | copy-start | bytes 2820100
  72.2 13.3 %copy-start = (f32[3,9,17,512]{3,0,2,1:T(4,128)S(1)}, f32[3,9,17,512]{3,0,2,1:T(4,128)}, u32[]{:S(2)}) copy-start(f32[3,9,17,512]{3,0,2,1:T(4,128)} %param.14) | copy-start | bytes 2820100
  72.2 9.3 %collective-permute-start.6 = (f32[30,8,128]{2,1,0:T(8,128)S(1)}, f32[30,8,128]{2,1,0:T(8,128)S(1)}, u32[]{:S(2)}, u32[]{:S(2)}) collective-permute-start(f32[30,8,128]{2,1,0:T(8,128)S(1)} %get-tuple-element.61), channel_id=1, source_target_pairs={{0,2},{2,0},{4,6},{6,4},{8,10},{10,8},{12,14},{14,12},{1,3},{3,1},... | collective-permute-start | bytes 368648 | tf_op jit(solution)/shard_map/ppermute | solution.py:602
  72.3 9.2 %collective-permute-start.7 = (f32[30,8,128]{2,1,0:T(8,128)S(1)}, f32[30,8,128]{2,1,0:T(8,128)S(1)}, u32[]{:S(2)}, u32[]{:S(2)}) collective-permute-start(f32[30,8,128]{2,1,0:T(8,128)S(1)} %get-tuple-element.62), channel_id=1, source_target_pairs={{2,4},{6,8},{10,12},{4,2},{8,6},{12,10},{3,5},{7,9},{11,13},{5,3},... | collective-permute-start | bytes 368648 | tf_op jit(solution)/shard_map/ppermute | solution.py:603
  81.6 7.4 %collective-permute-start.8 = (f32[15,8,128]{2,1,0:T(8,128)S(1)}, f32[15,8,128]{2,1,0:T(8,128)S(1)}, u32[]{:S(2)}, u32[]{:S(2)}) collective-permute-start(f32[15,8,128]{2,1,0:T(8,128)S(1)} %get-tuple-element.68), channel_id=1, source_target_pairs={{0,1},{1,0},{16,17},{17,16},{2,3},{3,2},{18,19},{19,18},{4,5},{5,4... | collective-permute-start | bytes 184328 | tf_op jit(solution)/shard_map/ppermute | solution.py:602
  81.7 7.3 %collective-permute-start.9 = (f32[15,8,128]{2,1,0:T(8,128)S(1)}, f32[15,8,128]{2,1,0:T(8,128)S(1)}, u32[]{:S(2)}, u32[]{:S(2)}) collective-permute-start(f32[15,8,128]{2,1,0:T(8,128)S(1)} %get-tuple-element.69), channel_id=1, source_target_pairs={{1,16},{16,1},{3,18},{18,3},{5,20},{20,5},{7,22},{22,7},{9,24},{24... | collective-permute-start | bytes 184328 | tf_op jit(solution)/shard_map/ppermute | solution.py:603

commit v9 on v8

--- a/solution.py
+++ b/solution.py
@@ -392,7 +392,7 @@
     return float(-1.0 / (half_size**3 * quad[i] * quad[j] * quad[k]))
 
 
-def first_kernel(nodes_y, u, v, a, density, momentum, energy, dest, slot, region, material,
+def first_kernel(nodes_y, u, v, a, density, momentum, energy, dest, slot, region, material, after,
                  b_out, bottoms, f_out, x1, x2, y_low, y_high, rows_low, rows_high, region_out,
                  elem, gx, gz, cross, planes, side, u_in, v_in, a_in, wide_u, wide_b, kept_u, kept_b, b_held,
                  cells, copies_held, dest_in, slot_in, region_in, semaphores):
@@ -797,7 +797,7 @@
     return [g - jnp.where(ends[0], 2.0 * f, pltpu.roll(g, 1, axis)) for f, g in zip(fluxes, upper)]
 
 
-def planes_kernel(density, momentum, energy, first, second, semaphores):
+def planes_kernel(density, momentum, energy, first, second, token, semaphores):
     odd = parity_x()
     pairs = []
     for out, down in ((first, odd), (second, 1 - odd)):
@@ -806,6 +806,7 @@
             pairs.append((density.at[plane], out.at[0, rows]))
             pairs.append((momentum.at[:, plane], out.at[pl.ds(1, 3), rows]))
             pairs.append((energy.at[plane], out.at[4, rows]))
+    token[...] = jnp.zeros((8, 128), f32)
     for copy in fetch(pairs, semaphores):
         copy.wait()
 
@@ -1059,14 +1060,14 @@
     crater = (density, momentum, energy)
     u, v, a = [jnp.transpose(x, (1, 2, 0, 3)) for x in (displacement, velocity_field, acceleration)]
     register, held_shape = (8, 128), (4, 1224, 128)
-    crater1, crater2 = call(
-        planes_kernel, crater, [(5, 64, 256), (5, 64, 256)], [], away=(0, 1, 2), out_away=(0, 1), mib=56, copies=12
+    crater1, crater2, token = call(
+        planes_kernel, crater, [(5, 64, 256), (5, 64, 256), register], [], away=(0, 1, 2), mib=56, copies=12
     )
     crater1, crater2 = exchange("gx", crater1, crater2)
     vectors = pltpu.VMEM((1, 128), jnp.int32)
     b, bottoms, f, x1, x2, y_low, y_high, rows_low, rows_high, region = call(
         functools.partial(first_kernel, float(nodes_y)),
-        (u, v, a) + crater + (face_dest.reshape(1, -1), face_slot, element_region_index, material),
+        (u, v, a) + crater + (face_dest.reshape(1, -1), face_slot, element_region_index, material, token),
         [element_shape, (devices, 24, 128), element_shape, (31, 8, 128), (31, 8, 128), (16, 8, 128), (15, 8, 128),
          (10, 8, 128), (10, 8, 128), register],
         internal_scratch

time: 92 us -> 76 us (0.83)
  Pallas kernels: 51.6 us -> 32.8 us
  waiting for transfers between devices: 11.2 us -> 13.8 us
    pallas_call x10, Pallas kernels: 51.6 us -> 32.8 us  [call(): pl.pallas_call(kernel, out_shape=[jax.ShapeDtypeStruct(s, f32) for s in o...]
    all_to_all x1, waiting for transfers between devices: 0.01 us -> 3.35 us  [shards(): bottoms = lax.all_to_all(bottoms, rank, 0, 0, tiled=True)]
  transfers between devices with their start and end apart: 11 -> 11, of which waited for: 2 -> 3; matrix products, arithmetic and copies ran while one was open for 0% -> 0% of each run, Pallas kernels for 38% -> 18%
where the time goes in v9:
time: 76 us; the launch traced here: 75.7 us
  Pallas kernels  32.8 us (43%)
  starting transfers between devices  27.1 us (36%)
  waiting for transfers between devices  13.8 us (18%)
  between operations  1.19 us (2%)
  local copies, waits for them, and re-layouts  0.77 us (1%)
    pallas_call x10, Pallas kernels, call(): pl.pallas_call(kernel, out_shape=[jax.ShapeDtypeStruct(s, f32) for s in o...  32.8 us
    ppermute x5, starting transfers between devices, exchange(): lax.ppermute(second, axis, pairs + [(j, i) for i, j in pairs])  19.5 us
    ppermute x5, waiting for transfers between devices, exchange(): first = lax.ppermute(first, axis, [(i, i ^ 1) for i in range(count)])  9.42 us
    all_to_all x1, starting transfers between devices, shards(): bottoms = lax.all_to_all(bottoms, rank, 0, 0, tiled=True)  6.45 us
    all_to_all x1, waiting for transfers between devices, shards(): bottoms = lax.all_to_all(bottoms, rank, 0, 0, tiled=True)  3.35 us
  transfers between devices with their start and end apart: 11, of which 3 were waited for; matrix products, arithmetic and copies ran while one was open for 0% of the time, Pallas kernels for 18%

profile of v9, /device:TPU:3, one launch (start us, length us, event | category | flops | bytes accessed | tf_op | source)
XLA Modules:
  0.0 75.7 jit_solution(11471512010696806828)
XLA Ops:
  0.6 2.1 %shard_map.138 = (f32[5,64,256]{2,1,0:T(8,128)}, f32[5,64,256]{2,1,0:T(8,128)}, f32[8,128]{1,0:T(8,128)}) custom-call(f32[4,32,256]{2,1,0:T(8,128)} %density.5, f32[3,4,32,256]{3,2,1,0:T(8,128)} %momentum.5, f32[4,32,256]{2,1,0:T(8,128)} %energy.5), custom_call_target="tpu_custom_call" | custom-call | tf_op jit(solution)/shard_map/pallas_call | solution.py:577
  2.8 0.0 copy-start.16
  2.8 0.0 copy-start.15
  2.8 10.3 %shard_map.139 = (f32[3,5,5,4,8,128]{5,4,3,2,1,0:T(8,128)}, f32[32,24,128]{2,1,0:T(8,128)}, f32[3,5,5,4,8,128]{5,4,3,2,1,0:T(8,128)}, f32[31,8,128]{2,1,0:T(8,12...) custom-call(f32[9,17,3,512]{3,2,1,0:T(4,128)} %bitcast.8, ...), custom_call_target="tpu_custom_call" | custom-call | tf_op jit(solution)/shard_map/pallas_call | solution.py:577
  13.1 0.0 copy-start.9
  13.1 0.0 copy-start.10
  13.1 0.0 copy-start.11
  13.1 0.0 copy-start.12
  13.1 0.0 copy-start.8
  13.1 0.0 copy-start.13
  13.2 6.4 %all-to-all-start = ((f32[32,24,128]{2,1,0:T(8,128)}), f32[32,24,128]{2,1,0:T(8,128)S(1)}, u32[]{:S(2)}, u32[]{:S(2)}) async-start(f32[32,24,128]{2,1,0:T(8,128)} %get-tuple-element.49), calls=%async_computation | async-start | bytes 786432 | tf_op jit(solution)/shard_map/all_to_all | solution.py:1083
  19.6 0.0 copy-done.16
  19.6 0.1 collective-permute-start
  19.8 0.0 copy-done.15
  19.8 4.2 %collective-permute-start.1 = (f32[5,64,256]{2,1,0:T(8,128)S(1)}, f32[5,64,256]{2,1,0:T(8,128)S(1)}, u32[]{:S(2)}, u32[]{:S(2)}) collective-permute-start(f32[5,64,256]{2,1,0:T(8,128)S(1)} %copy-done.15), channel_id=1, source_target_pairs={{2,4},{6,8},{10,12},{4,2},{8,6},{12,10},{3,5},{7,9},{11,13},{5,3},... | collective-permute-start | bytes 983048 | tf_op jit(solution)/shard_map/ppermute | solution.py:603
  24.0 0.1 collective-permute-start.2
  24.0 4.3 %collective-permute-start.3 = (f32[31,8,128]{2,1,0:T(8,128)}, f32[31,8,128]{2,1,0:T(8,128)S(1)}, u32[]{:S(2)}, u32[]{:S(2)}) collective-permute-start(f32[31,8,128]{2,1,0:T(8,128)} %get-tuple-element.46), channel_id=1, source_target_pairs={{2,4},{6,8},{10,12},{4,2},{8,6},{12,10},{3,5},{7,9},{11,13},{5,3},... | collective-permute-start | bytes 380936 | tf_op jit(solution)/shard_map/ppermute | solution.py:603
  28.3 3.4 %all-to-all-done.bottoms = f32[32,24,128]{2,1,0:T(8,128)S(1)} async-done(((f32[32,24,128]{2,1,0:T(8,128)}), f32[32,24,128]{2,1,0:T(8,128)S(1)}, u32[]{:S(2)}, u32[]{:S(2)}) %all-to-all-start) | async-done | bytes 393248 | tf_op jit(solution)/shard_map/all_to_all | solution.py:1083
  31.7 0.7 copy-done.14
  32.3 2.8 %shard_map.140.after.total = f32[360,128]{1,0:T(8,128)S(1)} custom-call(f32[768,128]{1,0:T(8,128)S(1)} %bitcast.14, f32[8,128]{1,0:T(8,128)S(1)} %copy-done.14), custom_call_target="tpu_custom_call" | custom-call | tf_op jit(solution)/shard_map/pallas_call | solution.py:577
  35.1 0.0 copy-start.4
  35.1 9.4 %collective-permute-done.2.came1.came_x1 = f32[31,8,128]{2,1,0:T(8,128)S(1)} collective-permute-done((f32[31,8,128]{2,1,0:T(8,128)}, f32[31,8,128]{2,1,0:T(8,128)S(1)}, u32[]{:S(2)}, u32[]{:S(2)}) %collective-permute-start.2) | collective-permute-done | bytes 127008 | tf_op jit(solution)/shard_map/ppermute | solution.py:602
  44.5 0.0 collective-permute-done.3.came2.came_x2
  44.5 0.0 collective-permute-done.crater1.came1
  44.5 0.0 collective-permute-done.1.crater2.came2
  44.6 0.2 shard_map.141
  44.8 0.8 %collective-permute-start.4 = (f32[38,8,128]{2,1,0:T(8,128)S(1)}, f32[38,8,128]{2,1,0:T(8,128)S(1)}, u32[]{:S(2)}, u32[]{:S(2)}) collective-permute-start(f32[38,8,128]{2,1,0:T(8,128)S(1)} %get-tuple-element.51), channel_id=1, source_target_pairs={{0,1},{1,0},{16,17},{17,16},{2,3},{3,2},{18,19},{19,18},{4,5},{5,4... | collective-permute-start | bytes 466952 | tf_op jit(solution)/shard_map/ppermute | solution.py:602
  45.6 3.0 %collective-permute-start.5 = (f32[38,8,128]{2,1,0:T(8,128)S(1)}, f32[38,8,128]{2,1,0:T(8,128)S(1)}, u32[]{:S(2)}, u32[]{:S(2)}) collective-permute-start(f32[38,8,128]{2,1,0:T(8,128)S(1)} %get-tuple-element.52), channel_id=1, source_target_pairs={{1,16},{16,1},{3,18},{18,3},{5,20},{20,5},{7,22},{22,7},{9,24},{24... | collective-permute-start | bytes 466952 | tf_op jit(solution)/shard_map/ppermute | solution.py:603
  48.7 0.0 copy-start.7
  48.7 2.5 %shard_map.142 = (f32[24,256]{1,0:T(8,128)S(1)}, f32[24,256]{1,0:T(8,128)S(1)}, f32[8,128]{1,0:T(8,128)S(1)}) custom-call(f32[360,128]{1,0:T(8,128)S(1)} %shard_map.140.after.total, f32[32,24,128]{2,1,0:T(8,128)S(1)} %all-to-all-done.bottoms, f32[3,8]{1,0:T(4,128)S(1)} %copy-done.13, f32[6,128,128]{2,1,0:T(8,128)S(1)} %copy-done.8, ...), custom_call_target="tpu_custom_call" | custom-call | tf_op jit(solution)/shard_map/pallas_call | solution.py:577
  51.1 0.0 collective-permute-done.4.came_y1.rows1
  51.1 1.0 %collective-permute-done.5.came_y2.rows2 = f32[38,8,128]{2,1,0:T(8,128)S(1)} collective-permute-done((f32[38,8,128]{2,1,0:T(8,128)S(1)}, f32[38,8,128]{2,1,0:T(8,128)S(1)}, u32[]{:S(2)}, u32[]{:S(2)}) %collective-permute-start.5) | collective-permute-done | bytes 155680 | tf_op jit(solution)/shard_map/ppermute | solution.py:603
  52.2 0.0 copy-start.1
  52.2 0.0 copy-start.2
  52.2 4.1 %shard_map.143 = (f32[3,5,5,4,8,128]{5,4,3,2,1,0:T(8,128)S(1)}, f32[3,5,5,4,8,128]{5,4,3,2,1,0:T(8,128)S(1)}, f32[30,8,128]{2,1,0:T(8,128)S(1)}, f32[30,8,128]{2...) custom-call(f32[3,5,5,4,8,128]{5,4,3,2,1,0:T(8,128)S(1)} %copy-done., ...), custom_call_target="tpu_custom_call" | custom-call | tf_op jit(solution)/shard_map/pallas_call | solution.py:577
  56.2 0.0 copy-start
  56.3 0.1 collective-permute-start.6
  56.3 4.4 %collective-permute-start.7 = (f32[30,8,128]{2,1,0:T(8,128)S(1)}, f32[30,8,128]{2,1,0:T(8,128)S(1)}, u32[]{:S(2)}, u32[]{:S(2)}) collective-permute-start(f32[30,8,128]{2,1,0:T(8,128)S(1)} %get-tuple-element.64), channel_id=1, source_target_pairs={{2,4},{6,8},{10,12},{4,2},{8,6},{12,10},{3,5},{7,9},{11,13},{5,3},... | collective-permute-start | bytes 368648 | tf_op jit(solution)/shard_map/ppermute | solution.py:603
  60.8 4.9 %shard_map.144 = (f32[5,4,32,256]{3,2,1,0:T(8,128)}, f32[8,128]{1,0:T(8,128)S(1)}) custom-call(f32[4,32,256]{2,1,0:T(8,128)S(1)} %copy-done.6, f32[3,4,32,256]{3,2,1,0:T(8,128)S(1)} %copy-done.3, f32[4,32,256]{2,1,0:T(8,128)S(1)} %copy-done.7, f32[5,64,256]{2,1,0:T(8,128)S(1)} %collective-permute-done.crater1.came1, ...), custom_call_target="tpu_custom_call" | custom-call | tf_op jit(solution)/shard_map/pallas_call | solution.py:577
  65.7 0.0 collective-permute-done.6.came1.x1
  65.7 0.0 collective-permute-done.7.came2.x2
  65.7 0.1 shard_map.145
  65.8 0.1 collective-permute-start.8
  65.9 3.6 %collective-permute-start.9 = (f32[15,8,128]{2,1,0:T(8,128)S(1)}, f32[15,8,128]{2,1,0:T(8,128)S(1)}, u32[]{:S(2)}, u32[]{:S(2)}) collective-permute-start(f32[15,8,128]{2,1,0:T(8,128)S(1)} %get-tuple-element.71), channel_id=1, source_target_pairs={{1,16},{16,1},{3,18},{18,3},{5,20},{20,5},{7,22},{22,7},{9,24},{24... | collective-permute-start | bytes 184328 | tf_op jit(solution)/shard_map/ppermute | solution.py:603
  69.5 3.5 %shard_map.146 = (f32[9,17,3,512]{3,2,1,0:T(4,128)}, f32[4,1224,128]{2,1,0:T(8,128)S(1)}) custom-call(f32[3,5,5,4,8,128]{5,4,3,2,1,0:T(8,128)S(1)} %get-tuple-element.59.a1, f32[24,256]{1,0:T(8,128)S(1)} %get-tuple-element.60.surf1, f32[9,17,3,512]{3,2,1,0:T(4,128)S(1)} %bitcast.9, f32[9,17,3,512]{3,2,1,0:T(4,128)S(1)} %bitcast.11, ...), custom_call_target="tpu_custom_call" | custom-call | tf_op jit(solution)/shard_map/pallas_call | solution.py:577
  73.0 0.0 collective-permute-done.8.y1
  73.1 0.0 collective-permute-done.9.y2
  73.1 2.4 %shard_map.147 = (f32[9,17,3,512]{3,2,1,0:T(4,128)}, f32[9,17,3,512]{3,2,1,0:T(4,128)}) custom-call(f32[4,1224,128]{2,1,0:T(8,128)S(1)} %get-tuple-element.68.v_part, f32[3,5,5,4,8,128]{5,4,3,2,1,0:T(8,128)S(1)} %get-tuple-element.69.f, f32[30,8,128]{2,1,0:T(8,128)S(1)} %collective-permute-done.6.came1.x1, ...), custom_call_target="tpu_custom_call" | custom-call | tf_op jit(solution)/shard_map/pallas_call | solution.py:577
  (18 shorter events, 0.0 us)
Async XLA Ops:
  2.8 16.9 %copy-start.16 = (f32[5,64,256]{2,1,0:T(8,128)S(1)}, f32[5,64,256]{2,1,0:T(8,128)}, u32[]{:S(2)}) copy-start(f32[5,64,256]{2,1,0:T(8,128)} %get-tuple-element.40) | copy-start | bytes 983044
  2.8 17.0 %copy-start.15 = (f32[5,64,256]{2,1,0:T(8,128)S(1)}, f32[5,64,256]{2,1,0:T(8,128)}, u32[]{:S(2)}) copy-start(f32[5,64,256]{2,1,0:T(8,128)} %get-tuple-element.41) | copy-start | bytes 983044
  13.1 31.5 %copy-start.9 = (f32[16,8,128]{2,1,0:T(8,128)S(1)}, f32[16,8,128]{2,1,0:T(8,128)}, u32[]{:S(2)}) copy-start(f32[16,8,128]{2,1,0:T(8,128)} %get-tuple-element.43.low) | copy-start | bytes 196612
  13.1 31.5 %copy-start.10 = (f32[15,8,128]{2,1,0:T(8,128)S(1)}, f32[15,8,128]{2,1,0:T(8,128)}, u32[]{:S(2)}) copy-start(f32[15,8,128]{2,1,0:T(8,128)} %get-tuple-element.44.high) | copy-start | bytes 184324
  13.1 31.5 %copy-start.11 = (f32[10,8,128]{2,1,0:T(8,128)S(1)}, f32[10,8,128]{2,1,0:T(8,128)}, u32[]{:S(2)}) copy-start(f32[10,8,128]{2,1,0:T(8,128)} %get-tuple-element.47.rows_low) | copy-start | bytes 122884
  13.1 31.5 %copy-start.12 = (f32[10,8,128]{2,1,0:T(8,128)S(1)}, f32[10,8,128]{2,1,0:T(8,128)}, u32[]{:S(2)}) copy-start(f32[10,8,128]{2,1,0:T(8,128)} %get-tuple-element.48.rows_high) | copy-start | bytes 122884
  13.1 35.5 %copy-start.8 = (f32[6,128,128]{2,1,0:T(8,128)S(1)}, f32[6,128,128]{2,1,0:T(8,128)}, u32[]{:S(2)}) copy-start(f32[6,128,128]{2,1,0:T(8,128)} %constant.2.clone.tables) | copy-start | bytes 1179652
  13.1 35.5 %copy-start.13 = (f32[3,8]{1,0:T(4,128)S(1)}, f32[3,8]{1,0:T(4,128)}, u32[]{:S(2)}) copy-start(f32[3,8]{1,0:T(4,128)} %material.5) | copy-start | bytes 292
  13.2 18.5 %all-to-all-start = ((f32[32,24,128]{2,1,0:T(8,128)}), f32[32,24,128]{2,1,0:T(8,128)S(1)}, u32[]{:S(2)}, u32[]{:S(2)}) async-start(f32[32,24,128]{2,1,0:T(8,128)} %get-tuple-element.49), calls=%async_computation | async-start | bytes 786432 | tf_op jit(solution)/shard_map/all_to_all | solution.py:1083
  19.6 24.9 %collective-permute-start = (f32[5,64,256]{2,1,0:T(8,128)S(1)}, f32[5,64,256]{2,1,0:T(8,128)S(1)}, u32[]{:S(2)}, u32[]{:S(2)}) collective-permute-start(f32[5,64,256]{2,1,0:T(8,128)S(1)} %copy-done.16), channel_id=1, source_target_pairs={{0,2},{2,0},{4,6},{6,4},{8,10},{10,8},{12,14},{14,12},{1,3},{3,1},... | collective-permute-start | bytes 983048 | tf_op jit(solution)/shard_map/ppermute | solution.py:602
  19.8 24.8 %collective-permute-start.1 = (f32[5,64,256]{2,1,0:T(8,128)S(1)}, f32[5,64,256]{2,1,0:T(8,128)S(1)}, u32[]{:S(2)}, u32[]{:S(2)}) collective-permute-start(f32[5,64,256]{2,1,0:T(8,128)S(1)} %copy-done.15), channel_id=1, source_target_pairs={{2,4},{6,8},{10,12},{4,2},{8,6},{12,10},{3,5},{7,9},{11,13},{5,3},... | collective-permute-start | bytes 983048 | tf_op jit(solution)/shard_map/ppermute | solution.py:603
  24.0 20.6 %collective-permute-start.2 = (f32[31,8,128]{2,1,0:T(8,128)}, f32[31,8,128]{2,1,0:T(8,128)S(1)}, u32[]{:S(2)}, u32[]{:S(2)}) collective-permute-start(f32[31,8,128]{2,1,0:T(8,128)} %get-tuple-element.45), channel_id=1, source_target_pairs={{0,2},{2,0},{4,6},{6,4},{8,10},{10,8},{12,14},{14,12},{1,3},{3,1},... | collective-permute-start | bytes 380936 | tf_op jit(solution)/shard_map/ppermute | solution.py:602
  24.0 20.5 %collective-permute-start.3 = (f32[31,8,128]{2,1,0:T(8,128)}, f32[31,8,128]{2,1,0:T(8,128)S(1)}, u32[]{:S(2)}, u32[]{:S(2)}) collective-permute-start(f32[31,8,128]{2,1,0:T(8,128)} %get-tuple-element.46), channel_id=1, source_target_pairs={{2,4},{6,8},{10,12},{4,2},{8,6},{12,10},{3,5},{7,9},{11,13},{5,3},... | collective-permute-start | bytes 380936 | tf_op jit(solution)/shard_map/ppermute | solution.py:603
  31.6 0.7 copy-start.14
  32.3 19.8 %copy-start.5 = (f32[3,5,5,4,8,128]{5,4,3,2,1,0:T(8,128)S(1)}, f32[3,5,5,4,8,128]{5,4,3,2,1,0:T(8,128)}, u32[]{:S(2)}) copy-start(f32[3,5,5,4,8,128]{5,4,3,2,1,0:T(8,128)} %get-tuple-element.54.f) | copy-start | bytes 3686404
  35.1 17.0 %copy-start.4 = (f32[3,5,5,4,8,128]{5,4,3,2,1,0:T(8,128)S(1)}, f32[3,5,5,4,8,128]{5,4,3,2,1,0:T(8,128)}, u32[]{:S(2)}) copy-start(f32[3,5,5,4,8,128]{5,4,3,2,1,0:T(8,128)} %get-tuple-element.53.b) | copy-start | bytes 3686404
  44.8 6.4 %collective-permute-start.4 = (f32[38,8,128]{2,1,0:T(8,128)S(1)}, f32[38,8,128]{2,1,0:T(8,128)S(1)}, u32[]{:S(2)}, u32[]{:S(2)}) collective-permute-start(f32[38,8,128]{2,1,0:T(8,128)S(1)} %get-tuple-element.51), channel_id=1, source_target_pairs={{0,1},{1,0},{16,17},{17,16},{2,3},{3,2},{18,19},{19,18},{4,5},{5,4... | collective-permute-start | bytes 466952 | tf_op jit(solution)/shard_map/ppermute | solution.py:602
  45.6 6.5 %collective-permute-start.5 = (f32[38,8,128]{2,1,0:T(8,128)S(1)}, f32[38,8,128]{2,1,0:T(8,128)S(1)}, u32[]{:S(2)}, u32[]{:S(2)}) collective-permute-start(f32[38,8,128]{2,1,0:T(8,128)S(1)} %get-tuple-element.52), channel_id=1, source_target_pairs={{1,16},{16,1},{3,18},{18,3},{5,20},{20,5},{7,22},{22,7},{9,24},{24... | collective-permute-start | bytes 466952 | tf_op jit(solution)/shard_map/ppermute | solution.py:603
  48.7 12.1 %copy-start.7 = (f32[4,32,256]{2,1,0:T(8,128)S(1)}, f32[4,32,256]{2,1,0:T(8,128)}, u32[]{:S(2)}) copy-start(f32[4,32,256]{2,1,0:T(8,128)} %energy.5) | copy-start | bytes 393220
  52.1 8.6 %copy-start.3 = (f32[3,4,32,256]{3,2,1,0:T(8,128)S(1)}, f32[3,4,32,256]{3,2,1,0:T(8,128)}, u32[]{:S(2)}) copy-start(f32[3,4,32,256]{3,2,1,0:T(8,128)} %momentum.5) | copy-start | bytes 1179652
  52.1 8.6 %copy-start.6 = (f32[4,32,256]{2,1,0:T(8,128)S(1)}, f32[4,32,256]{2,1,0:T(8,128)}, u32[]{:S(2)}) copy-start(f32[4,32,256]{2,1,0:T(8,128)} %density.5) | copy-start | bytes 393220
  52.2 17.3 %copy-start.1 = (f32[3,9,17,512]{3,0,2,1:T(4,128)S(1)}, f32[3,9,17,512]{3,0,2,1:T(4,128)}, u32[]{:S(2)}) copy-start(f32[3,9,17,512]{3,0,2,1:T(4,128)} %param.15) | copy-start | bytes 2820100
  52.2 17.3 %copy-start.2 = (f32[3,9,17,512]{3,0,2,1:T(4,128)S(1)}, f32[3,9,17,512]{3,0,2,1:T(4,128)}, u32[]{:S(2)}) copy-start(f32[3,9,17,512]{3,0,2,1:T(4,128)} %param.16) | copy-start | bytes 2820100
  56.2 13.3 %copy-start = (f32[3,9,17,512]{3,0,2,1:T(4,128)S(1)}, f32[3,9,17,512]{3,0,2,1:T(4,128)}, u32[]{:S(2)}) copy-start(f32[3,9,17,512]{3,0,2,1:T(4,128)} %param.14) | copy-start | bytes 2820100
  56.3 9.5 %collective-permute-start.6 = (f32[30,8,128]{2,1,0:T(8,128)S(1)}, f32[30,8,128]{2,1,0:T(8,128)S(1)}, u32[]{:S(2)}, u32[]{:S(2)}) collective-permute-start(f32[30,8,128]{2,1,0:T(8,128)S(1)} %get-tuple-element.63), channel_id=1, source_target_pairs={{0,2},{2,0},{4,6},{6,4},{8,10},{10,8},{12,14},{14,12},{1,3},{3,1},... | collective-permute-start | bytes 368648 | tf_op jit(solution)/shard_map/ppermute | solution.py:602
  56.3 9.4 %collective-permute-start.7 = (f32[30,8,128]{2,1,0:T(8,128)S(1)}, f32[30,8,128]{2,1,0:T(8,128)S(1)}, u32[]{:S(2)}, u32[]{:S(2)}) collective-permute-start(f32[30,8,128]{2,1,0:T(8,128)S(1)} %get-tuple-element.64), channel_id=1, source_target_pairs={{2,4},{6,8},{10,12},{4,2},{8,6},{12,10},{3,5},{7,9},{11,13},{5,3},... | collective-permute-start | bytes 368648 | tf_op jit(solution)/shard_map/ppermute | solution.py:603
  65.8 7.2 %collective-permute-start.8 = (f32[15,8,128]{2,1,0:T(8,128)S(1)}, f32[15,8,128]{2,1,0:T(8,128)S(1)}, u32[]{:S(2)}, u32[]{:S(2)}) collective-permute-start(f32[15,8,128]{2,1,0:T(8,128)S(1)} %get-tuple-element.70), channel_id=1, source_target_pairs={{0,1},{1,0},{16,17},{17,16},{2,3},{3,2},{18,19},{19,18},{4,5},{5,4... | collective-permute-start | bytes 184328 | tf_op jit(solution)/shard_map/ppermute | solution.py:602
  65.9 7.2 %collective-permute-start.9 = (f32[15,8,128]{2,1,0:T(8,128)S(1)}, f32[15,8,128]{2,1,0:T(8,128)S(1)}, u32[]{:S(2)}, u32[]{:S(2)}) collective-permute-start(f32[15,8,128]{2,1,0:T(8,128)S(1)} %get-tuple-element.71), channel_id=1, source_target_pairs={{1,16},{16,1},{3,18},{18,3},{5,20},{20,5},{7,22},{22,7},{9,24},{24... | collective-permute-start | bytes 184328 | tf_op jit(solution)/shard_map/ppermute | solution.py:603

commit v10 on v9

--- a/solution.py
+++ b/solution.py
@@ -581,6 +581,7 @@
         out_specs=[pl.BlockSpec(memory_space=pltpu.HBM) if n in out_away else whole() for n in range(len(outs))],
         scratch_shapes=scratch + ([pltpu.SemaphoreType.DMA((copies,))] if copies else []),
         compiler_params=pltpu.CompilerParams(vmem_limit_bytes=mib * 1024 * 1024),
+        cost_estimate=pl.CostEstimate(flops=0, bytes_accessed=0, transcendentals=0),
     )(*ins)
 
 

time: 76 us -> 76 us (level)
  no operation moved by 1% of the time
where the time goes in v10:
time: 76 us; the launch traced here: 75.7 us
  Pallas kernels  32.8 us (43%)
  starting transfers between devices  27.1 us (36%)
  waiting for transfers between devices  13.8 us (18%)
  between operations  1.19 us (2%)
  local copies, waits for them, and re-layouts  0.77 us (1%)
    pallas_call x10, Pallas kernels, call(): pl.pallas_call(kernel, out_shape=[jax.ShapeDtypeStruct(s, f32) for s in o...  32.8 us
    ppermute x5, starting transfers between devices, exchange(): lax.ppermute(second, axis, pairs + [(j, i) for i, j in pairs])  19.5 us
    ppermute x5, waiting for transfers between devices, exchange(): first = lax.ppermute(first, axis, [(i, i ^ 1) for i in range(count)])  9.42 us
    all_to_all x1, starting transfers between devices, shards(): bottoms = lax.all_to_all(bottoms, rank, 0, 0, tiled=True)  6.45 us
    all_to_all x1, waiting for transfers between devices, shards(): bottoms = lax.all_to_all(bottoms, rank, 0, 0, tiled=True)  3.35 us
  transfers between devices with their start and end apart: 11, of which 3 were waited for; matrix products, arithmetic and copies ran while one was open for 0% of the time, Pallas kernels for 18%

profile of v10, /device:TPU:3, one launch (start us, length us, event | category | flops | bytes accessed | tf_op | source)
XLA Modules:
  0.0 75.7 jit_solution(11471512010696806828)
XLA Ops:
  0.6 2.1 %shard_map.138 = (f32[5,64,256]{2,1,0:T(8,128)}, f32[5,64,256]{2,1,0:T(8,128)}, f32[8,128]{1,0:T(8,128)}) custom-call(f32[4,32,256]{2,1,0:T(8,128)} %density.5, f32[3,4,32,256]{3,2,1,0:T(8,128)} %momentum.5, f32[4,32,256]{2,1,0:T(8,128)} %energy.5), custom_call_target="tpu_custom_call" | custom-call | tf_op jit(solution)/shard_map/pallas_call | solution.py:577
  2.8 0.0 copy-start.16
  2.8 0.0 copy-start.15
  2.8 10.3 %shard_map.139 = (f32[3,5,5,4,8,128]{5,4,3,2,1,0:T(8,128)}, f32[32,24,128]{2,1,0:T(8,128)}, f32[3,5,5,4,8,128]{5,4,3,2,1,0:T(8,128)}, f32[31,8,128]{2,1,0:T(8,12...) custom-call(f32[9,17,3,512]{3,2,1,0:T(4,128)} %bitcast.8, ...), custom_call_target="tpu_custom_call" | custom-call | tf_op jit(solution)/shard_map/pallas_call | solution.py:577
  13.1 0.0 copy-start.9
  13.1 0.0 copy-start.10
  13.1 0.0 copy-start.11
  13.1 0.0 copy-start.12
  13.1 0.0 copy-start.8
  13.1 0.0 copy-start.13
  13.2 6.4 %all-to-all-start = ((f32[32,24,128]{2,1,0:T(8,128)}), f32[32,24,128]{2,1,0:T(8,128)S(1)}, u32[]{:S(2)}, u32[]{:S(2)}) async-start(f32[32,24,128]{2,1,0:T(8,128)} %get-tuple-element.49), calls=%async_computation | async-start | bytes 786432 | tf_op jit(solution)/shard_map/all_to_all | solution.py:1084
  19.6 0.0 copy-done.16
  19.6 0.1 collective-permute-start
  19.8 0.0 copy-done.15
  19.8 4.2 %collective-permute-start.1 = (f32[5,64,256]{2,1,0:T(8,128)S(1)}, f32[5,64,256]{2,1,0:T(8,128)S(1)}, u32[]{:S(2)}, u32[]{:S(2)}) collective-permute-start(f32[5,64,256]{2,1,0:T(8,128)S(1)} %copy-done.15), channel_id=1, source_target_pairs={{2,4},{6,8},{10,12},{4,2},{8,6},{12,10},{3,5},{7,9},{11,13},{5,3},... | collective-permute-start | bytes 983048 | tf_op jit(solution)/shard_map/ppermute | solution.py:604
  24.0 0.1 collective-permute-start.2
  24.0 4.3 %collective-permute-start.3 = (f32[31,8,128]{2,1,0:T(8,128)}, f32[31,8,128]{2,1,0:T(8,128)S(1)}, u32[]{:S(2)}, u32[]{:S(2)}) collective-permute-start(f32[31,8,128]{2,1,0:T(8,128)} %get-tuple-element.46), channel_id=1, source_target_pairs={{2,4},{6,8},{10,12},{4,2},{8,6},{12,10},{3,5},{7,9},{11,13},{5,3},... | collective-permute-start | bytes 380936 | tf_op jit(solution)/shard_map/ppermute | solution.py:604
  28.3 3.4 %all-to-all-done.bottoms = f32[32,24,128]{2,1,0:T(8,128)S(1)} async-done(((f32[32,24,128]{2,1,0:T(8,128)}), f32[32,24,128]{2,1,0:T(8,128)S(1)}, u32[]{:S(2)}, u32[]{:S(2)}) %all-to-all-start) | async-done | bytes 393248 | tf_op jit(solution)/shard_map/all_to_all | solution.py:1084
  31.7 0.7 copy-done.14
  32.3 2.8 %shard_map.140.after.total = f32[360,128]{1,0:T(8,128)S(1)} custom-call(f32[768,128]{1,0:T(8,128)S(1)} %bitcast.14, f32[8,128]{1,0:T(8,128)S(1)} %copy-done.14), custom_call_target="tpu_custom_call" | custom-call | tf_op jit(solution)/shard_map/pallas_call | solution.py:577
  35.1 0.0 copy-start.4
  35.1 9.4 %collective-permute-done.2.came1.came_x1 = f32[31,8,128]{2,1,0:T(8,128)S(1)} collective-permute-done((f32[31,8,128]{2,1,0:T(8,128)}, f32[31,8,128]{2,1,0:T(8,128)S(1)}, u32[]{:S(2)}, u32[]{:S(2)}) %collective-permute-start.2) | collective-permute-done | bytes 127008 | tf_op jit(solution)/shard_map/ppermute | solution.py:603
  44.5 0.0 collective-permute-done.3.came2.came_x2
  44.5 0.0 collective-permute-done.crater1.came1
  44.5 0.0 collective-permute-done.1.crater2.came2
  44.6 0.2 shard_map.141
  44.8 0.8 %collective-permute-start.4 = (f32[38,8,128]{2,1,0:T(8,128)S(1)}, f32[38,8,128]{2,1,0:T(8,128)S(1)}, u32[]{:S(2)}, u32[]{:S(2)}) collective-permute-start(f32[38,8,128]{2,1,0:T(8,128)S(1)} %get-tuple-element.51), channel_id=1, source_target_pairs={{0,1},{1,0},{16,17},{17,16},{2,3},{3,2},{18,19},{19,18},{4,5},{5,4... | collective-permute-start | bytes 466952 | tf_op jit(solution)/shard_map/ppermute | solution.py:603
  45.6 3.0 %collective-permute-start.5 = (f32[38,8,128]{2,1,0:T(8,128)S(1)}, f32[38,8,128]{2,1,0:T(8,128)S(1)}, u32[]{:S(2)}, u32[]{:S(2)}) collective-permute-start(f32[38,8,128]{2,1,0:T(8,128)S(1)} %get-tuple-element.52), channel_id=1, source_target_pairs={{1,16},{16,1},{3,18},{18,3},{5,20},{20,5},{7,22},{22,7},{9,24},{24... | collective-permute-start | bytes 466952 | tf_op jit(solution)/shard_map/ppermute | solution.py:604
  48.7 0.0 copy-start.7
  48.7 2.5 %shard_map.142 = (f32[24,256]{1,0:T(8,128)S(1)}, f32[24,256]{1,0:T(8,128)S(1)}, f32[8,128]{1,0:T(8,128)S(1)}) custom-call(f32[360,128]{1,0:T(8,128)S(1)} %shard_map.140.after.total, f32[32,24,128]{2,1,0:T(8,128)S(1)} %all-to-all-done.bottoms, f32[3,8]{1,0:T(4,128)S(1)} %copy-done.13, f32[6,128,128]{2,1,0:T(8,128)S(1)} %copy-done.8, ...), custom_call_target="tpu_custom_call" | custom-call | tf_op jit(solution)/shard_map/pallas_call | solution.py:577
  51.1 0.0 collective-permute-done.4.came_y1.rows1
  51.1 1.0 %collective-permute-done.5.came_y2.rows2 = f32[38,8,128]{2,1,0:T(8,128)S(1)} collective-permute-done((f32[38,8,128]{2,1,0:T(8,128)S(1)}, f32[38,8,128]{2,1,0:T(8,128)S(1)}, u32[]{:S(2)}, u32[]{:S(2)}) %collective-permute-start.5) | collective-permute-done | bytes 155680 | tf_op jit(solution)/shard_map/ppermute | solution.py:604
  52.2 0.0 copy-start.1
  52.2 0.0 copy-start.2
  52.2 4.1 %shard_map.143 = (f32[3,5,5,4,8,128]{5,4,3,2,1,0:T(8,128)S(1)}, f32[3,5,5,4,8,128]{5,4,3,2,1,0:T(8,128)S(1)}, f32[30,8,128]{2,1,0:T(8,128)S(1)}, f32[30,8,128]{2...) custom-call(f32[3,5,5,4,8,128]{5,4,3,2,1,0:T(8,128)S(1)} %copy-done., ...), custom_call_target="tpu_custom_call" | custom-call | tf_op jit(solution)/shard_map/pallas_call | solution.py:577
  56.2 0.0 copy-start
  56.3 0.1 collective-permute-start.6
  56.3 4.4 %collective-permute-start.7 = (f32[30,8,128]{2,1,0:T(8,128)S(1)}, f32[30,8,128]{2,1,0:T(8,128)S(1)}, u32[]{:S(2)}, u32[]{:S(2)}) collective-permute-start(f32[30,8,128]{2,1,0:T(8,128)S(1)} %get-tuple-element.64), channel_id=1, source_target_pairs={{2,4},{6,8},{10,12},{4,2},{8,6},{12,10},{3,5},{7,9},{11,13},{5,3},... | collective-permute-start | bytes 368648 | tf_op jit(solution)/shard_map/ppermute | solution.py:604
  60.8 4.9 %shard_map.144 = (f32[5,4,32,256]{3,2,1,0:T(8,128)}, f32[8,128]{1,0:T(8,128)S(1)}) custom-call(f32[4,32,256]{2,1,0:T(8,128)S(1)} %copy-done.6, f32[3,4,32,256]{3,2,1,0:T(8,128)S(1)} %copy-done.3, f32[4,32,256]{2,1,0:T(8,128)S(1)} %copy-done.7, f32[5,64,256]{2,1,0:T(8,128)S(1)} %collective-permute-done.crater1.came1, ...), custom_call_target="tpu_custom_call" | custom-call | tf_op jit(solution)/shard_map/pallas_call | solution.py:577
  65.7 0.0 collective-permute-done.6.came1.x1
  65.7 0.0 collective-permute-done.7.came2.x2
  65.7 0.1 shard_map.145
  65.8 0.1 collective-permute-start.8
  65.9 3.6 %collective-permute-start.9 = (f32[15,8,128]{2,1,0:T(8,128)S(1)}, f32[15,8,128]{2,1,0:T(8,128)S(1)}, u32[]{:S(2)}, u32[]{:S(2)}) collective-permute-start(f32[15,8,128]{2,1,0:T(8,128)S(1)} %get-tuple-element.71), channel_id=1, source_target_pairs={{1,16},{16,1},{3,18},{18,3},{5,20},{20,5},{7,22},{22,7},{9,24},{24... | collective-permute-start | bytes 184328 | tf_op jit(solution)/shard_map/ppermute | solution.py:604
  69.5 3.5 %shard_map.146 = (f32[9,17,3,512]{3,2,1,0:T(4,128)}, f32[4,1224,128]{2,1,0:T(8,128)S(1)}) custom-call(f32[3,5,5,4,8,128]{5,4,3,2,1,0:T(8,128)S(1)} %get-tuple-element.59.a1, f32[24,256]{1,0:T(8,128)S(1)} %get-tuple-element.60.surf1, f32[9,17,3,512]{3,2,1,0:T(4,128)S(1)} %bitcast.9, f32[9,17,3,512]{3,2,1,0:T(4,128)S(1)} %bitcast.11, ...), custom_call_target="tpu_custom_call" | custom-call | tf_op jit(solution)/shard_map/pallas_call | solution.py:577
  73.0 0.0 collective-permute-done.8.y1
  73.1 0.0 collective-permute-done.9.y2
  73.1 2.4 %shard_map.147 = (f32[9,17,3,512]{3,2,1,0:T(4,128)}, f32[9,17,3,512]{3,2,1,0:T(4,128)}) custom-call(f32[4,1224,128]{2,1,0:T(8,128)S(1)} %get-tuple-element.68.v_part, f32[3,5,5,4,8,128]{5,4,3,2,1,0:T(8,128)S(1)} %get-tuple-element.69.f, f32[30,8,128]{2,1,0:T(8,128)S(1)} %collective-permute-done.6.came1.x1, ...), custom_call_target="tpu_custom_call" | custom-call | tf_op jit(solution)/shard_map/pallas_call | solution.py:577
  (18 shorter events, 0.0 us)
Async XLA Ops:
  2.8 16.9 %copy-start.16 = (f32[5,64,256]{2,1,0:T(8,128)S(1)}, f32[5,64,256]{2,1,0:T(8,128)}, u32[]{:S(2)}) copy-start(f32[5,64,256]{2,1,0:T(8,128)} %get-tuple-element.40) | copy-start | bytes 983044
  2.8 17.0 %copy-start.15 = (f32[5,64,256]{2,1,0:T(8,128)S(1)}, f32[5,64,256]{2,1,0:T(8,128)}, u32[]{:S(2)}) copy-start(f32[5,64,256]{2,1,0:T(8,128)} %get-tuple-element.41) | copy-start | bytes 983044
  13.1 31.5 %copy-start.9 = (f32[16,8,128]{2,1,0:T(8,128)S(1)}, f32[16,8,128]{2,1,0:T(8,128)}, u32[]{:S(2)}) copy-start(f32[16,8,128]{2,1,0:T(8,128)} %get-tuple-element.43.low) | copy-start | bytes 196612
  13.1 31.5 %copy-start.10 = (f32[15,8,128]{2,1,0:T(8,128)S(1)}, f32[15,8,128]{2,1,0:T(8,128)}, u32[]{:S(2)}) copy-start(f32[15,8,128]{2,1,0:T(8,128)} %get-tuple-element.44.high) | copy-start | bytes 184324
  13.1 31.5 %copy-start.11 = (f32[10,8,128]{2,1,0:T(8,128)S(1)}, f32[10,8,128]{2,1,0:T(8,128)}, u32[]{:S(2)}) copy-start(f32[10,8,128]{2,1,0:T(8,128)} %get-tuple-element.47.rows_low) | copy-start | bytes 122884
  13.1 31.5 %copy-start.12 = (f32[10,8,128]{2,1,0:T(8,128)S(1)}, f32[10,8,128]{2,1,0:T(8,128)}, u32[]{:S(2)}) copy-start(f32[10,8,128]{2,1,0:T(8,128)} %get-tuple-element.48.rows_high) | copy-start | bytes 122884
  13.1 35.5 %copy-start.8 = (f32[6,128,128]{2,1,0:T(8,128)S(1)}, f32[6,128,128]{2,1,0:T(8,128)}, u32[]{:S(2)}) copy-start(f32[6,128,128]{2,1,0:T(8,128)} %constant.2.clone.tables) | copy-start | bytes 1179652
  13.1 35.5 %copy-start.13 = (f32[3,8]{1,0:T(4,128)S(1)}, f32[3,8]{1,0:T(4,128)}, u32[]{:S(2)}) copy-start(f32[3,8]{1,0:T(4,128)} %material.5) | copy-start | bytes 292
  13.2 18.5 %all-to-all-start = ((f32[32,24,128]{2,1,0:T(8,128)}), f32[32,24,128]{2,1,0:T(8,128)S(1)}, u32[]{:S(2)}, u32[]{:S(2)}) async-start(f32[32,24,128]{2,1,0:T(8,128)} %get-tuple-element.49), calls=%async_computation | async-start | bytes 786432 | tf_op jit(solution)/shard_map/all_to_all | solution.py:1084
  19.6 24.9 %collective-permute-start = (f32[5,64,256]{2,1,0:T(8,128)S(1)}, f32[5,64,256]{2,1,0:T(8,128)S(1)}, u32[]{:S(2)}, u32[]{:S(2)}) collective-permute-start(f32[5,64,256]{2,1,0:T(8,128)S(1)} %copy-done.16), channel_id=1, source_target_pairs={{0,2},{2,0},{4,6},{6,4},{8,10},{10,8},{12,14},{14,12},{1,3},{3,1},... | collective-permute-start | bytes 983048 | tf_op jit(solution)/shard_map/ppermute | solution.py:603
  19.8 24.8 %collective-permute-start.1 = (f32[5,64,256]{2,1,0:T(8,128)S(1)}, f32[5,64,256]{2,1,0:T(8,128)S(1)}, u32[]{:S(2)}, u32[]{:S(2)}) collective-permute-start(f32[5,64,256]{2,1,0:T(8,128)S(1)} %copy-done.15), channel_id=1, source_target_pairs={{2,4},{6,8},{10,12},{4,2},{8,6},{12,10},{3,5},{7,9},{11,13},{5,3},... | collective-permute-start | bytes 983048 | tf_op jit(solution)/shard_map/ppermute | solution.py:604
  24.0 20.6 %collective-permute-start.2 = (f32[31,8,128]{2,1,0:T(8,128)}, f32[31,8,128]{2,1,0:T(8,128)S(1)}, u32[]{:S(2)}, u32[]{:S(2)}) collective-permute-start(f32[31,8,128]{2,1,0:T(8,128)} %get-tuple-element.45), channel_id=1, source_target_pairs={{0,2},{2,0},{4,6},{6,4},{8,10},{10,8},{12,14},{14,12},{1,3},{3,1},... | collective-permute-start | bytes 380936 | tf_op jit(solution)/shard_map/ppermute | solution.py:603
  24.0 20.5 %collective-permute-start.3 = (f32[31,8,128]{2,1,0:T(8,128)}, f32[31,8,128]{2,1,0:T(8,128)S(1)}, u32[]{:S(2)}, u32[]{:S(2)}) collective-permute-start(f32[31,8,128]{2,1,0:T(8,128)} %get-tuple-element.46), channel_id=1, source_target_pairs={{2,4},{6,8},{10,12},{4,2},{8,6},{12,10},{3,5},{7,9},{11,13},{5,3},... | collective-permute-start | bytes 380936 | tf_op jit(solution)/shard_map/ppermute | solution.py:604
  31.6 0.7 copy-start.14
  32.3 19.8 %copy-start.5 = (f32[3,5,5,4,8,128]{5,4,3,2,1,0:T(8,128)S(1)}, f32[3,5,5,4,8,128]{5,4,3,2,1,0:T(8,128)}, u32[]{:S(2)}) copy-start(f32[3,5,5,4,8,128]{5,4,3,2,1,0:T(8,128)} %get-tuple-element.54.f) | copy-start | bytes 3686404
  35.1 17.0 %copy-start.4 = (f32[3,5,5,4,8,128]{5,4,3,2,1,0:T(8,128)S(1)}, f32[3,5,5,4,8,128]{5,4,3,2,1,0:T(8,128)}, u32[]{:S(2)}) copy-start(f32[3,5,5,4,8,128]{5,4,3,2,1,0:T(8,128)} %get-tuple-element.53.b) | copy-start | bytes 3686404
  44.8 6.4 %collective-permute-start.4 = (f32[38,8,128]{2,1,0:T(8,128)S(1)}, f32[38,8,128]{2,1,0:T(8,128)S(1)}, u32[]{:S(2)}, u32[]{:S(2)}) collective-permute-start(f32[38,8,128]{2,1,0:T(8,128)S(1)} %get-tuple-element.51), channel_id=1, source_target_pairs={{0,1},{1,0},{16,17},{17,16},{2,3},{3,2},{18,19},{19,18},{4,5},{5,4... | collective-permute-start | bytes 466952 | tf_op jit(solution)/shard_map/ppermute | solution.py:603
  45.6 6.5 %collective-permute-start.5 = (f32[38,8,128]{2,1,0:T(8,128)S(1)}, f32[38,8,128]{2,1,0:T(8,128)S(1)}, u32[]{:S(2)}, u32[]{:S(2)}) collective-permute-start(f32[38,8,128]{2,1,0:T(8,128)S(1)} %get-tuple-element.52), channel_id=1, source_target_pairs={{1,16},{16,1},{3,18},{18,3},{5,20},{20,5},{7,22},{22,7},{9,24},{24... | collective-permute-start | bytes 466952 | tf_op jit(solution)/shard_map/ppermute | solution.py:604
  48.7 12.1 %copy-start.7 = (f32[4,32,256]{2,1,0:T(8,128)S(1)}, f32[4,32,256]{2,1,0:T(8,128)}, u32[]{:S(2)}) copy-start(f32[4,32,256]{2,1,0:T(8,128)} %energy.5) | copy-start | bytes 393220
  52.1 8.6 %copy-start.3 = (f32[3,4,32,256]{3,2,1,0:T(8,128)S(1)}, f32[3,4,32,256]{3,2,1,0:T(8,128)}, u32[]{:S(2)}) copy-start(f32[3,4,32,256]{3,2,1,0:T(8,128)} %momentum.5) | copy-start | bytes 1179652
  52.1 8.6 %copy-start.6 = (f32[4,32,256]{2,1,0:T(8,128)S(1)}, f32[4,32,256]{2,1,0:T(8,128)}, u32[]{:S(2)}) copy-start(f32[4,32,256]{2,1,0:T(8,128)} %density.5) | copy-start | bytes 393220
  52.2 17.3 %copy-start.1 = (f32[3,9,17,512]{3,0,2,1:T(4,128)S(1)}, f32[3,9,17,512]{3,0,2,1:T(4,128)}, u32[]{:S(2)}) copy-start(f32[3,9,17,512]{3,0,2,1:T(4,128)} %param.15) | copy-start | bytes 2820100
  52.2 17.3 %copy-start.2 = (f32[3,9,17,512]{3,0,2,1:T(4,128)S(1)}, f32[3,9,17,512]{3,0,2,1:T(4,128)}, u32[]{:S(2)}) copy-start(f32[3,9,17,512]{3,0,2,1:T(4,128)} %param.16) | copy-start | bytes 2820100
  56.2 13.3 %copy-start = (f32[3,9,17,512]{3,0,2,1:T(4,128)S(1)}, f32[3,9,17,512]{3,0,2,1:T(4,128)}, u32[]{:S(2)}) copy-start(f32[3,9,17,512]{3,0,2,1:T(4,128)} %param.14) | copy-start | bytes 2820100
  56.3 9.5 %collective-permute-start.6 = (f32[30,8,128]{2,1,0:T(8,128)S(1)}, f32[30,8,128]{2,1,0:T(8,128)S(1)}, u32[]{:S(2)}, u32[]{:S(2)}) collective-permute-start(f32[30,8,128]{2,1,0:T(8,128)S(1)} %get-tuple-element.63), channel_id=1, source_target_pairs={{0,2},{2,0},{4,6},{6,4},{8,10},{10,8},{12,14},{14,12},{1,3},{3,1},... | collective-permute-start | bytes 368648 | tf_op jit(solution)/shard_map/ppermute | solution.py:603
  56.3 9.4 %collective-permute-start.7 = (f32[30,8,128]{2,1,0:T(8,128)S(1)}, f32[30,8,128]{2,1,0:T(8,128)S(1)}, u32[]{:S(2)}, u32[]{:S(2)}) collective-permute-start(f32[30,8,128]{2,1,0:T(8,128)S(1)} %get-tuple-element.64), channel_id=1, source_target_pairs={{2,4},{6,8},{10,12},{4,2},{8,6},{12,10},{3,5},{7,9},{11,13},{5,3},... | collective-permute-start | bytes 368648 | tf_op jit(solution)/shard_map/ppermute | solution.py:604
  65.8 7.2 %collective-permute-start.8 = (f32[15,8,128]{2,1,0:T(8,128)S(1)}, f32[15,8,128]{2,1,0:T(8,128)S(1)}, u32[]{:S(2)}, u32[]{:S(2)}) collective-permute-start(f32[15,8,128]{2,1,0:T(8,128)S(1)} %get-tuple-element.70), channel_id=1, source_target_pairs={{0,1},{1,0},{16,17},{17,16},{2,3},{3,2},{18,19},{19,18},{4,5},{5,4... | collective-permute-start | bytes 184328 | tf_op jit(solution)/shard_map/ppermute | solution.py:603
  65.9 7.2 %collective-permute-start.9 = (f32[15,8,128]{2,1,0:T(8,128)S(1)}, f32[15,8,128]{2,1,0:T(8,128)S(1)}, u32[]{:S(2)}, u32[]{:S(2)}) collective-permute-start(f32[15,8,128]{2,1,0:T(8,128)S(1)} %get-tuple-element.71), channel_id=1, source_target_pairs={{1,16},{16,1},{3,18},{18,3},{5,20},{20,5},{7,22},{22,7},{9,24},{24... | collective-permute-start | bytes 184328 | tf_op jit(solution)/shard_map/ppermute | solution.py:604

commit v11 on v7

--- a/solution.py
+++ b/solution.py
@@ -1069,7 +1069,7 @@
         smem=(4,),
         away=(0, 1, 2),
         out_away=(0,),
-        mib=56,
+        mib=28,
         copies=13,
     )
     (total,) = call(

time: 67.7 us -> 73.5 us (1.086)
  local copies, waits for them, and re-layouts: 2.4 us -> 8.89 us
  waiting for transfers between devices: 3.84 us -> 1.05 us
  starting transfers between devices: 27 us -> 28.2 us
    unnamed x32 -> x40, local copies, waits for them, and re-layouts: 2.4 us -> 8.89 us
    ppermute x5, waiting for transfers between devices: 2.8 us -> 0.01 us  [exchange(): first = lax.ppermute(first, axis, [(i, i ^ 1) for i in range(count)])]
    ppermute x5, starting transfers between devices: 1.22 us -> 2.08 us  [exchange(): first = lax.ppermute(first, axis, [(i, i ^ 1) for i in range(count)])]
  transfers between devices with their start and end apart: 11 -> 11, of which waited for: 2 -> 1; matrix products, arithmetic and copies ran while one was open for 0% -> 0% of each run, Pallas kernels for 35% -> 31%
where the time goes in v11:
time: 73.5 us; the launch traced here: 72.7 us
  Pallas kernels  33.3 us (45%)
  starting transfers between devices  28.2 us (38%)
  local copies, waits for them, and re-layouts  8.89 us (12%)
  between operations  1.17 us (2%)
  waiting for transfers between devices  1.05 us (1%)
    pallas_call x10, Pallas kernels, call(): pl.pallas_call(kernel, out_shape=[jax.ShapeDtypeStruct(s, f32) for s in o...  33.3 us
    ppermute x5, starting transfers between devices, exchange(): lax.ppermute(second, axis, pairs + [(j, i) for i, j in pairs])  19.7 us
    unnamed x40, local copies, waits for them, and re-layouts  8.89 us
    all_to_all x1, starting transfers between devices, shards(): bottoms = lax.all_to_all(bottoms, rank, 0, 0, tiled=True)  6.45 us
    ppermute x5, starting transfers between devices, exchange(): first = lax.ppermute(first, axis, [(i, i ^ 1) for i in range(count)])  2.08 us
  transfers between devices with their start and end apart: 11, of which 1 were waited for; matrix products, arithmetic and copies ran while one was open for 0% of the time, Pallas kernels for 31%

profile of v11, /device:TPU:3, one launch (start us, length us, event | category | flops | bytes accessed | tf_op | source)
XLA Modules:
  0.0 72.7 jit_solution(3901007625400626775)
XLA Ops:
  0.7 2.8 %shard_map.138 = (f32[32,24,128]{2,1,0:T(8,128)}, f32[5,64,256]{2,1,0:T(8,128)}, f32[5,64,256]{2,1,0:T(8,128)}, f32[10,8,128]{2,1,0:T(8,128)}, f32[10,8,128]{2,1,0:T(8,128)}, /*index=5*/f32[8,128]{1,0:T(8,128)}) custom-call(f32[4,32,256]{2,1,0:T(8,128)} %density.3, f32[3,4,32,256]{3,2,1,0:T(8,128)} %momentum.3, f32[4,32,256]{2,1,0:T(8,128)} %energy.3, ...), custom_call_target="tpu_custom_call" | custom-call | tf_op jit(solution)/shard_map/pallas_call | solution.py:562
  3.5 6.4 %all-to-all-start = ((f32[32,24,128]{2,1,0:T(8,128)}), f32[32,24,128]{2,1,0:T(8,128)S(1)}, u32[]{:S(2)}, u32[]{:S(2)}) async-start(f32[32,24,128]{2,1,0:T(8,128)} %get-tuple-element.49), calls=%async_computation | async-start | bytes 786432 | tf_op jit(solution)/shard_map/all_to_all | solution.py:1060
  9.9 0.1 collective-permute-start
  10.1 4.2 %collective-permute-start.1 = (f32[5,64,256]{2,1,0:T(8,128)}, f32[5,64,256]{2,1,0:T(8,128)S(1)}, u32[]{:S(2)}, u32[]{:S(2)}) collective-permute-start(f32[5,64,256]{2,1,0:T(8,128)} %get-tuple-element.41), channel_id=1, source_target_pairs={{2,4},{6,8},{10,12},{4,2},{8,6},{12,10},{3,5},{7,9},{11,13},{5,3},... | collective-permute-start | bytes 983048 | tf_op jit(solution)/shard_map/ppermute | solution.py:588
  14.3 0.0 copy-start.1
  14.3 1.3 %copy-done.1 = f32[3,9,17,512]{3,0,2,1:T(4,128)S(1)} copy-done((f32[3,9,17,512]{3,0,2,1:T(4,128)S(1)}, f32[3,9,17,512]{3,0,2,1:T(4,128)}, u32[]{:S(2)}) %copy-start.1) | copy-done | bytes 940056
  15.6 1.3 %copy-done.3 = f32[3,9,17,512]{3,0,2,1:T(4,128)S(1)} copy-done((f32[3,9,17,512]{3,0,2,1:T(4,128)S(1)}, f32[3,9,17,512]{3,0,2,1:T(4,128)}, u32[]{:S(2)}) %copy-start.3) | copy-done | bytes 940056
  16.9 0.7 copy-done.18
  17.5 8.7 %shard_map.139 = (f32[3,5,5,4,8,128]{5,4,3,2,1,0:T(8,128)S(1)}, f32[3,5,5,4,8,128]{5,4,3,2,1,0:T(8,128)S(1)}, f32[31,8,128]{2,1,0:T(8,128)}, f32[31,8,128]{2,1,0...) custom-call(f32[9,17,3,512]{3,2,1,0:T(4,128)S(1)} %bitcast.8, ...), custom_call_target="tpu_custom_call" | custom-call | tf_op jit(solution)/shard_map/pallas_call | solution.py:562
  26.2 0.0 copy-start.6
  26.2 1.0 %copy-done.6 = f32[3,5,5,4,8,128]{5,4,3,2,1,0:T(8,128)} copy-done((f32[3,5,5,4,8,128]{5,4,3,2,1,0:T(8,128)}, f32[3,5,5,4,8,128]{5,4,3,2,1,0:T(8,128)S(1)}, u32[]{:S(2)}) %copy-start.6) | copy-done | bytes 1228824
  27.2 0.6 copy-done.11
  27.9 0.6 copy-done.13
  28.5 0.0 collective-permute-start.2
  28.5 4.3 %collective-permute-start.3 = (f32[31,8,128]{2,1,0:T(8,128)}, f32[31,8,128]{2,1,0:T(8,128)}, u32[]{:S(2)}, u32[]{:S(2)}) collective-permute-start(f32[31,8,128]{2,1,0:T(8,128)} %get-tuple-element.46), channel_id=1, source_target_pairs={{2,4},{6,8},{10,12},{4,2},{8,6},{12,10},{3,5},{7,9},{11,13},{5,3},... | collective-permute-start | bytes 380936 | tf_op jit(solution)/shard_map/ppermute | solution.py:588
  32.8 0.0 all-to-all-done.bottoms
  32.8 0.0 copy-start.10
  32.8 2.8 %shard_map.140.after.total = f32[360,128]{1,0:T(8,128)S(1)} custom-call(f32[768,128]{1,0:T(8,128)S(1)} %bitcast.14, f32[8,128]{1,0:T(8,128)S(1)} %get-tuple-element.50.after), custom_call_target="tpu_custom_call" | custom-call | tf_op jit(solution)/shard_map/pallas_call | solution.py:562
  35.6 0.0 copy-start.7
  35.6 0.0 collective-permute-done.2.came1.came_x1
  35.6 0.0 collective-permute-done.3.came2.came_x2
  35.6 0.0 collective-permute-done.crater1.came1
  35.6 0.0 collective-permute-done.1.crater2.came2
  35.7 0.9 %copy-done.12 = f32[16,8,128]{2,1,0:T(8,128)S(1)} copy-done((f32[16,8,128]{2,1,0:T(8,128)S(1)}, f32[16,8,128]{2,1,0:T(8,128)}, u32[]{:S(2)}) %copy-start.12) | copy-done | bytes 65560
  36.6 0.8 %copy-done.14 = f32[15,8,128]{2,1,0:T(8,128)S(1)} copy-done((f32[15,8,128]{2,1,0:T(8,128)S(1)}, f32[15,8,128]{2,1,0:T(8,128)}, u32[]{:S(2)}) %copy-start.14) | copy-done | bytes 61464
  37.4 0.8 %copy-done.15 = f32[10,8,128]{2,1,0:T(8,128)S(1)} copy-done((f32[10,8,128]{2,1,0:T(8,128)S(1)}, f32[10,8,128]{2,1,0:T(8,128)}, u32[]{:S(2)}) %copy-start.15) | copy-done | bytes 40984
  38.2 0.8 %copy-done.16 = f32[10,8,128]{2,1,0:T(8,128)S(1)} copy-done((f32[10,8,128]{2,1,0:T(8,128)S(1)}, f32[10,8,128]{2,1,0:T(8,128)}, u32[]{:S(2)}) %copy-start.16) | copy-done | bytes 40984
  39.0 1.1 %shard_map.141 = (f32[38,8,128]{2,1,0:T(8,128)S(1)}, f32[38,8,128]{2,1,0:T(8,128)S(1)}, f32[8,128]{1,0:T(8,128)S(1)}) custom-call(f32[16,8,128]{2,1,0:T(8,128)S(1)} %copy-done.12, f32[15,8,128]{2,1,0:T(8,128)S(1)} %copy-done.14, f32[31,8,128]{2,1,0:T(8,128)} %collective-permute-done.2.came1.came_x1, f32[31,8,128]{2,1,0:T(8,128)} %collective-permute-done.3.came2.came_x2, ...), custom_call_target="tpu_custom_call" | custom-call | tf_op jit(solution)/shard_map/pallas_call | solution.py:562
  40.1 1.8 %collective-permute-start.4 = (f32[38,8,128]{2,1,0:T(8,128)S(1)}, f32[38,8,128]{2,1,0:T(8,128)S(1)}, u32[]{:S(2)}, u32[]{:S(2)}) collective-permute-start(f32[38,8,128]{2,1,0:T(8,128)S(1)} %get-tuple-element.51), channel_id=1, source_target_pairs={{0,1},{1,0},{16,17},{17,16},{2,3},{3,2},{18,19},{19,18},{4,5},{5,4... | collective-permute-start | bytes 466952 | tf_op jit(solution)/shard_map/ppermute | solution.py:587
  41.9 3.0 %collective-permute-start.5 = (f32[38,8,128]{2,1,0:T(8,128)S(1)}, f32[38,8,128]{2,1,0:T(8,128)S(1)}, u32[]{:S(2)}, u32[]{:S(2)}) collective-permute-start(f32[38,8,128]{2,1,0:T(8,128)S(1)} %get-tuple-element.52), channel_id=1, source_target_pairs={{1,16},{16,1},{3,18},{18,3},{5,20},{20,5},{7,22},{22,7},{9,24},{24... | collective-permute-start | bytes 466952 | tf_op jit(solution)/shard_map/ppermute | solution.py:588
  44.9 2.5 %shard_map.142 = (f32[24,256]{1,0:T(8,128)S(1)}, f32[24,256]{1,0:T(8,128)S(1)}, f32[8,128]{1,0:T(8,128)S(1)}) custom-call(f32[360,128]{1,0:T(8,128)S(1)} %shard_map.140.after.total, f32[32,24,128]{2,1,0:T(8,128)S(1)} %all-to-all-done.bottoms, f32[3,8]{1,0:T(4,128)S(1)} %copy-done.17, f32[6,128,128]{2,1,0:T(8,128)S(1)} %copy-done.10, ...), custom_call_target="tpu_custom_call" | custom-call | tf_op jit(solution)/shard_map/pallas_call | solution.py:562
  47.4 0.0 collective-permute-done.4.came_y1.rows1
  47.4 1.0 %collective-permute-done.5.came_y2.rows2 = f32[38,8,128]{2,1,0:T(8,128)S(1)} collective-permute-done((f32[38,8,128]{2,1,0:T(8,128)S(1)}, f32[38,8,128]{2,1,0:T(8,128)S(1)}, u32[]{:S(2)}, u32[]{:S(2)}) %collective-permute-start.5) | collective-permute-done | bytes 155680 | tf_op jit(solution)/shard_map/ppermute | solution.py:588
  48.4 0.0 copy-start.9
  48.5 0.0 copy-start.4
  48.5 4.6 %shard_map.143 = (f32[3,5,5,4,8,128]{5,4,3,2,1,0:T(8,128)S(1)}, f32[3,5,5,4,8,128]{5,4,3,2,1,0:T(8,128)S(1)}, f32[30,8,128]{2,1,0:T(8,128)S(1)}, f32[30,8,128]{2...) custom-call(f32[3,5,5,4,8,128]{5,4,3,2,1,0:T(8,128)S(1)} %get-tuple-, ...), custom_call_target="tpu_custom_call" | custom-call | tf_op jit(solution)/shard_map/pallas_call | solution.py:562
  53.1 0.0 copy-start.2
  53.1 0.1 collective-permute-start.6
  53.2 4.7 %collective-permute-start.7 = (f32[30,8,128]{2,1,0:T(8,128)S(1)}, f32[30,8,128]{2,1,0:T(8,128)S(1)}, u32[]{:S(2)}, u32[]{:S(2)}) collective-permute-start(f32[30,8,128]{2,1,0:T(8,128)S(1)} %get-tuple-element.64), channel_id=1, source_target_pairs={{2,4},{6,8},{10,12},{4,2},{8,6},{12,10},{3,5},{7,9},{11,13},{5,3},... | collective-permute-start | bytes 368648 | tf_op jit(solution)/shard_map/ppermute | solution.py:588
  57.9 4.9 %shard_map.144 = (f32[5,4,32,256]{3,2,1,0:T(8,128)}, f32[8,128]{1,0:T(8,128)S(1)}) custom-call(f32[4,32,256]{2,1,0:T(8,128)S(1)} %copy-done.8, f32[3,4,32,256]{3,2,1,0:T(8,128)S(1)} %copy-done.5, f32[4,32,256]{2,1,0:T(8,128)S(1)} %copy-done.9, f32[5,64,256]{2,1,0:T(8,128)S(1)} %collective-permute-done.crater1.came1, ...), custom_call_target="tpu_custom_call" | custom-call | tf_op jit(solution)/shard_map/pallas_call | solution.py:562
  62.8 0.0 collective-permute-done.6.came1.x1
  62.8 0.0 collective-permute-done.7.came2.x2
  62.8 0.1 shard_map.145
  62.9 0.1 collective-permute-start.8
  63.0 3.5 %collective-permute-start.9 = (f32[15,8,128]{2,1,0:T(8,128)S(1)}, f32[15,8,128]{2,1,0:T(8,128)S(1)}, u32[]{:S(2)}, u32[]{:S(2)}) collective-permute-start(f32[15,8,128]{2,1,0:T(8,128)S(1)} %get-tuple-element.71), channel_id=1, source_target_pairs={{1,16},{16,1},{3,18},{18,3},{5,20},{20,5},{7,22},{22,7},{9,24},{24... | collective-permute-start | bytes 184328 | tf_op jit(solution)/shard_map/ppermute | solution.py:588
  66.5 3.5 %shard_map.146 = (f32[9,17,3,512]{3,2,1,0:T(4,128)}, f32[4,1224,128]{2,1,0:T(8,128)S(1)}) custom-call(f32[3,5,5,4,8,128]{5,4,3,2,1,0:T(8,128)S(1)} %get-tuple-element.59.a1, f32[24,256]{1,0:T(8,128)S(1)} %get-tuple-element.60.surf1, f32[9,17,3,512]{3,2,1,0:T(4,128)S(1)} %bitcast.9, f32[9,17,3,512]{3,2,1,0:T(4,128)S(1)} %bitcast.11, ...), custom_call_target="tpu_custom_call" | custom-call | tf_op jit(solution)/shard_map/pallas_call | solution.py:562
  70.1 0.0 collective-permute-done.9.y2
  70.1 2.4 %shard_map.147 = (f32[9,17,3,512]{3,2,1,0:T(4,128)}, f32[9,17,3,512]{3,2,1,0:T(4,128)}) custom-call(f32[4,1224,128]{2,1,0:T(8,128)S(1)} %get-tuple-element.68.v_part, f32[3,5,5,4,8,128]{5,4,3,2,1,0:T(8,128)S(1)} %get-tuple-element.69.f, f32[30,8,128]{2,1,0:T(8,128)S(1)} %collective-permute-done.6.came1.x1, ...), custom_call_target="tpu_custom_call" | custom-call | tf_op jit(solution)/shard_map/pallas_call | solution.py:562
  (24 shorter events, 0.0 us)
Async XLA Ops:
  0.6 13.6 %copy-start.17 = (f32[3,8]{1,0:T(4,128)S(1)}, f32[3,8]{1,0:T(4,128)}, u32[]{:S(2)}) copy-start(f32[3,8]{1,0:T(4,128)} %material.5) | copy-start | bytes 292
  0.6 13.6 %copy-start = (f32[3,9,17,512]{3,0,2,1:T(4,128)S(1)}, f32[3,9,17,512]{3,0,2,1:T(4,128)}, u32[]{:S(2)}) copy-start(f32[3,9,17,512]{3,0,2,1:T(4,128)} %param.14) | copy-start | bytes 2820100
  3.5 29.3 %all-to-all-start = ((f32[32,24,128]{2,1,0:T(8,128)}), f32[32,24,128]{2,1,0:T(8,128)S(1)}, u32[]{:S(2)}, u32[]{:S(2)}) async-start(f32[32,24,128]{2,1,0:T(8,128)} %get-tuple-element.49), calls=%async_computation | async-start | bytes 786432 | tf_op jit(solution)/shard_map/all_to_all | solution.py:1060
  9.9 25.7 %collective-permute-start = (f32[5,64,256]{2,1,0:T(8,128)}, f32[5,64,256]{2,1,0:T(8,128)S(1)}, u32[]{:S(2)}, u32[]{:S(2)}) collective-permute-start(f32[5,64,256]{2,1,0:T(8,128)} %get-tuple-element.40), channel_id=1, source_target_pairs={{0,2},{2,0},{4,6},{6,4},{8,10},{10,8},{12,14},{14,12},{1,3},{3,1},... | collective-permute-start | bytes 983048 | tf_op jit(solution)/shard_map/ppermute | solution.py:587
  10.1 25.6 %collective-permute-start.1 = (f32[5,64,256]{2,1,0:T(8,128)}, f32[5,64,256]{2,1,0:T(8,128)S(1)}, u32[]{:S(2)}, u32[]{:S(2)}) collective-permute-start(f32[5,64,256]{2,1,0:T(8,128)} %get-tuple-element.41), channel_id=1, source_target_pairs={{2,4},{6,8},{10,12},{4,2},{8,6},{12,10},{3,5},{7,9},{11,13},{5,3},... | collective-permute-start | bytes 983048 | tf_op jit(solution)/shard_map/ppermute | solution.py:588
  14.3 1.3 %copy-start.1 = (f32[3,9,17,512]{3,0,2,1:T(4,128)S(1)}, f32[3,9,17,512]{3,0,2,1:T(4,128)}, u32[]{:S(2)}) copy-start(f32[3,9,17,512]{3,0,2,1:T(4,128)} %param.15) | copy-start | bytes 2820100
  15.6 1.3 %copy-start.3 = (f32[3,9,17,512]{3,0,2,1:T(4,128)S(1)}, f32[3,9,17,512]{3,0,2,1:T(4,128)}, u32[]{:S(2)}) copy-start(f32[3,9,17,512]{3,0,2,1:T(4,128)} %param.16) | copy-start | bytes 2820100
  16.9 0.7 copy-start.18
  26.2 1.0 %copy-start.6 = (f32[3,5,5,4,8,128]{5,4,3,2,1,0:T(8,128)}, f32[3,5,5,4,8,128]{5,4,3,2,1,0:T(8,128)S(1)}, u32[]{:S(2)}) copy-start(f32[3,5,5,4,8,128]{5,4,3,2,1,0:T(8,128)S(1)} %get-tuple-element.54.f) | copy-start | bytes 3686404
  27.2 0.6 copy-start.11
  27.9 0.6 copy-start.13
  28.5 7.1 %collective-permute-start.2 = (f32[31,8,128]{2,1,0:T(8,128)}, f32[31,8,128]{2,1,0:T(8,128)}, u32[]{:S(2)}, u32[]{:S(2)}) collective-permute-start(f32[31,8,128]{2,1,0:T(8,128)} %get-tuple-element.45), channel_id=1, source_target_pairs={{0,2},{2,0},{4,6},{6,4},{8,10},{10,8},{12,14},{14,12},{1,3},{3,1},... | collective-permute-start | bytes 380936 | tf_op jit(solution)/shard_map/ppermute | solution.py:587
  28.5 7.1 %collective-permute-start.3 = (f32[31,8,128]{2,1,0:T(8,128)}, f32[31,8,128]{2,1,0:T(8,128)}, u32[]{:S(2)}, u32[]{:S(2)}) collective-permute-start(f32[31,8,128]{2,1,0:T(8,128)} %get-tuple-element.46), channel_id=1, source_target_pairs={{2,4},{6,8},{10,12},{4,2},{8,6},{12,10},{3,5},{7,9},{11,13},{5,3},... | collective-permute-start | bytes 380936 | tf_op jit(solution)/shard_map/ppermute | solution.py:588
  32.8 12.1 %copy-start.10 = (f32[6,128,128]{2,1,0:T(8,128)S(1)}, f32[6,128,128]{2,1,0:T(8,128)}, u32[]{:S(2)}) copy-start(f32[6,128,128]{2,1,0:T(8,128)} %constant.2.clone.tables) | copy-start | bytes 1179652
  32.8 15.6 %copy-start.19 = (f32[8,128]{1,0:T(8,128)S(1)}, f32[8,128]{1,0:T(8,128)}, u32[]{:S(2)}) copy-start(f32[8,128]{1,0:T(8,128)} %get-tuple-element.42.region) | copy-start | bytes 12292
  35.6 12.8 %copy-start.7 = (f32[3,5,5,4,8,128]{5,4,3,2,1,0:T(8,128)S(1)}, f32[3,5,5,4,8,128]{5,4,3,2,1,0:T(8,128)}, u32[]{:S(2)}) copy-start(f32[3,5,5,4,8,128]{5,4,3,2,1,0:T(8,128)} %copy-done.6) | copy-start | bytes 3686404
  35.6 0.9 %copy-start.12 = (f32[16,8,128]{2,1,0:T(8,128)S(1)}, f32[16,8,128]{2,1,0:T(8,128)}, u32[]{:S(2)}) copy-start(f32[16,8,128]{2,1,0:T(8,128)} %copy-done.11) | copy-start | bytes 196612
  36.6 0.8 %copy-start.14 = (f32[15,8,128]{2,1,0:T(8,128)S(1)}, f32[15,8,128]{2,1,0:T(8,128)}, u32[]{:S(2)}) copy-start(f32[15,8,128]{2,1,0:T(8,128)} %copy-done.13) | copy-start | bytes 184324
  37.4 0.8 %copy-start.15 = (f32[10,8,128]{2,1,0:T(8,128)S(1)}, f32[10,8,128]{2,1,0:T(8,128)}, u32[]{:S(2)}) copy-start(f32[10,8,128]{2,1,0:T(8,128)} %get-tuple-element.47.rows_low) | copy-start | bytes 122884
  38.2 0.8 %copy-start.16 = (f32[10,8,128]{2,1,0:T(8,128)S(1)}, f32[10,8,128]{2,1,0:T(8,128)}, u32[]{:S(2)}) copy-start(f32[10,8,128]{2,1,0:T(8,128)} %get-tuple-element.48.rows_high) | copy-start | bytes 122884
  40.1 7.3 %collective-permute-start.4 = (f32[38,8,128]{2,1,0:T(8,128)S(1)}, f32[38,8,128]{2,1,0:T(8,128)S(1)}, u32[]{:S(2)}, u32[]{:S(2)}) collective-permute-start(f32[38,8,128]{2,1,0:T(8,128)S(1)} %get-tuple-element.51), channel_id=1, source_target_pairs={{0,1},{1,0},{16,17},{17,16},{2,3},{3,2},{18,19},{19,18},{4,5},{5,4... | collective-permute-start | bytes 466952 | tf_op jit(solution)/shard_map/ppermute | solution.py:587
  41.9 6.5 %collective-permute-start.5 = (f32[38,8,128]{2,1,0:T(8,128)S(1)}, f32[38,8,128]{2,1,0:T(8,128)S(1)}, u32[]{:S(2)}, u32[]{:S(2)}) collective-permute-start(f32[38,8,128]{2,1,0:T(8,128)S(1)} %get-tuple-element.52), channel_id=1, source_target_pairs={{1,16},{16,1},{3,18},{18,3},{5,20},{20,5},{7,22},{22,7},{9,24},{24... | collective-permute-start | bytes 466952 | tf_op jit(solution)/shard_map/ppermute | solution.py:588
  48.4 9.4 %copy-start.5 = (f32[3,4,32,256]{3,2,1,0:T(8,128)S(1)}, f32[3,4,32,256]{3,2,1,0:T(8,128)}, u32[]{:S(2)}) copy-start(f32[3,4,32,256]{3,2,1,0:T(8,128)} %momentum.3) | copy-start | bytes 1179652
  48.4 9.4 %copy-start.8 = (f32[4,32,256]{2,1,0:T(8,128)S(1)}, f32[4,32,256]{2,1,0:T(8,128)}, u32[]{:S(2)}) copy-start(f32[4,32,256]{2,1,0:T(8,128)} %density.3) | copy-start | bytes 393220
  48.4 9.4 %copy-start.9 = (f32[4,32,256]{2,1,0:T(8,128)S(1)}, f32[4,32,256]{2,1,0:T(8,128)}, u32[]{:S(2)}) copy-start(f32[4,32,256]{2,1,0:T(8,128)} %energy.3) | copy-start | bytes 393220
  48.5 18.1 %copy-start.4 = (f32[3,9,17,512]{3,0,2,1:T(4,128)S(1)}, f32[3,9,17,512]{3,0,2,1:T(4,128)}, u32[]{:S(2)}) copy-start(f32[3,9,17,512]{3,0,2,1:T(4,128)} %param.16) | copy-start | bytes 2820100
  53.1 13.5 %copy-start.2 = (f32[3,9,17,512]{3,0,2,1:T(4,128)S(1)}, f32[3,9,17,512]{3,0,2,1:T(4,128)}, u32[]{:S(2)}) copy-start(f32[3,9,17,512]{3,0,2,1:T(4,128)} %param.15) | copy-start | bytes 2820100
  53.1 9.7 %collective-permute-start.6 = (f32[30,8,128]{2,1,0:T(8,128)S(1)}, f32[30,8,128]{2,1,0:T(8,128)S(1)}, u32[]{:S(2)}, u32[]{:S(2)}) collective-permute-start(f32[30,8,128]{2,1,0:T(8,128)S(1)} %get-tuple-element.63), channel_id=1, source_target_pairs={{0,2},{2,0},{4,6},{6,4},{8,10},{10,8},{12,14},{14,12},{1,3},{3,1},... | collective-permute-start | bytes 368648 | tf_op jit(solution)/shard_map/ppermute | solution.py:587
  53.2 9.7 %collective-permute-start.7 = (f32[30,8,128]{2,1,0:T(8,128)S(1)}, f32[30,8,128]{2,1,0:T(8,128)S(1)}, u32[]{:S(2)}, u32[]{:S(2)}) collective-permute-start(f32[30,8,128]{2,1,0:T(8,128)S(1)} %get-tuple-element.64), channel_id=1, source_target_pairs={{2,4},{6,8},{10,12},{4,2},{8,6},{12,10},{3,5},{7,9},{11,13},{5,3},... | collective-permute-start | bytes 368648 | tf_op jit(solution)/shard_map/ppermute | solution.py:588
  62.9 7.2 %collective-permute-start.8 = (f32[15,8,128]{2,1,0:T(8,128)S(1)}, f32[15,8,128]{2,1,0:T(8,128)S(1)}, u32[]{:S(2)}, u32[]{:S(2)}) collective-permute-start(f32[15,8,128]{2,1,0:T(8,128)S(1)} %get-tuple-element.70), channel_id=1, source_target_pairs={{0,1},{1,0},{16,17},{17,16},{2,3},{3,2},{18,19},{19,18},{4,5},{5,4... | collective-permute-start | bytes 184328 | tf_op jit(solution)/shard_map/ppermute | solution.py:587
  63.0 7.1 %collective-permute-start.9 = (f32[15,8,128]{2,1,0:T(8,128)S(1)}, f32[15,8,128]{2,1,0:T(8,128)S(1)}, u32[]{:S(2)}, u32[]{:S(2)}) collective-permute-start(f32[15,8,128]{2,1,0:T(8,128)S(1)} %get-tuple-element.71), channel_id=1, source_target_pairs={{1,16},{16,1},{3,18},{18,3},{5,20},{20,5},{7,22},{22,7},{9,24},{24... | collective-permute-start | bytes 184328 | tf_op jit(solution)/shard_map/ppermute | solution.py:588

commit v12 on v7

--- a/solution.py
+++ b/solution.py
@@ -320,30 +320,32 @@
             first[c * 5 + i], second[c * 5 + i] = sort_out(odd_y, *rows)
 
 
-def first_edge_kernel(low, high, came1, came2, rows_low, rows_high, crater1, crater2, after, first, second, token, ends, semaphores):
+def first_edge_kernel(y_rows, came1, came2, rows_low, rows_high, crater1, crater2, after, first, second, token, ends, semaphores):
     token[...] = after[0:8]
     copies = fetch(
         [(c.at[:, pl.ds(24 * h, 8), :], ends.at[n, :, pl.ds(8 * h, 8), :]) for n, c in enumerate((crater1, crater2)) for h in range(2)],
         semaphores,
     )
-    edge_rows(low, high, came1, came2, first, second)
+    edge_rows(y_rows.at[pl.ds(0, 15)], y_rows.at[pl.ds(16, 15)], came1, came2, first, second)
     odd, odd_y = parity_x(), parity_y()
     regions = sort_out(odd, came1[30], came2[30])
-    for n, value in enumerate((low[15], regions[0], regions[1])):
+    for n, value in enumerate((y_rows[15], regions[0], regions[1])):
         first[15 + n] = value
         second[15 + n] = value
     for copy in copies:
         copy.wait()
     for f in range(5):
         for t in range(2):
-            lanes = slice(128 * t, 128 * t + 128)
-            at = 18 + f * 4 + t * 2
+            at = 18 + f * 2 + t
             first[at], second[at] = sort_out(odd_y, rows_low[f * 2 + t], rows_high[f * 2 + t])
-            found = []
-            for row in (0, 15):
-                sides = sort_out(odd, ends[0, f, row : row + 1, lanes], ends[1, f, row : row + 1, lanes])
-                found.append(jnp.concatenate(list(sides) * 4, axis=0))
-            first[at + 1], second[at + 1] = sort_out(odd_y, *found)
+        found = []
+        for row in (0, 15):
+            sides = []
+            for t in range(2):
+                lanes = slice(128 * t, 128 * t + 128)
+                sides += sort_out(odd, ends[0, f, row : row + 1, lanes], ends[1, f, row : row + 1, lanes])
+            found.append(jnp.concatenate(sides * 2, axis=0))
+        first[28 + f], second[28 + f] = sort_out(odd_y, *found)
 
 
 def second_edge_kernel(low, high, came1, came2, after, first, second, token):
@@ -392,7 +394,7 @@
     return float(-1.0 / (half_size**3 * quad[i] * quad[j] * quad[k]))
 
 
-def first_kernel(u, v, a, region, material, b_out, f_out, x1, x2, y_low, y_high, token,
+def first_kernel(u, v, a, region, material, b_out, f_out, x1, x2, y_rows,
                  elem, gx, gz, cross, planes, side, u_in, v_in, a_in, wide_u, wide_b, kept_u, kept_b, b_held, semaphores):
     copies = [tile_copies(f, h, semaphores, 4 * n) for n, (f, h) in enumerate(((u, u_in), (v, v_in), (a, a_in)))]
     for t in range(4):
@@ -435,11 +437,10 @@
     save_b.start()
     internal(elem, f_out, lookup(material, 1, region_now), lookup(material, 2, region_now), gx, gz, cross, planes, side)
     pack_x(f_out, x1, x2)
-    pack_y(f_out, y_low, y_high)
+    pack_y(f_out, y_rows.at[pl.ds(0, 15)], y_rows.at[pl.ds(16, 15)])
     x1[30] = region_now
     x2[30] = region_now
-    y_low[15] = region_now
-    token[...] = region_now
+    y_rows[15] = region_now
     save_b.wait()
 
 
@@ -849,9 +850,9 @@
             wide[f, 2 + x, 32:40, :] = wide[f, 2 + x, 24:32, :]
         for t in range(2):
             lanes = slice(128 * t, 128 * t + 128)
-            at = 18 + f * 4 + t * 2
+            at = 18 + f * 2 + t
             below, above = sort_out(odd_y, rows1[at], rows2[at])
-            sides_below, sides_above = sort_out(odd_y, rows1[at + 1], rows2[at + 1])
+            sides_below, sides_above = sort_out(odd_y, rows1[28 + f], rows2[28 + f])
 
             def put(p, row, edge, value):
                 clamped = jnp.where(edge == 0, place == 0, place == last_y)
@@ -863,7 +864,7 @@
                 put(2 + x, 38, 0, below[4 + x : 5 + x])
                 put(2 + x, 32, 1, above[x : x + 1])
                 put(2 + x, 33, 1, above[4 + x : 5 + x])
-            for p, n in ((1, 0), (6, 1)):
+            for p, n in ((1, 2 * t), (6, 2 * t + 1)):
                 put(p, 39, 0, sides_below[n : n + 1])
                 put(p, 32, 1, sides_above[n : n + 1])
 
@@ -1059,10 +1060,10 @@
     )
     bottoms = lax.all_to_all(bottoms, rank, 0, 0, tiled=True)
     crater1, crater2 = exchange("gx", crater1, crater2)
-    b, f, x1, x2, y_low, y_high, token = call(
+    b, f, x1, x2, y_rows = call(
         first_kernel,
         (u, v, a, region, material),
-        [element_shape, element_shape, (31, 8, 128), (31, 8, 128), (16, 8, 128), (15, 8, 128), register],
+        [element_shape, element_shape, (31, 8, 128), (31, 8, 128), (31, 8, 128)],
         internal_scratch
         + [held_shape] * 3
         + [(3, 5, 5, 8, 256), (3, 5, 5, 8, 256), (600, 256), (600, 256), element_shape],
@@ -1074,17 +1075,17 @@
     )
     (total,) = call(
         functools.partial(deposit_kernel, float(nodes_y), count_x),
-        (bottoms.reshape(devices * 24, 128), token),
+        (bottoms.reshape(devices * 24, 128), y_rows),
         [(360, 128)],
         [(4, 4 * count_x, 128)],
     )
     x1, x2 = exchange("gx", x1, x2)
     y1, y2, token = call(
         first_edge_kernel,
-        (y_low, y_high, x1, x2, rows_low, rows_high, crater1, crater2, total),
-        [(38, 8, 128), (38, 8, 128), register],
+        (y_rows, x1, x2, rows_low, rows_high, crater1, crater2, total),
+        [(33, 8, 128), (33, 8, 128), register],
         [(2, 5, 16, 256)],
-        away=(6, 7),
+        away=(5, 6),
         copies=4,
     )
     surf1, surf2, token = call(

time: 67.7 us -> 66.6 us (0.984)
    unnamed x32 -> x30, local copies, waits for them, and re-layouts: 2.4 us -> 1.86 us
  transfers between devices with their start and end apart: 11 -> 11, of which waited for: 2 -> 2; matrix products, arithmetic and copies ran while one was open for 0% -> 0% of each run, Pallas kernels for 35% -> 36%
where the time goes in v12:
time: 66.6 us; the launch traced here: 66.1 us
  Pallas kernels  32.9 us (49%)
  starting transfers between devices  26.9 us (40%)
  waiting for transfers between devices  3.5 us (5%)
  local copies, waits for them, and re-layouts  1.86 us (3%)
  between operations  1.01 us (2%)
    pallas_call x10, Pallas kernels, call(): pl.pallas_call(kernel, out_shape=[jax.ShapeDtypeStruct(s, f32) for s in o...  32.9 us
    ppermute x5, starting transfers between devices, exchange(): lax.ppermute(second, axis, pairs + [(j, i) for i, j in pairs])  19.2 us
    all_to_all x1, starting transfers between devices, shards(): bottoms = lax.all_to_all(bottoms, rank, 0, 0, tiled=True)  6.45 us
    ppermute x5, waiting for transfers between devices, exchange(): first = lax.ppermute(first, axis, [(i, i ^ 1) for i in range(count)])  2.69 us
    unnamed x30, local copies, waits for them, and re-layouts  1.86 us
  transfers between devices with their start and end apart: 11, of which 2 were waited for; matrix products, arithmetic and copies ran while one was open for 0% of the time, Pallas kernels for 36%

profile of v12, /device:TPU:3, one launch (start us, length us, event | category | flops | bytes accessed | tf_op | source)
XLA Modules:
  0.0 66.1 jit_solution(13415599867025363144)
XLA Ops:
  0.6 2.7 %shard_map.138 = (f32[32,24,128]{2,1,0:T(8,128)}, f32[5,64,256]{2,1,0:T(8,128)}, f32[5,64,256]{2,1,0:T(8,128)}, f32[10,8,128]{2,1,0:T(8,128)}, f32[10,8,128]{2,1,0:T(8,128)}, /*index=5*/f32[8,128]{1,0:T(8,128)}) custom-call(f32[4,32,256]{2,1,0:T(8,128)} %density.3, f32[3,4,32,256]{3,2,1,0:T(8,128)} %momentum.3, f32[4,32,256]{2,1,0:T(8,128)} %energy.3, ...), custom_call_target="tpu_custom_call" | custom-call | tf_op jit(solution)/shard_map/pallas_call | solution.py:563
  3.3 6.4 %all-to-all-start = ((f32[32,24,128]{2,1,0:T(8,128)}), f32[32,24,128]{2,1,0:T(8,128)S(1)}, u32[]{:S(2)}, u32[]{:S(2)}) async-start(f32[32,24,128]{2,1,0:T(8,128)} %get-tuple-element.46), calls=%async_computation | async-start | bytes 786432 | tf_op jit(solution)/shard_map/all_to_all | solution.py:1061
  9.8 0.1 collective-permute-start
  9.9 4.2 %collective-permute-start.1 = (f32[5,64,256]{2,1,0:T(8,128)}, f32[5,64,256]{2,1,0:T(8,128)S(1)}, u32[]{:S(2)}, u32[]{:S(2)}) collective-permute-start(f32[5,64,256]{2,1,0:T(8,128)} %get-tuple-element.39), channel_id=1, source_target_pairs={{2,4},{6,8},{10,12},{4,2},{8,6},{12,10},{3,5},{7,9},{11,13},{5,3},... | collective-permute-start | bytes 983048 | tf_op jit(solution)/shard_map/ppermute | solution.py:589
  14.1 0.0 copy-start.11
  14.1 0.0 copy-start.12
  14.2 0.0 copy-start.10
  14.2 9.8 %shard_map.139 = (f32[3,5,5,4,8,128]{5,4,3,2,1,0:T(8,128)}, f32[3,5,5,4,8,128]{5,4,3,2,1,0:T(8,128)}, f32[31,8,128]{2,1,0:T(8,128)}, f32[31,8,128]{2,1,0:T(8,128)}, f32[31,8,128]{2,1,0:T(8,128)}) custom-call(f32[9,17,3,512]{3,2,1,0:T(4,128)} %bitcast.8, f32[9,17,3,512]{3,2,1,0:T(4,128)} %bitcast.10, f32[9,17,3,512]{3,2,1,0:T(4,128)} %bitcast.12, ...), custom_call_target="tpu_custom_call" | custom-call | tf_op jit(solution)/shard_map/pallas_call | solution.py:563
  24.0 0.0 copy-start.13
  24.0 0.1 collective-permute-start.2
  24.1 4.3 %collective-permute-start.3 = (f32[31,8,128]{2,1,0:T(8,128)}, f32[31,8,128]{2,1,0:T(8,128)S(1)}, u32[]{:S(2)}, u32[]{:S(2)}) collective-permute-start(f32[31,8,128]{2,1,0:T(8,128)} %get-tuple-element.43), channel_id=1, source_target_pairs={{2,4},{6,8},{10,12},{4,2},{8,6},{12,10},{3,5},{7,9},{11,13},{5,3},... | collective-permute-start | bytes 380936 | tf_op jit(solution)/shard_map/ppermute | solution.py:589
  28.4 0.0 all-to-all-done.bottoms
  28.4 0.0 copy-start.8
  28.4 0.9 %copy-done.8 = f32[31,8,128]{2,1,0:T(8,128)S(1)} copy-done((f32[31,8,128]{2,1,0:T(8,128)S(1)}, f32[31,8,128]{2,1,0:T(8,128)}, u32[]{:S(2)}) %copy-start.8) | copy-done | bytes 127000
  29.3 2.8 %shard_map.140.after.total = f32[360,128]{1,0:T(8,128)S(1)} custom-call(f32[768,128]{1,0:T(8,128)S(1)} %bitcast.14, f32[31,8,128]{2,1,0:T(8,128)S(1)} %copy-done.8), custom_call_target="tpu_custom_call" | custom-call | tf_op jit(solution)/shard_map/pallas_call | solution.py:563
  32.1 0.0 copy-start.4
  32.1 2.7 %collective-permute-done.2.came1.came_x1 = f32[31,8,128]{2,1,0:T(8,128)S(1)} collective-permute-done((f32[31,8,128]{2,1,0:T(8,128)}, f32[31,8,128]{2,1,0:T(8,128)S(1)}, u32[]{:S(2)}, u32[]{:S(2)}) %collective-permute-start.2) | collective-permute-done | bytes 127008 | tf_op jit(solution)/shard_map/ppermute | solution.py:588
  34.8 0.0 collective-permute-done.3.came2.came_x2
  34.8 0.0 collective-permute-done.crater1.came1
  34.8 0.0 collective-permute-done.1.crater2.came2
  34.8 0.0 copy-done.11
  34.8 0.9 %copy-done.9 = f32[31,8,128]{2,1,0:T(8,128)S(1)} copy-done((f32[31,8,128]{2,1,0:T(8,128)S(1)}, f32[31,8,128]{2,1,0:T(8,128)}, u32[]{:S(2)}) %copy-start.9) | copy-done | bytes 127000
  35.7 0.2 shard_map.141
  35.9 0.9 %collective-permute-start.4 = (f32[33,8,128]{2,1,0:T(8,128)S(1)}, f32[33,8,128]{2,1,0:T(8,128)S(1)}, u32[]{:S(2)}, u32[]{:S(2)}) collective-permute-start(f32[33,8,128]{2,1,0:T(8,128)S(1)} %get-tuple-element.47), channel_id=1, source_target_pairs={{0,1},{1,0},{16,17},{17,16},{2,3},{3,2},{18,19},{19,18},{4,5},{5,4... | collective-permute-start | bytes 405512 | tf_op jit(solution)/shard_map/ppermute | solution.py:588
  36.7 3.0 %collective-permute-start.5 = (f32[33,8,128]{2,1,0:T(8,128)S(1)}, f32[33,8,128]{2,1,0:T(8,128)S(1)}, u32[]{:S(2)}, u32[]{:S(2)}) collective-permute-start(f32[33,8,128]{2,1,0:T(8,128)S(1)} %get-tuple-element.48), channel_id=1, source_target_pairs={{1,16},{16,1},{3,18},{18,3},{5,20},{20,5},{7,22},{22,7},{9,24},{24... | collective-permute-start | bytes 405512 | tf_op jit(solution)/shard_map/ppermute | solution.py:589
  39.7 0.0 copy-start.6
  39.8 0.0 copy-start.7
  39.8 2.5 %shard_map.142 = (f32[24,256]{1,0:T(8,128)S(1)}, f32[24,256]{1,0:T(8,128)S(1)}, f32[8,128]{1,0:T(8,128)S(1)}) custom-call(f32[360,128]{1,0:T(8,128)S(1)} %shard_map.140.after.total, f32[32,24,128]{2,1,0:T(8,128)S(1)} %all-to-all-done.bottoms, f32[3,8]{1,0:T(4,128)S(1)} %copy-done.13, f32[6,128,128]{2,1,0:T(8,128)S(1)} %copy-done.10, ...), custom_call_target="tpu_custom_call" | custom-call | tf_op jit(solution)/shard_map/pallas_call | solution.py:563
  42.2 0.0 collective-permute-done.4.came_y1.rows1
  42.2 0.8 %collective-permute-done.5.came_y2.rows2 = f32[33,8,128]{2,1,0:T(8,128)S(1)} collective-permute-done((f32[33,8,128]{2,1,0:T(8,128)S(1)}, f32[33,8,128]{2,1,0:T(8,128)S(1)}, u32[]{:S(2)}, u32[]{:S(2)}) %collective-permute-start.5) | collective-permute-done | bytes 135200 | tf_op jit(solution)/shard_map/ppermute | solution.py:589
  43.0 0.0 copy-done.4
  43.1 0.0 copy-start.3
  43.1 0.0 copy-start.1
  43.1 0.0 copy-start.2
  43.1 4.1 %shard_map.143 = (f32[3,5,5,4,8,128]{5,4,3,2,1,0:T(8,128)S(1)}, f32[3,5,5,4,8,128]{5,4,3,2,1,0:T(8,128)S(1)}, f32[30,8,128]{2,1,0:T(8,128)S(1)}, f32[30,8,128]{2...) custom-call(f32[3,5,5,4,8,128]{5,4,3,2,1,0:T(8,128)S(1)} %copy-done., ...), custom_call_target="tpu_custom_call" | custom-call | tf_op jit(solution)/shard_map/pallas_call | solution.py:563
  47.2 0.0 copy-start
  47.2 0.1 collective-permute-start.6
  47.2 4.3 %collective-permute-start.7 = (f32[30,8,128]{2,1,0:T(8,128)S(1)}, f32[30,8,128]{2,1,0:T(8,128)S(1)}, u32[]{:S(2)}, u32[]{:S(2)}) collective-permute-start(f32[30,8,128]{2,1,0:T(8,128)S(1)} %get-tuple-element.60), channel_id=1, source_target_pairs={{2,4},{6,8},{10,12},{4,2},{8,6},{12,10},{3,5},{7,9},{11,13},{5,3},... | collective-permute-start | bytes 368648 | tf_op jit(solution)/shard_map/ppermute | solution.py:589
  51.6 4.9 %shard_map.144 = (f32[5,4,32,256]{3,2,1,0:T(8,128)}, f32[8,128]{1,0:T(8,128)S(1)}) custom-call(f32[4,32,256]{2,1,0:T(8,128)S(1)} %copy-done.6, f32[3,4,32,256]{3,2,1,0:T(8,128)S(1)} %copy-done.3, f32[4,32,256]{2,1,0:T(8,128)S(1)} %copy-done.7, f32[5,64,256]{2,1,0:T(8,128)S(1)} %collective-permute-done.crater1.came1, ...), custom_call_target="tpu_custom_call" | custom-call | tf_op jit(solution)/shard_map/pallas_call | solution.py:563
  56.6 0.0 collective-permute-done.6.came1.x1
  56.6 0.0 collective-permute-done.7.came2.x2
  56.6 0.1 shard_map.145
  56.6 0.1 collective-permute-start.8
  56.7 3.4 %collective-permute-start.9 = (f32[15,8,128]{2,1,0:T(8,128)S(1)}, f32[15,8,128]{2,1,0:T(8,128)S(1)}, u32[]{:S(2)}, u32[]{:S(2)}) collective-permute-start(f32[15,8,128]{2,1,0:T(8,128)S(1)} %get-tuple-element.67), channel_id=1, source_target_pairs={{1,16},{16,1},{3,18},{18,3},{5,20},{20,5},{7,22},{22,7},{9,24},{24... | collective-permute-start | bytes 184328 | tf_op jit(solution)/shard_map/ppermute | solution.py:589
  60.2 3.5 %shard_map.146 = (f32[9,17,3,512]{3,2,1,0:T(4,128)}, f32[4,1224,128]{2,1,0:T(8,128)S(1)}) custom-call(f32[3,5,5,4,8,128]{5,4,3,2,1,0:T(8,128)S(1)} %get-tuple-element.55.a1, f32[24,256]{1,0:T(8,128)S(1)} %get-tuple-element.56.surf1, f32[9,17,3,512]{3,2,1,0:T(4,128)S(1)} %bitcast.9, f32[9,17,3,512]{3,2,1,0:T(4,128)S(1)} %bitcast.11, ...), custom_call_target="tpu_custom_call" | custom-call | tf_op jit(solution)/shard_map/pallas_call | solution.py:563
  63.7 0.0 collective-permute-done.8.y1
  63.7 0.0 collective-permute-done.9.y2
  63.7 2.4 %shard_map.147 = (f32[9,17,3,512]{3,2,1,0:T(4,128)}, f32[9,17,3,512]{3,2,1,0:T(4,128)}) custom-call(f32[4,1224,128]{2,1,0:T(8,128)S(1)} %get-tuple-element.64.v_part, f32[3,5,5,4,8,128]{5,4,3,2,1,0:T(8,128)S(1)} %get-tuple-element.65.f, f32[30,8,128]{2,1,0:T(8,128)S(1)} %collective-permute-done.6.came1.x1, ...), custom_call_target="tpu_custom_call" | custom-call | tf_op jit(solution)/shard_map/pallas_call | solution.py:563
  (14 shorter events, 0.0 us)
Async XLA Ops:
  3.3 25.0 %all-to-all-start = ((f32[32,24,128]{2,1,0:T(8,128)}), f32[32,24,128]{2,1,0:T(8,128)S(1)}, u32[]{:S(2)}, u32[]{:S(2)}) async-start(f32[32,24,128]{2,1,0:T(8,128)} %get-tuple-element.46), calls=%async_computation | async-start | bytes 786432 | tf_op jit(solution)/shard_map/all_to_all | solution.py:1061
  9.8 25.0 %collective-permute-start = (f32[5,64,256]{2,1,0:T(8,128)}, f32[5,64,256]{2,1,0:T(8,128)S(1)}, u32[]{:S(2)}, u32[]{:S(2)}) collective-permute-start(f32[5,64,256]{2,1,0:T(8,128)} %get-tuple-element.38), channel_id=1, source_target_pairs={{0,2},{2,0},{4,6},{6,4},{8,10},{10,8},{12,14},{14,12},{1,3},{3,1},... | collective-permute-start | bytes 983048 | tf_op jit(solution)/shard_map/ppermute | solution.py:588
  9.9 24.8 %collective-permute-start.1 = (f32[5,64,256]{2,1,0:T(8,128)}, f32[5,64,256]{2,1,0:T(8,128)S(1)}, u32[]{:S(2)}, u32[]{:S(2)}) collective-permute-start(f32[5,64,256]{2,1,0:T(8,128)} %get-tuple-element.39), channel_id=1, source_target_pairs={{2,4},{6,8},{10,12},{4,2},{8,6},{12,10},{3,5},{7,9},{11,13},{5,3},... | collective-permute-start | bytes 983048 | tf_op jit(solution)/shard_map/ppermute | solution.py:589
  14.1 20.6 %copy-start.11 = (f32[10,8,128]{2,1,0:T(8,128)S(1)}, f32[10,8,128]{2,1,0:T(8,128)}, u32[]{:S(2)}) copy-start(f32[10,8,128]{2,1,0:T(8,128)} %get-tuple-element.44.rows_low) | copy-start | bytes 122884
  14.1 20.6 %copy-start.12 = (f32[10,8,128]{2,1,0:T(8,128)S(1)}, f32[10,8,128]{2,1,0:T(8,128)}, u32[]{:S(2)}) copy-start(f32[10,8,128]{2,1,0:T(8,128)} %get-tuple-element.45.rows_high) | copy-start | bytes 122884
  14.2 25.6 %copy-start.10 = (f32[6,128,128]{2,1,0:T(8,128)S(1)}, f32[6,128,128]{2,1,0:T(8,128)}, u32[]{:S(2)}) copy-start(f32[6,128,128]{2,1,0:T(8,128)} %constant.2.clone.tables) | copy-start | bytes 1179652
  24.0 15.7 %copy-start.13 = (f32[3,8]{1,0:T(4,128)S(1)}, f32[3,8]{1,0:T(4,128)}, u32[]{:S(2)}) copy-start(f32[3,8]{1,0:T(4,128)} %material.5) | copy-start | bytes 292
  24.0 10.7 %collective-permute-start.2 = (f32[31,8,128]{2,1,0:T(8,128)}, f32[31,8,128]{2,1,0:T(8,128)S(1)}, u32[]{:S(2)}, u32[]{:S(2)}) collective-permute-start(f32[31,8,128]{2,1,0:T(8,128)} %get-tuple-element.42), channel_id=1, source_target_pairs={{0,2},{2,0},{4,6},{6,4},{8,10},{10,8},{12,14},{14,12},{1,3},{3,1},... | collective-permute-start | bytes 380936 | tf_op jit(solution)/shard_map/ppermute | solution.py:588
  24.1 10.7 %collective-permute-start.3 = (f32[31,8,128]{2,1,0:T(8,128)}, f32[31,8,128]{2,1,0:T(8,128)S(1)}, u32[]{:S(2)}, u32[]{:S(2)}) collective-permute-start(f32[31,8,128]{2,1,0:T(8,128)} %get-tuple-element.43), channel_id=1, source_target_pairs={{2,4},{6,8},{10,12},{4,2},{8,6},{12,10},{3,5},{7,9},{11,13},{5,3},... | collective-permute-start | bytes 380936 | tf_op jit(solution)/shard_map/ppermute | solution.py:589
  28.4 0.9 %copy-start.8 = (f32[31,8,128]{2,1,0:T(8,128)S(1)}, f32[31,8,128]{2,1,0:T(8,128)}, u32[]{:S(2)}) copy-start(f32[31,8,128]{2,1,0:T(8,128)} %get-tuple-element.41.after.y_rows) | copy-start | bytes 380932
  29.3 13.8 %copy-start.5 = (f32[3,5,5,4,8,128]{5,4,3,2,1,0:T(8,128)S(1)}, f32[3,5,5,4,8,128]{5,4,3,2,1,0:T(8,128)}, u32[]{:S(2)}) copy-start(f32[3,5,5,4,8,128]{5,4,3,2,1,0:T(8,128)} %get-tuple-element.50.f) | copy-start | bytes 3686404
  32.1 11.0 %copy-start.4 = (f32[3,5,5,4,8,128]{5,4,3,2,1,0:T(8,128)S(1)}, f32[3,5,5,4,8,128]{5,4,3,2,1,0:T(8,128)}, u32[]{:S(2)}) copy-start(f32[3,5,5,4,8,128]{5,4,3,2,1,0:T(8,128)} %get-tuple-element.49.b) | copy-start | bytes 3686404
  34.8 0.9 %copy-start.9 = (f32[31,8,128]{2,1,0:T(8,128)S(1)}, f32[31,8,128]{2,1,0:T(8,128)}, u32[]{:S(2)}) copy-start(f32[31,8,128]{2,1,0:T(8,128)} %get-tuple-element.41.after.y_rows) | copy-start | bytes 380932
  35.7 7.4 %copy-start.14 = (f32[8,128]{1,0:T(8,128)S(1)}, f32[8,128]{1,0:T(8,128)}, u32[]{:S(2)}) copy-start(f32[8,128]{1,0:T(8,128)} %get-tuple-element.40.region) | copy-start | bytes 12292
  35.9 6.4 %collective-permute-start.4 = (f32[33,8,128]{2,1,0:T(8,128)S(1)}, f32[33,8,128]{2,1,0:T(8,128)S(1)}, u32[]{:S(2)}, u32[]{:S(2)}) collective-permute-start(f32[33,8,128]{2,1,0:T(8,128)S(1)} %get-tuple-element.47), channel_id=1, source_target_pairs={{0,1},{1,0},{16,17},{17,16},{2,3},{3,2},{18,19},{19,18},{4,5},{5,4... | collective-permute-start | bytes 405512 | tf_op jit(solution)/shard_map/ppermute | solution.py:588
  36.7 6.3 %collective-permute-start.5 = (f32[33,8,128]{2,1,0:T(8,128)S(1)}, f32[33,8,128]{2,1,0:T(8,128)S(1)}, u32[]{:S(2)}, u32[]{:S(2)}) collective-permute-start(f32[33,8,128]{2,1,0:T(8,128)S(1)} %get-tuple-element.48), channel_id=1, source_target_pairs={{1,16},{16,1},{3,18},{18,3},{5,20},{20,5},{7,22},{22,7},{9,24},{24... | collective-permute-start | bytes 405512 | tf_op jit(solution)/shard_map/ppermute | solution.py:589
  39.7 11.9 %copy-start.6 = (f32[4,32,256]{2,1,0:T(8,128)S(1)}, f32[4,32,256]{2,1,0:T(8,128)}, u32[]{:S(2)}) copy-start(f32[4,32,256]{2,1,0:T(8,128)} %density.3) | copy-start | bytes 393220
  39.8 11.9 %copy-start.7 = (f32[4,32,256]{2,1,0:T(8,128)S(1)}, f32[4,32,256]{2,1,0:T(8,128)}, u32[]{:S(2)}) copy-start(f32[4,32,256]{2,1,0:T(8,128)} %energy.3) | copy-start | bytes 393220
  43.1 8.6 %copy-start.3 = (f32[3,4,32,256]{3,2,1,0:T(8,128)S(1)}, f32[3,4,32,256]{3,2,1,0:T(8,128)}, u32[]{:S(2)}) copy-start(f32[3,4,32,256]{3,2,1,0:T(8,128)} %momentum.3) | copy-start | bytes 1179652
  43.1 17.1 %copy-start.1 = (f32[3,9,17,512]{3,0,2,1:T(4,128)S(1)}, f32[3,9,17,512]{3,0,2,1:T(4,128)}, u32[]{:S(2)}) copy-start(f32[3,9,17,512]{3,0,2,1:T(4,128)} %param.15) | copy-start | bytes 2820100
  43.1 17.1 %copy-start.2 = (f32[3,9,17,512]{3,0,2,1:T(4,128)S(1)}, f32[3,9,17,512]{3,0,2,1:T(4,128)}, u32[]{:S(2)}) copy-start(f32[3,9,17,512]{3,0,2,1:T(4,128)} %param.16) | copy-start | bytes 2820100
  47.2 13.0 %copy-start = (f32[3,9,17,512]{3,0,2,1:T(4,128)S(1)}, f32[3,9,17,512]{3,0,2,1:T(4,128)}, u32[]{:S(2)}) copy-start(f32[3,9,17,512]{3,0,2,1:T(4,128)} %param.14) | copy-start | bytes 2820100
  47.2 9.4 %collective-permute-start.6 = (f32[30,8,128]{2,1,0:T(8,128)S(1)}, f32[30,8,128]{2,1,0:T(8,128)S(1)}, u32[]{:S(2)}, u32[]{:S(2)}) collective-permute-start(f32[30,8,128]{2,1,0:T(8,128)S(1)} %get-tuple-element.59), channel_id=1, source_target_pairs={{0,2},{2,0},{4,6},{6,4},{8,10},{10,8},{12,14},{14,12},{1,3},{3,1},... | collective-permute-start | bytes 368648 | tf_op jit(solution)/shard_map/ppermute | solution.py:588
  47.2 9.3 %collective-permute-start.7 = (f32[30,8,128]{2,1,0:T(8,128)S(1)}, f32[30,8,128]{2,1,0:T(8,128)S(1)}, u32[]{:S(2)}, u32[]{:S(2)}) collective-permute-start(f32[30,8,128]{2,1,0:T(8,128)S(1)} %get-tuple-element.60), channel_id=1, source_target_pairs={{2,4},{6,8},{10,12},{4,2},{8,6},{12,10},{3,5},{7,9},{11,13},{5,3},... | collective-permute-start | bytes 368648 | tf_op jit(solution)/shard_map/ppermute | solution.py:589
  56.6 7.1 %collective-permute-start.8 = (f32[15,8,128]{2,1,0:T(8,128)S(1)}, f32[15,8,128]{2,1,0:T(8,128)S(1)}, u32[]{:S(2)}, u32[]{:S(2)}) collective-permute-start(f32[15,8,128]{2,1,0:T(8,128)S(1)} %get-tuple-element.66), channel_id=1, source_target_pairs={{0,1},{1,0},{16,17},{17,16},{2,3},{3,2},{18,19},{19,18},{4,5},{5,4... | collective-permute-start | bytes 184328 | tf_op jit(solution)/shard_map/ppermute | solution.py:588
  56.7 7.0 %collective-permute-start.9 = (f32[15,8,128]{2,1,0:T(8,128)S(1)}, f32[15,8,128]{2,1,0:T(8,128)S(1)}, u32[]{:S(2)}, u32[]{:S(2)}) collective-permute-start(f32[15,8,128]{2,1,0:T(8,128)S(1)} %get-tuple-element.67), channel_id=1, source_target_pairs={{1,16},{16,1},{3,18},{18,3},{5,20},{20,5},{7,22},{22,7},{9,24},{24... | collective-permute-start | bytes 184328 | tf_op jit(solution)/shard_map/ppermute | solution.py:589
